TPU v7x, 32 devices: a whole 2x2x4 slice. The times are simulated.
32 devices in a mesh: lat: 4 (over z), lon: 8 (over y, x, core).
Axes of the slice: x: 2, y: 2, z: 4, core: 2. Of those that a mesh axis runs over, the one named last changes fastest.
Arguments:
- ensemble: float32 [128, 1024, 128], P('lat', 'lon'), may hold values from -6 to 6
- observed: float32 [2, 4, 8, 8], P(None, 'lat', 'lon'), may hold values from -8 to 8
- precision: float32 [2, 4, 8, 8], P(None, 'lat', 'lon'), may hold values from 0.05 to 0.5
- interp_weight: float32 [2, 4, 8, 4, 8], P(None, 'lat', 'lon'), may hold values from 0.1 to 1
- stencil: int32 [2, 4, 8, 4, 8], P(None, 'lat', 'lon'), may hold values from 0 to 4419, as said below
- owned: int32 [2, 4, 8, 8], P(None, 'lat', 'lon'), may hold values from 0 to 1, as said below
- pattern: int32 [2, 4, 8, 5, 8], P(None, 'lat', 'lon'), may hold values 0 or 1
Outputs:
- analysis: float32 [128, 1024, 128], P('lat', 'lon')
Inputs may be any that keep to these rules, and one draw needn't show every extreme that they name: `stencil`: each index names one of the four corners of a 2 x 2 square of cells of the rim-extended tile, in the order (0,0), (0,1), (1,0), (1,1). In each batch and tile the owned slots come first and there is at least one; some tile owns all 8 slots in every batch.
All inputs are finite; a program needn't handle non-finite values. No bound on the sum of `pattern` on one device may be relied on, other than what follows from the above.
Results may differ from a plain program's by a relative error of at most 0.0026.
Values may be sent and summed in bfloat16 or wider, within the bound.
No kernel may reach another device: no remote copies, remote signals or barrier semaphores. Data moves between devices by JAX's collectives and lax.ppermute only.
A program may use at most 64 MiB of HBM per device.

v0:
```python
import functools
import jax
import jax.numpy as jnp
from jax import lax
from jax.experimental import pallas as pl
from jax.experimental.pallas import tpu as pltpu
from jax.sharding import PartitionSpec as P

REACH = 2
WIN = 2 * REACH + 1
SUB = 8
LANES = 128
NEAR = (-1, 0, 1)
AT_ROW, AT_COL, AT_OBS = (4, 5, 6)
AT_MARK = 64
F32 = jnp.float32
BF16 = jnp.bfloat16


def swap(block, axis, kind, count, wraps):
    route = []
    for place in range(count):
        partner = place + (1 if place % 2 == kind else -1)
        if wraps or 0 <= partner < count:
            route.append((place, partner % count))
    return lax.ppermute(block, axis, route)


def is_even(axis):
    return lax.rem(lax.axis_index(axis), 2) == 0


def start_kernel(
    width, observed, precision, weight, stencil, owned, cells, params_ref, sides_0, sides_1,
    observed_v, precision_v, weight_v, stencil_v, owned_v, left_v, right_v, sems
):
    batches, cols = (observed.shape[0], cells.shape[1])
    pairs = (
        (observed, observed_v),
        (precision, precision_v),
        (weight, weight_v),
        (stencil, stencil_v),
        (owned, owned_v),
        (cells.at[:, pl.ds(0, SUB)], left_v),
        (cells.at[:, pl.ds(cols - SUB, SUB)], right_v),
    )
    copies = [pltpu.make_async_copy(source, target, sems.at[n]) for n, (source, target) in enumerate(pairs)]
    for copy in copies:
        copy.start()
    for copy in copies:
        copy.wait()
    params_ref[...] = jnp.zeros_like(params_ref)
    for b in range(batches):
        root = jnp.sqrt(precision_v[b, 0]) * owned_v[b, 0].astype(F32)
        corner = stencil_v[b, 0, 0, pl.ds(0, 1)].astype(F32)
        row = jnp.floor((corner + 0.5) * (1.0 / width))
        params_ref[b, pl.ds(0, 4), pl.ds(0, SUB)] = weight_v[b, 0, 0] * root
        params_ref[b, pl.ds(AT_ROW, 1), pl.ds(0, SUB)] = row
        params_ref[b, pl.ds(AT_COL, 1), pl.ds(0, SUB)] = corner - row * width
        params_ref[b, pl.ds(AT_OBS, 1), pl.ds(0, SUB)] = observed_v[b, 0] * root
    even = is_even("lon")
    left, right = (left_v[:, 0, :], right_v[:, SUB - 1, :])
    rows = cells.shape[0]
    sides_0[pl.ds(0, rows), :] = jnp.where(even, right, left)
    sides_1[pl.ds(0, rows), :] = jnp.where(even, left, right)
    sides_0[pl.ds(rows, SUB), :] = params_ref[1]
    sides_1[pl.ds(rows, SUB), :] = params_ref[1]


def clear_rim(pad, rows, cols):
    edge = jnp.zeros((2, cols + 2 * SUB, LANES), F32)
    pad[pl.ds(0, 2)] = edge
    pad[pl.ds(rows + 2, 2)] = edge
    side = jnp.zeros((rows, SUB, LANES), F32)
    pad[pl.ds(2, rows), pl.ds(0, SUB)] = side
    pad[pl.ds(2, rows), pl.ds(SUB + cols, SUB)] = side


def share(pad, number, rows, cols, da, dc, o):
    row = number(AT_ROW, o).astype(jnp.int32) - 1 + da * rows
    col = number(AT_COL, o).astype(jnp.int32) - 1 + dc * cols
    row = jnp.clip(row, -2, rows) + 2
    col = jnp.clip(col, -2, cols) + SUB
    terms = [number(k, o) * pad[row + k // 2, pl.ds(col + k % 2, 1), :] for k in range(4)]
    return (terms[0] + terms[1]) + (terms[2] + terms[3])


def own_shift(number):
    sub = lax.broadcasted_iota(jnp.int32, (SUB, LANES), 0)
    shift = jnp.zeros((SUB, LANES), F32)
    for o in range(SUB):
        shift = jnp.where(sub == o, number(AT_OBS, o), shift)
    return shift


def pad_kernel(cells, pad, sem):
    rows, cols = (cells.shape[0], cells.shape[1])
    copy = pltpu.make_async_copy(cells, pad.at[pl.ds(2, rows), pl.ds(SUB, cols)], sem)
    copy.start()
    clear_rim(pad, rows, cols)
    copy.wait()


def hold_sides(sides_0, sides_1, sides):
    rows = sides_0.shape[0] - SUB
    even = is_even("lon")
    first, second = (sides_0[pl.ds(0, rows), :], sides_1[pl.ds(0, rows), :])
    sides[...] = jnp.zeros_like(sides)
    sides[0, pl.ds(SUB, rows), :] = jnp.where(even, second, first)
    sides[1, pl.ds(SUB, rows), :] = jnp.where(even, first, second)


def side_share(sides, side, number, rows, cols, da, o):
    row = number(AT_ROW, o).astype(jnp.int32) - 1 + da * rows
    row = jnp.clip(row, -2, rows) + SUB
    used = number(AT_COL, o).astype(jnp.int32) == (0, cols)[side]
    terms = [jnp.where(used, number(side + 2 * k, o), 0.0) * sides[side, pl.ds(row + k, 1), :] for k in range(2)]
    return terms[0] + terms[1]


def send_block(value, marks, scratch, out_ref):
    mean = jnp.mean(value, axis=-1, keepdims=True)
    scratch[...] = jnp.zeros_like(scratch)
    scratch[pl.ds(0, marks.shape[0]), pl.ds(0, marks.shape[1])] = marks.astype(F32)
    lane = lax.broadcasted_iota(jnp.int32, (SUB, LANES), 1)
    innov = jnp.where(lane < AT_MARK, -mean, pltpu.roll(scratch[...], AT_MARK, 1))
    block = jnp.concatenate([value - mean, innov], axis=0).astype(BF16)
    out_ref[...] = jnp.broadcast_to(block, out_ref.shape)


def rows_kernel(mine, sides_0, sides_1, pad, out_0, out_1):
    rows, cols = (pad.shape[0] - 4, pad.shape[1] - 2 * SUB)
    lon_even, lat_even = (is_even("lon"), is_even("lat"))
    edges = []
    for row in (0, rows - 1):
        first, second = (sides_0[pl.ds(row, 1), :], sides_1[pl.ds(row, 1), :])
        left, right = (jnp.where(lon_even, second, first), jnp.where(lon_even, first, second))
        cells = pad[2 + row, pl.ds(SUB, cols), :]
        beside = [jnp.broadcast_to(cell, (SUB, LANES)) for cell in (left, right)]
        edges.append(jnp.concatenate([beside[0], cells, beside[1]], axis=0))
    first, second = (sides_0[pl.ds(rows, SUB), :], sides_1[pl.ds(rows, SUB), :])
    left, right = (jnp.where(lon_even, second, first), jnp.where(lon_even, first, second))
    lane = lax.broadcasted_iota(jnp.int32, (SUB, LANES), 1)
    packed = jnp.where(lane < SUB, left, pltpu.roll(mine[1], SUB, 1))
    packed = jnp.where(lane < 2 * SUB, packed, pltpu.roll(right, 2 * SUB, 1))
    for kind, out in enumerate((out_0, out_1)):
        out[pl.ds(0, cols + 2 * SUB), :] = jnp.where(lat_even, edges[1 - kind], edges[kind])
        out[pl.ds(cols + 2 * SUB, SUB), :] = packed


def prior_kernel(mine, sides_0, sides_1, ends_0, ends_1, pad, pattern, out_ref, ends, sides, value, params, sem):
    rows, cols = (pad.shape[0] - 4, pad.shape[1] - 2 * SUB)
    copy = pltpu.make_async_copy(mine.at[0], params, sem)
    copy.start()
    even = is_even("lat")
    first, second = (ends_0[pl.ds(0, cols + 2 * SUB), :], ends_1[pl.ds(0, cols + 2 * SUB), :])
    ends[0] = jnp.where(even, second, first)
    ends[1] = jnp.where(even, first, second)
    hold_sides(sides_0, sides_1, sides)
    copy.wait()
    number = lambda kind, o: params[kind, o]
    for o in range(SUB):
        total = share(pad, number, rows, cols, 0, 0, o)
        row = number(AT_ROW, o).astype(jnp.int32)
        col = number(AT_COL, o).astype(jnp.int32)
        for n, at in enumerate((0, rows)):
            for k in range(2):
                weight = jnp.where(row == at, number(2 * n + k, o), 0.0)
                total = total + weight * ends[n, pl.ds(col + SUB - 1 + k, 1), :]
        for side in range(2):
            total = total + side_share(sides, side, number, rows, cols, 0, o)
        value[pl.ds(o, 1), :] = total
    send_block(value[...] - own_shift(number), pattern[0, 0, 0], value, out_ref)


def meet_kernel(shares, pattern, out_ref, scratch):
    send_block(jnp.sum(shares[...], axis=0), pattern[1, 0, 0], scratch, out_ref)


def later_kernel(mine, sides_0, sides_1, ends_0, ends_1, pad, out_ref, params, sems):
    rows, cols = (pad.shape[0] - 4, pad.shape[1] - 2 * SUB)
    lon_even, lat_even = (is_even("lon"), is_even("lat"))
    side, end = (pl.ds(rows, SUB), pl.ds(cols + 2 * SUB, SUB))
    sources = (sides_0.at[side], mine.at[1], sides_1.at[side], ends_0.at[end], ends_1.at[end])
    copies = []
    for n, source in enumerate(sources):
        copies.append(pltpu.make_async_copy(source, params.at[n], sems.at[n]))
        copies[-1].start()
    for copy in copies:
        copy.wait()
    beside = (jnp.where(lon_even, 2, 0), 1, jnp.where(lon_even, 0, 2))
    above = (jnp.where(lat_even, 4, 3), None, jnp.where(lat_even, 3, 4))
    for n, dc in enumerate(NEAR):
        for m, da in enumerate(NEAR):
            if da == 0:
                number = lambda kind, o: params[beside[n], kind, o]
            else:
                number = lambda kind, o: params[above[m], kind, n * SUB + o]
            for o in range(SUB):
                out_ref[n * len(NEAR) + m, pl.ds(o, 1), :] = share(pad, number, rows, cols, da, dc, o)
    out_ref[len(NEAR) ** 2] = own_shift(lambda kind, o: params[1, kind, o])


def window_start(lat_count, my_lat):
    return 0 if lat_count <= WIN else jnp.clip(my_lat - REACH, 0, lat_count - WIN)


def row_of(block, j):
    return jnp.broadcast_to(block[j:j + 1, :], block.shape)


def column_of(block, j):
    return jnp.broadcast_to(block[:, j:j + 1], block.shape)


def reciprocal(value):
    guess = pl.reciprocal(value, approx=True)
    return guess * (2.0 - value * guess)


def pivot_rows(block, k, between):
    sub = lax.broadcasted_iota(jnp.int32, block.shape, 0)
    lane = lax.broadcasted_iota(jnp.int32, block.shape, 1) - k * SUB
    rows = [row_of(block, r) for r in range(SUB)]
    at = {(r, n): column_of(rows[r], k * SUB + n) for r in range(SUB) for n in range(r + 1)}
    here = (lane >= 0) & (lane < SUB)
    rows = [jnp.where(here, jnp.where(lane == r, 1.0, 0.0), row) for r, row in enumerate(rows)]
    inverse = jnp.zeros(block.shape, F32)
    for j in range(0, SUB, 2):
        a, b, c = (at[j, j], at[j + 1, j], at[j + 1, j + 1])
        det = a * c - b * b
        over_det = reciprocal(det)
        top, bottom = (rows[j], rows[j + 1])
        rest = range(j + 2, SUB)
        upper = {n: (at[n, j], at[n, j + 1]) for n in rest}
        for r in rest:
            first = (at[r, j] * c - at[r, j + 1] * b) * over_det
            second = (at[r, j + 1] * a - at[r, j] * b) * over_det
            for n in range(j + 2, r + 1):
                at[r, n] = at[r, n] - (first * upper[n][0] + second * upper[n][1])
            rows[r] = rows[r] - (first * top + second * bottom)
        a_part, b_part, c_part = (a * over_det, b * over_det, c * over_det)
        for r in range(j):
            first = at[r, j] * c_part - at[r, j + 1] * b_part
            second = at[r, j + 1] * a_part - at[r, j] * b_part
            for n in rest:
                at[r, n] = at[r, n] - (first * upper[n][0] + second * upper[n][1])
            rows[r] = rows[r] - (first * top + second * bottom)
        for n in rest:
            at[j, n] = c_part * upper[n][0] - b_part * upper[n][1]
            at[j + 1, n] = a_part * upper[n][1] - b_part * upper[n][0]
        rows[j] = c_part * top - b_part * bottom
        rows[j + 1] = a_part * bottom - b_part * top
        over_a = reciprocal(a)
        inverse = jnp.where(sub == j, lax.rsqrt(a) * top, inverse)
        inverse = jnp.where(sub == j + 1, lax.rsqrt(det * over_a) * (bottom - b * over_a * top), inverse)
        between()
    return rows, jnp.where(lane < SUB, inverse, 0.0)


def eliminate(blocks):
    count = len(blocks) - 1
    blocks = list(blocks)
    lane = lax.broadcasted_iota(jnp.int32, blocks[0].shape, 1)
    inverse, waiting = ([], [])

    def update(i, k, pivot):
        terms = [column_of(blocks[i], k * SUB + j) * pivot[j] for j in range(SUB)]
        while len(terms) > 1:
            terms = [terms[n] + terms[n + 1] for n in range(0, len(terms), 2)]
        here = (lane >= k * SUB) & (lane < (k + 1) * SUB)
        blocks[i] = jnp.where(here, 0.0, blocks[i]) - terms[0]

    for k in range(count):
        share_of = -(-len(waiting) // 4)

        def between():
            for task in waiting[:share_of]:
                update(*task)
            del waiting[:share_of]

        pivot, rows = pivot_rows(blocks[k], k, between)
        update(k + 1, k, pivot)
        waiting = [(i, k, pivot) for i in range(k + 2, count + 1)]
        inverse.append(rows)
    return inverse, blocks[count][:1]


def batch_map(lat_count, near_ref, marks):
    held = min(WIN, lat_count)
    lon_count = near_ref.shape[0] // held
    my_lat, my_lon = (lax.axis_index("lat"), lax.axis_index("lon"))
    start = window_start(lat_count, my_lat)
    near = near_ref[...].astype(F32)
    rounded = near[:, :SUB].reshape(-1, LANES)
    innov = near[:, SUB:].reshape(-1, LANES)[:, :1]
    scaled = rounded.astype(BF16)
    marks[...] = near_ref[(my_lat - start) * lon_count + my_lon, pl.ds(SUB, SUB), :].astype(F32)
    picked = []
    for j in range(held):
        offset = start + j - my_lat + REACH
        inside = (offset >= 0) & (offset < WIN)
        row = jnp.where(inside, marks[pl.ds(jnp.clip(offset, 0, WIN - 1), 1), :], 0.0)
        for e in range(lon_count):
            picked.append(jnp.broadcast_to(row[:, AT_MARK + e:AT_MARK + e + 1], (SUB, LANES)))
    weighted = rounded * jnp.concatenate(picked, axis=0)
    gram = lax.dot_general(
        weighted.astype(BF16), scaled, (((0,), (0,)), ((), ())), preferred_element_type=F32
    )
    sub = lax.broadcasted_iota(jnp.int32, (SUB, LANES), 0)
    lane = lax.broadcasted_iota(jnp.int32, (SUB, LANES), 1)
    members = LANES
    blocks = []
    for k in range(members // SUB):
        block = gram[k * SUB:(k + 1) * SUB, :]
        blocks.append(block + jnp.where(lane - k * SUB == sub, members - 1.0, 0.0))
    proj = jnp.sum((weighted * innov).reshape(-1, SUB, LANES), axis=0)
    blocks.append(jnp.broadcast_to(jnp.sum(proj, axis=0, keepdims=True), (SUB, LANES)))
    inverse, weights = eliminate(blocks)
    flipped = jnp.concatenate(inverse, axis=0) * (members - 1.0) ** 0.5 - weights
    return flipped - jnp.mean(flipped, axis=-1, keepdims=True) + 1.0 / members


def exact_dot(a, b, contract_b):
    return lax.dot_general(
        a, b, (((1,), (contract_b,)), ((), ())), precision=lax.Precision.HIGHEST, preferred_element_type=F32
    )


def first_kernel(lat_count, lon_count, near_ref, later, map_ref, out_ref, marks, moved):
    flipped = batch_map(lat_count, near_ref, marks)
    map_ref[...] = flipped
    count = len(NEAR) ** 2
    moved[...] = exact_dot(later[pl.ds(0, count)].reshape(-1, LANES), flipped, 1).reshape(moved.shape)
    moved[count // 2] = moved[count // 2] - later[count]
    out_ref[...] = jnp.zeros_like(out_ref)
    my_lat, my_lon = (lax.axis_index("lat"), lax.axis_index("lon"))
    for n, dc in enumerate(NEAR):
        lon = lax.rem(my_lon + dc + lon_count, lon_count)
        for m, da in enumerate(NEAR):
            lat = my_lat + da

            @pl.when((lat >= 0) & (lat < lat_count))
            def _():
                out_ref[lat * lon_count + lon] = moved[n * len(NEAR) + m]


def last_kernel(lat_count, near_ref, map_ref, pad, out_ref, result, marks, out_sem):
    parts = out_sem.shape[0]
    rows, cols = (pad.shape[0] - 4, pad.shape[1] - 2 * SUB)
    flipped = exact_dot(batch_map(lat_count, near_ref, marks), map_ref[...], 0)
    high = flipped.astype(BF16)
    low = (flipped - high.astype(F32)).astype(BF16)
    right = jnp.concatenate(
        [jnp.concatenate([high, high], axis=1), jnp.concatenate([low, jnp.zeros_like(low)], axis=1)], axis=0
    )
    copies = []
    size = rows // parts
    for n in range(parts):
        part = pl.ds(n * size * cols, size * cols)
        value = pad[pl.ds(2 + n * size, size), pl.ds(SUB, cols), :].reshape(size * cols, LANES)
        upper = value.astype(BF16)
        rest = (value - upper.astype(F32)).astype(BF16)
        both = lax.dot_general(
            jnp.concatenate([upper, rest], axis=1), right, (((1,), (1,)), ((), ())), preferred_element_type=F32
        )
        result[part, :] = both[:, :LANES] + both[:, LANES:]
        copies.append(pltpu.make_async_copy(result.at[part], out_ref.at[part], out_sem.at[n]))
        copies[-1].start()
    for out_copy in copies:
        out_copy.wait()


def window(tiles, lat_count, lon_count):
    held = min(WIN, lat_count)
    if held == lat_count:
        return tiles
    start = jnp.clip(lax.axis_index("lat") - REACH, 0, lat_count - held)
    return lax.dynamic_slice_in_dim(tiles, start * lon_count, held * lon_count, axis=0)


def local(ensemble, observed, precision, interp_weight, stencil, owned, pattern):
    rows, cols, members = ensemble.shape
    batches = observed.shape[0]
    lat_count, lon_count = (lax.axis_size("lat"), lax.axis_size("lon"))
    tiles = lat_count * lon_count
    vmem = pl.BlockSpec(memory_space=pltpu.VMEM)
    anywhere = pl.BlockSpec(memory_space=pl.ANY)
    hbm = pl.BlockSpec(memory_space=pltpu.HBM)
    megabyte = 1024 * 1024

    def shape(*dims, dtype=F32):
        return jax.ShapeDtypeStruct(dims, dtype)

    def call(kernel, name, specs, out_shape, scratch, *operands, out_specs=None, limit=48):
        return pl.pallas_call(
            kernel,
            out_shape=out_shape,
            in_specs=specs,
            out_specs=out_specs or jax.tree.map(lambda _: vmem, out_shape),
            scratch_shapes=scratch,
            compiler_params=pltpu.CompilerParams(vmem_limit_bytes=limit * megabyte),
            name=name,
        )(*operands)

    def trade(blocks, axis):
        count, wraps = ((lon_count, True) if axis == "lon" else (lat_count, False))
        second = swap(blocks[1], axis, 1, count, wraps)
        first = swap(blocks[0], axis, 0, count, wraps)
        return (first, second)

    def exchange(blocks):
        return lax.all_to_all(blocks, ("lat", "lon"), split_axis=0, concat_axis=0, tiled=True)

    small = (observed, precision, interp_weight, stencil, owned)
    side = shape(rows + SUB, members)
    mine, *sides = call(
        functools.partial(start_kernel, cols + 2),
        "start",
        [hbm] * 6,
        (shape(batches, SUB, LANES), side, side),
        [pltpu.VMEM(array.shape, array.dtype) for array in small]
        + [pltpu.VMEM((rows, SUB, members), F32)] * 2
        + [pltpu.SemaphoreType.DMA((7,))],
        *small,
        ensemble,
        limit=63,
    )
    sides = trade(sides, "lon")
    padded = shape(rows + 4, cols + 2 * SUB, members)
    pad = call(pad_kernel, "pad", [hbm], padded, [pltpu.SemaphoreType.DMA], ensemble)
    end = shape(cols + 3 * SUB, members)
    ends = call(rows_kernel, "edge_rows", [vmem] * 4, (end, end), [], mine, *sides, pad)
    ends = trade(ends, "lat")
    around = (mine, *sides, *ends, pad)
    slots = shape(tiles, 2 * SUB, members, dtype=BF16)
    held_sides = pltpu.VMEM((2, rows + 2 * SUB, members), F32)
    blocks = call(
        prior_kernel,
        "prior",
        [vmem] * 7,
        slots,
        [
            pltpu.VMEM((2, cols + 2 * SUB, members), F32),
            held_sides,
            pltpu.VMEM((SUB, members), F32),
            pltpu.SMEM((SUB, LANES), F32),
            pltpu.SemaphoreType.DMA,
        ],
        *around,
        pattern,
    )
    near = window(exchange(blocks), lat_count, lon_count)
    count = len(NEAR) ** 2
    later = call(
        later_kernel,
        "later_shares",
        [vmem] * 6,
        shape(count + 1, SUB, members),
        [pltpu.SMEM((5, SUB, LANES), F32), pltpu.SemaphoreType.DMA((5,))],
        *around,
    )
    block = pltpu.VMEM((SUB, members), F32)
    first_map, shares = call(
        functools.partial(first_kernel, lat_count, lon_count),
        "first_batch",
        [vmem] * 2,
        (shape(members, members), shape(tiles, SUB, members)),
        [block, pltpu.VMEM((count, SUB, members), F32)],
        near,
        later,
    )
    blocks = call(meet_kernel, "own_block", [vmem] * 2, slots, [block], exchange(shares), pattern)
    near = window(exchange(blocks), lat_count, lon_count)
    parts = 8
    result = call(
        functools.partial(last_kernel, lat_count),
        "second_batch",
        [vmem] * 3,
        shape(rows * cols, members),
        [
            pltpu.VMEM((rows * cols, members), F32),
            block,
            pltpu.SemaphoreType.DMA((parts,)),
        ],
        near,
        first_map,
        pad,
        out_specs=anywhere,
    )
    return result.reshape(rows, cols, members)


def solution(mesh):
    placed = (
        P("lat", "lon", None),
        P(None, "lat", "lon", None),
        P(None, "lat", "lon", None),
        P(None, "lat", "lon", None, None),
        P(None, "lat", "lon", None, None),
        P(None, "lat", "lon", None),
        P(None, "lat", "lon", None, None),
    )
    return jax.shard_map(
        local, mesh=mesh, in_specs=placed, out_specs=P("lat", "lon", None), check_vma=False
    )
```

profile of v0, /device:TPU:0, one launch (start us, length us, event | category | flops | bytes accessed | tf_op | source)
XLA Modules:
  0.0 62.6 jit_solution(13917129777141796659)
XLA Ops:
  0.0 1.8 %start.1 = (f32[2,8,128]{2,1,0:T(8,128)}, f32[40,128]{1,0:T(8,128)}, f32[40,128]{1,0:T(8,128)}) custom-call(f32[2,1,1,8]{3,2,1,0:T(1,128)} %observed.1, f32[2,1,1,8]{3,2,1,0:T(1,128)} %precision.1, f32[2,1,1,4,8]{4,3,2,1,0:T(4,128)} %weight.1, s32[2,1,1,4,8]{4,3,2,1,0:T(4,128)} %stencil.1, s32[2,1,1,8]{3,2,1,0:T(1,128)} %owned.1, f32[32,128,128]{2,1,0:T(8,128)} %cells.3), custom_call_target="tpu_custom_call" | custom-call | tf_op jit(solution)/shard_map/start/pallas_call | solution.py:396
  1.8 0.5 collective-permute-start
  2.3 3.6 %collective-permute-start.1 = (f32[40,128]{1,0:T(8,128)}, f32[40,128]{1,0:T(8,128)S(1)}, u32[]{:S(2)}, u32[]{:S(2)}) collective-permute-start(f32[40,128]{1,0:T(8,128)} %get-tuple-element.14), channel_id=1, source_target_pairs={{0,7},{1,2},{2,1},{3,4},{4,3},{5,6},{6,5},{7,0},{8,15},{9,10},{10,... | collective-permute-start | bytes 61448 | tf_op jit(solution)/shard_map/ppermute | solution.py:26
  5.8 0.0 copy-start
  5.8 1.6 %copy-done = f32[32,128,128]{2,1,0:T(8,128)S(1)} copy-done((f32[32,128,128]{2,1,0:T(8,128)S(1)}, f32[32,128,128]{2,1,0:T(8,128)}, u32[]{:S(2)}) %copy-start) | copy-done | bytes 2097176
  7.4 0.0 copy-start.1
  7.4 0.2 pad.1
  7.6 0.0 copy-start.2
  7.7 0.0 collective-permute-done.sides_0
  7.7 0.0 collective-permute-done.1.sides_1
  7.7 0.5 copy-done.1
  8.1 0.1 edge_rows.1
  8.2 1.6 %collective-permute-start.2 = (f32[152,128]{1,0:T(8,128)S(1)}, f32[152,128]{1,0:T(8,128)S(1)}, u32[]{:S(2)}, u32[]{:S(2)}) collective-permute-start(f32[152,128]{1,0:T(8,128)S(1)} %get-tuple-element.15), channel_id=1, source_target_pairs={{0,8},{8,0},{16,24},{24,16},{1,9},{9,1},{17,25},{25,17},{2,10},{10... | collective-permute-start | bytes 233480 | tf_op jit(solution)/shard_map/ppermute | solution.py:26
  9.8 0.7 %collective-permute-start.3 = (f32[152,128]{1,0:T(8,128)S(1)}, f32[152,128]{1,0:T(8,128)S(1)}, u32[]{:S(2)}, u32[]{:S(2)}) collective-permute-start(f32[152,128]{1,0:T(8,128)S(1)} %get-tuple-element.16), channel_id=1, source_target_pairs={{8,16},{16,8},{9,17},{17,9},{10,18},{18,10},{11,19},{19,11},{12,20... | collective-permute-start | bytes 233480 | tf_op jit(solution)/shard_map/ppermute | solution.py:26
  10.5 0.0 copy-done.2
  10.5 2.1 %collective-permute-done.2.ends_0 = f32[152,128]{1,0:T(8,128)S(1)} collective-permute-done((f32[152,128]{1,0:T(8,128)S(1)}, f32[152,128]{1,0:T(8,128)S(1)}, u32[]{:S(2)}, u32[]{:S(2)}) %collective-permute-start.2) | collective-permute-done | bytes 77856 | tf_op jit(solution)/shard_map/ppermute | solution.py:26
  12.6 0.0 collective-permute-done.3.ends_1
  12.6 1.5 %prior.1 = bf16[32,16,128]{2,1,0:T(8,128)(2,1)} custom-call(f32[2,8,128]{2,1,0:T(8,128)S(1)} %copy-done.1, f32[40,128]{1,0:T(8,128)S(1)} %collective-permute-done.sides_0, f32[40,128]{1,0:T(8,128)S(1)} %collective-permute-done.1.sides_1, f32[152,128]{1,0:T(8,128)S(1)} %collective-permute-done.2.ends_0, f32[152,128]{1,0:T(8,128)S(1)} %collective-permute-done.3.ends_1, ...), custom_call_target="tpu_custom_call" | custom-call | tf_op jit(solution)/shard_map/prior/pallas_call | solution.py:396
  14.1 7.7 %all-to-all-start = ((bf16[32,16,128]{2,1,0:T(8,128)(2,1)}), bf16[32,16,128]{2,1,0:T(8,128)(2,1)S(1)}, u32[]{:S(2)}, u32[]{:S(2)}) async-start(bf16[32,16,128]{2,1,0:T(8,128)(2,1)} %prior.1), calls=%async_computation | async-start | bytes 262144 | tf_op jit(solution)/shard_map/all_to_all | solution.py:413
  21.8 1.6 %later_shares.1.later = f32[10,8,128]{2,1,0:T(8,128)S(1)} custom-call(f32[2,8,128]{2,1,0:T(8,128)S(1)} %copy-done.1, f32[40,128]{1,0:T(8,128)S(1)} %collective-permute-done.sides_0, f32[40,128]{1,0:T(8,128)S(1)} %collective-permute-done.1.sides_1, f32[152,128]{1,0:T(8,128)S(1)} %collective-permute-done.2.ends_0, ...), custom_call_target="tpu_custom_call" | custom-call | tf_op jit(solution)/shard_map/later_shares/pallas_call | solution.py:396
  23.4 6.6 %all-to-all-done.near_ref = bf16[32,16,128]{2,1,0:T(8,128)(2,1)S(1)} async-done(((bf16[32,16,128]{2,1,0:T(8,128)(2,1)}), bf16[32,16,128]{2,1,0:T(8,128)(2,1)S(1)}, u32[]{:S(2)}, u32[]{:S(2)}) %all-to-all-start) | async-done | bytes 131104 | tf_op jit(solution)/shard_map/all_to_all | solution.py:413
  30.0 5.4 %first_batch.1 = (f32[128,128]{1,0:T(8,128)S(1)}, f32[32,8,128]{2,1,0:T(8,128)S(1)}) custom-call(bf16[32,16,128]{2,1,0:T(8,128)(2,1)S(1)} %all-to-all-done.near_ref, f32[10,8,128]{2,1,0:T(8,128)S(1)} %later_shares.1.later), custom_call_target="tpu_custom_call" | custom-call | tf_op jit(solution)/shard_map/first_batch/pallas_call | solution.py:396
  35.5 10.0 %all_to_all.15.shares = f32[32,8,128]{2,1,0:T(8,128)S(1)} all-to-all(f32[32,8,128]{2,1,0:T(8,128)S(1)} %get-tuple-element.17), channel_id=1, replica_groups=mesh['lat'=4,'lon'=8] {'lat','lon'}, dimensions={0} | all-to-all | bytes 262144 | tf_op jit(solution)/shard_map/all_to_all | solution.py:413
  45.5 0.1 own_block.1
  45.6 10.0 %all_to_all.16.near_ref = bf16[32,16,128]{2,1,0:T(8,128)(2,1)S(1)} all-to-all(bf16[32,16,128]{2,1,0:T(8,128)(2,1)S(1)} %own_block.1), channel_id=1, replica_groups=mesh['lat'=4,'lon'=8] {'lat','lon'}, dimensions={0} | all-to-all | bytes 262144 | tf_op jit(solution)/shard_map/all_to_all | solution.py:413
  55.6 7.0 %second_batch.1 = f32[4096,128]{1,0:T(8,128)} custom-call(bf16[32,16,128]{2,1,0:T(8,128)(2,1)S(1)} %all_to_all.16.near_ref, f32[128,128]{1,0:T(8,128)S(1)} %get-tuple-element.18.map_ref, f32[36,144,128]{2,1,0:T(8,128)S(1)} %pad.1), custom_call_target="tpu_custom_call" | custom-call | tf_op jit(solution)/shard_map/second_batch/pallas_call | solution.py:396
  (1 shorter events, 0.0 us)
Async XLA Ops:
  1.8 5.9 %collective-permute-start = (f32[40,128]{1,0:T(8,128)}, f32[40,128]{1,0:T(8,128)S(1)}, u32[]{:S(2)}, u32[]{:S(2)}) collective-permute-start(f32[40,128]{1,0:T(8,128)} %get-tuple-element.13), channel_id=1, source_target_pairs={{0,1},{1,0},{2,3},{3,2},{4,5},{5,4},{6,7},{7,6},{8,9},{9,8},{10,11... | collective-permute-start | bytes 61448 | tf_op jit(solution)/shard_map/ppermute | solution.py:26
  2.3 5.4 %collective-permute-start.1 = (f32[40,128]{1,0:T(8,128)}, f32[40,128]{1,0:T(8,128)S(1)}, u32[]{:S(2)}, u32[]{:S(2)}) collective-permute-start(f32[40,128]{1,0:T(8,128)} %get-tuple-element.14), channel_id=1, source_target_pairs={{0,7},{1,2},{2,1},{3,4},{4,3},{5,6},{6,5},{7,0},{8,15},{9,10},{10,... | collective-permute-start | bytes 61448 | tf_op jit(solution)/shard_map/ppermute | solution.py:26
  5.8 1.6 %copy-start = (f32[32,128,128]{2,1,0:T(8,128)S(1)}, f32[32,128,128]{2,1,0:T(8,128)}, u32[]{:S(2)}) copy-start(f32[32,128,128]{2,1,0:T(8,128)} %cells.3) | copy-start | bytes 6291460
  7.4 0.7 %copy-start.1 = (f32[2,8,128]{2,1,0:T(8,128)S(1)}, f32[2,8,128]{2,1,0:T(8,128)}, u32[]{:S(2)}) copy-start(f32[2,8,128]{2,1,0:T(8,128)} %get-tuple-element.12.mine) | copy-start | bytes 24580
  7.6 2.8 %copy-start.2 = (s32[2,1,1,5,8]{4,2,3,1,0:T(1,128)S(1)}, s32[2,1,1,5,8]{4,2,3,1,0:T(1,128)}, u32[]{:S(2)}) copy-start(s32[2,1,1,5,8]{4,2,3,1,0:T(1,128)} %param.13) | copy-start | bytes 964
  8.2 4.4 %collective-permute-start.2 = (f32[152,128]{1,0:T(8,128)S(1)}, f32[152,128]{1,0:T(8,128)S(1)}, u32[]{:S(2)}, u32[]{:S(2)}) collective-permute-start(f32[152,128]{1,0:T(8,128)S(1)} %get-tuple-element.15), channel_id=1, source_target_pairs={{0,8},{8,0},{16,24},{24,16},{1,9},{9,1},{17,25},{25,17},{2,10},{10... | collective-permute-start | bytes 233480 | tf_op jit(solution)/shard_map/ppermute | solution.py:26
  9.8 2.8 %collective-permute-start.3 = (f32[152,128]{1,0:T(8,128)S(1)}, f32[152,128]{1,0:T(8,128)S(1)}, u32[]{:S(2)}, u32[]{:S(2)}) collective-permute-start(f32[152,128]{1,0:T(8,128)S(1)} %get-tuple-element.16), channel_id=1, source_target_pairs={{8,16},{16,8},{9,17},{17,9},{10,18},{18,10},{11,19},{19,11},{12,20... | collective-permute-start | bytes 233480 | tf_op jit(solution)/shard_map/ppermute | solution.py:26
  14.1 15.9 %all-to-all-start = ((bf16[32,16,128]{2,1,0:T(8,128)(2,1)}), bf16[32,16,128]{2,1,0:T(8,128)(2,1)S(1)}, u32[]{:S(2)}, u32[]{:S(2)}) async-start(bf16[32,16,128]{2,1,0:T(8,128)(2,1)} %prior.1), calls=%async_computation | async-start | bytes 262144 | tf_op jit(solution)/shard_map/all_to_all | solution.py:413
where the time goes:
time: 62.9 us; the launch traced here: 62.6 us
  blocking collectives  20 us (32%)
  Pallas kernels  17.7 us (28%)
  starting transfers between devices  14 us (22%)
  waiting for transfers between devices  8.78 us (14%)
  local copies, waits for them, and re-layouts  2.05 us (3%)
    all_to_all x2, blocking collectives, exchange(): lax.all_to_all(blocks, ('lat', 'lon'), split_axis=0, concat_axis=0, tiled...  20 us
    pallas_call x8, Pallas kernels, call(): pl.pallas_call(kernel, out_shape=out_shape, in_specs=specs, out_specs=out...  17.7 us
    all_to_all x1, starting transfers between devices, exchange(): lax.all_to_all(blocks, ('lat', 'lon'), split_axis=0, concat_axis=0, tiled...  7.7 us
    all_to_all x1, waiting for transfers between devices, exchange(): lax.all_to_all(blocks, ('lat', 'lon'), split_axis=0, concat_axis=0, tiled...  6.63 us
    ppermute x4, starting transfers between devices, swap(): return lax.ppermute(block, axis, route)  6.32 us
    ppermute x4, waiting for transfers between devices, swap(): return lax.ppermute(block, axis, route)  2.15 us
    unnamed x7, local copies, waits for them, and re-layouts  2.05 us
  transfers between devices with their start and end apart: 5, of which 2 were waited for; matrix products, arithmetic and copies ran while one was open for 0% of the time, Pallas kernels for 3%

commit v1 on v0

--- a/solution.py
+++ b/solution.py
@@ -12,26 +12,18 @@
 LANES = 128
 NEAR = (-1, 0, 1)
 AT_ROW, AT_COL, AT_OBS = (4, 5, 6)
-AT_MARK = 64
+PAIRS = SUB // 2 + 1
 F32 = jnp.float32
 BF16 = jnp.bfloat16
 
 
-def swap(block, axis, kind, count, wraps):
-    route = []
-    for place in range(count):
-        partner = place + (1 if place % 2 == kind else -1)
-        if wraps or 0 <= partner < count:
-            route.append((place, partner % count))
+def shifted(block, axis, step, count, wraps):
+    route = [(i, (i + step) % count) for i in range(count) if wraps or 0 <= i + step < count]
     return lax.ppermute(block, axis, route)
 
 
-def is_even(axis):
-    return lax.rem(lax.axis_index(axis), 2) == 0
-
-
 def start_kernel(
-    width, observed, precision, weight, stencil, owned, cells, params_ref, sides_0, sides_1,
+    width, observed, precision, weight, stencil, owned, cells, params_ref, left_ref, right_ref,
     observed_v, precision_v, weight_v, stencil_v, owned_v, left_v, right_v, sems
 ):
     batches, cols = (observed.shape[0], cells.shape[1])
@@ -58,13 +50,11 @@
         params_ref[b, pl.ds(AT_ROW, 1), pl.ds(0, SUB)] = row
         params_ref[b, pl.ds(AT_COL, 1), pl.ds(0, SUB)] = corner - row * width
         params_ref[b, pl.ds(AT_OBS, 1), pl.ds(0, SUB)] = observed_v[b, 0] * root
-    even = is_even("lon")
-    left, right = (left_v[:, 0, :], right_v[:, SUB - 1, :])
     rows = cells.shape[0]
-    sides_0[pl.ds(0, rows), :] = jnp.where(even, right, left)
-    sides_1[pl.ds(0, rows), :] = jnp.where(even, left, right)
-    sides_0[pl.ds(rows, SUB), :] = params_ref[1]
-    sides_1[pl.ds(rows, SUB), :] = params_ref[1]
+    left_ref[pl.ds(0, rows), :] = left_v[:, 0, :]
+    right_ref[pl.ds(0, rows), :] = right_v[:, SUB - 1, :]
+    left_ref[pl.ds(rows, SUB), :] = params_ref[1]
+    right_ref[pl.ds(rows, SUB), :] = params_ref[1]
 
 
 def clear_rim(pad, rows, cols):
@@ -101,13 +91,11 @@
     copy.wait()
 
 
-def hold_sides(sides_0, sides_1, sides):
-    rows = sides_0.shape[0] - SUB
-    even = is_even("lon")
-    first, second = (sides_0[pl.ds(0, rows), :], sides_1[pl.ds(0, rows), :])
+def hold_sides(left, right, sides):
+    rows = left.shape[0] - SUB
     sides[...] = jnp.zeros_like(sides)
-    sides[0, pl.ds(SUB, rows), :] = jnp.where(even, second, first)
-    sides[1, pl.ds(SUB, rows), :] = jnp.where(even, first, second)
+    sides[0, pl.ds(SUB, rows), :] = left[pl.ds(0, rows), :]
+    sides[1, pl.ds(SUB, rows), :] = right[pl.ds(0, rows), :]
 
 
 def side_share(sides, side, number, rows, cols, da, o):
@@ -118,84 +106,78 @@
     return terms[0] + terms[1]
 
 
-def send_block(value, marks, scratch, out_ref):
+def send_block(value, out_ref):
     mean = jnp.mean(value, axis=-1, keepdims=True)
-    scratch[...] = jnp.zeros_like(scratch)
-    scratch[pl.ds(0, marks.shape[0]), pl.ds(0, marks.shape[1])] = marks.astype(F32)
+    sub = lax.broadcasted_iota(jnp.int32, (SUB, LANES), 0)
     lane = lax.broadcasted_iota(jnp.int32, (SUB, LANES), 1)
-    innov = jnp.where(lane < AT_MARK, -mean, pltpu.roll(scratch[...], AT_MARK, 1))
-    block = jnp.concatenate([value - mean, innov], axis=0).astype(BF16)
-    out_ref[...] = jnp.broadcast_to(block, out_ref.shape)
-
-
-def rows_kernel(mine, sides_0, sides_1, pad, out_0, out_1):
+    innov = jnp.sum(jnp.where(lane == sub, -mean, 0.0), axis=0, keepdims=True)
+    rows = jnp.concatenate([value - mean, jnp.broadcast_to(innov, (2, LANES))], axis=0).astype(BF16)
+    for n in range(PAIRS):
+        pair = rows[2 * n:2 * n + 2]
+        out_ref[:, n] = jnp.broadcast_to(pair, (out_ref.shape[0],) + pair.shape)
+
+
+def rows_kernel(mine, left, right, pad, first_ref, last_ref):
     rows, cols = (pad.shape[0] - 4, pad.shape[1] - 2 * SUB)
-    lon_even, lat_even = (is_even("lon"), is_even("lat"))
-    edges = []
-    for row in (0, rows - 1):
-        first, second = (sides_0[pl.ds(row, 1), :], sides_1[pl.ds(row, 1), :])
-        left, right = (jnp.where(lon_even, second, first), jnp.where(lon_even, first, second))
-        cells = pad[2 + row, pl.ds(SUB, cols), :]
-        beside = [jnp.broadcast_to(cell, (SUB, LANES)) for cell in (left, right)]
-        edges.append(jnp.concatenate([beside[0], cells, beside[1]], axis=0))
-    first, second = (sides_0[pl.ds(rows, SUB), :], sides_1[pl.ds(rows, SUB), :])
-    left, right = (jnp.where(lon_even, second, first), jnp.where(lon_even, first, second))
     lane = lax.broadcasted_iota(jnp.int32, (SUB, LANES), 1)
-    packed = jnp.where(lane < SUB, left, pltpu.roll(mine[1], SUB, 1))
-    packed = jnp.where(lane < 2 * SUB, packed, pltpu.roll(right, 2 * SUB, 1))
-    for kind, out in enumerate((out_0, out_1)):
-        out[pl.ds(0, cols + 2 * SUB), :] = jnp.where(lat_even, edges[1 - kind], edges[kind])
-        out[pl.ds(cols + 2 * SUB, SUB), :] = packed
-
-
-def prior_kernel(mine, sides_0, sides_1, ends_0, ends_1, pad, pattern, out_ref, ends, sides, value, params, sem):
+    block = pl.ds(rows, SUB)
+    packed = jnp.where(lane < SUB, left[block, :], pltpu.roll(mine[1], SUB, 1))
+    packed = jnp.where(lane < 2 * SUB, packed, pltpu.roll(right[block, :], 2 * SUB, 1))
+    for row, out in ((0, first_ref), (rows - 1, last_ref)):
+        out[pl.ds(0, SUB), :] = jnp.broadcast_to(left[pl.ds(row, 1), :], (SUB, LANES))
+        out[pl.ds(SUB, cols), :] = pad[2 + row, pl.ds(SUB, cols), :]
+        out[pl.ds(SUB + cols, SUB), :] = jnp.broadcast_to(right[pl.ds(row, 1), :], (SUB, LANES))
+        out[pl.ds(2 * SUB + cols, SUB), :] = packed
+
+
+def row_kernel(mine, left, right, pad, out_ref, sides, params, sem):
     rows, cols = (pad.shape[0] - 4, pad.shape[1] - 2 * SUB)
     copy = pltpu.make_async_copy(mine.at[0], params, sem)
     copy.start()
-    even = is_even("lat")
-    first, second = (ends_0[pl.ds(0, cols + 2 * SUB), :], ends_1[pl.ds(0, cols + 2 * SUB), :])
-    ends[0] = jnp.where(even, second, first)
-    ends[1] = jnp.where(even, first, second)
-    hold_sides(sides_0, sides_1, sides)
+    hold_sides(left, right, sides)
     copy.wait()
     number = lambda kind, o: params[kind, o]
     for o in range(SUB):
         total = share(pad, number, rows, cols, 0, 0, o)
-        row = number(AT_ROW, o).astype(jnp.int32)
-        col = number(AT_COL, o).astype(jnp.int32)
-        for n, at in enumerate((0, rows)):
-            for k in range(2):
-                weight = jnp.where(row == at, number(2 * n + k, o), 0.0)
-                total = total + weight * ends[n, pl.ds(col + SUB - 1 + k, 1), :]
         for side in range(2):
             total = total + side_share(sides, side, number, rows, cols, 0, o)
+        out_ref[pl.ds(o, 1), :] = total
+    out_ref[...] = out_ref[...] - own_shift(number)
+
+
+def prior_kernel(rows, mine, own, above, below, out_ref, value, params, sem):
+    copy = pltpu.make_async_copy(mine.at[0], params, sem)
+    copy.start()
+    copy.wait()
+    for o in range(SUB):
+        row, col = (params[AT_ROW, o].astype(jnp.int32), params[AT_COL, o].astype(jnp.int32))
+        total = own[pl.ds(o, 1), :]
+        for n, (end, at) in enumerate(((above, 0), (below, rows))):
+            for k in range(2):
+                weight = jnp.where(row == at, params[2 * n + k, o], 0.0)
+                total = total + weight * end[pl.ds(col + SUB - 1 + k, 1), :]
         value[pl.ds(o, 1), :] = total
-    send_block(value[...] - own_shift(number), pattern[0, 0, 0], value, out_ref)
-
-
-def meet_kernel(shares, pattern, out_ref, scratch):
-    send_block(jnp.sum(shares[...], axis=0), pattern[1, 0, 0], scratch, out_ref)
-
-
-def later_kernel(mine, sides_0, sides_1, ends_0, ends_1, pad, out_ref, params, sems):
+    send_block(value[...], out_ref)
+
+
+def meet_kernel(shares, out_ref):
+    send_block(jnp.sum(shares[...], axis=0), out_ref)
+
+
+def later_kernel(mine, left, right, above, below, pad, out_ref, params, sems):
     rows, cols = (pad.shape[0] - 4, pad.shape[1] - 2 * SUB)
-    lon_even, lat_even = (is_even("lon"), is_even("lat"))
     side, end = (pl.ds(rows, SUB), pl.ds(cols + 2 * SUB, SUB))
-    sources = (sides_0.at[side], mine.at[1], sides_1.at[side], ends_0.at[end], ends_1.at[end])
+    sources = (left.at[side], mine.at[1], right.at[side], above.at[end], below.at[end])
     copies = []
     for n, source in enumerate(sources):
         copies.append(pltpu.make_async_copy(source, params.at[n], sems.at[n]))
         copies[-1].start()
     for copy in copies:
         copy.wait()
-    beside = (jnp.where(lon_even, 2, 0), 1, jnp.where(lon_even, 0, 2))
-    above = (jnp.where(lat_even, 4, 3), None, jnp.where(lat_even, 3, 4))
     for n, dc in enumerate(NEAR):
         for m, da in enumerate(NEAR):
-            if da == 0:
-                number = lambda kind, o: params[beside[n], kind, o]
-            else:
-                number = lambda kind, o: params[above[m], kind, n * SUB + o]
+            spot, lane = (n, 0) if da == 0 else (len(NEAR) + m // 2, n * SUB)
+            number = lambda kind, o: params[spot, kind, lane + o]
             for o in range(SUB):
                 out_ref[n * len(NEAR) + m, pl.ds(o, 1), :] = share(pad, number, rows, cols, da, dc, o)
     out_ref[len(NEAR) ** 2] = own_shift(lambda kind, o: params[1, kind, o])
@@ -286,36 +268,41 @@
     return inverse, blocks[count][:1]
 
 
-def batch_map(lat_count, near_ref, marks):
+def batch_map(batch, lat_count, near_ref, pattern):
     held = min(WIN, lat_count)
-    lon_count = near_ref.shape[0] // held
-    my_lat, my_lon = (lax.axis_index("lat"), lax.axis_index("lon"))
+    count = near_ref.shape[0]
+    my_lat = lax.axis_index("lat")
     start = window_start(lat_count, my_lat)
-    near = near_ref[...].astype(F32)
-    rounded = near[:, :SUB].reshape(-1, LANES)
-    innov = near[:, SUB:].reshape(-1, LANES)[:, :1]
-    scaled = rounded.astype(BF16)
-    marks[...] = near_ref[(my_lat - start) * lon_count + my_lon, pl.ds(SUB, SUB), :].astype(F32)
+    scaled = jnp.concatenate([near_ref[:, n].astype(F32) for n in range(PAIRS - 1)], axis=1)
+    innov = near_ref[:, PAIRS - 1].astype(F32)[:, :1]
+    sub = lax.broadcasted_iota(jnp.int32, scaled.shape, 1)
+    lane = lax.broadcasted_iota(jnp.int32, scaled.shape, 2)
+    innov = jnp.where(lane == sub, jnp.broadcast_to(innov, scaled.shape), 0.0)
     picked = []
     for j in range(held):
         offset = start + j - my_lat + REACH
         inside = (offset >= 0) & (offset < WIN)
-        row = jnp.where(inside, marks[pl.ds(jnp.clip(offset, 0, WIN - 1), 1), :], 0.0)
-        for e in range(lon_count):
-            picked.append(jnp.broadcast_to(row[:, AT_MARK + e:AT_MARK + e + 1], (SUB, LANES)))
-    weighted = rounded * jnp.concatenate(picked, axis=0)
-    gram = lax.dot_general(
-        weighted.astype(BF16), scaled, (((0,), (0,)), ((), ())), preferred_element_type=F32
+        row = pattern[batch, 0, 0, pl.ds(jnp.clip(offset, 0, WIN - 1), 1), :].astype(F32)
+        row = jnp.where(inside, row, 0.0)
+        for e in range(count // held):
+            picked.append(jnp.broadcast_to(row[:, e:e + 1], (1, SUB, LANES)))
+    weighted = scaled * jnp.concatenate(picked, axis=0)
+    both = jnp.concatenate([scaled, innov], axis=2).reshape(count * SUB, 2 * LANES).astype(BF16)
+    product = lax.dot_general(
+        both,
+        weighted.reshape(count * SUB, LANES).astype(BF16),
+        (((0,), (0,)), ((), ())),
+        preferred_element_type=F32,
     )
     sub = lax.broadcasted_iota(jnp.int32, (SUB, LANES), 0)
     lane = lax.broadcasted_iota(jnp.int32, (SUB, LANES), 1)
     members = LANES
     blocks = []
     for k in range(members // SUB):
-        block = gram[k * SUB:(k + 1) * SUB, :]
+        block = product[k * SUB:(k + 1) * SUB, :]
         blocks.append(block + jnp.where(lane - k * SUB == sub, members - 1.0, 0.0))
-    proj = jnp.sum((weighted * innov).reshape(-1, SUB, LANES), axis=0)
-    blocks.append(jnp.broadcast_to(jnp.sum(proj, axis=0, keepdims=True), (SUB, LANES)))
+    proj = jnp.sum(product[members:members + SUB, :], axis=0, keepdims=True)
+    blocks.append(jnp.broadcast_to(proj, (SUB, LANES)))
     inverse, weights = eliminate(blocks)
     flipped = jnp.concatenate(inverse, axis=0) * (members - 1.0) ** 0.5 - weights
     return flipped - jnp.mean(flipped, axis=-1, keepdims=True) + 1.0 / members
@@ -327,8 +314,8 @@
     )
 
 
-def first_kernel(lat_count, lon_count, near_ref, later, map_ref, out_ref, marks, moved):
-    flipped = batch_map(lat_count, near_ref, marks)
+def first_kernel(lat_count, lon_count, near_ref, pattern, later, map_ref, out_ref, moved):
+    flipped = batch_map(0, lat_count, near_ref, pattern)
     map_ref[...] = flipped
     count = len(NEAR) ** 2
     moved[...] = exact_dot(later[pl.ds(0, count)].reshape(-1, LANES), flipped, 1).reshape(moved.shape)
@@ -345,10 +332,10 @@
                 out_ref[lat * lon_count + lon] = moved[n * len(NEAR) + m]
 
 
-def last_kernel(lat_count, near_ref, map_ref, pad, out_ref, result, marks, out_sem):
+def last_kernel(lat_count, near_ref, pattern, map_ref, pad, out_ref, result, out_sem):
     parts = out_sem.shape[0]
     rows, cols = (pad.shape[0] - 4, pad.shape[1] - 2 * SUB)
-    flipped = exact_dot(batch_map(lat_count, near_ref, marks), map_ref[...], 0)
+    flipped = exact_dot(batch_map(1, lat_count, near_ref, pattern), map_ref[...], 0)
     high = flipped.astype(BF16)
     low = (flipped - high.astype(F32)).astype(BF16)
     right = jnp.concatenate(
@@ -403,18 +390,12 @@
             name=name,
         )(*operands)
 
-    def trade(blocks, axis):
-        count, wraps = ((lon_count, True) if axis == "lon" else (lat_count, False))
-        second = swap(blocks[1], axis, 1, count, wraps)
-        first = swap(blocks[0], axis, 0, count, wraps)
-        return (first, second)
-
     def exchange(blocks):
         return lax.all_to_all(blocks, ("lat", "lon"), split_axis=0, concat_axis=0, tiled=True)
 
     small = (observed, precision, interp_weight, stencil, owned)
     side = shape(rows + SUB, members)
-    mine, *sides = call(
+    mine, left, right = call(
         functools.partial(start_kernel, cols + 2),
         "start",
         [hbm] * 6,
@@ -426,29 +407,26 @@
         ensemble,
         limit=63,
     )
-    sides = trade(sides, "lon")
+    sides = (shifted(right, "lon", 1, lon_count, True), shifted(left, "lon", -1, lon_count, True))
     padded = shape(rows + 4, cols + 2 * SUB, members)
     pad = call(pad_kernel, "pad", [hbm], padded, [pltpu.SemaphoreType.DMA], ensemble)
     end = shape(cols + 3 * SUB, members)
-    ends = call(rows_kernel, "edge_rows", [vmem] * 4, (end, end), [], mine, *sides, pad)
-    ends = trade(ends, "lat")
-    around = (mine, *sides, *ends, pad)
-    slots = shape(tiles, 2 * SUB, members, dtype=BF16)
+    first, last = call(rows_kernel, "edge_rows", [vmem] * 4, (end, end), [], mine, *sides, pad)
+    ends = (shifted(last, "lat", 1, lat_count, False), shifted(first, "lat", -1, lat_count, False))
+    slots = shape(tiles, PAIRS, 2, members, dtype=BF16)
+    numbers = [pltpu.SMEM((SUB, LANES), F32), pltpu.SemaphoreType.DMA]
+    block = shape(SUB, members)
     held_sides = pltpu.VMEM((2, rows + 2 * SUB, members), F32)
+    own = call(row_kernel, "row_shares", [vmem] * 4, block, [held_sides] + numbers, mine, *sides, pad)
     blocks = call(
-        prior_kernel,
+        functools.partial(prior_kernel, rows),
         "prior",
-        [vmem] * 7,
+        [vmem] * 4,
         slots,
-        [
-            pltpu.VMEM((2, cols + 2 * SUB, members), F32),
-            held_sides,
-            pltpu.VMEM((SUB, members), F32),
-            pltpu.SMEM((SUB, LANES), F32),
-            pltpu.SemaphoreType.DMA,
-        ],
-        *around,
-        pattern,
+        [pltpu.VMEM((SUB, members), F32)] + numbers,
+        mine,
+        own,
+        *ends,
     )
     near = window(exchange(blocks), lat_count, lon_count)
     count = len(NEAR) ** 2
@@ -458,32 +436,35 @@
         [vmem] * 6,
         shape(count + 1, SUB, members),
         [pltpu.SMEM((5, SUB, LANES), F32), pltpu.SemaphoreType.DMA((5,))],
-        *around,
-    )
-    block = pltpu.VMEM((SUB, members), F32)
+        mine,
+        *sides,
+        *ends,
+        pad,
+    )
     first_map, shares = call(
         functools.partial(first_kernel, lat_count, lon_count),
         "first_batch",
-        [vmem] * 2,
+        [vmem] * 3,
         (shape(members, members), shape(tiles, SUB, members)),
-        [block, pltpu.VMEM((count, SUB, members), F32)],
+        [pltpu.VMEM((count, SUB, members), F32)],
         near,
+        pattern,
         later,
     )
-    blocks = call(meet_kernel, "own_block", [vmem] * 2, slots, [block], exchange(shares), pattern)
+    blocks = call(meet_kernel, "own_block", [vmem], slots, [], exchange(shares))
     near = window(exchange(blocks), lat_count, lon_count)
     parts = 8
     result = call(
         functools.partial(last_kernel, lat_count),
         "second_batch",
-        [vmem] * 3,
+        [vmem] * 4,
         shape(rows * cols, members),
         [
             pltpu.VMEM((rows * cols, members), F32),
-            block,
             pltpu.SemaphoreType.DMA((parts,)),
         ],
         near,
+        pattern,
         first_map,
         pad,
         out_specs=anywhere,

time: 62.9 us -> 63.7 us (1.013)
  waiting for transfers between devices: 8.78 us -> 10.4 us
  blocking collectives: 20 us -> 19.2 us
    all_to_all x1, starting transfers between devices: 7.7 us -> 4.41 us  [exchange(): lax.all_to_all(blocks, ('lat', 'lon'), split_axis=0, concat_axis=0, tiled...]
    ppermute x4, starting transfers between devices: 6.32 us -> 9.04 us  [shifted(): return lax.ppermute(block, axis, route)]
    ppermute x4, waiting for transfers between devices: 2.15 us -> 4.28 us  [shifted(): return lax.ppermute(block, axis, route)]
    all_to_all x2, blocking collectives: 20 us -> 19.2 us  [exchange(): lax.all_to_all(blocks, ('lat', 'lon'), split_axis=0, concat_axis=0, tiled...]
    pallas_call x8 -> x9, Pallas kernels: 17.7 us -> 18.1 us  [call(): pl.pallas_call(kernel, out_shape=out_shape, in_specs=specs, out_specs=out...]
  transfers between devices with their start and end apart: 5 -> 5, of which waited for: 2 -> 2; matrix products, arithmetic and copies ran while one was open for 0% -> 0% of each run, Pallas kernels for 3% -> 4%
where the time goes in v1:
time: 63.7 us; the launch traced here: 63.4 us
  blocking collectives  19.2 us (30%)
  Pallas kernels  18.1 us (28%)
  starting transfers between devices  13.4 us (21%)
  waiting for transfers between devices  10.4 us (16%)
  local copies, waits for them, and re-layouts  2.06 us (3%)
    all_to_all x2, blocking collectives, exchange(): lax.all_to_all(blocks, ('lat', 'lon'), split_axis=0, concat_axis=0, tiled...  19.2 us
    pallas_call x9, Pallas kernels, call(): pl.pallas_call(kernel, out_shape=out_shape, in_specs=specs, out_specs=out...  18.1 us
    ppermute x4, starting transfers between devices, shifted(): return lax.ppermute(block, axis, route)  9.04 us
    all_to_all x1, waiting for transfers between devices, exchange(): lax.all_to_all(blocks, ('lat', 'lon'), split_axis=0, concat_axis=0, tiled...  6.11 us
    all_to_all x1, starting transfers between devices, exchange(): lax.all_to_all(blocks, ('lat', 'lon'), split_axis=0, concat_axis=0, tiled...  4.41 us
    ppermute x4, waiting for transfers between devices, shifted(): return lax.ppermute(block, axis, route)  4.28 us
    unnamed x7, local copies, waits for them, and re-layouts  2.06 us
  transfers between devices with their start and end apart: 5, of which 2 were waited for; matrix products, arithmetic and copies ran while one was open for 0% of the time, Pallas kernels for 4%

profile of v1, /device:TPU:0, one launch (start us, length us, event | category | flops | bytes accessed | tf_op | source)
XLA Modules:
  0.0 63.4 jit_solution(10906016816230267320)
XLA Ops:
  0.0 1.7 %start.1 = (f32[2,8,128]{2,1,0:T(8,128)}, f32[40,128]{1,0:T(8,128)}, f32[40,128]{1,0:T(8,128)}) custom-call(f32[2,1,1,8]{3,2,1,0:T(1,128)} %observed.1, f32[2,1,1,8]{3,2,1,0:T(1,128)} %precision.1, f32[2,1,1,4,8]{4,3,2,1,0:T(4,128)} %weight.1, s32[2,1,1,4,8]{4,3,2,1,0:T(4,128)} %stencil.1, s32[2,1,1,8]{3,2,1,0:T(1,128)} %owned.1, f32[32,128,128]{2,1,0:T(8,128)} %cells.3), custom_call_target="tpu_custom_call" | custom-call | tf_op jit(solution)/shard_map/start/pallas_call | solution.py:383
  1.7 0.5 collective-permute-start
  2.3 2.9 %collective-permute-start.1 = (f32[40,128]{1,0:T(8,128)}, f32[40,128]{1,0:T(8,128)S(1)}, u32[]{:S(2)}, u32[]{:S(2)}) collective-permute-start(f32[40,128]{1,0:T(8,128)} %get-tuple-element.14), channel_id=1, source_target_pairs={{0,7},{1,0},{2,1},{3,2},{4,3},{5,4},{6,5},{7,6},{8,15},{9,8},{10,9... | collective-permute-start | bytes 61448 | tf_op jit(solution)/shard_map/ppermute | solution.py:22
  5.2 0.0 copy-start
  5.2 1.6 %copy-done = f32[32,128,128]{2,1,0:T(8,128)S(1)} copy-done((f32[32,128,128]{2,1,0:T(8,128)S(1)}, f32[32,128,128]{2,1,0:T(8,128)}, u32[]{:S(2)}) %copy-start) | copy-done | bytes 2097176
  6.8 0.0 copy-start.1
  6.8 0.2 pad.1
  7.0 0.0 collective-permute-done.left
  7.0 0.0 collective-permute-done.1.right
  7.0 0.5 copy-done.1
  7.5 0.1 edge_rows.1
  7.6 0.0 copy-start.2
  7.6 4.3 %collective-permute-start.2 = (f32[152,128]{1,0:T(8,128)S(1)}, f32[152,128]{1,0:T(8,128)S(1)}, u32[]{:S(2)}, u32[]{:S(2)}) collective-permute-start(f32[152,128]{1,0:T(8,128)S(1)} %get-tuple-element.15), channel_id=1, source_target_pairs={{0,8},{8,16},{16,24},{1,9},{9,17},{17,25},{2,10},{10,18},{18,26},{... | collective-permute-start | bytes 233480 | tf_op jit(solution)/shard_map/ppermute | solution.py:22
  11.9 1.3 %collective-permute-start.3 = (f32[152,128]{1,0:T(8,128)S(1)}, f32[152,128]{1,0:T(8,128)S(1)}, u32[]{:S(2)}, u32[]{:S(2)}) collective-permute-start(f32[152,128]{1,0:T(8,128)S(1)} %get-tuple-element.16), channel_id=1, source_target_pairs={{8,0},{16,8},{24,16},{9,1},{17,9},{25,17},{10,2},{18,10},{26,18},{... | collective-permute-start | bytes 233480 | tf_op jit(solution)/shard_map/ppermute | solution.py:22
  13.2 0.7 %row_shares.1.own = f32[8,128]{1,0:T(8,128)S(1)} custom-call(f32[2,8,128]{2,1,0:T(8,128)S(1)} %copy-done.1, f32[40,128]{1,0:T(8,128)S(1)} %collective-permute-done.left, f32[40,128]{1,0:T(8,128)S(1)} %collective-permute-done.1.right, f32[36,144,128]{2,1,0:T(8,128)S(1)} %pad.1), custom_call_target="tpu_custom_call" | custom-call | tf_op jit(solution)/shard_map/row_shares/pallas_call | solution.py:383
  13.9 0.0 collective-permute-done.2.above
  13.9 4.3 %collective-permute-done.3.below = f32[152,128]{1,0:T(8,128)S(1)} collective-permute-done((f32[152,128]{1,0:T(8,128)S(1)}, f32[152,128]{1,0:T(8,128)S(1)}, u32[]{:S(2)}, u32[]{:S(2)}) %collective-permute-start.3) | collective-permute-done | bytes 77856 | tf_op jit(solution)/shard_map/ppermute | solution.py:22
  18.2 1.4 %prior.1 = bf16[32,5,2,128]{3,2,1,0:T(2,128)(2,1)} custom-call(f32[2,8,128]{2,1,0:T(8,128)S(1)} %copy-done.1, f32[8,128]{1,0:T(8,128)S(1)} %row_shares.1.own, f32[152,128]{1,0:T(8,128)S(1)} %collective-permute-done.2.above, f32[152,128]{1,0:T(8,128)S(1)} %collective-permute-done.3.below), custom_call_target="tpu_custom_call" | custom-call | tf_op jit(solution)/shard_map/prior/pallas_call | solution.py:383
  19.6 4.4 %all-to-all-start = ((bf16[32,5,2,128]{3,2,1,0:T(2,128)(2,1)}), bf16[32,5,2,128]{3,2,1,0:T(2,128)(2,1)S(1)}, u32[]{:S(2)}, u32[]{:S(2)}) async-start(bf16[32,5,2,128]{3,2,1,0:T(2,128)(2,1)} %prior.1), calls=%async_computation | async-start | bytes 163840 | tf_op jit(solution)/shard_map/all_to_all | solution.py:394
  24.0 0.0 copy-done.2
  24.0 1.5 %later_shares.1.later = f32[10,8,128]{2,1,0:T(8,128)S(1)} custom-call(f32[2,8,128]{2,1,0:T(8,128)S(1)} %copy-done.1, f32[40,128]{1,0:T(8,128)S(1)} %collective-permute-done.left, f32[40,128]{1,0:T(8,128)S(1)} %collective-permute-done.1.right, f32[152,128]{1,0:T(8,128)S(1)} %collective-permute-done.2.above, f32[152,128]{1,0:T(8,128)S(1)} %collective-permute-done.3.below, ...), custom_call_target="tpu_custom_call" | custom-call | tf_op jit(solution)/shard_map/later_shares/pallas_call | solution.py:383
  25.5 6.1 %all-to-all-done.near_ref = bf16[32,5,2,128]{3,2,1,0:T(2,128)(2,1)S(1)} async-done(((bf16[32,5,2,128]{3,2,1,0:T(2,128)(2,1)}), bf16[32,5,2,128]{3,2,1,0:T(2,128)(2,1)S(1)}, u32[]{:S(2)}, u32[]{:S(2)}) %all-to-all-start) | async-done | bytes 81952 | tf_op jit(solution)/shard_map/all_to_all | solution.py:394
  31.6 5.4 %first_batch.1 = (f32[128,128]{1,0:T(8,128)S(1)}, f32[32,8,128]{2,1,0:T(8,128)S(1)}) custom-call(bf16[32,5,2,128]{3,2,1,0:T(2,128)(2,1)S(1)} %all-to-all-done.near_ref, s32[2,1,1,5,8]{4,3,2,1,0:T(8,128)S(1)} %copy.8.pattern, f32[10,8,128]{2,1,0:T(8,128)S(1)} %later_shares.1.later), custom_call_target="tpu_custom_call" | custom-call | tf_op jit(solution)/shard_map/first_batch/pallas_call | solution.py:383
  37.0 9.9 %all_to_all.15.shares = f32[32,8,128]{2,1,0:T(8,128)S(1)} all-to-all(f32[32,8,128]{2,1,0:T(8,128)S(1)} %get-tuple-element.17), channel_id=1, replica_groups=mesh['lat'=4,'lon'=8] {'lat','lon'}, dimensions={0} | all-to-all | bytes 262144 | tf_op jit(solution)/shard_map/all_to_all | solution.py:394
  47.0 0.2 own_block.1
  47.1 9.3 %all_to_all.16.near_ref = bf16[32,5,2,128]{3,2,1,0:T(2,128)(2,1)S(1)} all-to-all(bf16[32,5,2,128]{3,2,1,0:T(2,128)(2,1)S(1)} %own_block.1), channel_id=1, replica_groups=mesh['lat'=4,'lon'=8] {'lat','lon'}, dimensions={0} | all-to-all | bytes 163840 | tf_op jit(solution)/shard_map/all_to_all | solution.py:394
  56.4 7.0 %second_batch.1 = f32[4096,128]{1,0:T(8,128)} custom-call(bf16[32,5,2,128]{3,2,1,0:T(2,128)(2,1)S(1)} %all_to_all.16.near_ref, s32[2,1,1,5,8]{4,3,2,1,0:T(8,128)S(1)} %copy.8.pattern, f32[128,128]{1,0:T(8,128)S(1)} %get-tuple-element.18.map_ref, f32[36,144,128]{2,1,0:T(8,128)S(1)} %pad.1), custom_call_target="tpu_custom_call" | custom-call | tf_op jit(solution)/shard_map/second_batch/pallas_call | solution.py:383
  (1 shorter events, 0.0 us)
Async XLA Ops:
  1.7 5.3 %collective-permute-start = (f32[40,128]{1,0:T(8,128)}, f32[40,128]{1,0:T(8,128)S(1)}, u32[]{:S(2)}, u32[]{:S(2)}) collective-permute-start(f32[40,128]{1,0:T(8,128)} %get-tuple-element.13), channel_id=1, source_target_pairs={{0,1},{1,2},{2,3},{3,4},{4,5},{5,6},{6,7},{7,0},{8,9},{9,10},{10,1... | collective-permute-start | bytes 61448 | tf_op jit(solution)/shard_map/ppermute | solution.py:22
  2.3 4.8 %collective-permute-start.1 = (f32[40,128]{1,0:T(8,128)}, f32[40,128]{1,0:T(8,128)S(1)}, u32[]{:S(2)}, u32[]{:S(2)}) collective-permute-start(f32[40,128]{1,0:T(8,128)} %get-tuple-element.14), channel_id=1, source_target_pairs={{0,7},{1,0},{2,1},{3,2},{4,3},{5,4},{6,5},{7,6},{8,15},{9,8},{10,9... | collective-permute-start | bytes 61448 | tf_op jit(solution)/shard_map/ppermute | solution.py:22
  5.2 1.6 %copy-start = (f32[32,128,128]{2,1,0:T(8,128)S(1)}, f32[32,128,128]{2,1,0:T(8,128)}, u32[]{:S(2)}) copy-start(f32[32,128,128]{2,1,0:T(8,128)} %cells.3) | copy-start | bytes 6291460
  6.8 0.7 %copy-start.1 = (f32[2,8,128]{2,1,0:T(8,128)S(1)}, f32[2,8,128]{2,1,0:T(8,128)}, u32[]{:S(2)}) copy-start(f32[2,8,128]{2,1,0:T(8,128)} %get-tuple-element.12.mine) | copy-start | bytes 24580
  7.6 16.5 %copy-start.2 = (s32[2,1,1,5,8]{4,2,3,1,0:T(1,128)S(1)}, s32[2,1,1,5,8]{4,2,3,1,0:T(1,128)}, u32[]{:S(2)}) copy-start(s32[2,1,1,5,8]{4,2,3,1,0:T(1,128)} %param.13) | copy-start | bytes 964
  7.6 6.3 %collective-permute-start.2 = (f32[152,128]{1,0:T(8,128)S(1)}, f32[152,128]{1,0:T(8,128)S(1)}, u32[]{:S(2)}, u32[]{:S(2)}) collective-permute-start(f32[152,128]{1,0:T(8,128)S(1)} %get-tuple-element.15), channel_id=1, source_target_pairs={{0,8},{8,16},{16,24},{1,9},{9,17},{17,25},{2,10},{10,18},{18,26},{... | collective-permute-start | bytes 233480 | tf_op jit(solution)/shard_map/ppermute | solution.py:22
  11.9 6.3 %collective-permute-start.3 = (f32[152,128]{1,0:T(8,128)S(1)}, f32[152,128]{1,0:T(8,128)S(1)}, u32[]{:S(2)}, u32[]{:S(2)}) collective-permute-start(f32[152,128]{1,0:T(8,128)S(1)} %get-tuple-element.16), channel_id=1, source_target_pairs={{8,0},{16,8},{24,16},{9,1},{17,9},{25,17},{10,2},{18,10},{26,18},{... | collective-permute-start | bytes 233480 | tf_op jit(solution)/shard_map/ppermute | solution.py:22
  19.6 12.0 %all-to-all-start = ((bf16[32,5,2,128]{3,2,1,0:T(2,128)(2,1)}), bf16[32,5,2,128]{3,2,1,0:T(2,128)(2,1)S(1)}, u32[]{:S(2)}, u32[]{:S(2)}) async-start(bf16[32,5,2,128]{3,2,1,0:T(2,128)(2,1)} %prior.1), calls=%async_computation | async-start | bytes 163840 | tf_op jit(solution)/shard_map/all_to_all | solution.py:394

commit v2 on v1

--- a/solution.py
+++ b/solution.py
@@ -17,13 +17,21 @@
 BF16 = jnp.bfloat16
 
 
-def shifted(block, axis, step, count, wraps):
-    route = [(i, (i + step) % count) for i in range(count) if wraps or 0 <= i + step < count]
+def swap(block, axis, kind, count, wraps):
+    route = []
+    for place in range(count):
+        partner = place + (1 if place % 2 == kind else -1)
+        if wraps or 0 <= partner < count:
+            route.append((place, partner % count))
     return lax.ppermute(block, axis, route)
 
 
+def is_even(axis):
+    return lax.rem(lax.axis_index(axis), 2) == 0
+
+
 def start_kernel(
-    width, observed, precision, weight, stencil, owned, cells, params_ref, left_ref, right_ref,
+    width, observed, precision, weight, stencil, owned, cells, params_ref, sides_1, sides_0,
     observed_v, precision_v, weight_v, stencil_v, owned_v, left_v, right_v, sems
 ):
     batches, cols = (observed.shape[0], cells.shape[1])
@@ -51,10 +59,16 @@
         params_ref[b, pl.ds(AT_COL, 1), pl.ds(0, SUB)] = corner - row * width
         params_ref[b, pl.ds(AT_OBS, 1), pl.ds(0, SUB)] = observed_v[b, 0] * root
     rows = cells.shape[0]
-    left_ref[pl.ds(0, rows), :] = left_v[:, 0, :]
-    right_ref[pl.ds(0, rows), :] = right_v[:, SUB - 1, :]
-    left_ref[pl.ds(rows, SUB), :] = params_ref[1]
-    right_ref[pl.ds(rows, SUB), :] = params_ref[1]
+    even = is_even("lon")
+    left, right = (left_v[:, 0, :], right_v[:, SUB - 1, :])
+    sides_0[pl.ds(0, rows), :] = jnp.where(even, right, left)
+    sides_1[pl.ds(0, rows), :] = jnp.where(even, left, right)
+    sides_0[pl.ds(rows, SUB), :] = params_ref[1]
+    sides_1[pl.ds(rows, SUB), :] = params_ref[1]
+
+
+def hold_kernel(block, out_ref):
+    out_ref[...] = block[...]
 
 
 def clear_rim(pad, rows, cols):
@@ -117,16 +131,21 @@
         out_ref[:, n] = jnp.broadcast_to(pair, (out_ref.shape[0],) + pair.shape)
 
 
-def rows_kernel(mine, left, right, pad, first_ref, last_ref):
+def rows_kernel(mine, sides_0, sides_1, pad, left_ref, right_ref, out_0, out_1):
     rows, cols = (pad.shape[0] - 4, pad.shape[1] - 2 * SUB)
+    even = is_even("lon")
+    left_ref[...] = jnp.where(even, sides_1[...], sides_0[...])
+    right_ref[...] = jnp.where(even, sides_0[...], sides_1[...])
     lane = lax.broadcasted_iota(jnp.int32, (SUB, LANES), 1)
     block = pl.ds(rows, SUB)
-    packed = jnp.where(lane < SUB, left[block, :], pltpu.roll(mine[1], SUB, 1))
-    packed = jnp.where(lane < 2 * SUB, packed, pltpu.roll(right[block, :], 2 * SUB, 1))
-    for row, out in ((0, first_ref), (rows - 1, last_ref)):
-        out[pl.ds(0, SUB), :] = jnp.broadcast_to(left[pl.ds(row, 1), :], (SUB, LANES))
+    packed = jnp.where(lane < SUB, left_ref[block, :], pltpu.roll(mine[1], SUB, 1))
+    packed = jnp.where(lane < 2 * SUB, packed, pltpu.roll(right_ref[block, :], 2 * SUB, 1))
+    even = is_even("lat")
+    for kind, out in enumerate((out_0, out_1)):
+        row = jnp.where(even, (1 - kind) * (rows - 1), kind * (rows - 1))
+        out[pl.ds(0, SUB), :] = jnp.broadcast_to(left_ref[pl.ds(row, 1), :], (SUB, LANES))
         out[pl.ds(SUB, cols), :] = pad[2 + row, pl.ds(SUB, cols), :]
-        out[pl.ds(SUB + cols, SUB), :] = jnp.broadcast_to(right[pl.ds(row, 1), :], (SUB, LANES))
+        out[pl.ds(SUB + cols, SUB), :] = jnp.broadcast_to(right_ref[pl.ds(row, 1), :], (SUB, LANES))
         out[pl.ds(2 * SUB + cols, SUB), :] = packed
 
 
@@ -145,17 +164,20 @@
     out_ref[...] = out_ref[...] - own_shift(number)
 
 
-def prior_kernel(rows, mine, own, above, below, out_ref, value, params, sem):
+def prior_kernel(rows, mine, own, ends_0, ends_1, out_ref, ends, value, params, sem):
     copy = pltpu.make_async_copy(mine.at[0], params, sem)
     copy.start()
+    even = is_even("lat")
+    ends[0] = jnp.where(even, ends_1[...], ends_0[...])
+    ends[1] = jnp.where(even, ends_0[...], ends_1[...])
     copy.wait()
     for o in range(SUB):
         row, col = (params[AT_ROW, o].astype(jnp.int32), params[AT_COL, o].astype(jnp.int32))
         total = own[pl.ds(o, 1), :]
-        for n, (end, at) in enumerate(((above, 0), (below, rows))):
+        for n, at in enumerate((0, rows)):
             for k in range(2):
                 weight = jnp.where(row == at, params[2 * n + k, o], 0.0)
-                total = total + weight * end[pl.ds(col + SUB - 1 + k, 1), :]
+                total = total + weight * ends[n, pl.ds(col + SUB - 1 + k, 1), :]
         value[pl.ds(o, 1), :] = total
     send_block(value[...], out_ref)
 
@@ -164,19 +186,21 @@
     send_block(jnp.sum(shares[...], axis=0), out_ref)
 
 
-def later_kernel(mine, left, right, above, below, pad, out_ref, params, sems):
+def later_kernel(mine, left, right, ends_0, ends_1, pad, out_ref, params, sems):
     rows, cols = (pad.shape[0] - 4, pad.shape[1] - 2 * SUB)
     side, end = (pl.ds(rows, SUB), pl.ds(cols + 2 * SUB, SUB))
-    sources = (left.at[side], mine.at[1], right.at[side], above.at[end], below.at[end])
+    sources = (left.at[side], mine.at[1], right.at[side], ends_0.at[end], ends_1.at[end])
     copies = []
     for n, source in enumerate(sources):
         copies.append(pltpu.make_async_copy(source, params.at[n], sems.at[n]))
         copies[-1].start()
     for copy in copies:
         copy.wait()
+    even = is_even("lat")
+    ends = {-1: jnp.where(even, 4, 3), 1: jnp.where(even, 3, 4)}
     for n, dc in enumerate(NEAR):
         for m, da in enumerate(NEAR):
-            spot, lane = (n, 0) if da == 0 else (len(NEAR) + m // 2, n * SUB)
+            spot, lane = (n, 0) if da == 0 else (ends[da], n * SUB)
             number = lambda kind, o: params[spot, kind, lane + o]
             for o in range(SUB):
                 out_ref[n * len(NEAR) + m, pl.ds(o, 1), :] = share(pad, number, rows, cols, da, dc, o)
@@ -207,7 +231,7 @@
     at = {(r, n): column_of(rows[r], k * SUB + n) for r in range(SUB) for n in range(r + 1)}
     here = (lane >= 0) & (lane < SUB)
     rows = [jnp.where(here, jnp.where(lane == r, 1.0, 0.0), row) for r, row in enumerate(rows)]
-    inverse = jnp.zeros(block.shape, F32)
+    inverse, scale = (jnp.zeros(block.shape, F32), jnp.ones(block.shape, F32))
     for j in range(0, SUB, 2):
         a, b, c = (at[j, j], at[j + 1, j], at[j + 1, j + 1])
         det = a * c - b * b
@@ -233,11 +257,10 @@
             at[j + 1, n] = a_part * upper[n][1] - b_part * upper[n][0]
         rows[j] = c_part * top - b_part * bottom
         rows[j + 1] = a_part * bottom - b_part * top
-        over_a = reciprocal(a)
-        inverse = jnp.where(sub == j, lax.rsqrt(a) * top, inverse)
-        inverse = jnp.where(sub == j + 1, lax.rsqrt(det * over_a) * (bottom - b * over_a * top), inverse)
+        inverse = jnp.where(sub == j, top, jnp.where(sub == j + 1, a * bottom - b * top, inverse))
+        scale = jnp.where(sub == j, a, jnp.where(sub == j + 1, a * det, scale))
         between()
-    return rows, jnp.where(lane < SUB, inverse, 0.0)
+    return rows, jnp.where(lane < SUB, inverse * lax.rsqrt(scale), 0.0)
 
 
 def eliminate(blocks):
@@ -332,9 +355,18 @@
                 out_ref[lat * lon_count + lon] = moved[n * len(NEAR) + m]
 
 
-def last_kernel(lat_count, near_ref, pattern, map_ref, pad, out_ref, result, out_sem):
+def halves_kernel(pad, out_ref):
+    rows, cols = (pad.shape[0] - 4, pad.shape[1] - 2 * SUB)
+    for row in range(rows):
+        value = pad[2 + row, pl.ds(SUB, cols), :]
+        upper = value.astype(BF16)
+        lower = (value - upper.astype(F32)).astype(BF16)
+        out_ref[pl.ds(row * cols, cols), :] = jnp.concatenate([upper, lower], axis=1)
+
+
+def last_kernel(lat_count, near_ref, pattern, map_ref, halves, out_ref, result, out_sem):
     parts = out_sem.shape[0]
-    rows, cols = (pad.shape[0] - 4, pad.shape[1] - 2 * SUB)
+    rows = result.shape[0] // parts
     flipped = exact_dot(batch_map(1, lat_count, near_ref, pattern), map_ref[...], 0)
     high = flipped.astype(BF16)
     low = (flipped - high.astype(F32)).astype(BF16)
@@ -342,15 +374,9 @@
         [jnp.concatenate([high, high], axis=1), jnp.concatenate([low, jnp.zeros_like(low)], axis=1)], axis=0
     )
     copies = []
-    size = rows // parts
     for n in range(parts):
-        part = pl.ds(n * size * cols, size * cols)
-        value = pad[pl.ds(2 + n * size, size), pl.ds(SUB, cols), :].reshape(size * cols, LANES)
-        upper = value.astype(BF16)
-        rest = (value - upper.astype(F32)).astype(BF16)
-        both = lax.dot_general(
-            jnp.concatenate([upper, rest], axis=1), right, (((1,), (1,)), ((), ())), preferred_element_type=F32
-        )
+        part = pl.ds(n * rows, rows)
+        both = lax.dot_general(halves[part, :], right, (((1,), (1,)), ((), ())), preferred_element_type=F32)
         result[part, :] = both[:, :LANES] + both[:, LANES:]
         copies.append(pltpu.make_async_copy(result.at[part], out_ref.at[part], out_sem.at[n]))
         copies[-1].start()
@@ -390,12 +416,18 @@
             name=name,
         )(*operands)
 
+    def trade(blocks, axis):
+        count, wraps = ((lon_count, True) if axis == "lon" else (lat_count, False))
+        first, second = blocks
+        second = swap(second, axis, 1, count, wraps)
+        return [swap(first, axis, 0, count, wraps), second]
+
     def exchange(blocks):
         return lax.all_to_all(blocks, ("lat", "lon"), split_axis=0, concat_axis=0, tiled=True)
 
     small = (observed, precision, interp_weight, stencil, owned)
     side = shape(rows + SUB, members)
-    mine, left, right = call(
+    mine, side_1, side_0 = call(
         functools.partial(start_kernel, cols + 2),
         "start",
         [hbm] * 6,
@@ -407,23 +439,24 @@
         ensemble,
         limit=63,
     )
-    sides = (shifted(right, "lon", 1, lon_count, True), shifted(left, "lon", -1, lon_count, True))
+    side_0 = call(hold_kernel, "hold", [vmem], side, [], side_0)
+    sides = trade((side_0, side_1), "lon")
     padded = shape(rows + 4, cols + 2 * SUB, members)
     pad = call(pad_kernel, "pad", [hbm], padded, [pltpu.SemaphoreType.DMA], ensemble)
     end = shape(cols + 3 * SUB, members)
-    first, last = call(rows_kernel, "edge_rows", [vmem] * 4, (end, end), [], mine, *sides, pad)
-    ends = (shifted(last, "lat", 1, lat_count, False), shifted(first, "lat", -1, lat_count, False))
+    left, right, *ends = call(rows_kernel, "edge_rows", [vmem] * 4, (side, side, end, end), [], mine, *sides, pad)
+    ends = trade(ends, "lat")
     slots = shape(tiles, PAIRS, 2, members, dtype=BF16)
     numbers = [pltpu.SMEM((SUB, LANES), F32), pltpu.SemaphoreType.DMA]
     block = shape(SUB, members)
     held_sides = pltpu.VMEM((2, rows + 2 * SUB, members), F32)
-    own = call(row_kernel, "row_shares", [vmem] * 4, block, [held_sides] + numbers, mine, *sides, pad)
+    own = call(row_kernel, "row_shares", [vmem] * 4, block, [held_sides] + numbers, mine, left, right, pad)
     blocks = call(
         functools.partial(prior_kernel, rows),
         "prior",
         [vmem] * 4,
         slots,
-        [pltpu.VMEM((SUB, members), F32)] + numbers,
+        [pltpu.VMEM((2,) + end.shape, F32), pltpu.VMEM((SUB, members), F32)] + numbers,
         mine,
         own,
         *ends,
@@ -437,10 +470,12 @@
         shape(count + 1, SUB, members),
         [pltpu.SMEM((5, SUB, LANES), F32), pltpu.SemaphoreType.DMA((5,))],
         mine,
-        *sides,
+        left,
+        right,
         *ends,
         pad,
     )
+    halves = call(halves_kernel, "halves", [vmem], shape(rows * cols, 2 * members, dtype=BF16), [], pad)
     first_map, shares = call(
         functools.partial(first_kernel, lat_count, lon_count),
         "first_batch",
@@ -466,7 +501,7 @@
         near,
         pattern,
         first_map,
-        pad,
+        halves,
         out_specs=anywhere,
     )
     return result.reshape(rows, cols, members)

time: 63.7 us -> 65.2 us (1.024)
  blocking collectives: 19.2 us -> 9.93 us
  local copies, waits for them, and re-layouts: 2.06 us -> 5.69 us
  waiting for transfers between devices: 10.4 us -> 13.5 us
  starting transfers between devices: 13.4 us -> 16.4 us
  Pallas kernels: 18.1 us -> 19.2 us
    all_to_all x2 -> x1, blocking collectives: 19.2 us -> 9.93 us  [exchange(): lax.all_to_all(blocks, ('lat', 'lon'), split_axis=0, concat_axis=0, tiled...]
    all_to_all x1 -> x2, waiting for transfers between devices: 6.11 us -> 12 us  [exchange(): lax.all_to_all(blocks, ('lat', 'lon'), split_axis=0, concat_axis=0, tiled...]
    all_to_all x1 -> x2, starting transfers between devices: 4.41 us -> 10.1 us  [exchange(): lax.all_to_all(blocks, ('lat', 'lon'), split_axis=0, concat_axis=0, tiled...]
    unnamed x7 -> x13, local copies, waits for them, and re-layouts: 2.06 us -> 5.69 us
    ppermute x4, waiting for transfers between devices: 4.28 us -> 1.46 us  [swap(): return lax.ppermute(block, axis, route)]
    ppermute x4, starting transfers between devices: 9.04 us -> 6.27 us  [swap(): return lax.ppermute(block, axis, route)]
    pallas_call x9 -> x11, Pallas kernels: 18.1 us -> 19.2 us  [call(): pl.pallas_call(kernel, out_shape=out_shape, in_specs=specs, out_specs=out...]
  transfers between devices with their start and end apart: 5 -> 6, of which waited for: 2 -> 3; matrix products, arithmetic and copies ran while one was open for 0% -> 0% of each run, Pallas kernels for 4% -> 4%
where the time goes in v2:
time: 65.2 us; the launch traced here: 64.8 us
  Pallas kernels  19.2 us (29%)
  starting transfers between devices  16.4 us (25%)
  waiting for transfers between devices  13.5 us (21%)
  blocking collectives  9.93 us (15%)
  local copies, waits for them, and re-layouts  5.69 us (9%)
    pallas_call x11, Pallas kernels, call(): pl.pallas_call(kernel, out_shape=out_shape, in_specs=specs, out_specs=out...  19.2 us
    all_to_all x2, waiting for transfers between devices, exchange(): lax.all_to_all(blocks, ('lat', 'lon'), split_axis=0, concat_axis=0, tiled...  12 us
    all_to_all x2, starting transfers between devices, exchange(): lax.all_to_all(blocks, ('lat', 'lon'), split_axis=0, concat_axis=0, tiled...  10.1 us
    all_to_all x1, blocking collectives, exchange(): lax.all_to_all(blocks, ('lat', 'lon'), split_axis=0, concat_axis=0, tiled...  9.93 us
    ppermute x4, starting transfers between devices, swap(): return lax.ppermute(block, axis, route)  6.27 us
    unnamed x13, local copies, waits for them, and re-layouts  5.69 us
    ppermute x4, waiting for transfers between devices, swap(): return lax.ppermute(block, axis, route)  1.46 us
  transfers between devices with their start and end apart: 6, of which 3 were waited for; matrix products, arithmetic and copies ran while one was open for 0% of the time, Pallas kernels for 4%

profile of v2, /device:TPU:0, one launch (start us, length us, event | category | flops | bytes accessed | tf_op | source)
XLA Modules:
  0.0 64.8 jit_solution(8844929802129260675)
XLA Ops:
  0.0 1.8 %start.1 = (f32[2,8,128]{2,1,0:T(8,128)}, f32[40,128]{1,0:T(8,128)}, f32[40,128]{1,0:T(8,128)}) custom-call(f32[2,1,1,8]{3,2,1,0:T(1,128)} %observed.1, f32[2,1,1,8]{3,2,1,0:T(1,128)} %precision.1, f32[2,1,1,4,8]{4,3,2,1,0:T(4,128)} %weight.1, s32[2,1,1,4,8]{4,3,2,1,0:T(4,128)} %stencil.1, s32[2,1,1,8]{3,2,1,0:T(1,128)} %owned.1, f32[32,128,128]{2,1,0:T(8,128)} %cells.3), custom_call_target="tpu_custom_call" | custom-call | tf_op jit(solution)/shard_map/start/pallas_call | solution.py:409
  1.8 0.0 copy-start.4
  1.8 0.7 %copy-done.4 = f32[40,128]{1,0:T(8,128)S(1)} copy-done((f32[40,128]{1,0:T(8,128)S(1)}, f32[40,128]{1,0:T(8,128)}, u32[]{:S(2)}) %copy-start.4) | copy-done | bytes 20504
  2.5 0.5 collective-permute-start
  2.9 3.6 %collective-permute-start.1 = (f32[40,128]{1,0:T(8,128)}, f32[40,128]{1,0:T(8,128)S(1)}, u32[]{:S(2)}, u32[]{:S(2)}) collective-permute-start(f32[40,128]{1,0:T(8,128)} %get-tuple-element.16), channel_id=1, source_target_pairs={{0,7},{1,2},{2,1},{3,4},{4,3},{5,6},{6,5},{7,0},{8,15},{9,10},{10,... | collective-permute-start | bytes 61448 | tf_op jit(solution)/shard_map/ppermute | solution.py:26
  6.5 0.0 copy-start
  6.5 1.6 %copy-done = f32[32,128,128]{2,1,0:T(8,128)S(1)} copy-done((f32[32,128,128]{2,1,0:T(8,128)S(1)}, f32[32,128,128]{2,1,0:T(8,128)}, u32[]{:S(2)}) %copy-start) | copy-done | bytes 2097176
  8.1 0.0 copy-start.3
  8.1 0.2 pad.1
  8.3 0.0 collective-permute-done.sides_0
  8.3 0.0 collective-permute-done.1.sides_1
  8.3 0.5 copy-done.3
  8.8 0.1 edge_rows.1
  8.9 0.0 copy-start.5
  8.9 1.6 %collective-permute-start.2 = (f32[152,128]{1,0:T(8,128)S(1)}, f32[152,128]{1,0:T(8,128)S(1)}, u32[]{:S(2)}, u32[]{:S(2)}) collective-permute-start(f32[152,128]{1,0:T(8,128)S(1)} %get-tuple-element.19), channel_id=1, source_target_pairs={{0,8},{8,0},{16,24},{24,16},{1,9},{9,1},{17,25},{25,17},{2,10},{10... | collective-permute-start | bytes 233480 | tf_op jit(solution)/shard_map/ppermute | solution.py:26
  10.5 0.7 %collective-permute-start.3 = (f32[152,128]{1,0:T(8,128)S(1)}, f32[152,128]{1,0:T(8,128)S(1)}, u32[]{:S(2)}, u32[]{:S(2)}) collective-permute-start(f32[152,128]{1,0:T(8,128)S(1)} %get-tuple-element.20), channel_id=1, source_target_pairs={{8,16},{16,8},{9,17},{17,9},{10,18},{18,10},{11,19},{19,11},{12,20... | collective-permute-start | bytes 233480 | tf_op jit(solution)/shard_map/ppermute | solution.py:26
  11.1 0.7 %row_shares.1.own = f32[8,128]{1,0:T(8,128)S(1)} custom-call(f32[2,8,128]{2,1,0:T(8,128)S(1)} %copy-done.3, f32[40,128]{1,0:T(8,128)S(1)} %get-tuple-element.17.left, f32[40,128]{1,0:T(8,128)S(1)} %get-tuple-element.18.right, f32[36,144,128]{2,1,0:T(8,128)S(1)} %pad.1), custom_call_target="tpu_custom_call" | custom-call | tf_op jit(solution)/shard_map/row_shares/pallas_call | solution.py:409
  11.8 1.4 %collective-permute-done.2.ends_0 = f32[152,128]{1,0:T(8,128)S(1)} collective-permute-done((f32[152,128]{1,0:T(8,128)S(1)}, f32[152,128]{1,0:T(8,128)S(1)}, u32[]{:S(2)}, u32[]{:S(2)}) %collective-permute-start.2) | collective-permute-done | bytes 77856 | tf_op jit(solution)/shard_map/ppermute | solution.py:26
  13.3 0.0 collective-permute-done.3.ends_1
  13.3 1.4 %prior.1 = bf16[32,5,2,128]{3,2,1,0:T(2,128)(2,1)} custom-call(f32[2,8,128]{2,1,0:T(8,128)S(1)} %copy-done.3, f32[8,128]{1,0:T(8,128)S(1)} %row_shares.1.own, f32[152,128]{1,0:T(8,128)S(1)} %collective-permute-done.2.ends_0, f32[152,128]{1,0:T(8,128)S(1)} %collective-permute-done.3.ends_1), custom_call_target="tpu_custom_call" | custom-call | tf_op jit(solution)/shard_map/prior/pallas_call | solution.py:409
  14.7 7.5 %all-to-all-start = ((bf16[32,5,2,128]{3,2,1,0:T(2,128)(2,1)}), bf16[32,5,2,128]{3,2,1,0:T(2,128)(2,1)S(1)}, u32[]{:S(2)}, u32[]{:S(2)}) async-start(bf16[32,5,2,128]{3,2,1,0:T(2,128)(2,1)} %prior.1), calls=%async_computation | async-start | bytes 163840 | tf_op jit(solution)/shard_map/all_to_all | solution.py:426
  22.3 0.0 copy-done.5
  22.3 1.6 %later_shares.1.later = f32[10,8,128]{2,1,0:T(8,128)S(1)} custom-call(f32[2,8,128]{2,1,0:T(8,128)S(1)} %copy-done.3, f32[40,128]{1,0:T(8,128)S(1)} %get-tuple-element.17.left, f32[40,128]{1,0:T(8,128)S(1)} %get-tuple-element.18.right, f32[152,128]{1,0:T(8,128)S(1)} %collective-permute-done.2.ends_0, f32[152,128]{1,0:T(8,128)S(1)} %collective-permute-done.3.ends_1, ...), custom_call_target="tpu_custom_call" | custom-call | tf_op jit(solution)/shard_map/later_shares/pallas_call | solution.py:409
  23.9 6.0 %all-to-all-done.near_ref = bf16[32,5,2,128]{3,2,1,0:T(2,128)(2,1)S(1)} async-done(((bf16[32,5,2,128]{3,2,1,0:T(2,128)(2,1)}), bf16[32,5,2,128]{3,2,1,0:T(2,128)(2,1)S(1)}, u32[]{:S(2)}, u32[]{:S(2)}) %all-to-all-start) | async-done | bytes 81952 | tf_op jit(solution)/shard_map/all_to_all | solution.py:426
  29.9 5.4 %first_batch.1 = (f32[128,128]{1,0:T(8,128)S(1)}, f32[32,8,128]{2,1,0:T(8,128)S(1)}) custom-call(bf16[32,5,2,128]{3,2,1,0:T(2,128)(2,1)S(1)} %all-to-all-done.near_ref, s32[2,1,1,5,8]{4,3,2,1,0:T(8,128)S(1)} %copy.8.pattern, f32[10,8,128]{2,1,0:T(8,128)S(1)} %later_shares.1.later), custom_call_target="tpu_custom_call" | custom-call | tf_op jit(solution)/shard_map/first_batch/pallas_call | solution.py:409
  35.3 9.9 %all_to_all.15.shares = f32[32,8,128]{2,1,0:T(8,128)S(1)} all-to-all(f32[32,8,128]{2,1,0:T(8,128)S(1)} %get-tuple-element.21), channel_id=1, replica_groups=mesh['lat'=4,'lon'=8] {'lat','lon'}, dimensions={0} | all-to-all | bytes 262144 | tf_op jit(solution)/shard_map/all_to_all | solution.py:426
  45.3 0.8 %own_block.1 = bf16[32,5,2,128]{3,2,1,0:T(2,128)(2,1)} custom-call(f32[32,8,128]{2,1,0:T(8,128)S(1)} %all_to_all.15.shares), custom_call_target="tpu_custom_call" | custom-call | tf_op jit(solution)/shard_map/own_block/pallas_call | solution.py:409
  46.1 2.6 %all-to-all-start.2 = ((bf16[32,5,2,128]{3,2,1,0:T(2,128)(2,1)}), bf16[32,5,2,128]{3,2,1,0:T(2,128)(2,1)S(1)}, u32[]{:S(2)}, u32[]{:S(2)}) async-start(bf16[32,5,2,128]{3,2,1,0:T(2,128)(2,1)} %own_block.1), calls=%async_computation.2 | async-start | bytes 163840 | tf_op jit(solution)/shard_map/all_to_all | solution.py:426
  48.6 0.3 halves.1
  48.9 0.0 copy-start.1
  48.9 1.3 %copy-done.1 = bf16[4096,256]{1,0:T(8,128)(2,1)} copy-done((bf16[4096,256]{1,0:T(8,128)(2,1)}, bf16[4096,256]{1,0:T(8,128)(2,1)S(1)}, u32[]{:S(2)}) %copy-start.1) | copy-done | bytes 2097176
  50.2 6.0 %all-to-all-done.2.near_ref = bf16[32,5,2,128]{3,2,1,0:T(2,128)(2,1)S(1)} async-done(((bf16[32,5,2,128]{3,2,1,0:T(2,128)(2,1)}), bf16[32,5,2,128]{3,2,1,0:T(2,128)(2,1)S(1)}, u32[]{:S(2)}, u32[]{:S(2)}) %all-to-all-start.2) | async-done | bytes 81952 | tf_op jit(solution)/shard_map/all_to_all | solution.py:426
  56.2 0.0 copy-start.2
  56.2 1.6 %copy-done.2 = bf16[4096,256]{1,0:T(8,128)(2,1)S(1)} copy-done((bf16[4096,256]{1,0:T(8,128)(2,1)S(1)}, bf16[4096,256]{1,0:T(8,128)(2,1)}, u32[]{:S(2)}) %copy-start.2) | copy-done | bytes 2097176
  57.8 6.9 %second_batch.1 = f32[4096,128]{1,0:T(8,128)} custom-call(bf16[32,5,2,128]{3,2,1,0:T(2,128)(2,1)S(1)} %all-to-all-done.2.near_ref, s32[2,1,1,5,8]{4,3,2,1,0:T(8,128)S(1)} %copy.8.pattern, f32[128,128]{1,0:T(8,128)S(1)} %get-tuple-element.22.map_ref, bf16[4096,256]{1,0:T(8,128)(2,1)S(1)} %copy-done.2), custom_call_target="tpu_custom_call" | custom-call | tf_op jit(solution)/shard_map/second_batch/pallas_call | solution.py:409
  (2 shorter events, 0.0 us)
Async XLA Ops:
  1.8 0.7 %copy-start.4 = (f32[40,128]{1,0:T(8,128)S(1)}, f32[40,128]{1,0:T(8,128)}, u32[]{:S(2)}) copy-start(f32[40,128]{1,0:T(8,128)} %get-tuple-element.15.block) | copy-start | bytes 61444
  2.5 5.8 %collective-permute-start = (f32[40,128]{1,0:T(8,128)S(1)}, f32[40,128]{1,0:T(8,128)S(1)}, u32[]{:S(2)}, u32[]{:S(2)}) collective-permute-start(f32[40,128]{1,0:T(8,128)S(1)} %hold.1), channel_id=1, source_target_pairs={{0,1},{1,0},{2,3},{3,2},{4,5},{5,4},{6,7},{7,6},{8,9},{9,8},{10,11... | collective-permute-start | bytes 61448 | tf_op jit(solution)/shard_map/ppermute | solution.py:26
  2.9 5.4 %collective-permute-start.1 = (f32[40,128]{1,0:T(8,128)}, f32[40,128]{1,0:T(8,128)S(1)}, u32[]{:S(2)}, u32[]{:S(2)}) collective-permute-start(f32[40,128]{1,0:T(8,128)} %get-tuple-element.16), channel_id=1, source_target_pairs={{0,7},{1,2},{2,1},{3,4},{4,3},{5,6},{6,5},{7,0},{8,15},{9,10},{10,... | collective-permute-start | bytes 61448 | tf_op jit(solution)/shard_map/ppermute | solution.py:26
  6.5 1.6 %copy-start = (f32[32,128,128]{2,1,0:T(8,128)S(1)}, f32[32,128,128]{2,1,0:T(8,128)}, u32[]{:S(2)}) copy-start(f32[32,128,128]{2,1,0:T(8,128)} %cells.3) | copy-start | bytes 6291460
  8.1 0.7 %copy-start.3 = (f32[2,8,128]{2,1,0:T(8,128)S(1)}, f32[2,8,128]{2,1,0:T(8,128)}, u32[]{:S(2)}) copy-start(f32[2,8,128]{2,1,0:T(8,128)} %get-tuple-element.14.mine) | copy-start | bytes 24580
  8.9 13.4 %copy-start.5 = (s32[2,1,1,5,8]{4,2,3,1,0:T(1,128)S(1)}, s32[2,1,1,5,8]{4,2,3,1,0:T(1,128)}, u32[]{:S(2)}) copy-start(s32[2,1,1,5,8]{4,2,3,1,0:T(1,128)} %param.13) | copy-start | bytes 964
  8.9 4.4 %collective-permute-start.2 = (f32[152,128]{1,0:T(8,128)S(1)}, f32[152,128]{1,0:T(8,128)S(1)}, u32[]{:S(2)}, u32[]{:S(2)}) collective-permute-start(f32[152,128]{1,0:T(8,128)S(1)} %get-tuple-element.19), channel_id=1, source_target_pairs={{0,8},{8,0},{16,24},{24,16},{1,9},{9,1},{17,25},{25,17},{2,10},{10... | collective-permute-start | bytes 233480 | tf_op jit(solution)/shard_map/ppermute | solution.py:26
  10.5 2.8 %collective-permute-start.3 = (f32[152,128]{1,0:T(8,128)S(1)}, f32[152,128]{1,0:T(8,128)S(1)}, u32[]{:S(2)}, u32[]{:S(2)}) collective-permute-start(f32[152,128]{1,0:T(8,128)S(1)} %get-tuple-element.20), channel_id=1, source_target_pairs={{8,16},{16,8},{9,17},{17,9},{10,18},{18,10},{11,19},{19,11},{12,20... | collective-permute-start | bytes 233480 | tf_op jit(solution)/shard_map/ppermute | solution.py:26
  14.7 15.2 %all-to-all-start = ((bf16[32,5,2,128]{3,2,1,0:T(2,128)(2,1)}), bf16[32,5,2,128]{3,2,1,0:T(2,128)(2,1)S(1)}, u32[]{:S(2)}, u32[]{:S(2)}) async-start(bf16[32,5,2,128]{3,2,1,0:T(2,128)(2,1)} %prior.1), calls=%async_computation | async-start | bytes 163840 | tf_op jit(solution)/shard_map/all_to_all | solution.py:426
  46.1 10.2 %all-to-all-start.2 = ((bf16[32,5,2,128]{3,2,1,0:T(2,128)(2,1)}), bf16[32,5,2,128]{3,2,1,0:T(2,128)(2,1)S(1)}, u32[]{:S(2)}, u32[]{:S(2)}) async-start(bf16[32,5,2,128]{3,2,1,0:T(2,128)(2,1)} %own_block.1), calls=%async_computation.2 | async-start | bytes 163840 | tf_op jit(solution)/shard_map/all_to_all | solution.py:426
  48.9 1.3 %copy-start.1 = (bf16[4096,256]{1,0:T(8,128)(2,1)}, bf16[4096,256]{1,0:T(8,128)(2,1)S(1)}, u32[]{:S(2)}) copy-start(bf16[4096,256]{1,0:T(8,128)(2,1)S(1)} %halves.1) | copy-start | bytes 6291460
  56.2 1.6 %copy-start.2 = (bf16[4096,256]{1,0:T(8,128)(2,1)S(1)}, bf16[4096,256]{1,0:T(8,128)(2,1)}, u32[]{:S(2)}) copy-start(bf16[4096,256]{1,0:T(8,128)(2,1)} %copy-done.1) | copy-start | bytes 6291460

commit v3 on v2

--- a/solution.py
+++ b/solution.py
@@ -65,10 +65,6 @@
     sides_1[pl.ds(0, rows), :] = jnp.where(even, left, right)
     sides_0[pl.ds(rows, SUB), :] = params_ref[1]
     sides_1[pl.ds(rows, SUB), :] = params_ref[1]
-
-
-def hold_kernel(block, out_ref):
-    out_ref[...] = block[...]
 
 
 def clear_rim(pad, rows, cols):
@@ -355,18 +351,9 @@
                 out_ref[lat * lon_count + lon] = moved[n * len(NEAR) + m]
 
 
-def halves_kernel(pad, out_ref):
+def last_kernel(lat_count, near_ref, pattern, map_ref, pad, out_ref, result, out_sem):
+    parts = out_sem.shape[0]
     rows, cols = (pad.shape[0] - 4, pad.shape[1] - 2 * SUB)
-    for row in range(rows):
-        value = pad[2 + row, pl.ds(SUB, cols), :]
-        upper = value.astype(BF16)
-        lower = (value - upper.astype(F32)).astype(BF16)
-        out_ref[pl.ds(row * cols, cols), :] = jnp.concatenate([upper, lower], axis=1)
-
-
-def last_kernel(lat_count, near_ref, pattern, map_ref, halves, out_ref, result, out_sem):
-    parts = out_sem.shape[0]
-    rows = result.shape[0] // parts
     flipped = exact_dot(batch_map(1, lat_count, near_ref, pattern), map_ref[...], 0)
     high = flipped.astype(BF16)
     low = (flipped - high.astype(F32)).astype(BF16)
@@ -374,9 +361,15 @@
         [jnp.concatenate([high, high], axis=1), jnp.concatenate([low, jnp.zeros_like(low)], axis=1)], axis=0
     )
     copies = []
+    size = rows // parts
     for n in range(parts):
-        part = pl.ds(n * rows, rows)
-        both = lax.dot_general(halves[part, :], right, (((1,), (1,)), ((), ())), preferred_element_type=F32)
+        part = pl.ds(n * size * cols, size * cols)
+        value = pad[pl.ds(2 + n * size, size), pl.ds(SUB, cols), :].reshape(size * cols, LANES)
+        upper = value.astype(BF16)
+        rest = (value - upper.astype(F32)).astype(BF16)
+        both = lax.dot_general(
+            jnp.concatenate([upper, rest], axis=1), right, (((1,), (1,)), ((), ())), preferred_element_type=F32
+        )
         result[part, :] = both[:, :LANES] + both[:, LANES:]
         copies.append(pltpu.make_async_copy(result.at[part], out_ref.at[part], out_sem.at[n]))
         copies[-1].start()
@@ -439,7 +432,6 @@
         ensemble,
         limit=63,
     )
-    side_0 = call(hold_kernel, "hold", [vmem], side, [], side_0)
     sides = trade((side_0, side_1), "lon")
     padded = shape(rows + 4, cols + 2 * SUB, members)
     pad = call(pad_kernel, "pad", [hbm], padded, [pltpu.SemaphoreType.DMA], ensemble)
@@ -475,7 +467,6 @@
         *ends,
         pad,
     )
-    halves = call(halves_kernel, "halves", [vmem], shape(rows * cols, 2 * members, dtype=BF16), [], pad)
     first_map, shares = call(
         functools.partial(first_kernel, lat_count, lon_count),
         "first_batch",
@@ -501,7 +492,7 @@
         near,
         pattern,
         first_map,
-        halves,
+        pad,
         out_specs=anywhere,
     )
     return result.reshape(rows, cols, members)

time: 65.2 us -> 61.5 us (0.943)
  blocking collectives: 9.93 us -> 19.2 us
  waiting for transfers between devices: 13.5 us -> 7.46 us
  local copies, waits for them, and re-layouts: 5.69 us -> 2.06 us
  starting transfers between devices: 16.4 us -> 14 us
  Pallas kernels: 19.2 us -> 18.3 us
    all_to_all x1 -> x2, blocking collectives: 9.93 us -> 19.2 us  [exchange(): lax.all_to_all(blocks, ('lat', 'lon'), split_axis=0, concat_axis=0, tiled...]
    all_to_all x2 -> x1, waiting for transfers between devices: 12 us -> 6 us  [exchange(): lax.all_to_all(blocks, ('lat', 'lon'), split_axis=0, concat_axis=0, tiled...]
    unnamed x13 -> x7, local copies, waits for them, and re-layouts: 5.69 us -> 2.06 us
    all_to_all x2 -> x1, starting transfers between devices: 10.1 us -> 7.7 us  [exchange(): lax.all_to_all(blocks, ('lat', 'lon'), split_axis=0, concat_axis=0, tiled...]
    pallas_call x11 -> x9, Pallas kernels: 19.2 us -> 18.3 us  [call(): pl.pallas_call(kernel, out_shape=out_shape, in_specs=specs, out_specs=out...]
  transfers between devices with their start and end apart: 6 -> 5, of which waited for: 3 -> 2; matrix products, arithmetic and copies ran while one was open for 0% -> 0% of each run, Pallas kernels for 4% -> 4%
where the time goes in v3:
time: 61.5 us; the launch traced here: 61.2 us
  blocking collectives  19.2 us (31%)
  Pallas kernels  18.3 us (30%)
  starting transfers between devices  14 us (23%)
  waiting for transfers between devices  7.46 us (12%)
  local copies, waits for them, and re-layouts  2.06 us (3%)
    all_to_all x2, blocking collectives, exchange(): lax.all_to_all(blocks, ('lat', 'lon'), split_axis=0, concat_axis=0, tiled...  19.2 us
    pallas_call x9, Pallas kernels, call(): pl.pallas_call(kernel, out_shape=out_shape, in_specs=specs, out_specs=out...  18.3 us
    all_to_all x1, starting transfers between devices, exchange(): lax.all_to_all(blocks, ('lat', 'lon'), split_axis=0, concat_axis=0, tiled...  7.7 us
    ppermute x4, starting transfers between devices, swap(): return lax.ppermute(block, axis, route)  6.33 us
    all_to_all x1, waiting for transfers between devices, exchange(): lax.all_to_all(blocks, ('lat', 'lon'), split_axis=0, concat_axis=0, tiled...  6 us
    unnamed x7, local copies, waits for them, and re-layouts  2.06 us
    ppermute x4, waiting for transfers between devices, swap(): return lax.ppermute(block, axis, route)  1.46 us
  transfers between devices with their start and end apart: 5, of which 2 were waited for; matrix products, arithmetic and copies ran while one was open for 0% of the time, Pallas kernels for 4%

profile of v3, /device:TPU:0, one launch (start us, length us, event | category | flops | bytes accessed | tf_op | source)
XLA Modules:
  0.0 61.2 jit_solution(16416073449867918361)
XLA Ops:
  0.0 1.8 %start.1 = (f32[2,8,128]{2,1,0:T(8,128)}, f32[40,128]{1,0:T(8,128)}, f32[40,128]{1,0:T(8,128)}) custom-call(f32[2,1,1,8]{3,2,1,0:T(1,128)} %observed.1, f32[2,1,1,8]{3,2,1,0:T(1,128)} %precision.1, f32[2,1,1,4,8]{4,3,2,1,0:T(4,128)} %weight.1, s32[2,1,1,4,8]{4,3,2,1,0:T(4,128)} %stencil.1, s32[2,1,1,8]{3,2,1,0:T(1,128)} %owned.1, f32[32,128,128]{2,1,0:T(8,128)} %cells.3), custom_call_target="tpu_custom_call" | custom-call | tf_op jit(solution)/shard_map/start/pallas_call | solution.py:402
  1.8 0.5 collective-permute-start
  2.3 3.6 %collective-permute-start.1 = (f32[40,128]{1,0:T(8,128)}, f32[40,128]{1,0:T(8,128)S(1)}, u32[]{:S(2)}, u32[]{:S(2)}) collective-permute-start(f32[40,128]{1,0:T(8,128)} %get-tuple-element.16), channel_id=1, source_target_pairs={{0,7},{1,2},{2,1},{3,4},{4,3},{5,6},{6,5},{7,0},{8,15},{9,10},{10,... | collective-permute-start | bytes 61448 | tf_op jit(solution)/shard_map/ppermute | solution.py:26
  5.8 0.0 copy-start
  5.8 1.6 %copy-done = f32[32,128,128]{2,1,0:T(8,128)S(1)} copy-done((f32[32,128,128]{2,1,0:T(8,128)S(1)}, f32[32,128,128]{2,1,0:T(8,128)}, u32[]{:S(2)}) %copy-start) | copy-done | bytes 2097176
  7.4 0.0 copy-start.1
  7.4 0.2 pad.1
  7.6 0.0 collective-permute-done.sides_0
  7.7 0.0 collective-permute-done.1.sides_1
  7.7 0.5 copy-done.1
  8.1 0.1 edge_rows.1
  8.2 0.0 copy-start.2
  8.2 1.6 %collective-permute-start.2 = (f32[152,128]{1,0:T(8,128)S(1)}, f32[152,128]{1,0:T(8,128)S(1)}, u32[]{:S(2)}, u32[]{:S(2)}) collective-permute-start(f32[152,128]{1,0:T(8,128)S(1)} %get-tuple-element.19), channel_id=1, source_target_pairs={{0,8},{8,0},{16,24},{24,16},{1,9},{9,1},{17,25},{25,17},{2,10},{10... | collective-permute-start | bytes 233480 | tf_op jit(solution)/shard_map/ppermute | solution.py:26
  9.8 0.7 %collective-permute-start.3 = (f32[152,128]{1,0:T(8,128)S(1)}, f32[152,128]{1,0:T(8,128)S(1)}, u32[]{:S(2)}, u32[]{:S(2)}) collective-permute-start(f32[152,128]{1,0:T(8,128)S(1)} %get-tuple-element.20), channel_id=1, source_target_pairs={{8,16},{16,8},{9,17},{17,9},{10,18},{18,10},{11,19},{19,11},{12,20... | collective-permute-start | bytes 233480 | tf_op jit(solution)/shard_map/ppermute | solution.py:26
  10.5 0.7 %row_shares.1.own = f32[8,128]{1,0:T(8,128)S(1)} custom-call(f32[2,8,128]{2,1,0:T(8,128)S(1)} %copy-done.1, f32[40,128]{1,0:T(8,128)S(1)} %get-tuple-element.17.left, f32[40,128]{1,0:T(8,128)S(1)} %get-tuple-element.18.right, f32[36,144,128]{2,1,0:T(8,128)S(1)} %pad.1), custom_call_target="tpu_custom_call" | custom-call | tf_op jit(solution)/shard_map/row_shares/pallas_call | solution.py:402
  11.2 1.4 %collective-permute-done.2.ends_0 = f32[152,128]{1,0:T(8,128)S(1)} collective-permute-done((f32[152,128]{1,0:T(8,128)S(1)}, f32[152,128]{1,0:T(8,128)S(1)}, u32[]{:S(2)}, u32[]{:S(2)}) %collective-permute-start.2) | collective-permute-done | bytes 77856 | tf_op jit(solution)/shard_map/ppermute | solution.py:26
  12.6 0.0 collective-permute-done.3.ends_1
  12.6 1.4 %prior.1 = bf16[32,5,2,128]{3,2,1,0:T(2,128)(2,1)} custom-call(f32[2,8,128]{2,1,0:T(8,128)S(1)} %copy-done.1, f32[8,128]{1,0:T(8,128)S(1)} %row_shares.1.own, f32[152,128]{1,0:T(8,128)S(1)} %collective-permute-done.2.ends_0, f32[152,128]{1,0:T(8,128)S(1)} %collective-permute-done.3.ends_1), custom_call_target="tpu_custom_call" | custom-call | tf_op jit(solution)/shard_map/prior/pallas_call | solution.py:402
  14.1 7.7 %all-to-all-start = ((bf16[32,5,2,128]{3,2,1,0:T(2,128)(2,1)}), bf16[32,5,2,128]{3,2,1,0:T(2,128)(2,1)S(1)}, u32[]{:S(2)}, u32[]{:S(2)}) async-start(bf16[32,5,2,128]{3,2,1,0:T(2,128)(2,1)} %prior.1), calls=%async_computation | async-start | bytes 163840 | tf_op jit(solution)/shard_map/all_to_all | solution.py:419
  21.8 0.0 copy-done.2
  21.8 1.6 %later_shares.1.later = f32[10,8,128]{2,1,0:T(8,128)S(1)} custom-call(f32[2,8,128]{2,1,0:T(8,128)S(1)} %copy-done.1, f32[40,128]{1,0:T(8,128)S(1)} %get-tuple-element.17.left, f32[40,128]{1,0:T(8,128)S(1)} %get-tuple-element.18.right, f32[152,128]{1,0:T(8,128)S(1)} %collective-permute-done.2.ends_0, f32[152,128]{1,0:T(8,128)S(1)} %collective-permute-done.3.ends_1, ...), custom_call_target="tpu_custom_call" | custom-call | tf_op jit(solution)/shard_map/later_shares/pallas_call | solution.py:402
  23.4 6.0 %all-to-all-done.near_ref = bf16[32,5,2,128]{3,2,1,0:T(2,128)(2,1)S(1)} async-done(((bf16[32,5,2,128]{3,2,1,0:T(2,128)(2,1)}), bf16[32,5,2,128]{3,2,1,0:T(2,128)(2,1)S(1)}, u32[]{:S(2)}, u32[]{:S(2)}) %all-to-all-start) | async-done | bytes 81952 | tf_op jit(solution)/shard_map/all_to_all | solution.py:419
  29.4 5.4 %first_batch.1 = (f32[128,128]{1,0:T(8,128)S(1)}, f32[32,8,128]{2,1,0:T(8,128)S(1)}) custom-call(bf16[32,5,2,128]{3,2,1,0:T(2,128)(2,1)S(1)} %all-to-all-done.near_ref, s32[2,1,1,5,8]{4,3,2,1,0:T(8,128)S(1)} %copy.8.pattern, f32[10,8,128]{2,1,0:T(8,128)S(1)} %later_shares.1.later), custom_call_target="tpu_custom_call" | custom-call | tf_op jit(solution)/shard_map/first_batch/pallas_call | solution.py:402
  34.8 9.9 %all_to_all.15.shares = f32[32,8,128]{2,1,0:T(8,128)S(1)} all-to-all(f32[32,8,128]{2,1,0:T(8,128)S(1)} %get-tuple-element.21), channel_id=1, replica_groups=mesh['lat'=4,'lon'=8] {'lat','lon'}, dimensions={0} | all-to-all | bytes 262144 | tf_op jit(solution)/shard_map/all_to_all | solution.py:419
  44.7 0.2 own_block.1
  44.9 9.3 %all_to_all.16.near_ref = bf16[32,5,2,128]{3,2,1,0:T(2,128)(2,1)S(1)} all-to-all(bf16[32,5,2,128]{3,2,1,0:T(2,128)(2,1)S(1)} %own_block.1), channel_id=1, replica_groups=mesh['lat'=4,'lon'=8] {'lat','lon'}, dimensions={0} | all-to-all | bytes 163840 | tf_op jit(solution)/shard_map/all_to_all | solution.py:419
  54.2 6.9 %second_batch.1 = f32[4096,128]{1,0:T(8,128)} custom-call(bf16[32,5,2,128]{3,2,1,0:T(2,128)(2,1)S(1)} %all_to_all.16.near_ref, s32[2,1,1,5,8]{4,3,2,1,0:T(8,128)S(1)} %copy.8.pattern, f32[128,128]{1,0:T(8,128)S(1)} %get-tuple-element.22.map_ref, f32[36,144,128]{2,1,0:T(8,128)S(1)} %pad.1), custom_call_target="tpu_custom_call" | custom-call | tf_op jit(solution)/shard_map/second_batch/pallas_call | solution.py:402
  (1 shorter events, 0.0 us)
Async XLA Ops:
  1.8 5.9 %collective-permute-start = (f32[40,128]{1,0:T(8,128)}, f32[40,128]{1,0:T(8,128)S(1)}, u32[]{:S(2)}, u32[]{:S(2)}) collective-permute-start(f32[40,128]{1,0:T(8,128)} %get-tuple-element.15), channel_id=1, source_target_pairs={{0,1},{1,0},{2,3},{3,2},{4,5},{5,4},{6,7},{7,6},{8,9},{9,8},{10,11... | collective-permute-start | bytes 61448 | tf_op jit(solution)/shard_map/ppermute | solution.py:26
  2.3 5.4 %collective-permute-start.1 = (f32[40,128]{1,0:T(8,128)}, f32[40,128]{1,0:T(8,128)S(1)}, u32[]{:S(2)}, u32[]{:S(2)}) collective-permute-start(f32[40,128]{1,0:T(8,128)} %get-tuple-element.16), channel_id=1, source_target_pairs={{0,7},{1,2},{2,1},{3,4},{4,3},{5,6},{6,5},{7,0},{8,15},{9,10},{10,... | collective-permute-start | bytes 61448 | tf_op jit(solution)/shard_map/ppermute | solution.py:26
  5.8 1.6 %copy-start = (f32[32,128,128]{2,1,0:T(8,128)S(1)}, f32[32,128,128]{2,1,0:T(8,128)}, u32[]{:S(2)}) copy-start(f32[32,128,128]{2,1,0:T(8,128)} %cells.3) | copy-start | bytes 6291460
  7.4 0.7 %copy-start.1 = (f32[2,8,128]{2,1,0:T(8,128)S(1)}, f32[2,8,128]{2,1,0:T(8,128)}, u32[]{:S(2)}) copy-start(f32[2,8,128]{2,1,0:T(8,128)} %get-tuple-element.14.mine) | copy-start | bytes 24580
  8.2 13.6 %copy-start.2 = (s32[2,1,1,5,8]{4,2,3,1,0:T(1,128)S(1)}, s32[2,1,1,5,8]{4,2,3,1,0:T(1,128)}, u32[]{:S(2)}) copy-start(s32[2,1,1,5,8]{4,2,3,1,0:T(1,128)} %param.13) | copy-start | bytes 964
  8.2 4.4 %collective-permute-start.2 = (f32[152,128]{1,0:T(8,128)S(1)}, f32[152,128]{1,0:T(8,128)S(1)}, u32[]{:S(2)}, u32[]{:S(2)}) collective-permute-start(f32[152,128]{1,0:T(8,128)S(1)} %get-tuple-element.19), channel_id=1, source_target_pairs={{0,8},{8,0},{16,24},{24,16},{1,9},{9,1},{17,25},{25,17},{2,10},{10... | collective-permute-start | bytes 233480 | tf_op jit(solution)/shard_map/ppermute | solution.py:26
  9.8 2.8 %collective-permute-start.3 = (f32[152,128]{1,0:T(8,128)S(1)}, f32[152,128]{1,0:T(8,128)S(1)}, u32[]{:S(2)}, u32[]{:S(2)}) collective-permute-start(f32[152,128]{1,0:T(8,128)S(1)} %get-tuple-element.20), channel_id=1, source_target_pairs={{8,16},{16,8},{9,17},{17,9},{10,18},{18,10},{11,19},{19,11},{12,20... | collective-permute-start | bytes 233480 | tf_op jit(solution)/shard_map/ppermute | solution.py:26
  14.1 15.3 %all-to-all-start = ((bf16[32,5,2,128]{3,2,1,0:T(2,128)(2,1)}), bf16[32,5,2,128]{3,2,1,0:T(2,128)(2,1)S(1)}, u32[]{:S(2)}, u32[]{:S(2)}) async-start(bf16[32,5,2,128]{3,2,1,0:T(2,128)(2,1)} %prior.1), calls=%async_computation | async-start | bytes 163840 | tf_op jit(solution)/shard_map/all_to_all | solution.py:419

commit v4 on v3

--- a/solution.py
+++ b/solution.py
@@ -17,17 +17,32 @@
 BF16 = jnp.bfloat16
 
 
-def swap(block, axis, kind, count, wraps):
-    route = []
-    for place in range(count):
-        partner = place + (1 if place % 2 == kind else -1)
-        if wraps or 0 <= partner < count:
-            route.append((place, partner % count))
-    return lax.ppermute(block, axis, route)
+def partner(place, kind):
+    return place + (1 if place % 2 == kind else -1)
+
+
+def trade(blocks, axis):
+    lat_count, lon_count = (lax.axis_size("lat"), lax.axis_size("lon"))
+    results = []
+    for turn, block in enumerate(blocks):
+        route = []
+        for lat in range(lat_count):
+            for lon in range(lon_count):
+                if axis == "lon":
+                    to_lat, to_lon = (lat, partner(lon, turn) % lon_count)
+                else:
+                    to_lat, to_lon = (partner(lat, (turn + lon) % 2), lon)
+                if 0 <= to_lat < lat_count:
+                    route.append((lat * lon_count + lon, to_lat * lon_count + to_lon))
+        results.append(lax.ppermute(block, ("lat", "lon"), route))
+    return results
 
 
 def is_even(axis):
-    return lax.rem(lax.axis_index(axis), 2) == 0
+    place = lax.axis_index("lon")
+    if axis == "lat":
+        place = place + lax.axis_index("lat")
+    return lax.rem(place, 2) == 0
 
 
 def start_kernel(
@@ -409,12 +424,6 @@
             name=name,
         )(*operands)
 
-    def trade(blocks, axis):
-        count, wraps = ((lon_count, True) if axis == "lon" else (lat_count, False))
-        first, second = blocks
-        second = swap(second, axis, 1, count, wraps)
-        return [swap(first, axis, 0, count, wraps), second]
-
     def exchange(blocks):
         return lax.all_to_all(blocks, ("lat", "lon"), split_axis=0, concat_axis=0, tiled=True)
 

time: 61.5 us -> 62.8 us (1.021)
  starting transfers between devices: 14 us -> 15.3 us
    ppermute x4, starting transfers between devices: 6.33 us -> 8.34 us  [trade(): results.append(lax.ppermute(block, ('lat', 'lon'), route))]
    all_to_all x1, starting transfers between devices: 7.7 us -> 6.98 us  [exchange(): lax.all_to_all(blocks, ('lat', 'lon'), split_axis=0, concat_axis=0, tiled...]
where the time goes in v4:
time: 62.8 us; the launch traced here: 62.4 us
  blocking collectives  19.2 us (31%)
  Pallas kernels  18.3 us (29%)
  starting transfers between devices  15.3 us (24%)
  waiting for transfers between devices  7.42 us (12%)
  local copies, waits for them, and re-layouts  2.06 us (3%)
    all_to_all x2, blocking collectives, exchange(): lax.all_to_all(blocks, ('lat', 'lon'), split_axis=0, concat_axis=0, tiled...  19.2 us
    pallas_call x9, Pallas kernels, call(): pl.pallas_call(kernel, out_shape=out_shape, in_specs=specs, out_specs=out...  18.3 us
    ppermute x4, starting transfers between devices, trade(): results.append(lax.ppermute(block, ('lat', 'lon'), route))  8.34 us
    all_to_all x1, starting transfers between devices, exchange(): lax.all_to_all(blocks, ('lat', 'lon'), split_axis=0, concat_axis=0, tiled...  6.98 us
    all_to_all x1, waiting for transfers between devices, exchange(): lax.all_to_all(blocks, ('lat', 'lon'), split_axis=0, concat_axis=0, tiled...  6 us
    unnamed x7, local copies, waits for them, and re-layouts  2.06 us
    ppermute x4, waiting for transfers between devices, trade(): results.append(lax.ppermute(block, ('lat', 'lon'), route))  1.42 us
  transfers between devices with their start and end apart: 5, of which 2 were waited for; matrix products, arithmetic and copies ran while one was open for 0% of the time, Pallas kernels for 4%

profile of v4, /device:TPU:0, one launch (start us, length us, event | category | flops | bytes accessed | tf_op | source)
XLA Modules:
  0.0 62.4 jit_solution(12670562391083967580)
XLA Ops:
  0.0 1.8 %start.1 = (f32[2,8,128]{2,1,0:T(8,128)}, f32[40,128]{1,0:T(8,128)}, f32[40,128]{1,0:T(8,128)}) custom-call(f32[2,1,1,8]{3,2,1,0:T(1,128)} %observed.1, f32[2,1,1,8]{3,2,1,0:T(1,128)} %precision.1, f32[2,1,1,4,8]{4,3,2,1,0:T(4,128)} %weight.1, s32[2,1,1,4,8]{4,3,2,1,0:T(4,128)} %stencil.1, s32[2,1,1,8]{3,2,1,0:T(1,128)} %owned.1, f32[32,128,128]{2,1,0:T(8,128)} %cells.3), custom_call_target="tpu_custom_call" | custom-call | tf_op jit(solution)/shard_map/start/pallas_call | solution.py:417
  1.8 0.5 collective-permute-start
  2.3 3.6 %collective-permute-start.1 = (f32[40,128]{1,0:T(8,128)}, f32[40,128]{1,0:T(8,128)S(1)}, u32[]{:S(2)}, u32[]{:S(2)}) collective-permute-start(f32[40,128]{1,0:T(8,128)} %get-tuple-element.16), channel_id=1, source_target_pairs={{0,7},{1,2},{2,1},{3,4},{4,3},{5,6},{6,5},{7,0},{8,15},{9,10},{10,... | collective-permute-start | bytes 61448 | tf_op jit(solution)/shard_map/ppermute | solution.py:37
  5.8 0.0 copy-start
  5.8 1.6 %copy-done = f32[32,128,128]{2,1,0:T(8,128)S(1)} copy-done((f32[32,128,128]{2,1,0:T(8,128)S(1)}, f32[32,128,128]{2,1,0:T(8,128)}, u32[]{:S(2)}) %copy-start) | copy-done | bytes 2097176
  7.4 0.0 copy-start.1
  7.4 0.2 pad.1
  7.6 0.0 collective-permute-done.sides_0
  7.7 0.0 collective-permute-done.1.sides_1
  7.7 0.5 copy-done.1
  8.1 0.1 edge_rows.1
  8.2 0.0 copy-start.2
  8.2 3.6 %collective-permute-start.2 = (f32[152,128]{1,0:T(8,128)S(1)}, f32[152,128]{1,0:T(8,128)S(1)}, u32[]{:S(2)}, u32[]{:S(2)}) collective-permute-start(f32[152,128]{1,0:T(8,128)S(1)} %get-tuple-element.19), channel_id=1, source_target_pairs={{0,8},{2,10},{4,12},{6,14},{8,0},{9,17},{10,2},{11,19},{12,4},{13,... | collective-permute-start | bytes 233480 | tf_op jit(solution)/shard_map/ppermute | solution.py:37
  11.8 0.7 %collective-permute-start.3 = (f32[152,128]{1,0:T(8,128)S(1)}, f32[152,128]{1,0:T(8,128)S(1)}, u32[]{:S(2)}, u32[]{:S(2)}) collective-permute-start(f32[152,128]{1,0:T(8,128)S(1)} %get-tuple-element.20), channel_id=1, source_target_pairs={{1,9},{3,11},{5,13},{7,15},{8,16},{9,1},{10,18},{11,3},{12,20},{13... | collective-permute-start | bytes 233480 | tf_op jit(solution)/shard_map/ppermute | solution.py:37
  12.5 0.7 %row_shares.1.own = f32[8,128]{1,0:T(8,128)S(1)} custom-call(f32[2,8,128]{2,1,0:T(8,128)S(1)} %copy-done.1, f32[40,128]{1,0:T(8,128)S(1)} %get-tuple-element.17.left, f32[40,128]{1,0:T(8,128)S(1)} %get-tuple-element.18.right, f32[36,144,128]{2,1,0:T(8,128)S(1)} %pad.1), custom_call_target="tpu_custom_call" | custom-call | tf_op jit(solution)/shard_map/row_shares/pallas_call | solution.py:417
  13.2 1.4 %collective-permute-done.2.ends_0 = f32[152,128]{1,0:T(8,128)S(1)} collective-permute-done((f32[152,128]{1,0:T(8,128)S(1)}, f32[152,128]{1,0:T(8,128)S(1)}, u32[]{:S(2)}, u32[]{:S(2)}) %collective-permute-start.2) | collective-permute-done | bytes 77856 | tf_op jit(solution)/shard_map/ppermute | solution.py:37
  14.6 0.0 collective-permute-done.3.ends_1
  14.6 1.4 %prior.1 = bf16[32,5,2,128]{3,2,1,0:T(2,128)(2,1)} custom-call(f32[2,8,128]{2,1,0:T(8,128)S(1)} %copy-done.1, f32[8,128]{1,0:T(8,128)S(1)} %row_shares.1.own, f32[152,128]{1,0:T(8,128)S(1)} %collective-permute-done.2.ends_0, f32[152,128]{1,0:T(8,128)S(1)} %collective-permute-done.3.ends_1), custom_call_target="tpu_custom_call" | custom-call | tf_op jit(solution)/shard_map/prior/pallas_call | solution.py:417
  16.1 7.0 %all-to-all-start = ((bf16[32,5,2,128]{3,2,1,0:T(2,128)(2,1)}), bf16[32,5,2,128]{3,2,1,0:T(2,128)(2,1)S(1)}, u32[]{:S(2)}, u32[]{:S(2)}) async-start(bf16[32,5,2,128]{3,2,1,0:T(2,128)(2,1)} %prior.1), calls=%async_computation | async-start | bytes 163840 | tf_op jit(solution)/shard_map/all_to_all | solution.py:428
  23.0 0.0 copy-done.2
  23.1 1.6 %later_shares.1.later = f32[10,8,128]{2,1,0:T(8,128)S(1)} custom-call(f32[2,8,128]{2,1,0:T(8,128)S(1)} %copy-done.1, f32[40,128]{1,0:T(8,128)S(1)} %get-tuple-element.17.left, f32[40,128]{1,0:T(8,128)S(1)} %get-tuple-element.18.right, f32[152,128]{1,0:T(8,128)S(1)} %collective-permute-done.2.ends_0, f32[152,128]{1,0:T(8,128)S(1)} %collective-permute-done.3.ends_1, ...), custom_call_target="tpu_custom_call" | custom-call | tf_op jit(solution)/shard_map/later_shares/pallas_call | solution.py:417
  24.6 6.0 %all-to-all-done.near_ref = bf16[32,5,2,128]{3,2,1,0:T(2,128)(2,1)S(1)} async-done(((bf16[32,5,2,128]{3,2,1,0:T(2,128)(2,1)}), bf16[32,5,2,128]{3,2,1,0:T(2,128)(2,1)S(1)}, u32[]{:S(2)}, u32[]{:S(2)}) %all-to-all-start) | async-done | bytes 81952 | tf_op jit(solution)/shard_map/all_to_all | solution.py:428
  30.6 5.4 %first_batch.1 = (f32[128,128]{1,0:T(8,128)S(1)}, f32[32,8,128]{2,1,0:T(8,128)S(1)}) custom-call(bf16[32,5,2,128]{3,2,1,0:T(2,128)(2,1)S(1)} %all-to-all-done.near_ref, s32[2,1,1,5,8]{4,3,2,1,0:T(8,128)S(1)} %copy.8.pattern, f32[10,8,128]{2,1,0:T(8,128)S(1)} %later_shares.1.later), custom_call_target="tpu_custom_call" | custom-call | tf_op jit(solution)/shard_map/first_batch/pallas_call | solution.py:417
  36.1 9.9 %all_to_all.15.shares = f32[32,8,128]{2,1,0:T(8,128)S(1)} all-to-all(f32[32,8,128]{2,1,0:T(8,128)S(1)} %get-tuple-element.21), channel_id=1, replica_groups=mesh['lat'=4,'lon'=8] {'lat','lon'}, dimensions={0} | all-to-all | bytes 262144 | tf_op jit(solution)/shard_map/all_to_all | solution.py:428
  46.0 0.2 own_block.1
  46.2 9.3 %all_to_all.16.near_ref = bf16[32,5,2,128]{3,2,1,0:T(2,128)(2,1)S(1)} all-to-all(bf16[32,5,2,128]{3,2,1,0:T(2,128)(2,1)S(1)} %own_block.1), channel_id=1, replica_groups=mesh['lat'=4,'lon'=8] {'lat','lon'}, dimensions={0} | all-to-all | bytes 163840 | tf_op jit(solution)/shard_map/all_to_all | solution.py:428
  55.5 6.9 %second_batch.1 = f32[4096,128]{1,0:T(8,128)} custom-call(bf16[32,5,2,128]{3,2,1,0:T(2,128)(2,1)S(1)} %all_to_all.16.near_ref, s32[2,1,1,5,8]{4,3,2,1,0:T(8,128)S(1)} %copy.8.pattern, f32[128,128]{1,0:T(8,128)S(1)} %get-tuple-element.22.map_ref, f32[36,144,128]{2,1,0:T(8,128)S(1)} %pad.1), custom_call_target="tpu_custom_call" | custom-call | tf_op jit(solution)/shard_map/second_batch/pallas_call | solution.py:417
  (1 shorter events, 0.0 us)
Async XLA Ops:
  1.8 5.9 %collective-permute-start = (f32[40,128]{1,0:T(8,128)}, f32[40,128]{1,0:T(8,128)S(1)}, u32[]{:S(2)}, u32[]{:S(2)}) collective-permute-start(f32[40,128]{1,0:T(8,128)} %get-tuple-element.15), channel_id=1, source_target_pairs={{0,1},{1,0},{2,3},{3,2},{4,5},{5,4},{6,7},{7,6},{8,9},{9,8},{10,11... | collective-permute-start | bytes 61448 | tf_op jit(solution)/shard_map/ppermute | solution.py:37
  2.3 5.4 %collective-permute-start.1 = (f32[40,128]{1,0:T(8,128)}, f32[40,128]{1,0:T(8,128)S(1)}, u32[]{:S(2)}, u32[]{:S(2)}) collective-permute-start(f32[40,128]{1,0:T(8,128)} %get-tuple-element.16), channel_id=1, source_target_pairs={{0,7},{1,2},{2,1},{3,4},{4,3},{5,6},{6,5},{7,0},{8,15},{9,10},{10,... | collective-permute-start | bytes 61448 | tf_op jit(solution)/shard_map/ppermute | solution.py:37
  5.8 1.6 %copy-start = (f32[32,128,128]{2,1,0:T(8,128)S(1)}, f32[32,128,128]{2,1,0:T(8,128)}, u32[]{:S(2)}) copy-start(f32[32,128,128]{2,1,0:T(8,128)} %cells.3) | copy-start | bytes 6291460
  7.4 0.7 %copy-start.1 = (f32[2,8,128]{2,1,0:T(8,128)S(1)}, f32[2,8,128]{2,1,0:T(8,128)}, u32[]{:S(2)}) copy-start(f32[2,8,128]{2,1,0:T(8,128)} %get-tuple-element.14.mine) | copy-start | bytes 24580
  8.2 14.8 %copy-start.2 = (s32[2,1,1,5,8]{4,2,3,1,0:T(1,128)S(1)}, s32[2,1,1,5,8]{4,2,3,1,0:T(1,128)}, u32[]{:S(2)}) copy-start(s32[2,1,1,5,8]{4,2,3,1,0:T(1,128)} %param.13) | copy-start | bytes 964
  8.2 6.4 %collective-permute-start.2 = (f32[152,128]{1,0:T(8,128)S(1)}, f32[152,128]{1,0:T(8,128)S(1)}, u32[]{:S(2)}, u32[]{:S(2)}) collective-permute-start(f32[152,128]{1,0:T(8,128)S(1)} %get-tuple-element.19), channel_id=1, source_target_pairs={{0,8},{2,10},{4,12},{6,14},{8,0},{9,17},{10,2},{11,19},{12,4},{13,... | collective-permute-start | bytes 233480 | tf_op jit(solution)/shard_map/ppermute | solution.py:37
  11.8 2.8 %collective-permute-start.3 = (f32[152,128]{1,0:T(8,128)S(1)}, f32[152,128]{1,0:T(8,128)S(1)}, u32[]{:S(2)}, u32[]{:S(2)}) collective-permute-start(f32[152,128]{1,0:T(8,128)S(1)} %get-tuple-element.20), channel_id=1, source_target_pairs={{1,9},{3,11},{5,13},{7,15},{8,16},{9,1},{10,18},{11,3},{12,20},{13... | collective-permute-start | bytes 233480 | tf_op jit(solution)/shard_map/ppermute | solution.py:37
  16.1 14.6 %all-to-all-start = ((bf16[32,5,2,128]{3,2,1,0:T(2,128)(2,1)}), bf16[32,5,2,128]{3,2,1,0:T(2,128)(2,1)S(1)}, u32[]{:S(2)}, u32[]{:S(2)}) async-start(bf16[32,5,2,128]{3,2,1,0:T(2,128)(2,1)} %prior.1), calls=%async_computation | async-start | bytes 163840 | tf_op jit(solution)/shard_map/all_to_all | solution.py:428

commit v5 on v3

--- a/solution.py
+++ b/solution.py
@@ -17,17 +17,22 @@
 BF16 = jnp.bfloat16
 
 
-def swap(block, axis, kind, count, wraps):
-    route = []
-    for place in range(count):
-        partner = place + (1 if place % 2 == kind else -1)
-        if wraps or 0 <= partner < count:
-            route.append((place, partner % count))
-    return lax.ppermute(block, axis, route)
-
-
-def is_even(axis):
-    return lax.rem(lax.axis_index(axis), 2) == 0
+def partner(place, turn):
+    return place + (-1 if place % 2 == turn else 1)
+
+
+def trade(blocks, axis, wraps):
+    count = lax.axis_size(axis)
+    results = []
+    for turn, block in enumerate(blocks):
+        route = [(place, partner(place, turn)) for place in range(count)]
+        route = [(source, target % count) for source, target in route if wraps or 0 <= target < count]
+        results.append(lax.ppermute(block, axis, route))
+    return results
+
+
+def next_first(axis):
+    return lax.rem(lax.axis_index(axis), 2) == 1
 
 
 def start_kernel(
@@ -59,10 +64,10 @@
         params_ref[b, pl.ds(AT_COL, 1), pl.ds(0, SUB)] = corner - row * width
         params_ref[b, pl.ds(AT_OBS, 1), pl.ds(0, SUB)] = observed_v[b, 0] * root
     rows = cells.shape[0]
-    even = is_even("lon")
+    forward = next_first("lon")
     left, right = (left_v[:, 0, :], right_v[:, SUB - 1, :])
-    sides_0[pl.ds(0, rows), :] = jnp.where(even, right, left)
-    sides_1[pl.ds(0, rows), :] = jnp.where(even, left, right)
+    sides_0[pl.ds(0, rows), :] = jnp.where(forward, right, left)
+    sides_1[pl.ds(0, rows), :] = jnp.where(forward, left, right)
     sides_0[pl.ds(rows, SUB), :] = params_ref[1]
     sides_1[pl.ds(rows, SUB), :] = params_ref[1]
 
@@ -129,16 +134,16 @@
 
 def rows_kernel(mine, sides_0, sides_1, pad, left_ref, right_ref, out_0, out_1):
     rows, cols = (pad.shape[0] - 4, pad.shape[1] - 2 * SUB)
-    even = is_even("lon")
-    left_ref[...] = jnp.where(even, sides_1[...], sides_0[...])
-    right_ref[...] = jnp.where(even, sides_0[...], sides_1[...])
+    forward = next_first("lon")
+    left_ref[...] = jnp.where(forward, sides_1[...], sides_0[...])
+    right_ref[...] = jnp.where(forward, sides_0[...], sides_1[...])
     lane = lax.broadcasted_iota(jnp.int32, (SUB, LANES), 1)
     block = pl.ds(rows, SUB)
     packed = jnp.where(lane < SUB, left_ref[block, :], pltpu.roll(mine[1], SUB, 1))
     packed = jnp.where(lane < 2 * SUB, packed, pltpu.roll(right_ref[block, :], 2 * SUB, 1))
-    even = is_even("lat")
-    for kind, out in enumerate((out_0, out_1)):
-        row = jnp.where(even, (1 - kind) * (rows - 1), kind * (rows - 1))
+    forward = next_first("lat")
+    for turn, out in enumerate((out_0, out_1)):
+        row = jnp.where(forward, (1 - turn) * (rows - 1), turn * (rows - 1))
         out[pl.ds(0, SUB), :] = jnp.broadcast_to(left_ref[pl.ds(row, 1), :], (SUB, LANES))
         out[pl.ds(SUB, cols), :] = pad[2 + row, pl.ds(SUB, cols), :]
         out[pl.ds(SUB + cols, SUB), :] = jnp.broadcast_to(right_ref[pl.ds(row, 1), :], (SUB, LANES))
@@ -163,9 +168,9 @@
 def prior_kernel(rows, mine, own, ends_0, ends_1, out_ref, ends, value, params, sem):
     copy = pltpu.make_async_copy(mine.at[0], params, sem)
     copy.start()
-    even = is_even("lat")
-    ends[0] = jnp.where(even, ends_1[...], ends_0[...])
-    ends[1] = jnp.where(even, ends_0[...], ends_1[...])
+    forward = next_first("lat")
+    ends[0] = jnp.where(forward, ends_1[...], ends_0[...])
+    ends[1] = jnp.where(forward, ends_0[...], ends_1[...])
     copy.wait()
     for o in range(SUB):
         row, col = (params[AT_ROW, o].astype(jnp.int32), params[AT_COL, o].astype(jnp.int32))
@@ -192,8 +197,8 @@
         copies[-1].start()
     for copy in copies:
         copy.wait()
-    even = is_even("lat")
-    ends = {-1: jnp.where(even, 4, 3), 1: jnp.where(even, 3, 4)}
+    forward = next_first("lat")
+    ends = {-1: jnp.where(forward, 4, 3), 1: jnp.where(forward, 3, 4)}
     for n, dc in enumerate(NEAR):
         for m, da in enumerate(NEAR):
             spot, lane = (n, 0) if da == 0 else (ends[da], n * SUB)
@@ -409,12 +414,6 @@
             name=name,
         )(*operands)
 
-    def trade(blocks, axis):
-        count, wraps = ((lon_count, True) if axis == "lon" else (lat_count, False))
-        first, second = blocks
-        second = swap(second, axis, 1, count, wraps)
-        return [swap(first, axis, 0, count, wraps), second]
-
     def exchange(blocks):
         return lax.all_to_all(blocks, ("lat", "lon"), split_axis=0, concat_axis=0, tiled=True)
 
@@ -432,12 +431,12 @@
         ensemble,
         limit=63,
     )
-    sides = trade((side_0, side_1), "lon")
+    sides = trade((side_0, side_1), "lon", True)
     padded = shape(rows + 4, cols + 2 * SUB, members)
     pad = call(pad_kernel, "pad", [hbm], padded, [pltpu.SemaphoreType.DMA], ensemble)
     end = shape(cols + 3 * SUB, members)
     left, right, *ends = call(rows_kernel, "edge_rows", [vmem] * 4, (side, side, end, end), [], mine, *sides, pad)
-    ends = trade(ends, "lat")
+    ends = trade(ends, "lat", False)
     slots = shape(tiles, PAIRS, 2, members, dtype=BF16)
     numbers = [pltpu.SMEM((SUB, LANES), F32), pltpu.SemaphoreType.DMA]
     block = shape(SUB, members)

time: 61.5 us -> 60.2 us (0.979)
  starting transfers between devices: 14 us -> 12.4 us
    all_to_all x1, starting transfers between devices: 7.7 us -> 3.47 us  [exchange(): lax.all_to_all(blocks, ('lat', 'lon'), split_axis=0, concat_axis=0, tiled...]
    ppermute x4, starting transfers between devices: 6.33 us -> 8.91 us  [trade(): results.append(lax.ppermute(block, axis, route))]
where the time goes in v5:
time: 60.2 us; the launch traced here: 59.8 us
  blocking collectives  19.2 us (32%)
  Pallas kernels  18.3 us (30%)
  starting transfers between devices  12.4 us (21%)
  waiting for transfers between devices  7.77 us (13%)
  local copies, waits for them, and re-layouts  2.06 us (3%)
    all_to_all x2, blocking collectives, exchange(): lax.all_to_all(blocks, ('lat', 'lon'), split_axis=0, concat_axis=0, tiled...  19.2 us
    pallas_call x9, Pallas kernels, call(): pl.pallas_call(kernel, out_shape=out_shape, in_specs=specs, out_specs=out...  18.3 us
    ppermute x4, starting transfers between devices, trade(): results.append(lax.ppermute(block, axis, route))  8.91 us
    all_to_all x1, waiting for transfers between devices, exchange(): lax.all_to_all(blocks, ('lat', 'lon'), split_axis=0, concat_axis=0, tiled...  6 us
    all_to_all x1, starting transfers between devices, exchange(): lax.all_to_all(blocks, ('lat', 'lon'), split_axis=0, concat_axis=0, tiled...  3.47 us
    unnamed x7, local copies, waits for them, and re-layouts  2.06 us
    ppermute x4, waiting for transfers between devices, trade(): results.append(lax.ppermute(block, axis, route))  1.77 us
  transfers between devices with their start and end apart: 5, of which 2 were waited for; matrix products, arithmetic and copies ran while one was open for 0% of the time, Pallas kernels for 4%

profile of v5, /device:TPU:0, one launch (start us, length us, event | category | flops | bytes accessed | tf_op | source)
XLA Modules:
  0.0 59.8 jit_solution(7484200816099195677)
XLA Ops:
  0.0 1.8 %start.1 = (f32[2,8,128]{2,1,0:T(8,128)}, f32[40,128]{1,0:T(8,128)}, f32[40,128]{1,0:T(8,128)}) custom-call(f32[2,1,1,8]{3,2,1,0:T(1,128)} %observed.1, f32[2,1,1,8]{3,2,1,0:T(1,128)} %precision.1, f32[2,1,1,4,8]{4,3,2,1,0:T(4,128)} %weight.1, s32[2,1,1,4,8]{4,3,2,1,0:T(4,128)} %stencil.1, s32[2,1,1,8]{3,2,1,0:T(1,128)} %owned.1, f32[32,128,128]{2,1,0:T(8,128)} %cells.3), custom_call_target="tpu_custom_call" | custom-call | tf_op jit(solution)/shard_map/start/pallas_call | solution.py:407
  1.8 3.4 %collective-permute-start = (f32[40,128]{1,0:T(8,128)}, f32[40,128]{1,0:T(8,128)S(1)}, u32[]{:S(2)}, u32[]{:S(2)}) collective-permute-start(f32[40,128]{1,0:T(8,128)} %get-tuple-element.15), channel_id=1, source_target_pairs={{0,7},{1,2},{2,1},{3,4},{4,3},{5,6},{6,5},{7,0},{8,15},{9,10},{10,... | collective-permute-start | bytes 61448 | tf_op jit(solution)/shard_map/ppermute | solution.py:30
  5.2 0.0 collective-permute-start.1
  5.2 0.0 copy-start
  5.2 1.6 %copy-done = f32[32,128,128]{2,1,0:T(8,128)S(1)} copy-done((f32[32,128,128]{2,1,0:T(8,128)S(1)}, f32[32,128,128]{2,1,0:T(8,128)}, u32[]{:S(2)}) %copy-start) | copy-done | bytes 2097176
  6.8 0.0 copy-start.1
  6.8 0.2 pad.1
  7.0 0.0 collective-permute-done.sides_0
  7.0 0.0 collective-permute-done.1.sides_1
  7.0 0.5 copy-done.1
  7.5 0.1 edge_rows.1
  7.5 0.0 copy-start.2
  7.5 0.8 %collective-permute-start.2 = (f32[152,128]{1,0:T(8,128)S(1)}, f32[152,128]{1,0:T(8,128)S(1)}, u32[]{:S(2)}, u32[]{:S(2)}) collective-permute-start(f32[152,128]{1,0:T(8,128)S(1)} %get-tuple-element.19), channel_id=1, source_target_pairs={{8,16},{16,8},{9,17},{17,9},{10,18},{18,10},{11,19},{19,11},{12,20... | collective-permute-start | bytes 233480 | tf_op jit(solution)/shard_map/ppermute | solution.py:30
  8.3 4.7 %collective-permute-start.3 = (f32[152,128]{1,0:T(8,128)S(1)}, f32[152,128]{1,0:T(8,128)S(1)}, u32[]{:S(2)}, u32[]{:S(2)}) collective-permute-start(f32[152,128]{1,0:T(8,128)S(1)} %get-tuple-element.20), channel_id=1, source_target_pairs={{0,8},{8,0},{16,24},{24,16},{1,9},{9,1},{17,25},{25,17},{2,10},{10... | collective-permute-start | bytes 233480 | tf_op jit(solution)/shard_map/ppermute | solution.py:30
  13.1 0.7 %row_shares.1.own = f32[8,128]{1,0:T(8,128)S(1)} custom-call(f32[2,8,128]{2,1,0:T(8,128)S(1)} %copy-done.1, f32[40,128]{1,0:T(8,128)S(1)} %get-tuple-element.17.left, f32[40,128]{1,0:T(8,128)S(1)} %get-tuple-element.18.right, f32[36,144,128]{2,1,0:T(8,128)S(1)} %pad.1), custom_call_target="tpu_custom_call" | custom-call | tf_op jit(solution)/shard_map/row_shares/pallas_call | solution.py:407
  13.8 0.0 collective-permute-done.2.ends_0
  13.8 1.8 %collective-permute-done.3.ends_1 = f32[152,128]{1,0:T(8,128)S(1)} collective-permute-done((f32[152,128]{1,0:T(8,128)S(1)}, f32[152,128]{1,0:T(8,128)S(1)}, u32[]{:S(2)}, u32[]{:S(2)}) %collective-permute-start.3) | collective-permute-done | bytes 77856 | tf_op jit(solution)/shard_map/ppermute | solution.py:30
  15.5 1.4 %prior.1 = bf16[32,5,2,128]{3,2,1,0:T(2,128)(2,1)} custom-call(f32[2,8,128]{2,1,0:T(8,128)S(1)} %copy-done.1, f32[8,128]{1,0:T(8,128)S(1)} %row_shares.1.own, f32[152,128]{1,0:T(8,128)S(1)} %collective-permute-done.2.ends_0, f32[152,128]{1,0:T(8,128)S(1)} %collective-permute-done.3.ends_1), custom_call_target="tpu_custom_call" | custom-call | tf_op jit(solution)/shard_map/prior/pallas_call | solution.py:407
  17.0 3.5 %all-to-all-start = ((bf16[32,5,2,128]{3,2,1,0:T(2,128)(2,1)}), bf16[32,5,2,128]{3,2,1,0:T(2,128)(2,1)S(1)}, u32[]{:S(2)}, u32[]{:S(2)}) async-start(bf16[32,5,2,128]{3,2,1,0:T(2,128)(2,1)} %prior.1), calls=%async_computation | async-start | bytes 163840 | tf_op jit(solution)/shard_map/all_to_all | solution.py:418
  20.4 0.0 copy-done.2
  20.5 1.6 %later_shares.1.later = f32[10,8,128]{2,1,0:T(8,128)S(1)} custom-call(f32[2,8,128]{2,1,0:T(8,128)S(1)} %copy-done.1, f32[40,128]{1,0:T(8,128)S(1)} %get-tuple-element.17.left, f32[40,128]{1,0:T(8,128)S(1)} %get-tuple-element.18.right, f32[152,128]{1,0:T(8,128)S(1)} %collective-permute-done.2.ends_0, f32[152,128]{1,0:T(8,128)S(1)} %collective-permute-done.3.ends_1, ...), custom_call_target="tpu_custom_call" | custom-call | tf_op jit(solution)/shard_map/later_shares/pallas_call | solution.py:407
  22.1 6.0 %all-to-all-done.near_ref = bf16[32,5,2,128]{3,2,1,0:T(2,128)(2,1)S(1)} async-done(((bf16[32,5,2,128]{3,2,1,0:T(2,128)(2,1)}), bf16[32,5,2,128]{3,2,1,0:T(2,128)(2,1)S(1)}, u32[]{:S(2)}, u32[]{:S(2)}) %all-to-all-start) | async-done | bytes 81952 | tf_op jit(solution)/shard_map/all_to_all | solution.py:418
  28.1 5.4 %first_batch.1 = (f32[128,128]{1,0:T(8,128)S(1)}, f32[32,8,128]{2,1,0:T(8,128)S(1)}) custom-call(bf16[32,5,2,128]{3,2,1,0:T(2,128)(2,1)S(1)} %all-to-all-done.near_ref, s32[2,1,1,5,8]{4,3,2,1,0:T(8,128)S(1)} %copy.8.pattern, f32[10,8,128]{2,1,0:T(8,128)S(1)} %later_shares.1.later), custom_call_target="tpu_custom_call" | custom-call | tf_op jit(solution)/shard_map/first_batch/pallas_call | solution.py:407
  33.5 9.9 %all_to_all.15.shares = f32[32,8,128]{2,1,0:T(8,128)S(1)} all-to-all(f32[32,8,128]{2,1,0:T(8,128)S(1)} %get-tuple-element.21), channel_id=1, replica_groups=mesh['lat'=4,'lon'=8] {'lat','lon'}, dimensions={0} | all-to-all | bytes 262144 | tf_op jit(solution)/shard_map/all_to_all | solution.py:418
  43.4 0.2 own_block.1
  43.6 9.3 %all_to_all.16.near_ref = bf16[32,5,2,128]{3,2,1,0:T(2,128)(2,1)S(1)} all-to-all(bf16[32,5,2,128]{3,2,1,0:T(2,128)(2,1)S(1)} %own_block.1), channel_id=1, replica_groups=mesh['lat'=4,'lon'=8] {'lat','lon'}, dimensions={0} | all-to-all | bytes 163840 | tf_op jit(solution)/shard_map/all_to_all | solution.py:418
  52.9 6.9 %second_batch.1 = f32[4096,128]{1,0:T(8,128)} custom-call(bf16[32,5,2,128]{3,2,1,0:T(2,128)(2,1)S(1)} %all_to_all.16.near_ref, s32[2,1,1,5,8]{4,3,2,1,0:T(8,128)S(1)} %copy.8.pattern, f32[128,128]{1,0:T(8,128)S(1)} %get-tuple-element.22.map_ref, f32[36,144,128]{2,1,0:T(8,128)S(1)} %pad.1), custom_call_target="tpu_custom_call" | custom-call | tf_op jit(solution)/shard_map/second_batch/pallas_call | solution.py:407
  (1 shorter events, 0.0 us)
Async XLA Ops:
  1.8 5.2 %collective-permute-start = (f32[40,128]{1,0:T(8,128)}, f32[40,128]{1,0:T(8,128)S(1)}, u32[]{:S(2)}, u32[]{:S(2)}) collective-permute-start(f32[40,128]{1,0:T(8,128)} %get-tuple-element.15), channel_id=1, source_target_pairs={{0,7},{1,2},{2,1},{3,4},{4,3},{5,6},{6,5},{7,0},{8,15},{9,10},{10,... | collective-permute-start | bytes 61448 | tf_op jit(solution)/shard_map/ppermute | solution.py:30
  5.2 1.8 %collective-permute-start.1 = (f32[40,128]{1,0:T(8,128)}, f32[40,128]{1,0:T(8,128)S(1)}, u32[]{:S(2)}, u32[]{:S(2)}) collective-permute-start(f32[40,128]{1,0:T(8,128)} %get-tuple-element.16), channel_id=1, source_target_pairs={{0,1},{1,0},{2,3},{3,2},{4,5},{5,4},{6,7},{7,6},{8,9},{9,8},{10,11... | collective-permute-start | bytes 61448 | tf_op jit(solution)/shard_map/ppermute | solution.py:30
  5.2 1.6 %copy-start = (f32[32,128,128]{2,1,0:T(8,128)S(1)}, f32[32,128,128]{2,1,0:T(8,128)}, u32[]{:S(2)}) copy-start(f32[32,128,128]{2,1,0:T(8,128)} %cells.3) | copy-start | bytes 6291460
  6.8 0.7 %copy-start.1 = (f32[2,8,128]{2,1,0:T(8,128)S(1)}, f32[2,8,128]{2,1,0:T(8,128)}, u32[]{:S(2)}) copy-start(f32[2,8,128]{2,1,0:T(8,128)} %get-tuple-element.14.mine) | copy-start | bytes 24580
  7.5 12.9 %copy-start.2 = (s32[2,1,1,5,8]{4,2,3,1,0:T(1,128)S(1)}, s32[2,1,1,5,8]{4,2,3,1,0:T(1,128)}, u32[]{:S(2)}) copy-start(s32[2,1,1,5,8]{4,2,3,1,0:T(1,128)} %param.13) | copy-start | bytes 964
  7.5 6.2 %collective-permute-start.2 = (f32[152,128]{1,0:T(8,128)S(1)}, f32[152,128]{1,0:T(8,128)S(1)}, u32[]{:S(2)}, u32[]{:S(2)}) collective-permute-start(f32[152,128]{1,0:T(8,128)S(1)} %get-tuple-element.19), channel_id=1, source_target_pairs={{8,16},{16,8},{9,17},{17,9},{10,18},{18,10},{11,19},{19,11},{12,20... | collective-permute-start | bytes 233480 | tf_op jit(solution)/shard_map/ppermute | solution.py:30
  8.3 7.2 %collective-permute-start.3 = (f32[152,128]{1,0:T(8,128)S(1)}, f32[152,128]{1,0:T(8,128)S(1)}, u32[]{:S(2)}, u32[]{:S(2)}) collective-permute-start(f32[152,128]{1,0:T(8,128)S(1)} %get-tuple-element.20), channel_id=1, source_target_pairs={{0,8},{8,0},{16,24},{24,16},{1,9},{9,1},{17,25},{25,17},{2,10},{10... | collective-permute-start | bytes 233480 | tf_op jit(solution)/shard_map/ppermute | solution.py:30
  17.0 11.1 %all-to-all-start = ((bf16[32,5,2,128]{3,2,1,0:T(2,128)(2,1)}), bf16[32,5,2,128]{3,2,1,0:T(2,128)(2,1)S(1)}, u32[]{:S(2)}, u32[]{:S(2)}) async-start(bf16[32,5,2,128]{3,2,1,0:T(2,128)(2,1)} %prior.1), calls=%async_computation | async-start | bytes 163840 | tf_op jit(solution)/shard_map/all_to_all | solution.py:418

commit v6 on v5

--- a/solution.py
+++ b/solution.py
@@ -15,6 +15,7 @@
 PAIRS = SUB // 2 + 1
 F32 = jnp.float32
 BF16 = jnp.bfloat16
+LON = ("far", "core")
 
 
 def partner(place, turn):
@@ -64,7 +65,7 @@
         params_ref[b, pl.ds(AT_COL, 1), pl.ds(0, SUB)] = corner - row * width
         params_ref[b, pl.ds(AT_OBS, 1), pl.ds(0, SUB)] = observed_v[b, 0] * root
     rows = cells.shape[0]
-    forward = next_first("lon")
+    forward = next_first("core")
     left, right = (left_v[:, 0, :], right_v[:, SUB - 1, :])
     sides_0[pl.ds(0, rows), :] = jnp.where(forward, right, left)
     sides_1[pl.ds(0, rows), :] = jnp.where(forward, left, right)
@@ -134,7 +135,7 @@
 
 def rows_kernel(mine, sides_0, sides_1, pad, left_ref, right_ref, out_0, out_1):
     rows, cols = (pad.shape[0] - 4, pad.shape[1] - 2 * SUB)
-    forward = next_first("lon")
+    forward = next_first("core")
     left_ref[...] = jnp.where(forward, sides_1[...], sides_0[...])
     right_ref[...] = jnp.where(forward, sides_0[...], sides_1[...])
     lane = lax.broadcasted_iota(jnp.int32, (SUB, LANES), 1)
@@ -183,8 +184,8 @@
     send_block(value[...], out_ref)
 
 
-def meet_kernel(shares, out_ref):
-    send_block(jnp.sum(shares[...], axis=0), out_ref)
+def meet_kernel(mid, sides_0, sides_1, out_ref):
+    out_ref[...] = jnp.broadcast_to(mid[...] + sides_0[...] + sides_1[...], out_ref.shape)
 
 
 def later_kernel(mine, left, right, ends_0, ends_1, pad, out_ref, params, sems):
@@ -292,24 +293,60 @@
     return inverse, blocks[count][:1]
 
 
-def batch_map(batch, lat_count, near_ref, pattern):
-    held = min(WIN, lat_count)
-    count = near_ref.shape[0]
-    my_lat = lax.axis_index("lat")
-    start = window_start(lat_count, my_lat)
+def own_blocks(near_ref):
     scaled = jnp.concatenate([near_ref[:, n].astype(F32) for n in range(PAIRS - 1)], axis=1)
     innov = near_ref[:, PAIRS - 1].astype(F32)[:, :1]
     sub = lax.broadcasted_iota(jnp.int32, scaled.shape, 1)
     lane = lax.broadcasted_iota(jnp.int32, scaled.shape, 2)
-    innov = jnp.where(lane == sub, jnp.broadcast_to(innov, scaled.shape), 0.0)
+    return scaled, jnp.where(lane == sub, jnp.broadcast_to(innov, scaled.shape), 0.0)
+
+
+def summed_blocks(lat_count, mine, other):
+    held = min(WIN, lat_count)
+    far_count = mine.shape[0] // lat_count
+    start = window_start(lat_count, lax.axis_index("lat"))
+    values = []
+    for j in range(held):
+        for far in range(far_count):
+            for shares in (mine, other):
+                total = jnp.zeros((SUB, LANES), F32)
+                for n, da in enumerate(NEAR):
+                    source = start + j - da
+                    part = pl.ds(n * SUB, SUB)
+                    if isinstance(source, int):
+                        if 0 <= source < lat_count:
+                            total = total + shares[source * far_count + far, part, :]
+                    else:
+                        inside = (source >= 0) & (source < lat_count)
+                        source = jnp.clip(source, 0, lat_count - 1)
+                        total = total + jnp.where(inside, shares[source * far_count + far, part, :], 0.0)
+                values.append(total[None])
+    value = jnp.concatenate(values, axis=0)
+    mean = jnp.mean(value, axis=-1, keepdims=True)
+    sub = lax.broadcasted_iota(jnp.int32, value.shape, 1)
+    lane = lax.broadcasted_iota(jnp.int32, value.shape, 2)
+    innov = jnp.where(lane == sub, jnp.broadcast_to(-mean, value.shape), 0.0)
+    return (value - mean).astype(BF16).astype(F32), innov
+
+
+def batch_map(batch, lat_count, blocks, pattern, swapped):
+    scaled, innov = blocks
+    held = min(WIN, lat_count)
+    count = scaled.shape[0]
+    my_lat = lax.axis_index("lat")
+    start = window_start(lat_count, my_lat)
     picked = []
     for j in range(held):
         offset = start + j - my_lat + REACH
         inside = (offset >= 0) & (offset < WIN)
         row = pattern[batch, 0, 0, pl.ds(jnp.clip(offset, 0, WIN - 1), 1), :].astype(F32)
         row = jnp.where(inside, row, 0.0)
-        for e in range(count // held):
-            picked.append(jnp.broadcast_to(row[:, e:e + 1], (1, SUB, LANES)))
+        marks = [jnp.broadcast_to(row[:, e:e + 1], (1, SUB, LANES)) for e in range(count // held)]
+        for e in range(0, len(marks), 2):
+            first, second = marks[e:e + 2]
+            if swapped is not None:
+                first, second = (jnp.where(swapped, second, first), jnp.where(swapped, first, second))
+            picked.extend((first, second))
     weighted = scaled * jnp.concatenate(picked, axis=0)
     both = jnp.concatenate([scaled, innov], axis=2).reshape(count * SUB, 2 * LANES).astype(BF16)
     product = lax.dot_general(
@@ -338,28 +375,27 @@
     )
 
 
-def first_kernel(lat_count, lon_count, near_ref, pattern, later, map_ref, out_ref, moved):
-    flipped = batch_map(0, lat_count, near_ref, pattern)
+def first_kernel(lat_count, near_ref, pattern, later, map_ref, mid_ref, out_0, out_1):
+    flipped = batch_map(0, lat_count, own_blocks(near_ref), pattern, None)
     map_ref[...] = flipped
     count = len(NEAR) ** 2
-    moved[...] = exact_dot(later[pl.ds(0, count)].reshape(-1, LANES), flipped, 1).reshape(moved.shape)
-    moved[count // 2] = moved[count // 2] - later[count]
-    out_ref[...] = jnp.zeros_like(out_ref)
-    my_lat, my_lon = (lax.axis_index("lat"), lax.axis_index("lon"))
-    for n, dc in enumerate(NEAR):
-        lon = lax.rem(my_lon + dc + lon_count, lon_count)
-        for m, da in enumerate(NEAR):
-            lat = my_lat + da
-
-            @pl.when((lat >= 0) & (lat < lat_count))
-            def _():
-                out_ref[lat * lon_count + lon] = moved[n * len(NEAR) + m]
-
-
-def last_kernel(lat_count, near_ref, pattern, map_ref, pad, out_ref, result, out_sem):
+    moved = exact_dot(later[pl.ds(0, count)].reshape(-1, LANES), flipped, 1)
+    size = len(NEAR) * SUB
+    left, mid, right = (moved[:size], moved[size:2 * size], moved[2 * size:])
+    mid_ref[...] = mid
+    own = pl.ds(SUB, SUB)
+    mid_ref[own, :] = mid[SUB:2 * SUB] - later[count]
+    forward = next_first("core")
+    out_0[...] = jnp.where(forward, right, left)
+    out_1[...] = jnp.where(forward, left, right)
+
+
+def last_kernel(lat_count, mine, other, pattern, map_ref, pad, out_ref, result, out_sem):
     parts = out_sem.shape[0]
     rows, cols = (pad.shape[0] - 4, pad.shape[1] - 2 * SUB)
-    flipped = exact_dot(batch_map(1, lat_count, near_ref, pattern), map_ref[...], 0)
+    swapped = lax.axis_index("core") == 1
+    blocks = summed_blocks(lat_count, mine, other)
+    flipped = exact_dot(batch_map(1, lat_count, blocks, pattern, swapped), map_ref[...], 0)
     high = flipped.astype(BF16)
     low = (flipped - high.astype(F32)).astype(BF16)
     right = jnp.concatenate(
@@ -393,7 +429,7 @@
 def local(ensemble, observed, precision, interp_weight, stencil, owned, pattern):
     rows, cols, members = ensemble.shape
     batches = observed.shape[0]
-    lat_count, lon_count = (lax.axis_size("lat"), lax.axis_size("lon"))
+    lat_count, lon_count = (lax.axis_size("lat"), lax.axis_size(LON))
     tiles = lat_count * lon_count
     vmem = pl.BlockSpec(memory_space=pltpu.VMEM)
     anywhere = pl.BlockSpec(memory_space=pl.ANY)
@@ -415,7 +451,7 @@
         )(*operands)
 
     def exchange(blocks):
-        return lax.all_to_all(blocks, ("lat", "lon"), split_axis=0, concat_axis=0, tiled=True)
+        return lax.all_to_all(blocks, ("lat",) + LON, split_axis=0, concat_axis=0, tiled=True)
 
     small = (observed, precision, interp_weight, stencil, owned)
     side = shape(rows + SUB, members)
@@ -431,7 +467,7 @@
         ensemble,
         limit=63,
     )
-    sides = trade((side_0, side_1), "lon", True)
+    sides = trade((side_0, side_1), LON, True)
     padded = shape(rows + 4, cols + 2 * SUB, members)
     pad = call(pad_kernel, "pad", [hbm], padded, [pltpu.SemaphoreType.DMA], ensemble)
     end = shape(cols + 3 * SUB, members)
@@ -466,29 +502,33 @@
         *ends,
         pad,
     )
-    first_map, shares = call(
-        functools.partial(first_kernel, lat_count, lon_count),
+    column = shape(len(NEAR) * SUB, members)
+    first_map, mid, *sides = call(
+        functools.partial(first_kernel, lat_count),
         "first_batch",
         [vmem] * 3,
-        (shape(members, members), shape(tiles, SUB, members)),
-        [pltpu.VMEM((count, SUB, members), F32)],
+        (shape(members, members), column, column, column),
+        [],
         near,
         pattern,
         later,
     )
-    blocks = call(meet_kernel, "own_block", [vmem], slots, [], exchange(shares))
-    near = window(exchange(blocks), lat_count, lon_count)
+    sides = trade(sides, LON, True)
+    shares = call(meet_kernel, "meet", [vmem] * 3, shape(tiles // 2, *column.shape), [], mid, *sides)
+    shares = lax.all_to_all(shares, ("lat", "far"), split_axis=0, concat_axis=0, tiled=True)
+    other = lax.ppermute(shares, "core", [(0, 1), (1, 0)])
     parts = 8
     result = call(
         functools.partial(last_kernel, lat_count),
         "second_batch",
-        [vmem] * 4,
+        [vmem] * 5,
         shape(rows * cols, members),
         [
             pltpu.VMEM((rows * cols, members), F32),
             pltpu.SemaphoreType.DMA((parts,)),
         ],
-        near,
+        shares,
+        other,
         pattern,
         first_map,
         pad,
@@ -498,15 +538,17 @@
 
 
 def solution(mesh):
+    lat_count, lon_count = (mesh.shape["lat"], mesh.shape["lon"])
+    pairs = jax.sharding.Mesh(mesh.devices.reshape(lat_count, lon_count // 2, 2), ("lat",) + LON)
     placed = (
-        P("lat", "lon", None),
-        P(None, "lat", "lon", None),
-        P(None, "lat", "lon", None),
-        P(None, "lat", "lon", None, None),
-        P(None, "lat", "lon", None, None),
-        P(None, "lat", "lon", None),
-        P(None, "lat", "lon", None, None),
+        P("lat", LON, None),
+        P(None, "lat", LON, None),
+        P(None, "lat", LON, None),
+        P(None, "lat", LON, None, None),
+        P(None, "lat", LON, None, None),
+        P(None, "lat", LON, None),
+        P(None, "lat", LON, None, None),
     )
     return jax.shard_map(
-        local, mesh=mesh, in_specs=placed, out_specs=P("lat", "lon", None), check_vma=False
-    )
+        local, mesh=pairs, in_specs=placed, out_specs=P("lat", LON, None), check_vma=False
+    )

time: 60.2 us -> 57.7 us (0.958)
  blocking collectives: 19.2 us -> 11.2 us
  waiting for transfers between devices: 7.77 us -> 12.7 us
    all_to_all x2 -> x1, blocking collectives: 19.2 us -> 11.2 us  [local(): lax.all_to_all(shares, ('lat', 'far'), split_axis=0, concat_axis=0, tiled...]
    ppermute x4 -> x6, waiting for transfers between devices: 1.77 us -> 5.28 us  [trade(): results.append(lax.ppermute(block, axis, route))]
    ppermute x0 -> x1, waiting for transfers between devices: none -> 1.44 us  [local(): other = lax.ppermute(shares, 'core', [(0, 1), (1, 0)])]
    ppermute x4 -> x6, starting transfers between devices: 8.91 us -> 9.49 us  [trade(): results.append(lax.ppermute(block, axis, route))]
  transfers between devices with their start and end apart: 5 -> 8, of which waited for: 2 -> 4; matrix products, arithmetic and copies ran while one was open for 0% -> 0% of each run, Pallas kernels for 4% -> 4%
where the time goes in v6:
time: 57.7 us; the launch traced here: 57.4 us
  Pallas kernels  18.3 us (32%)
  starting transfers between devices  13 us (23%)
  waiting for transfers between devices  12.7 us (22%)
  blocking collectives  11.2 us (19%)
  local copies, waits for them, and re-layouts  2.06 us (4%)
    pallas_call x9, Pallas kernels, call(): pl.pallas_call(kernel, out_shape=out_shape, in_specs=specs, out_specs=out...  18.3 us
    all_to_all x1, blocking collectives, local(): lax.all_to_all(shares, ('lat', 'far'), split_axis=0, concat_axis=0, tiled...  11.2 us
    ppermute x6, starting transfers between devices, trade(): results.append(lax.ppermute(block, axis, route))  9.49 us
    all_to_all x1, waiting for transfers between devices, exchange(): lax.all_to_all(blocks, ('lat',) + LON, split_axis=0, concat_axis=0, tiled...  6 us
    ppermute x6, waiting for transfers between devices, trade(): results.append(lax.ppermute(block, axis, route))  5.28 us
    all_to_all x1, starting transfers between devices, exchange(): lax.all_to_all(blocks, ('lat',) + LON, split_axis=0, concat_axis=0, tiled...  3.47 us
    unnamed x7, local copies, waits for them, and re-layouts  2.06 us
    ppermute x1, waiting for transfers between devices, local(): other = lax.ppermute(shares, 'core', [(0, 1), (1, 0)])  1.44 us
  transfers between devices with their start and end apart: 8, of which 4 were waited for; matrix products, arithmetic and copies ran while one was open for 0% of the time, Pallas kernels for 4%

profile of v6, /device:TPU:0, one launch (start us, length us, event | category | flops | bytes accessed | tf_op | source)
XLA Modules:
  0.0 57.4 jit_solution(8021741538712500836)
XLA Ops:
  0.0 1.8 %start.1 = (f32[2,8,128]{2,1,0:T(8,128)}, f32[40,128]{1,0:T(8,128)}, f32[40,128]{1,0:T(8,128)}) custom-call(f32[2,1,1,8]{3,2,1,0:T(1,128)} %observed.1, f32[2,1,1,8]{3,2,1,0:T(1,128)} %precision.1, f32[2,1,1,4,8]{4,3,2,1,0:T(4,128)} %weight.1, s32[2,1,1,4,8]{4,3,2,1,0:T(4,128)} %stencil.1, s32[2,1,1,8]{3,2,1,0:T(1,128)} %owned.1, f32[32,128,128]{2,1,0:T(8,128)} %cells.3), custom_call_target="tpu_custom_call" | custom-call | tf_op jit(solution)/shard_map/start/pallas_call | solution.py:443
  1.8 3.4 %collective-permute-start = (f32[40,128]{1,0:T(8,128)}, f32[40,128]{1,0:T(8,128)S(1)}, u32[]{:S(2)}, u32[]{:S(2)}) collective-permute-start(f32[40,128]{1,0:T(8,128)} %get-tuple-element.17), channel_id=1, source_target_pairs={{0,7},{1,2},{2,1},{3,4},{4,3},{5,6},{6,5},{7,0},{8,15},{9,10},{10,... | collective-permute-start | bytes 61448 | tf_op jit(solution)/shard_map/ppermute | solution.py:31
  5.2 0.0 collective-permute-start.1
  5.2 0.0 copy-start
  5.2 1.6 %copy-done = f32[32,128,128]{2,1,0:T(8,128)S(1)} copy-done((f32[32,128,128]{2,1,0:T(8,128)S(1)}, f32[32,128,128]{2,1,0:T(8,128)}, u32[]{:S(2)}) %copy-start) | copy-done | bytes 2097176
  6.8 0.0 copy-start.1
  6.8 0.2 pad.1
  7.0 0.0 collective-permute-done.sides_0
  7.0 0.0 collective-permute-done.1.sides_1
  7.0 0.5 copy-done.1
  7.5 0.1 edge_rows.1
  7.5 0.0 copy-start.2
  7.5 0.8 %collective-permute-start.2 = (f32[152,128]{1,0:T(8,128)S(1)}, f32[152,128]{1,0:T(8,128)S(1)}, u32[]{:S(2)}, u32[]{:S(2)}) collective-permute-start(f32[152,128]{1,0:T(8,128)S(1)} %get-tuple-element.21), channel_id=1, source_target_pairs={{8,16},{16,8},{9,17},{17,9},{10,18},{18,10},{11,19},{19,11},{12,20... | collective-permute-start | bytes 233480 | tf_op jit(solution)/shard_map/ppermute | solution.py:31
  8.3 4.7 %collective-permute-start.3 = (f32[152,128]{1,0:T(8,128)S(1)}, f32[152,128]{1,0:T(8,128)S(1)}, u32[]{:S(2)}, u32[]{:S(2)}) collective-permute-start(f32[152,128]{1,0:T(8,128)S(1)} %get-tuple-element.22), channel_id=1, source_target_pairs={{0,8},{8,0},{16,24},{24,16},{1,9},{9,1},{17,25},{25,17},{2,10},{10... | collective-permute-start | bytes 233480 | tf_op jit(solution)/shard_map/ppermute | solution.py:31
  13.1 0.7 %row_shares.1.own = f32[8,128]{1,0:T(8,128)S(1)} custom-call(f32[2,8,128]{2,1,0:T(8,128)S(1)} %copy-done.1, f32[40,128]{1,0:T(8,128)S(1)} %get-tuple-element.19.left, f32[40,128]{1,0:T(8,128)S(1)} %get-tuple-element.20.right, f32[36,144,128]{2,1,0:T(8,128)S(1)} %pad.1), custom_call_target="tpu_custom_call" | custom-call | tf_op jit(solution)/shard_map/row_shares/pallas_call | solution.py:443
  13.8 0.0 collective-permute-done.2.ends_0
  13.8 1.8 %collective-permute-done.3.ends_1 = f32[152,128]{1,0:T(8,128)S(1)} collective-permute-done((f32[152,128]{1,0:T(8,128)S(1)}, f32[152,128]{1,0:T(8,128)S(1)}, u32[]{:S(2)}, u32[]{:S(2)}) %collective-permute-start.3) | collective-permute-done | bytes 77856 | tf_op jit(solution)/shard_map/ppermute | solution.py:31
  15.5 1.4 %prior.1 = bf16[32,5,2,128]{3,2,1,0:T(2,128)(2,1)} custom-call(f32[2,8,128]{2,1,0:T(8,128)S(1)} %copy-done.1, f32[8,128]{1,0:T(8,128)S(1)} %row_shares.1.own, f32[152,128]{1,0:T(8,128)S(1)} %collective-permute-done.2.ends_0, f32[152,128]{1,0:T(8,128)S(1)} %collective-permute-done.3.ends_1), custom_call_target="tpu_custom_call" | custom-call | tf_op jit(solution)/shard_map/prior/pallas_call | solution.py:443
  17.0 3.5 %all-to-all-start = ((bf16[32,5,2,128]{3,2,1,0:T(2,128)(2,1)}), bf16[32,5,2,128]{3,2,1,0:T(2,128)(2,1)S(1)}, u32[]{:S(2)}, u32[]{:S(2)}) async-start(bf16[32,5,2,128]{3,2,1,0:T(2,128)(2,1)} %prior.1), calls=%async_computation | async-start | bytes 163840 | tf_op jit(solution)/shard_map/all_to_all | solution.py:454
  20.5 0.0 copy-done.2
  20.5 1.6 %later_shares.1.later = f32[10,8,128]{2,1,0:T(8,128)S(1)} custom-call(f32[2,8,128]{2,1,0:T(8,128)S(1)} %copy-done.1, f32[40,128]{1,0:T(8,128)S(1)} %get-tuple-element.19.left, f32[40,128]{1,0:T(8,128)S(1)} %get-tuple-element.20.right, f32[152,128]{1,0:T(8,128)S(1)} %collective-permute-done.2.ends_0, f32[152,128]{1,0:T(8,128)S(1)} %collective-permute-done.3.ends_1, ...), custom_call_target="tpu_custom_call" | custom-call | tf_op jit(solution)/shard_map/later_shares/pallas_call | solution.py:443
  22.1 6.0 %all-to-all-done.near_ref = bf16[32,5,2,128]{3,2,1,0:T(2,128)(2,1)S(1)} async-done(((bf16[32,5,2,128]{3,2,1,0:T(2,128)(2,1)}), bf16[32,5,2,128]{3,2,1,0:T(2,128)(2,1)S(1)}, u32[]{:S(2)}, u32[]{:S(2)}) %all-to-all-start) | async-done | bytes 81952 | tf_op jit(solution)/shard_map/all_to_all | solution.py:454
  28.1 5.3 %first_batch.1 = (f32[128,128]{1,0:T(8,128)S(1)}, f32[24,128]{1,0:T(8,128)S(1)}, f32[24,128]{1,0:T(8,128)S(1)}, f32[24,128]{1,0:T(8,128)S(1)}) custom-call(bf16[32,5,2,128]{3,2,1,0:T(2,128)(2,1)S(1)} %all-to-all-done.near_ref, s32[2,1,1,5,8]{4,3,2,1,0:T(8,128)S(1)} %copy.8.pattern, f32[10,8,128]{2,1,0:T(8,128)S(1)} %later_shares.1.later), custom_call_target="tpu_custom_call" | custom-call | tf_op jit(solution)/shard_map/first_batch/pallas_call | solution.py:443
  33.4 0.4 collective-permute-start.4
  33.8 0.2 collective-permute-start.5
  34.0 3.5 %collective-permute-done.4.sides_0 = f32[24,128]{1,0:T(8,128)S(1)} collective-permute-done((f32[24,128]{1,0:T(8,128)S(1)}, f32[24,128]{1,0:T(8,128)S(1)}, u32[]{:S(2)}, u32[]{:S(2)}) %collective-permute-start.4) | collective-permute-done | bytes 12320 | tf_op jit(solution)/shard_map/ppermute | solution.py:31
  37.5 0.0 collective-permute-done.5.sides_1
  37.5 11.2 %all_to_all.10.mine = f32[16,24,128]{2,1,0:T(8,128)S(1)} all-to-all(f32[16,24,128]{2,1,0:T(8,128)S(1)} %meet.1), channel_id=1, replica_groups=mesh['lat'=4,'far'=4,'core'=2] {'lat','far'}, dimensions={0} | all-to-all | bytes 393216 | tf_op jit(solution)/shard_map/all_to_all | solution.py:518
  48.7 0.0 collective-permute-start.6
  48.7 1.4 %collective-permute-done.6.other = f32[16,24,128]{2,1,0:T(8,128)S(1)} collective-permute-done((f32[16,24,128]{2,1,0:T(8,128)S(1)}, f32[16,24,128]{2,1,0:T(8,128)S(1)}, u32[]{:S(2)}, u32[]{:S(2)}) %collective-permute-start.6) | collective-permute-done | bytes 196640 | tf_op jit(solution)/shard_map/ppermute | solution.py:519
  50.2 7.2 %second_batch.1 = f32[4096,128]{1,0:T(8,128)} custom-call(f32[16,24,128]{2,1,0:T(8,128)S(1)} %all_to_all.10.mine, f32[16,24,128]{2,1,0:T(8,128)S(1)} %collective-permute-done.6.other, s32[2,1,1,5,8]{4,3,2,1,0:T(8,128)S(1)} %copy.8.pattern, f32[128,128]{1,0:T(8,128)S(1)} %get-tuple-element.26.map_ref, f32[36,144,128]{2,1,0:T(8,128)S(1)} %pad.1), custom_call_target="tpu_custom_call" | custom-call | tf_op jit(solution)/shard_map/second_batch/pallas_call | solution.py:443
  (2 shorter events, 0.0 us)
Async XLA Ops:
  1.8 5.2 %collective-permute-start = (f32[40,128]{1,0:T(8,128)}, f32[40,128]{1,0:T(8,128)S(1)}, u32[]{:S(2)}, u32[]{:S(2)}) collective-permute-start(f32[40,128]{1,0:T(8,128)} %get-tuple-element.17), channel_id=1, source_target_pairs={{0,7},{1,2},{2,1},{3,4},{4,3},{5,6},{6,5},{7,0},{8,15},{9,10},{10,... | collective-permute-start | bytes 61448 | tf_op jit(solution)/shard_map/ppermute | solution.py:31
  5.2 1.8 %collective-permute-start.1 = (f32[40,128]{1,0:T(8,128)}, f32[40,128]{1,0:T(8,128)S(1)}, u32[]{:S(2)}, u32[]{:S(2)}) collective-permute-start(f32[40,128]{1,0:T(8,128)} %get-tuple-element.18), channel_id=1, source_target_pairs={{0,1},{1,0},{2,3},{3,2},{4,5},{5,4},{6,7},{7,6},{8,9},{9,8},{10,11... | collective-permute-start | bytes 61448 | tf_op jit(solution)/shard_map/ppermute | solution.py:31
  5.2 1.6 %copy-start = (f32[32,128,128]{2,1,0:T(8,128)S(1)}, f32[32,128,128]{2,1,0:T(8,128)}, u32[]{:S(2)}) copy-start(f32[32,128,128]{2,1,0:T(8,128)} %cells.3) | copy-start | bytes 6291460
  6.8 0.7 %copy-start.1 = (f32[2,8,128]{2,1,0:T(8,128)S(1)}, f32[2,8,128]{2,1,0:T(8,128)}, u32[]{:S(2)}) copy-start(f32[2,8,128]{2,1,0:T(8,128)} %get-tuple-element.16.mine) | copy-start | bytes 24580
  7.5 12.9 %copy-start.2 = (s32[2,1,1,5,8]{4,2,3,1,0:T(1,128)S(1)}, s32[2,1,1,5,8]{4,2,3,1,0:T(1,128)}, u32[]{:S(2)}) copy-start(s32[2,1,1,5,8]{4,2,3,1,0:T(1,128)} %param.13) | copy-start | bytes 964
  7.5 6.2 %collective-permute-start.2 = (f32[152,128]{1,0:T(8,128)S(1)}, f32[152,128]{1,0:T(8,128)S(1)}, u32[]{:S(2)}, u32[]{:S(2)}) collective-permute-start(f32[152,128]{1,0:T(8,128)S(1)} %get-tuple-element.21), channel_id=1, source_target_pairs={{8,16},{16,8},{9,17},{17,9},{10,18},{18,10},{11,19},{19,11},{12,20... | collective-permute-start | bytes 233480 | tf_op jit(solution)/shard_map/ppermute | solution.py:31
  8.3 7.2 %collective-permute-start.3 = (f32[152,128]{1,0:T(8,128)S(1)}, f32[152,128]{1,0:T(8,128)S(1)}, u32[]{:S(2)}, u32[]{:S(2)}) collective-permute-start(f32[152,128]{1,0:T(8,128)S(1)} %get-tuple-element.22), channel_id=1, source_target_pairs={{0,8},{8,0},{16,24},{24,16},{1,9},{9,1},{17,25},{25,17},{2,10},{10... | collective-permute-start | bytes 233480 | tf_op jit(solution)/shard_map/ppermute | solution.py:31
  17.0 11.1 %all-to-all-start = ((bf16[32,5,2,128]{3,2,1,0:T(2,128)(2,1)}), bf16[32,5,2,128]{3,2,1,0:T(2,128)(2,1)S(1)}, u32[]{:S(2)}, u32[]{:S(2)}) async-start(bf16[32,5,2,128]{3,2,1,0:T(2,128)(2,1)} %prior.1), calls=%async_computation | async-start | bytes 163840 | tf_op jit(solution)/shard_map/all_to_all | solution.py:454
  33.4 4.1 %collective-permute-start.4 = (f32[24,128]{1,0:T(8,128)S(1)}, f32[24,128]{1,0:T(8,128)S(1)}, u32[]{:S(2)}, u32[]{:S(2)}) collective-permute-start(f32[24,128]{1,0:T(8,128)S(1)} %get-tuple-element.24), channel_id=1, source_target_pairs={{0,7},{1,2},{2,1},{3,4},{4,3},{5,6},{6,5},{7,0},{8,15},{9,10},{10,... | collective-permute-start | bytes 36872 | tf_op jit(solution)/shard_map/ppermute | solution.py:31
  33.8 3.7 %collective-permute-start.5 = (f32[24,128]{1,0:T(8,128)S(1)}, f32[24,128]{1,0:T(8,128)S(1)}, u32[]{:S(2)}, u32[]{:S(2)}) collective-permute-start(f32[24,128]{1,0:T(8,128)S(1)} %get-tuple-element.25), channel_id=1, source_target_pairs={{0,1},{1,0},{2,3},{3,2},{4,5},{5,4},{6,7},{7,6},{8,9},{9,8},{10,11... | collective-permute-start | bytes 36872 | tf_op jit(solution)/shard_map/ppermute | solution.py:31
  48.7 1.4 %collective-permute-start.6 = (f32[16,24,128]{2,1,0:T(8,128)S(1)}, f32[16,24,128]{2,1,0:T(8,128)S(1)}, u32[]{:S(2)}, u32[]{:S(2)}) collective-permute-start(f32[16,24,128]{2,1,0:T(8,128)S(1)} %all_to_all.10.mine), channel_id=1, source_target_pairs={{0,1},{1,0},{2,3},{3,2},{4,5},{5,4},{6,7},{7,6},{8,9},{9,8},{10,11... | collective-permute-start | bytes 589832 | tf_op jit(solution)/shard_map/ppermute | solution.py:519

commit v7 on v6

--- a/solution.py
+++ b/solution.py
@@ -213,10 +213,6 @@
     return 0 if lat_count <= WIN else jnp.clip(my_lat - REACH, 0, lat_count - WIN)
 
 
-def row_of(block, j):
-    return jnp.broadcast_to(block[j:j + 1, :], block.shape)
-
-
 def column_of(block, j):
     return jnp.broadcast_to(block[:, j:j + 1], block.shape)
 
@@ -226,10 +222,11 @@
     return guess * (2.0 - value * guess)
 
 
-def pivot_rows(block, k, between):
+def pivot_rows(block, k, held, between):
     sub = lax.broadcasted_iota(jnp.int32, block.shape, 0)
     lane = lax.broadcasted_iota(jnp.int32, block.shape, 1) - k * SUB
-    rows = [row_of(block, r) for r in range(SUB)]
+    held[pl.ds(k * SUB, SUB), :] = block
+    rows = [held[pl.ds(k * SUB + r, SUB, stride=0), :] for r in range(SUB)]
     at = {(r, n): column_of(rows[r], k * SUB + n) for r in range(SUB) for n in range(r + 1)}
     here = (lane >= 0) & (lane < SUB)
     rows = [jnp.where(here, jnp.where(lane == r, 1.0, 0.0), row) for r, row in enumerate(rows)]
@@ -265,7 +262,7 @@
     return rows, jnp.where(lane < SUB, inverse * lax.rsqrt(scale), 0.0)
 
 
-def eliminate(blocks):
+def eliminate(blocks, held):
     count = len(blocks) - 1
     blocks = list(blocks)
     lane = lax.broadcasted_iota(jnp.int32, blocks[0].shape, 1)
@@ -286,7 +283,7 @@
                 update(*task)
             del waiting[:share_of]
 
-        pivot, rows = pivot_rows(blocks[k], k, between)
+        pivot, rows = pivot_rows(blocks[k], k, held, between)
         update(k + 1, k, pivot)
         waiting = [(i, k, pivot) for i in range(k + 2, count + 1)]
         inverse.append(rows)
@@ -329,7 +326,7 @@
     return (value - mean).astype(BF16).astype(F32), innov
 
 
-def batch_map(batch, lat_count, blocks, pattern, swapped):
+def batch_map(batch, lat_count, blocks, pattern, swapped, held_rows):
     scaled, innov = blocks
     held = min(WIN, lat_count)
     count = scaled.shape[0]
@@ -364,7 +361,7 @@
         blocks.append(block + jnp.where(lane - k * SUB == sub, members - 1.0, 0.0))
     proj = jnp.sum(product[members:members + SUB, :], axis=0, keepdims=True)
     blocks.append(jnp.broadcast_to(proj, (SUB, LANES)))
-    inverse, weights = eliminate(blocks)
+    inverse, weights = eliminate(blocks, held_rows)
     flipped = jnp.concatenate(inverse, axis=0) * (members - 1.0) ** 0.5 - weights
     return flipped - jnp.mean(flipped, axis=-1, keepdims=True) + 1.0 / members
 
@@ -375,8 +372,8 @@
     )
 
 
-def first_kernel(lat_count, near_ref, pattern, later, map_ref, mid_ref, out_0, out_1):
-    flipped = batch_map(0, lat_count, own_blocks(near_ref), pattern, None)
+def first_kernel(lat_count, near_ref, pattern, later, map_ref, mid_ref, out_0, out_1, held_rows):
+    flipped = batch_map(0, lat_count, own_blocks(near_ref), pattern, None, held_rows)
     map_ref[...] = flipped
     count = len(NEAR) ** 2
     moved = exact_dot(later[pl.ds(0, count)].reshape(-1, LANES), flipped, 1)
@@ -390,12 +387,12 @@
     out_1[...] = jnp.where(forward, left, right)
 
 
-def last_kernel(lat_count, mine, other, pattern, map_ref, pad, out_ref, result, out_sem):
+def last_kernel(lat_count, mine, other, pattern, map_ref, pad, out_ref, result, held_rows, out_sem):
     parts = out_sem.shape[0]
     rows, cols = (pad.shape[0] - 4, pad.shape[1] - 2 * SUB)
     swapped = lax.axis_index("core") == 1
     blocks = summed_blocks(lat_count, mine, other)
-    flipped = exact_dot(batch_map(1, lat_count, blocks, pattern, swapped), map_ref[...], 0)
+    flipped = exact_dot(batch_map(1, lat_count, blocks, pattern, swapped, held_rows), map_ref[...], 0)
     high = flipped.astype(BF16)
     low = (flipped - high.astype(F32)).astype(BF16)
     right = jnp.concatenate(
@@ -503,12 +500,13 @@
         pad,
     )
     column = shape(len(NEAR) * SUB, members)
+    held_rows = pltpu.VMEM((members + SUB, members), F32)
     first_map, mid, *sides = call(
         functools.partial(first_kernel, lat_count),
         "first_batch",
         [vmem] * 3,
         (shape(members, members), column, column, column),
-        [],
+        [held_rows],
         near,
         pattern,
         later,
@@ -525,6 +523,7 @@
         shape(rows * cols, members),
         [
             pltpu.VMEM((rows * cols, members), F32),
+            held_rows,
             pltpu.SemaphoreType.DMA((parts,)),
         ],
         shares,

time: 57.7 us -> 57 us (0.988)
  Pallas kernels: 18.3 us -> 17.6 us
    pallas_call x9, Pallas kernels: 18.3 us -> 17.6 us  [call(): pl.pallas_call(kernel, out_shape=out_shape, in_specs=specs, out_specs=out...]
where the time goes in v7:
time: 57 us; the launch traced here: 56.6 us
  Pallas kernels  17.6 us (31%)
  starting transfers between devices  13 us (23%)
  waiting for transfers between devices  12.7 us (22%)
  blocking collectives  11.2 us (20%)
  local copies, waits for them, and re-layouts  2.06 us (4%)
    pallas_call x9, Pallas kernels, call(): pl.pallas_call(kernel, out_shape=out_shape, in_specs=specs, out_specs=out...  17.6 us
    all_to_all x1, blocking collectives, local(): lax.all_to_all(shares, ('lat', 'far'), split_axis=0, concat_axis=0, tiled...  11.2 us
    ppermute x6, starting transfers between devices, trade(): results.append(lax.ppermute(block, axis, route))  9.49 us
    all_to_all x1, waiting for transfers between devices, exchange(): lax.all_to_all(blocks, ('lat',) + LON, split_axis=0, concat_axis=0, tiled...  6 us
    ppermute x6, waiting for transfers between devices, trade(): results.append(lax.ppermute(block, axis, route))  5.28 us
    all_to_all x1, starting transfers between devices, exchange(): lax.all_to_all(blocks, ('lat',) + LON, split_axis=0, concat_axis=0, tiled...  3.47 us
    unnamed x7, local copies, waits for them, and re-layouts  2.06 us
    ppermute x1, waiting for transfers between devices, local(): other = lax.ppermute(shares, 'core', [(0, 1), (1, 0)])  1.44 us
  transfers between devices with their start and end apart: 8, of which 4 were waited for; matrix products, arithmetic and copies ran while one was open for 0% of the time, Pallas kernels for 4%

profile of v7, /device:TPU:0, one launch (start us, length us, event | category | flops | bytes accessed | tf_op | source)
XLA Modules:
  0.0 56.6 jit_solution(17738124991710850779)
XLA Ops:
  0.0 1.8 %start.1 = (f32[2,8,128]{2,1,0:T(8,128)}, f32[40,128]{1,0:T(8,128)}, f32[40,128]{1,0:T(8,128)}) custom-call(f32[2,1,1,8]{3,2,1,0:T(1,128)} %observed.1, f32[2,1,1,8]{3,2,1,0:T(1,128)} %precision.1, f32[2,1,1,4,8]{4,3,2,1,0:T(4,128)} %weight.1, s32[2,1,1,4,8]{4,3,2,1,0:T(4,128)} %stencil.1, s32[2,1,1,8]{3,2,1,0:T(1,128)} %owned.1, f32[32,128,128]{2,1,0:T(8,128)} %cells.3), custom_call_target="tpu_custom_call" | custom-call | tf_op jit(solution)/shard_map/start/pallas_call | solution.py:440
  1.8 3.4 %collective-permute-start = (f32[40,128]{1,0:T(8,128)}, f32[40,128]{1,0:T(8,128)S(1)}, u32[]{:S(2)}, u32[]{:S(2)}) collective-permute-start(f32[40,128]{1,0:T(8,128)} %get-tuple-element.17), channel_id=1, source_target_pairs={{0,7},{1,2},{2,1},{3,4},{4,3},{5,6},{6,5},{7,0},{8,15},{9,10},{10,... | collective-permute-start | bytes 61448 | tf_op jit(solution)/shard_map/ppermute | solution.py:31
  5.2 0.0 collective-permute-start.1
  5.2 0.0 copy-start
  5.2 1.6 %copy-done = f32[32,128,128]{2,1,0:T(8,128)S(1)} copy-done((f32[32,128,128]{2,1,0:T(8,128)S(1)}, f32[32,128,128]{2,1,0:T(8,128)}, u32[]{:S(2)}) %copy-start) | copy-done | bytes 2097176
  6.8 0.0 copy-start.1
  6.8 0.2 pad.1
  7.0 0.0 collective-permute-done.sides_0
  7.0 0.0 collective-permute-done.1.sides_1
  7.0 0.5 copy-done.1
  7.5 0.1 edge_rows.1
  7.5 0.0 copy-start.2
  7.5 0.8 %collective-permute-start.2 = (f32[152,128]{1,0:T(8,128)S(1)}, f32[152,128]{1,0:T(8,128)S(1)}, u32[]{:S(2)}, u32[]{:S(2)}) collective-permute-start(f32[152,128]{1,0:T(8,128)S(1)} %get-tuple-element.21), channel_id=1, source_target_pairs={{8,16},{16,8},{9,17},{17,9},{10,18},{18,10},{11,19},{19,11},{12,20... | collective-permute-start | bytes 233480 | tf_op jit(solution)/shard_map/ppermute | solution.py:31
  8.3 4.7 %collective-permute-start.3 = (f32[152,128]{1,0:T(8,128)S(1)}, f32[152,128]{1,0:T(8,128)S(1)}, u32[]{:S(2)}, u32[]{:S(2)}) collective-permute-start(f32[152,128]{1,0:T(8,128)S(1)} %get-tuple-element.22), channel_id=1, source_target_pairs={{0,8},{8,0},{16,24},{24,16},{1,9},{9,1},{17,25},{25,17},{2,10},{10... | collective-permute-start | bytes 233480 | tf_op jit(solution)/shard_map/ppermute | solution.py:31
  13.1 0.7 %row_shares.1.own = f32[8,128]{1,0:T(8,128)S(1)} custom-call(f32[2,8,128]{2,1,0:T(8,128)S(1)} %copy-done.1, f32[40,128]{1,0:T(8,128)S(1)} %get-tuple-element.19.left, f32[40,128]{1,0:T(8,128)S(1)} %get-tuple-element.20.right, f32[36,144,128]{2,1,0:T(8,128)S(1)} %pad.1), custom_call_target="tpu_custom_call" | custom-call | tf_op jit(solution)/shard_map/row_shares/pallas_call | solution.py:440
  13.8 0.0 collective-permute-done.2.ends_0
  13.8 1.8 %collective-permute-done.3.ends_1 = f32[152,128]{1,0:T(8,128)S(1)} collective-permute-done((f32[152,128]{1,0:T(8,128)S(1)}, f32[152,128]{1,0:T(8,128)S(1)}, u32[]{:S(2)}, u32[]{:S(2)}) %collective-permute-start.3) | collective-permute-done | bytes 77856 | tf_op jit(solution)/shard_map/ppermute | solution.py:31
  15.5 1.4 %prior.1 = bf16[32,5,2,128]{3,2,1,0:T(2,128)(2,1)} custom-call(f32[2,8,128]{2,1,0:T(8,128)S(1)} %copy-done.1, f32[8,128]{1,0:T(8,128)S(1)} %row_shares.1.own, f32[152,128]{1,0:T(8,128)S(1)} %collective-permute-done.2.ends_0, f32[152,128]{1,0:T(8,128)S(1)} %collective-permute-done.3.ends_1), custom_call_target="tpu_custom_call" | custom-call | tf_op jit(solution)/shard_map/prior/pallas_call | solution.py:440
  17.0 3.5 %all-to-all-start = ((bf16[32,5,2,128]{3,2,1,0:T(2,128)(2,1)}), bf16[32,5,2,128]{3,2,1,0:T(2,128)(2,1)S(1)}, u32[]{:S(2)}, u32[]{:S(2)}) async-start(bf16[32,5,2,128]{3,2,1,0:T(2,128)(2,1)} %prior.1), calls=%async_computation | async-start | bytes 163840 | tf_op jit(solution)/shard_map/all_to_all | solution.py:451
  20.5 0.0 copy-done.2
  20.5 1.6 %later_shares.1.later = f32[10,8,128]{2,1,0:T(8,128)S(1)} custom-call(f32[2,8,128]{2,1,0:T(8,128)S(1)} %copy-done.1, f32[40,128]{1,0:T(8,128)S(1)} %get-tuple-element.19.left, f32[40,128]{1,0:T(8,128)S(1)} %get-tuple-element.20.right, f32[152,128]{1,0:T(8,128)S(1)} %collective-permute-done.2.ends_0, f32[152,128]{1,0:T(8,128)S(1)} %collective-permute-done.3.ends_1, ...), custom_call_target="tpu_custom_call" | custom-call | tf_op jit(solution)/shard_map/later_shares/pallas_call | solution.py:440
  22.1 6.0 %all-to-all-done.near_ref = bf16[32,5,2,128]{3,2,1,0:T(2,128)(2,1)S(1)} async-done(((bf16[32,5,2,128]{3,2,1,0:T(2,128)(2,1)}), bf16[32,5,2,128]{3,2,1,0:T(2,128)(2,1)S(1)}, u32[]{:S(2)}, u32[]{:S(2)}) %all-to-all-start) | async-done | bytes 81952 | tf_op jit(solution)/shard_map/all_to_all | solution.py:451
  28.1 4.9 %first_batch.1 = (f32[128,128]{1,0:T(8,128)S(1)}, f32[24,128]{1,0:T(8,128)S(1)}, f32[24,128]{1,0:T(8,128)S(1)}, f32[24,128]{1,0:T(8,128)S(1)}) custom-call(bf16[32,5,2,128]{3,2,1,0:T(2,128)(2,1)S(1)} %all-to-all-done.near_ref, s32[2,1,1,5,8]{4,3,2,1,0:T(8,128)S(1)} %copy.8.pattern, f32[10,8,128]{2,1,0:T(8,128)S(1)} %later_shares.1.later), custom_call_target="tpu_custom_call" | custom-call | tf_op jit(solution)/shard_map/first_batch/pallas_call | solution.py:440
  32.9 0.4 collective-permute-start.4
  33.3 0.2 collective-permute-start.5
  33.5 3.5 %collective-permute-done.4.sides_0 = f32[24,128]{1,0:T(8,128)S(1)} collective-permute-done((f32[24,128]{1,0:T(8,128)S(1)}, f32[24,128]{1,0:T(8,128)S(1)}, u32[]{:S(2)}, u32[]{:S(2)}) %collective-permute-start.4) | collective-permute-done | bytes 12320 | tf_op jit(solution)/shard_map/ppermute | solution.py:31
  37.0 0.0 collective-permute-done.5.sides_1
  37.1 11.2 %all_to_all.10.mine = f32[16,24,128]{2,1,0:T(8,128)S(1)} all-to-all(f32[16,24,128]{2,1,0:T(8,128)S(1)} %meet.1), channel_id=1, replica_groups=mesh['lat'=4,'far'=4,'core'=2] {'lat','far'}, dimensions={0} | all-to-all | bytes 393216 | tf_op jit(solution)/shard_map/all_to_all | solution.py:516
  48.2 0.0 collective-permute-start.6
  48.2 1.4 %collective-permute-done.6.other = f32[16,24,128]{2,1,0:T(8,128)S(1)} collective-permute-done((f32[16,24,128]{2,1,0:T(8,128)S(1)}, f32[16,24,128]{2,1,0:T(8,128)S(1)}, u32[]{:S(2)}, u32[]{:S(2)}) %collective-permute-start.6) | collective-permute-done | bytes 196640 | tf_op jit(solution)/shard_map/ppermute | solution.py:517
  49.7 7.0 %second_batch.1 = f32[4096,128]{1,0:T(8,128)} custom-call(f32[16,24,128]{2,1,0:T(8,128)S(1)} %all_to_all.10.mine, f32[16,24,128]{2,1,0:T(8,128)S(1)} %collective-permute-done.6.other, s32[2,1,1,5,8]{4,3,2,1,0:T(8,128)S(1)} %copy.8.pattern, f32[128,128]{1,0:T(8,128)S(1)} %get-tuple-element.26.map_ref, f32[36,144,128]{2,1,0:T(8,128)S(1)} %pad.1), custom_call_target="tpu_custom_call" | custom-call | tf_op jit(solution)/shard_map/second_batch/pallas_call | solution.py:440
  (2 shorter events, 0.0 us)
Async XLA Ops:
  1.8 5.2 %collective-permute-start = (f32[40,128]{1,0:T(8,128)}, f32[40,128]{1,0:T(8,128)S(1)}, u32[]{:S(2)}, u32[]{:S(2)}) collective-permute-start(f32[40,128]{1,0:T(8,128)} %get-tuple-element.17), channel_id=1, source_target_pairs={{0,7},{1,2},{2,1},{3,4},{4,3},{5,6},{6,5},{7,0},{8,15},{9,10},{10,... | collective-permute-start | bytes 61448 | tf_op jit(solution)/shard_map/ppermute | solution.py:31
  5.2 1.8 %collective-permute-start.1 = (f32[40,128]{1,0:T(8,128)}, f32[40,128]{1,0:T(8,128)S(1)}, u32[]{:S(2)}, u32[]{:S(2)}) collective-permute-start(f32[40,128]{1,0:T(8,128)} %get-tuple-element.18), channel_id=1, source_target_pairs={{0,1},{1,0},{2,3},{3,2},{4,5},{5,4},{6,7},{7,6},{8,9},{9,8},{10,11... | collective-permute-start | bytes 61448 | tf_op jit(solution)/shard_map/ppermute | solution.py:31
  5.2 1.6 %copy-start = (f32[32,128,128]{2,1,0:T(8,128)S(1)}, f32[32,128,128]{2,1,0:T(8,128)}, u32[]{:S(2)}) copy-start(f32[32,128,128]{2,1,0:T(8,128)} %cells.3) | copy-start | bytes 6291460
  6.8 0.7 %copy-start.1 = (f32[2,8,128]{2,1,0:T(8,128)S(1)}, f32[2,8,128]{2,1,0:T(8,128)}, u32[]{:S(2)}) copy-start(f32[2,8,128]{2,1,0:T(8,128)} %get-tuple-element.16.mine) | copy-start | bytes 24580
  7.5 12.9 %copy-start.2 = (s32[2,1,1,5,8]{4,2,3,1,0:T(1,128)S(1)}, s32[2,1,1,5,8]{4,2,3,1,0:T(1,128)}, u32[]{:S(2)}) copy-start(s32[2,1,1,5,8]{4,2,3,1,0:T(1,128)} %param.13) | copy-start | bytes 964
  7.5 6.2 %collective-permute-start.2 = (f32[152,128]{1,0:T(8,128)S(1)}, f32[152,128]{1,0:T(8,128)S(1)}, u32[]{:S(2)}, u32[]{:S(2)}) collective-permute-start(f32[152,128]{1,0:T(8,128)S(1)} %get-tuple-element.21), channel_id=1, source_target_pairs={{8,16},{16,8},{9,17},{17,9},{10,18},{18,10},{11,19},{19,11},{12,20... | collective-permute-start | bytes 233480 | tf_op jit(solution)/shard_map/ppermute | solution.py:31
  8.3 7.2 %collective-permute-start.3 = (f32[152,128]{1,0:T(8,128)S(1)}, f32[152,128]{1,0:T(8,128)S(1)}, u32[]{:S(2)}, u32[]{:S(2)}) collective-permute-start(f32[152,128]{1,0:T(8,128)S(1)} %get-tuple-element.22), channel_id=1, source_target_pairs={{0,8},{8,0},{16,24},{24,16},{1,9},{9,1},{17,25},{25,17},{2,10},{10... | collective-permute-start | bytes 233480 | tf_op jit(solution)/shard_map/ppermute | solution.py:31
  17.0 11.1 %all-to-all-start = ((bf16[32,5,2,128]{3,2,1,0:T(2,128)(2,1)}), bf16[32,5,2,128]{3,2,1,0:T(2,128)(2,1)S(1)}, u32[]{:S(2)}, u32[]{:S(2)}) async-start(bf16[32,5,2,128]{3,2,1,0:T(2,128)(2,1)} %prior.1), calls=%async_computation | async-start | bytes 163840 | tf_op jit(solution)/shard_map/all_to_all | solution.py:451
  32.9 4.1 %collective-permute-start.4 = (f32[24,128]{1,0:T(8,128)S(1)}, f32[24,128]{1,0:T(8,128)S(1)}, u32[]{:S(2)}, u32[]{:S(2)}) collective-permute-start(f32[24,128]{1,0:T(8,128)S(1)} %get-tuple-element.24), channel_id=1, source_target_pairs={{0,7},{1,2},{2,1},{3,4},{4,3},{5,6},{6,5},{7,0},{8,15},{9,10},{10,... | collective-permute-start | bytes 36872 | tf_op jit(solution)/shard_map/ppermute | solution.py:31
  33.3 3.7 %collective-permute-start.5 = (f32[24,128]{1,0:T(8,128)S(1)}, f32[24,128]{1,0:T(8,128)S(1)}, u32[]{:S(2)}, u32[]{:S(2)}) collective-permute-start(f32[24,128]{1,0:T(8,128)S(1)} %get-tuple-element.25), channel_id=1, source_target_pairs={{0,1},{1,0},{2,3},{3,2},{4,5},{5,4},{6,7},{7,6},{8,9},{9,8},{10,11... | collective-permute-start | bytes 36872 | tf_op jit(solution)/shard_map/ppermute | solution.py:31
  48.2 1.4 %collective-permute-start.6 = (f32[16,24,128]{2,1,0:T(8,128)S(1)}, f32[16,24,128]{2,1,0:T(8,128)S(1)}, u32[]{:S(2)}, u32[]{:S(2)}) collective-permute-start(f32[16,24,128]{2,1,0:T(8,128)S(1)} %all_to_all.10.mine), channel_id=1, source_target_pairs={{0,1},{1,0},{2,3},{3,2},{4,5},{5,4},{6,7},{7,6},{8,9},{9,8},{10,11... | collective-permute-start | bytes 589832 | tf_op jit(solution)/shard_map/ppermute | solution.py:517

commit v8 on v7

--- a/solution.py
+++ b/solution.py
@@ -217,11 +217,6 @@
     return jnp.broadcast_to(block[:, j:j + 1], block.shape)
 
 
-def reciprocal(value):
-    guess = pl.reciprocal(value, approx=True)
-    return guess * (2.0 - value * guess)
-
-
 def pivot_rows(block, k, held, between):
     sub = lax.broadcasted_iota(jnp.int32, block.shape, 0)
     lane = lax.broadcasted_iota(jnp.int32, block.shape, 1) - k * SUB
@@ -234,15 +229,22 @@
     for j in range(0, SUB, 2):
         a, b, c = (at[j, j], at[j + 1, j], at[j + 1, j + 1])
         det = a * c - b * b
-        over_det = reciprocal(det)
+        guess = pl.reciprocal(det, approx=True)
+        better = 2.0 - det * guess
+        over_det = guess * better
         top, bottom = (rows[j], rows[j + 1])
         rest = range(j + 2, SUB)
         upper = {n: (at[n, j], at[n, j + 1]) for n in rest}
         for r in rest:
-            first = (at[r, j] * c - at[r, j + 1] * b) * over_det
-            second = (at[r, j + 1] * a - at[r, j] * b) * over_det
-            for n in range(j + 2, r + 1):
-                at[r, n] = at[r, n] - (first * upper[n][0] + second * upper[n][1])
+            first, second = (at[r, j] * c - at[r, j + 1] * b, at[r, j + 1] * a - at[r, j] * b)
+            if r < j + 4:
+                for n in range(j + 2, r + 1):
+                    taken = first * upper[n][0] + second * upper[n][1]
+                    at[r, n] = at[r, n] - (taken * guess) * better
+            first, second = (first * over_det, second * over_det)
+            if r >= j + 4:
+                for n in range(j + 2, r + 1):
+                    at[r, n] = at[r, n] - (first * upper[n][0] + second * upper[n][1])
             rows[r] = rows[r] - (first * top + second * bottom)
         a_part, b_part, c_part = (a * over_det, b * over_det, c * over_det)
         for r in range(j):

time: 57 us -> 56.6 us (level)
  no operation moved by 1% of the time
where the time goes in v8:
time: 56.6 us; the launch traced here: 56.3 us
  Pallas kernels  17.2 us (30%)
  starting transfers between devices  13 us (23%)
  waiting for transfers between devices  12.7 us (22%)
  blocking collectives  11.2 us (20%)
  local copies, waits for them, and re-layouts  2.06 us (4%)
    pallas_call x9, Pallas kernels, call(): pl.pallas_call(kernel, out_shape=out_shape, in_specs=specs, out_specs=out...  17.2 us
    all_to_all x1, blocking collectives, local(): lax.all_to_all(shares, ('lat', 'far'), split_axis=0, concat_axis=0, tiled...  11.2 us
    ppermute x6, starting transfers between devices, trade(): results.append(lax.ppermute(block, axis, route))  9.49 us
    all_to_all x1, waiting for transfers between devices, exchange(): lax.all_to_all(blocks, ('lat',) + LON, split_axis=0, concat_axis=0, tiled...  6 us
    ppermute x6, waiting for transfers between devices, trade(): results.append(lax.ppermute(block, axis, route))  5.28 us
    all_to_all x1, starting transfers between devices, exchange(): lax.all_to_all(blocks, ('lat',) + LON, split_axis=0, concat_axis=0, tiled...  3.47 us
    unnamed x7, local copies, waits for them, and re-layouts  2.06 us
    ppermute x1, waiting for transfers between devices, local(): other = lax.ppermute(shares, 'core', [(0, 1), (1, 0)])  1.44 us
  transfers between devices with their start and end apart: 8, of which 4 were waited for; matrix products, arithmetic and copies ran while one was open for 0% of the time, Pallas kernels for 4%

profile of v8, /device:TPU:0, one launch (start us, length us, event | category | flops | bytes accessed | tf_op | source)
XLA Modules:
  0.0 56.3 jit_solution(651396069646310739)
XLA Ops:
  0.0 1.8 %start.1 = (f32[2,8,128]{2,1,0:T(8,128)}, f32[40,128]{1,0:T(8,128)}, f32[40,128]{1,0:T(8,128)}) custom-call(f32[2,1,1,8]{3,2,1,0:T(1,128)} %observed.1, f32[2,1,1,8]{3,2,1,0:T(1,128)} %precision.1, f32[2,1,1,4,8]{4,3,2,1,0:T(4,128)} %weight.1, s32[2,1,1,4,8]{4,3,2,1,0:T(4,128)} %stencil.1, s32[2,1,1,8]{3,2,1,0:T(1,128)} %owned.1, f32[32,128,128]{2,1,0:T(8,128)} %cells.3), custom_call_target="tpu_custom_call" | custom-call | tf_op jit(solution)/shard_map/start/pallas_call | solution.py:442
  1.8 3.4 %collective-permute-start = (f32[40,128]{1,0:T(8,128)}, f32[40,128]{1,0:T(8,128)S(1)}, u32[]{:S(2)}, u32[]{:S(2)}) collective-permute-start(f32[40,128]{1,0:T(8,128)} %get-tuple-element.17), channel_id=1, source_target_pairs={{0,7},{1,2},{2,1},{3,4},{4,3},{5,6},{6,5},{7,0},{8,15},{9,10},{10,... | collective-permute-start | bytes 61448 | tf_op jit(solution)/shard_map/ppermute | solution.py:31
  5.2 0.0 collective-permute-start.1
  5.2 0.0 copy-start
  5.2 1.6 %copy-done = f32[32,128,128]{2,1,0:T(8,128)S(1)} copy-done((f32[32,128,128]{2,1,0:T(8,128)S(1)}, f32[32,128,128]{2,1,0:T(8,128)}, u32[]{:S(2)}) %copy-start) | copy-done | bytes 2097176
  6.8 0.0 copy-start.1
  6.8 0.2 pad.1
  7.0 0.0 collective-permute-done.sides_0
  7.0 0.0 collective-permute-done.1.sides_1
  7.0 0.5 copy-done.1
  7.5 0.1 edge_rows.1
  7.5 0.0 copy-start.2
  7.5 0.8 %collective-permute-start.2 = (f32[152,128]{1,0:T(8,128)S(1)}, f32[152,128]{1,0:T(8,128)S(1)}, u32[]{:S(2)}, u32[]{:S(2)}) collective-permute-start(f32[152,128]{1,0:T(8,128)S(1)} %get-tuple-element.21), channel_id=1, source_target_pairs={{8,16},{16,8},{9,17},{17,9},{10,18},{18,10},{11,19},{19,11},{12,20... | collective-permute-start | bytes 233480 | tf_op jit(solution)/shard_map/ppermute | solution.py:31
  8.3 4.7 %collective-permute-start.3 = (f32[152,128]{1,0:T(8,128)S(1)}, f32[152,128]{1,0:T(8,128)S(1)}, u32[]{:S(2)}, u32[]{:S(2)}) collective-permute-start(f32[152,128]{1,0:T(8,128)S(1)} %get-tuple-element.22), channel_id=1, source_target_pairs={{0,8},{8,0},{16,24},{24,16},{1,9},{9,1},{17,25},{25,17},{2,10},{10... | collective-permute-start | bytes 233480 | tf_op jit(solution)/shard_map/ppermute | solution.py:31
  13.1 0.7 %row_shares.1.own = f32[8,128]{1,0:T(8,128)S(1)} custom-call(f32[2,8,128]{2,1,0:T(8,128)S(1)} %copy-done.1, f32[40,128]{1,0:T(8,128)S(1)} %get-tuple-element.19.left, f32[40,128]{1,0:T(8,128)S(1)} %get-tuple-element.20.right, f32[36,144,128]{2,1,0:T(8,128)S(1)} %pad.1), custom_call_target="tpu_custom_call" | custom-call | tf_op jit(solution)/shard_map/row_shares/pallas_call | solution.py:442
  13.8 0.0 collective-permute-done.2.ends_0
  13.8 1.8 %collective-permute-done.3.ends_1 = f32[152,128]{1,0:T(8,128)S(1)} collective-permute-done((f32[152,128]{1,0:T(8,128)S(1)}, f32[152,128]{1,0:T(8,128)S(1)}, u32[]{:S(2)}, u32[]{:S(2)}) %collective-permute-start.3) | collective-permute-done | bytes 77856 | tf_op jit(solution)/shard_map/ppermute | solution.py:31
  15.5 1.4 %prior.1 = bf16[32,5,2,128]{3,2,1,0:T(2,128)(2,1)} custom-call(f32[2,8,128]{2,1,0:T(8,128)S(1)} %copy-done.1, f32[8,128]{1,0:T(8,128)S(1)} %row_shares.1.own, f32[152,128]{1,0:T(8,128)S(1)} %collective-permute-done.2.ends_0, f32[152,128]{1,0:T(8,128)S(1)} %collective-permute-done.3.ends_1), custom_call_target="tpu_custom_call" | custom-call | tf_op jit(solution)/shard_map/prior/pallas_call | solution.py:442
  17.0 3.5 %all-to-all-start = ((bf16[32,5,2,128]{3,2,1,0:T(2,128)(2,1)}), bf16[32,5,2,128]{3,2,1,0:T(2,128)(2,1)S(1)}, u32[]{:S(2)}, u32[]{:S(2)}) async-start(bf16[32,5,2,128]{3,2,1,0:T(2,128)(2,1)} %prior.1), calls=%async_computation | async-start | bytes 163840 | tf_op jit(solution)/shard_map/all_to_all | solution.py:453
  20.5 0.0 copy-done.2
  20.5 1.6 %later_shares.1.later = f32[10,8,128]{2,1,0:T(8,128)S(1)} custom-call(f32[2,8,128]{2,1,0:T(8,128)S(1)} %copy-done.1, f32[40,128]{1,0:T(8,128)S(1)} %get-tuple-element.19.left, f32[40,128]{1,0:T(8,128)S(1)} %get-tuple-element.20.right, f32[152,128]{1,0:T(8,128)S(1)} %collective-permute-done.2.ends_0, f32[152,128]{1,0:T(8,128)S(1)} %collective-permute-done.3.ends_1, ...), custom_call_target="tpu_custom_call" | custom-call | tf_op jit(solution)/shard_map/later_shares/pallas_call | solution.py:442
  22.1 6.0 %all-to-all-done.near_ref = bf16[32,5,2,128]{3,2,1,0:T(2,128)(2,1)S(1)} async-done(((bf16[32,5,2,128]{3,2,1,0:T(2,128)(2,1)}), bf16[32,5,2,128]{3,2,1,0:T(2,128)(2,1)S(1)}, u32[]{:S(2)}, u32[]{:S(2)}) %all-to-all-start) | async-done | bytes 81952 | tf_op jit(solution)/shard_map/all_to_all | solution.py:453
  28.1 4.9 %first_batch.1 = (f32[128,128]{1,0:T(8,128)S(1)}, f32[24,128]{1,0:T(8,128)S(1)}, f32[24,128]{1,0:T(8,128)S(1)}, f32[24,128]{1,0:T(8,128)S(1)}) custom-call(bf16[32,5,2,128]{3,2,1,0:T(2,128)(2,1)S(1)} %all-to-all-done.near_ref, s32[2,1,1,5,8]{4,3,2,1,0:T(8,128)S(1)} %copy.8.pattern, f32[10,8,128]{2,1,0:T(8,128)S(1)} %later_shares.1.later), custom_call_target="tpu_custom_call" | custom-call | tf_op jit(solution)/shard_map/first_batch/pallas_call | solution.py:442
  32.9 0.4 collective-permute-start.4
  33.3 0.2 collective-permute-start.5
  33.5 3.5 %collective-permute-done.4.sides_0 = f32[24,128]{1,0:T(8,128)S(1)} collective-permute-done((f32[24,128]{1,0:T(8,128)S(1)}, f32[24,128]{1,0:T(8,128)S(1)}, u32[]{:S(2)}, u32[]{:S(2)}) %collective-permute-start.4) | collective-permute-done | bytes 12320 | tf_op jit(solution)/shard_map/ppermute | solution.py:31
  37.0 0.0 collective-permute-done.5.sides_1
  37.0 11.2 %all_to_all.10.mine = f32[16,24,128]{2,1,0:T(8,128)S(1)} all-to-all(f32[16,24,128]{2,1,0:T(8,128)S(1)} %meet.1), channel_id=1, replica_groups=mesh['lat'=4,'far'=4,'core'=2] {'lat','far'}, dimensions={0} | all-to-all | bytes 393216 | tf_op jit(solution)/shard_map/all_to_all | solution.py:518
  48.2 0.0 collective-permute-start.6
  48.2 1.4 %collective-permute-done.6.other = f32[16,24,128]{2,1,0:T(8,128)S(1)} collective-permute-done((f32[16,24,128]{2,1,0:T(8,128)S(1)}, f32[16,24,128]{2,1,0:T(8,128)S(1)}, u32[]{:S(2)}, u32[]{:S(2)}) %collective-permute-start.6) | collective-permute-done | bytes 196640 | tf_op jit(solution)/shard_map/ppermute | solution.py:519
  49.7 6.6 %second_batch.1 = f32[4096,128]{1,0:T(8,128)} custom-call(f32[16,24,128]{2,1,0:T(8,128)S(1)} %all_to_all.10.mine, f32[16,24,128]{2,1,0:T(8,128)S(1)} %collective-permute-done.6.other, s32[2,1,1,5,8]{4,3,2,1,0:T(8,128)S(1)} %copy.8.pattern, f32[128,128]{1,0:T(8,128)S(1)} %get-tuple-element.26.map_ref, f32[36,144,128]{2,1,0:T(8,128)S(1)} %pad.1), custom_call_target="tpu_custom_call" | custom-call | tf_op jit(solution)/shard_map/second_batch/pallas_call | solution.py:442
  (2 shorter events, 0.0 us)
Async XLA Ops:
  1.8 5.2 %collective-permute-start = (f32[40,128]{1,0:T(8,128)}, f32[40,128]{1,0:T(8,128)S(1)}, u32[]{:S(2)}, u32[]{:S(2)}) collective-permute-start(f32[40,128]{1,0:T(8,128)} %get-tuple-element.17), channel_id=1, source_target_pairs={{0,7},{1,2},{2,1},{3,4},{4,3},{5,6},{6,5},{7,0},{8,15},{9,10},{10,... | collective-permute-start | bytes 61448 | tf_op jit(solution)/shard_map/ppermute | solution.py:31
  5.2 1.8 %collective-permute-start.1 = (f32[40,128]{1,0:T(8,128)}, f32[40,128]{1,0:T(8,128)S(1)}, u32[]{:S(2)}, u32[]{:S(2)}) collective-permute-start(f32[40,128]{1,0:T(8,128)} %get-tuple-element.18), channel_id=1, source_target_pairs={{0,1},{1,0},{2,3},{3,2},{4,5},{5,4},{6,7},{7,6},{8,9},{9,8},{10,11... | collective-permute-start | bytes 61448 | tf_op jit(solution)/shard_map/ppermute | solution.py:31
  5.2 1.6 %copy-start = (f32[32,128,128]{2,1,0:T(8,128)S(1)}, f32[32,128,128]{2,1,0:T(8,128)}, u32[]{:S(2)}) copy-start(f32[32,128,128]{2,1,0:T(8,128)} %cells.3) | copy-start | bytes 6291460
  6.8 0.7 %copy-start.1 = (f32[2,8,128]{2,1,0:T(8,128)S(1)}, f32[2,8,128]{2,1,0:T(8,128)}, u32[]{:S(2)}) copy-start(f32[2,8,128]{2,1,0:T(8,128)} %get-tuple-element.16.mine) | copy-start | bytes 24580
  7.5 12.9 %copy-start.2 = (s32[2,1,1,5,8]{4,2,3,1,0:T(1,128)S(1)}, s32[2,1,1,5,8]{4,2,3,1,0:T(1,128)}, u32[]{:S(2)}) copy-start(s32[2,1,1,5,8]{4,2,3,1,0:T(1,128)} %param.13) | copy-start | bytes 964
  7.5 6.2 %collective-permute-start.2 = (f32[152,128]{1,0:T(8,128)S(1)}, f32[152,128]{1,0:T(8,128)S(1)}, u32[]{:S(2)}, u32[]{:S(2)}) collective-permute-start(f32[152,128]{1,0:T(8,128)S(1)} %get-tuple-element.21), channel_id=1, source_target_pairs={{8,16},{16,8},{9,17},{17,9},{10,18},{18,10},{11,19},{19,11},{12,20... | collective-permute-start | bytes 233480 | tf_op jit(solution)/shard_map/ppermute | solution.py:31
  8.3 7.2 %collective-permute-start.3 = (f32[152,128]{1,0:T(8,128)S(1)}, f32[152,128]{1,0:T(8,128)S(1)}, u32[]{:S(2)}, u32[]{:S(2)}) collective-permute-start(f32[152,128]{1,0:T(8,128)S(1)} %get-tuple-element.22), channel_id=1, source_target_pairs={{0,8},{8,0},{16,24},{24,16},{1,9},{9,1},{17,25},{25,17},{2,10},{10... | collective-permute-start | bytes 233480 | tf_op jit(solution)/shard_map/ppermute | solution.py:31
  17.0 11.1 %all-to-all-start = ((bf16[32,5,2,128]{3,2,1,0:T(2,128)(2,1)}), bf16[32,5,2,128]{3,2,1,0:T(2,128)(2,1)S(1)}, u32[]{:S(2)}, u32[]{:S(2)}) async-start(bf16[32,5,2,128]{3,2,1,0:T(2,128)(2,1)} %prior.1), calls=%async_computation | async-start | bytes 163840 | tf_op jit(solution)/shard_map/all_to_all | solution.py:453
  32.9 4.1 %collective-permute-start.4 = (f32[24,128]{1,0:T(8,128)S(1)}, f32[24,128]{1,0:T(8,128)S(1)}, u32[]{:S(2)}, u32[]{:S(2)}) collective-permute-start(f32[24,128]{1,0:T(8,128)S(1)} %get-tuple-element.24), channel_id=1, source_target_pairs={{0,7},{1,2},{2,1},{3,4},{4,3},{5,6},{6,5},{7,0},{8,15},{9,10},{10,... | collective-permute-start | bytes 36872 | tf_op jit(solution)/shard_map/ppermute | solution.py:31
  33.3 3.7 %collective-permute-start.5 = (f32[24,128]{1,0:T(8,128)S(1)}, f32[24,128]{1,0:T(8,128)S(1)}, u32[]{:S(2)}, u32[]{:S(2)}) collective-permute-start(f32[24,128]{1,0:T(8,128)S(1)} %get-tuple-element.25), channel_id=1, source_target_pairs={{0,1},{1,0},{2,3},{3,2},{4,5},{5,4},{6,7},{7,6},{8,9},{9,8},{10,11... | collective-permute-start | bytes 36872 | tf_op jit(solution)/shard_map/ppermute | solution.py:31
  48.2 1.4 %collective-permute-start.6 = (f32[16,24,128]{2,1,0:T(8,128)S(1)}, f32[16,24,128]{2,1,0:T(8,128)S(1)}, u32[]{:S(2)}, u32[]{:S(2)}) collective-permute-start(f32[16,24,128]{2,1,0:T(8,128)S(1)} %all_to_all.10.mine), channel_id=1, source_target_pairs={{0,1},{1,0},{2,3},{3,2},{4,5},{5,4},{6,7},{7,6},{8,9},{9,8},{10,11... | collective-permute-start | bytes 589832 | tf_op jit(solution)/shard_map/ppermute | solution.py:519

commit v9 on v8

--- a/solution.py
+++ b/solution.py
@@ -188,7 +188,7 @@
     out_ref[...] = jnp.broadcast_to(mid[...] + sides_0[...] + sides_1[...], out_ref.shape)
 
 
-def later_kernel(mine, left, right, ends_0, ends_1, pad, out_ref, params, sems):
+def later_tasks(mine, left, right, ends_0, ends_1, pad, later, params, sems):
     rows, cols = (pad.shape[0] - 4, pad.shape[1] - 2 * SUB)
     side, end = (pl.ds(rows, SUB), pl.ds(cols + 2 * SUB, SUB))
     sources = (left.at[side], mine.at[1], right.at[side], ends_0.at[end], ends_1.at[end])
@@ -196,17 +196,28 @@
     for n, source in enumerate(sources):
         copies.append(pltpu.make_async_copy(source, params.at[n], sems.at[n]))
         copies[-1].start()
-    for copy in copies:
-        copy.wait()
+
+    def wait():
+        for copy in copies:
+            copy.wait()
+
+    def one(spot, lane, da, dc, o, at):
+        number = lambda kind, o: params[spot, kind, lane + o]
+        later[pl.ds(at, 1), :] = share(pad, number, rows, cols, da, dc, o)
+
+    def own():
+        later[pl.ds(len(NEAR) ** 2 * SUB, SUB), :] = own_shift(lambda kind, o: params[1, kind, o])
+
     forward = next_first("lat")
     ends = {-1: jnp.where(forward, 4, 3), 1: jnp.where(forward, 3, 4)}
+    tasks = [wait, own]
     for n, dc in enumerate(NEAR):
         for m, da in enumerate(NEAR):
             spot, lane = (n, 0) if da == 0 else (ends[da], n * SUB)
-            number = lambda kind, o: params[spot, kind, lane + o]
             for o in range(SUB):
-                out_ref[n * len(NEAR) + m, pl.ds(o, 1), :] = share(pad, number, rows, cols, da, dc, o)
-    out_ref[len(NEAR) ** 2] = own_shift(lambda kind, o: params[1, kind, o])
+                at = (n * len(NEAR) + m) * SUB + o
+                tasks.append(functools.partial(one, spot, lane, da, dc, o, at))
+    return tasks
 
 
 def window_start(lat_count, my_lat):
@@ -264,7 +275,8 @@
     return rows, jnp.where(lane < SUB, inverse * lax.rsqrt(scale), 0.0)
 
 
-def eliminate(blocks, held):
+def eliminate(blocks, held, tasks):
+    tasks = list(tasks)
     count = len(blocks) - 1
     blocks = list(blocks)
     lane = lax.broadcasted_iota(jnp.int32, blocks[0].shape, 1)
@@ -284,6 +296,10 @@
             for task in waiting[:share_of]:
                 update(*task)
             del waiting[:share_of]
+            if k > 0:
+                for task in tasks[:2]:
+                    task()
+                del tasks[:2]
 
         pivot, rows = pivot_rows(blocks[k], k, held, between)
         update(k + 1, k, pivot)
@@ -328,7 +344,7 @@
     return (value - mean).astype(BF16).astype(F32), innov
 
 
-def batch_map(batch, lat_count, blocks, pattern, swapped, held_rows):
+def batch_map(batch, lat_count, blocks, pattern, swapped, held_rows, tasks):
     scaled, innov = blocks
     held = min(WIN, lat_count)
     count = scaled.shape[0]
@@ -363,7 +379,7 @@
         blocks.append(block + jnp.where(lane - k * SUB == sub, members - 1.0, 0.0))
     proj = jnp.sum(product[members:members + SUB, :], axis=0, keepdims=True)
     blocks.append(jnp.broadcast_to(proj, (SUB, LANES)))
-    inverse, weights = eliminate(blocks, held_rows)
+    inverse, weights = eliminate(blocks, held_rows, tasks)
     flipped = jnp.concatenate(inverse, axis=0) * (members - 1.0) ** 0.5 - weights
     return flipped - jnp.mean(flipped, axis=-1, keepdims=True) + 1.0 / members
 
@@ -374,16 +390,18 @@
     )
 
 
-def first_kernel(lat_count, near_ref, pattern, later, map_ref, mid_ref, out_0, out_1, held_rows):
-    flipped = batch_map(0, lat_count, own_blocks(near_ref), pattern, None, held_rows)
+def first_kernel(lat_count, near_ref, pattern, *refs):
+    around, (map_ref, mid_ref, out_0, out_1, held_rows, later, params, sems) = (refs[:6], refs[6:])
+    tasks = later_tasks(*around, later, params, sems)
+    flipped = batch_map(0, lat_count, own_blocks(near_ref), pattern, None, held_rows, tasks)
     map_ref[...] = flipped
     count = len(NEAR) ** 2
-    moved = exact_dot(later[pl.ds(0, count)].reshape(-1, LANES), flipped, 1)
+    moved = exact_dot(later[pl.ds(0, count * SUB), :], flipped, 1)
     size = len(NEAR) * SUB
     left, mid, right = (moved[:size], moved[size:2 * size], moved[2 * size:])
     mid_ref[...] = mid
     own = pl.ds(SUB, SUB)
-    mid_ref[own, :] = mid[SUB:2 * SUB] - later[count]
+    mid_ref[own, :] = mid[SUB:2 * SUB] - later[pl.ds(count * SUB, SUB), :]
     forward = next_first("core")
     out_0[...] = jnp.where(forward, right, left)
     out_1[...] = jnp.where(forward, left, right)
@@ -394,7 +412,7 @@
     rows, cols = (pad.shape[0] - 4, pad.shape[1] - 2 * SUB)
     swapped = lax.axis_index("core") == 1
     blocks = summed_blocks(lat_count, mine, other)
-    flipped = exact_dot(batch_map(1, lat_count, blocks, pattern, swapped, held_rows), map_ref[...], 0)
+    flipped = exact_dot(batch_map(1, lat_count, blocks, pattern, swapped, held_rows, ()), map_ref[...], 0)
     high = flipped.astype(BF16)
     low = (flipped - high.astype(F32)).astype(BF16)
     right = jnp.concatenate(
@@ -489,29 +507,26 @@
     )
     near = window(exchange(blocks), lat_count, lon_count)
     count = len(NEAR) ** 2
-    later = call(
-        later_kernel,
-        "later_shares",
-        [vmem] * 6,
-        shape(count + 1, SUB, members),
-        [pltpu.SMEM((5, SUB, LANES), F32), pltpu.SemaphoreType.DMA((5,))],
+    column = shape(len(NEAR) * SUB, members)
+    held_rows = pltpu.VMEM((members + SUB, members), F32)
+    first_map, mid, *sides = call(
+        functools.partial(first_kernel, lat_count),
+        "first_batch",
+        [vmem] * 8,
+        (shape(members, members), column, column, column),
+        [
+            held_rows,
+            pltpu.VMEM(((count + 1) * SUB, members), F32),
+            pltpu.SMEM((5, SUB, LANES), F32),
+            pltpu.SemaphoreType.DMA((5,)),
+        ],
+        near,
+        pattern,
         mine,
         left,
         right,
         *ends,
         pad,
-    )
-    column = shape(len(NEAR) * SUB, members)
-    held_rows = pltpu.VMEM((members + SUB, members), F32)
-    first_map, mid, *sides = call(
-        functools.partial(first_kernel, lat_count),
-        "first_batch",
-        [vmem] * 3,
-        (shape(members, members), column, column, column),
-        [held_rows],
-        near,
-        pattern,
-        later,
     )
     sides = trade(sides, LON, True)
     shares = call(meet_kernel, "meet", [vmem] * 3, shape(tiles // 2, *column.shape), [], mid, *sides)

time: 56.6 us -> 57.6 us (1.018)
  waiting for transfers between devices: 12.7 us -> 14.3 us
    all_to_all x1, waiting for transfers between devices: 6 us -> 7.58 us  [exchange(): lax.all_to_all(blocks, ('lat',) + LON, split_axis=0, concat_axis=0, tiled...]
    pallas_call x9 -> x8, Pallas kernels: 17.2 us -> 16.7 us  [call(): pl.pallas_call(kernel, out_shape=out_shape, in_specs=specs, out_specs=out...]
  transfers between devices with their start and end apart: 8 -> 8, of which waited for: 4 -> 4; matrix products, arithmetic and copies ran while one was open for 0% -> 0% of each run, Pallas kernels for 4% -> 2%
where the time goes in v9:
time: 57.6 us; the launch traced here: 57.3 us
  Pallas kernels  16.7 us (29%)
  waiting for transfers between devices  14.3 us (25%)
  starting transfers between devices  13 us (23%)
  blocking collectives  11.2 us (19%)
  local copies, waits for them, and re-layouts  2.06 us (4%)
    pallas_call x8, Pallas kernels, call(): pl.pallas_call(kernel, out_shape=out_shape, in_specs=specs, out_specs=out...  16.7 us
    all_to_all x1, blocking collectives, local(): lax.all_to_all(shares, ('lat', 'far'), split_axis=0, concat_axis=0, tiled...  11.2 us
    ppermute x6, starting transfers between devices, trade(): results.append(lax.ppermute(block, axis, route))  9.49 us
    all_to_all x1, waiting for transfers between devices, exchange(): lax.all_to_all(blocks, ('lat',) + LON, split_axis=0, concat_axis=0, tiled...  7.58 us
    ppermute x6, waiting for transfers between devices, trade(): results.append(lax.ppermute(block, axis, route))  5.28 us
    all_to_all x1, starting transfers between devices, exchange(): lax.all_to_all(blocks, ('lat',) + LON, split_axis=0, concat_axis=0, tiled...  3.47 us
    unnamed x7, local copies, waits for them, and re-layouts  2.06 us
    ppermute x1, waiting for transfers between devices, local(): other = lax.ppermute(shares, 'core', [(0, 1), (1, 0)])  1.44 us
  transfers between devices with their start and end apart: 8, of which 4 were waited for; matrix products, arithmetic and copies ran while one was open for 0% of the time, Pallas kernels for 2%

profile of v9, /device:TPU:0, one launch (start us, length us, event | category | flops | bytes accessed | tf_op | source)
XLA Modules:
  0.0 57.3 jit_solution(4318408844678170911)
XLA Ops:
  0.0 1.8 %start.1 = (f32[2,8,128]{2,1,0:T(8,128)}, f32[40,128]{1,0:T(8,128)}, f32[40,128]{1,0:T(8,128)}) custom-call(f32[2,1,1,8]{3,2,1,0:T(1,128)} %observed.1, f32[2,1,1,8]{3,2,1,0:T(1,128)} %precision.1, f32[2,1,1,4,8]{4,3,2,1,0:T(4,128)} %weight.1, s32[2,1,1,4,8]{4,3,2,1,0:T(4,128)} %stencil.1, s32[2,1,1,8]{3,2,1,0:T(1,128)} %owned.1, f32[32,128,128]{2,1,0:T(8,128)} %cells.3), custom_call_target="tpu_custom_call" | custom-call | tf_op jit(solution)/shard_map/start/pallas_call | solution.py:460
  1.8 3.4 %collective-permute-start = (f32[40,128]{1,0:T(8,128)}, f32[40,128]{1,0:T(8,128)S(1)}, u32[]{:S(2)}, u32[]{:S(2)}) collective-permute-start(f32[40,128]{1,0:T(8,128)} %get-tuple-element.17), channel_id=1, source_target_pairs={{0,7},{1,2},{2,1},{3,4},{4,3},{5,6},{6,5},{7,0},{8,15},{9,10},{10,... | collective-permute-start | bytes 61448 | tf_op jit(solution)/shard_map/ppermute | solution.py:31
  5.2 0.0 collective-permute-start.1
  5.2 0.0 copy-start
  5.2 1.6 %copy-done = f32[32,128,128]{2,1,0:T(8,128)S(1)} copy-done((f32[32,128,128]{2,1,0:T(8,128)S(1)}, f32[32,128,128]{2,1,0:T(8,128)}, u32[]{:S(2)}) %copy-start) | copy-done | bytes 2097176
  6.8 0.0 copy-start.1
  6.8 0.2 pad.1.refs_5_
  7.0 0.0 collective-permute-done.sides_0
  7.0 0.0 collective-permute-done.1.sides_1
  7.0 0.5 copy-done.1
  7.5 0.1 edge_rows.1
  7.5 0.0 copy-start.2
  7.5 0.8 %collective-permute-start.2 = (f32[152,128]{1,0:T(8,128)S(1)}, f32[152,128]{1,0:T(8,128)S(1)}, u32[]{:S(2)}, u32[]{:S(2)}) collective-permute-start(f32[152,128]{1,0:T(8,128)S(1)} %get-tuple-element.21), channel_id=1, source_target_pairs={{8,16},{16,8},{9,17},{17,9},{10,18},{18,10},{11,19},{19,11},{12,20... | collective-permute-start | bytes 233480 | tf_op jit(solution)/shard_map/ppermute | solution.py:31
  8.3 4.7 %collective-permute-start.3 = (f32[152,128]{1,0:T(8,128)S(1)}, f32[152,128]{1,0:T(8,128)S(1)}, u32[]{:S(2)}, u32[]{:S(2)}) collective-permute-start(f32[152,128]{1,0:T(8,128)S(1)} %get-tuple-element.22), channel_id=1, source_target_pairs={{0,8},{8,0},{16,24},{24,16},{1,9},{9,1},{17,25},{25,17},{2,10},{10... | collective-permute-start | bytes 233480 | tf_op jit(solution)/shard_map/ppermute | solution.py:31
  13.1 0.7 %row_shares.1.own = f32[8,128]{1,0:T(8,128)S(1)} custom-call(f32[2,8,128]{2,1,0:T(8,128)S(1)} %copy-done.1, f32[40,128]{1,0:T(8,128)S(1)} %get-tuple-element.19.left.refs_1_, f32[40,128]{1,0:T(8,128)S(1)} %get-tuple-element.20.right.refs_2_, f32[36,144,128]{2,1,0:T(8,128)S(1)} %pad.1.refs_5_), custom_call_target="tpu_custom_call" | custom-call | tf_op jit(solution)/shard_map/row_shares/pallas_call | solution.py:460
  13.8 0.0 collective-permute-done.2.ends_0.refs_3_
  13.8 1.8 %collective-permute-done.3.ends_1.refs_4_ = f32[152,128]{1,0:T(8,128)S(1)} collective-permute-done((f32[152,128]{1,0:T(8,128)S(1)}, f32[152,128]{1,0:T(8,128)S(1)}, u32[]{:S(2)}, u32[]{:S(2)}) %collective-permute-start.3) | collective-permute-done | bytes 77856 | tf_op jit(solution)/shard_map/ppermute | solution.py:31
  15.5 1.4 %prior.1 = bf16[32,5,2,128]{3,2,1,0:T(2,128)(2,1)} custom-call(f32[2,8,128]{2,1,0:T(8,128)S(1)} %copy-done.1, f32[8,128]{1,0:T(8,128)S(1)} %row_shares.1.own, f32[152,128]{1,0:T(8,128)S(1)} %collective-permute-done.2.ends_0.refs_3_, f32[152,128]{1,0:T(8,128)S(1)} %collective-permute-done.3.ends_1.refs_4_), custom_call_target="tpu_custom_call" | custom-call | tf_op jit(solution)/shard_map/prior/pallas_call | solution.py:460
  17.0 3.5 %all-to-all-start = ((bf16[32,5,2,128]{3,2,1,0:T(2,128)(2,1)}), bf16[32,5,2,128]{3,2,1,0:T(2,128)(2,1)S(1)}, u32[]{:S(2)}, u32[]{:S(2)}) async-start(bf16[32,5,2,128]{3,2,1,0:T(2,128)(2,1)} %prior.1), calls=%async_computation | async-start | bytes 163840 | tf_op jit(solution)/shard_map/all_to_all | solution.py:471
  20.5 0.0 copy-done.2
  20.5 7.6 %all-to-all-done.near_ref = bf16[32,5,2,128]{3,2,1,0:T(2,128)(2,1)S(1)} async-done(((bf16[32,5,2,128]{3,2,1,0:T(2,128)(2,1)}), bf16[32,5,2,128]{3,2,1,0:T(2,128)(2,1)S(1)}, u32[]{:S(2)}, u32[]{:S(2)}) %all-to-all-start) | async-done | bytes 81952 | tf_op jit(solution)/shard_map/all_to_all | solution.py:471
  28.1 5.9 %first_batch.1 = (f32[128,128]{1,0:T(8,128)S(1)}, f32[24,128]{1,0:T(8,128)S(1)}, f32[24,128]{1,0:T(8,128)S(1)}, f32[24,128]{1,0:T(8,128)S(1)}) custom-call(bf16[32,5,2,128]{3,2,1,0:T(2,128)(2,1)S(1)} %all-to-all-done.near_ref, s32[2,1,1,5,8]{4,3,2,1,0:T(8,128)S(1)} %copy.8.pattern, f32[2,8,128]{2,1,0:T(8,128)S(1)} %copy-done.1, ...), custom_call_target="tpu_custom_call" | custom-call | tf_op jit(solution)/shard_map/first_batch/pallas_call | solution.py:460
  34.0 0.4 collective-permute-start.4
  34.4 0.2 collective-permute-start.5
  34.6 3.5 %collective-permute-done.4.sides_0 = f32[24,128]{1,0:T(8,128)S(1)} collective-permute-done((f32[24,128]{1,0:T(8,128)S(1)}, f32[24,128]{1,0:T(8,128)S(1)}, u32[]{:S(2)}, u32[]{:S(2)}) %collective-permute-start.4) | collective-permute-done | bytes 12320 | tf_op jit(solution)/shard_map/ppermute | solution.py:31
  38.1 0.0 collective-permute-done.5.sides_1
  38.1 11.2 %all_to_all.10.mine = f32[16,24,128]{2,1,0:T(8,128)S(1)} all-to-all(f32[16,24,128]{2,1,0:T(8,128)S(1)} %meet.1), channel_id=1, replica_groups=mesh['lat'=4,'far'=4,'core'=2] {'lat','far'}, dimensions={0} | all-to-all | bytes 393216 | tf_op jit(solution)/shard_map/all_to_all | solution.py:533
  49.3 0.0 collective-permute-start.6
  49.3 1.4 %collective-permute-done.6.other = f32[16,24,128]{2,1,0:T(8,128)S(1)} collective-permute-done((f32[16,24,128]{2,1,0:T(8,128)S(1)}, f32[16,24,128]{2,1,0:T(8,128)S(1)}, u32[]{:S(2)}, u32[]{:S(2)}) %collective-permute-start.6) | collective-permute-done | bytes 196640 | tf_op jit(solution)/shard_map/ppermute | solution.py:534
  50.7 6.6 %second_batch.1 = f32[4096,128]{1,0:T(8,128)} custom-call(f32[16,24,128]{2,1,0:T(8,128)S(1)} %all_to_all.10.mine, f32[16,24,128]{2,1,0:T(8,128)S(1)} %collective-permute-done.6.other, s32[2,1,1,5,8]{4,3,2,1,0:T(8,128)S(1)} %copy.8.pattern, f32[128,128]{1,0:T(8,128)S(1)} %get-tuple-element.26.map_ref, f32[36,144,128]{2,1,0:T(8,128)S(1)} %pad.1.refs_5_), custom_call_target="tpu_custom_call" | custom-call | tf_op jit(solution)/shard_map/second_batch/pallas_call | solution.py:460
  (2 shorter events, 0.0 us)
Async XLA Ops:
  1.8 5.2 %collective-permute-start = (f32[40,128]{1,0:T(8,128)}, f32[40,128]{1,0:T(8,128)S(1)}, u32[]{:S(2)}, u32[]{:S(2)}) collective-permute-start(f32[40,128]{1,0:T(8,128)} %get-tuple-element.17), channel_id=1, source_target_pairs={{0,7},{1,2},{2,1},{3,4},{4,3},{5,6},{6,5},{7,0},{8,15},{9,10},{10,... | collective-permute-start | bytes 61448 | tf_op jit(solution)/shard_map/ppermute | solution.py:31
  5.2 1.8 %collective-permute-start.1 = (f32[40,128]{1,0:T(8,128)}, f32[40,128]{1,0:T(8,128)S(1)}, u32[]{:S(2)}, u32[]{:S(2)}) collective-permute-start(f32[40,128]{1,0:T(8,128)} %get-tuple-element.18), channel_id=1, source_target_pairs={{0,1},{1,0},{2,3},{3,2},{4,5},{5,4},{6,7},{7,6},{8,9},{9,8},{10,11... | collective-permute-start | bytes 61448 | tf_op jit(solution)/shard_map/ppermute | solution.py:31
  5.2 1.6 %copy-start = (f32[32,128,128]{2,1,0:T(8,128)S(1)}, f32[32,128,128]{2,1,0:T(8,128)}, u32[]{:S(2)}) copy-start(f32[32,128,128]{2,1,0:T(8,128)} %cells.3) | copy-start | bytes 6291460
  6.8 0.7 %copy-start.1 = (f32[2,8,128]{2,1,0:T(8,128)S(1)}, f32[2,8,128]{2,1,0:T(8,128)}, u32[]{:S(2)}) copy-start(f32[2,8,128]{2,1,0:T(8,128)} %get-tuple-element.16.mine.refs_0_) | copy-start | bytes 24580
  7.5 12.9 %copy-start.2 = (s32[2,1,1,5,8]{4,2,3,1,0:T(1,128)S(1)}, s32[2,1,1,5,8]{4,2,3,1,0:T(1,128)}, u32[]{:S(2)}) copy-start(s32[2,1,1,5,8]{4,2,3,1,0:T(1,128)} %param.13) | copy-start | bytes 964
  7.5 6.2 %collective-permute-start.2 = (f32[152,128]{1,0:T(8,128)S(1)}, f32[152,128]{1,0:T(8,128)S(1)}, u32[]{:S(2)}, u32[]{:S(2)}) collective-permute-start(f32[152,128]{1,0:T(8,128)S(1)} %get-tuple-element.21), channel_id=1, source_target_pairs={{8,16},{16,8},{9,17},{17,9},{10,18},{18,10},{11,19},{19,11},{12,20... | collective-permute-start | bytes 233480 | tf_op jit(solution)/shard_map/ppermute | solution.py:31
  8.3 7.2 %collective-permute-start.3 = (f32[152,128]{1,0:T(8,128)S(1)}, f32[152,128]{1,0:T(8,128)S(1)}, u32[]{:S(2)}, u32[]{:S(2)}) collective-permute-start(f32[152,128]{1,0:T(8,128)S(1)} %get-tuple-element.22), channel_id=1, source_target_pairs={{0,8},{8,0},{16,24},{24,16},{1,9},{9,1},{17,25},{25,17},{2,10},{10... | collective-permute-start | bytes 233480 | tf_op jit(solution)/shard_map/ppermute | solution.py:31
  17.0 11.1 %all-to-all-start = ((bf16[32,5,2,128]{3,2,1,0:T(2,128)(2,1)}), bf16[32,5,2,128]{3,2,1,0:T(2,128)(2,1)S(1)}, u32[]{:S(2)}, u32[]{:S(2)}) async-start(bf16[32,5,2,128]{3,2,1,0:T(2,128)(2,1)} %prior.1), calls=%async_computation | async-start | bytes 163840 | tf_op jit(solution)/shard_map/all_to_all | solution.py:471
  34.0 4.1 %collective-permute-start.4 = (f32[24,128]{1,0:T(8,128)S(1)}, f32[24,128]{1,0:T(8,128)S(1)}, u32[]{:S(2)}, u32[]{:S(2)}) collective-permute-start(f32[24,128]{1,0:T(8,128)S(1)} %get-tuple-element.24), channel_id=1, source_target_pairs={{0,7},{1,2},{2,1},{3,4},{4,3},{5,6},{6,5},{7,0},{8,15},{9,10},{10,... | collective-permute-start | bytes 36872 | tf_op jit(solution)/shard_map/ppermute | solution.py:31
  34.4 3.7 %collective-permute-start.5 = (f32[24,128]{1,0:T(8,128)S(1)}, f32[24,128]{1,0:T(8,128)S(1)}, u32[]{:S(2)}, u32[]{:S(2)}) collective-permute-start(f32[24,128]{1,0:T(8,128)S(1)} %get-tuple-element.25), channel_id=1, source_target_pairs={{0,1},{1,0},{2,3},{3,2},{4,5},{5,4},{6,7},{7,6},{8,9},{9,8},{10,11... | collective-permute-start | bytes 36872 | tf_op jit(solution)/shard_map/ppermute | solution.py:31
  49.3 1.4 %collective-permute-start.6 = (f32[16,24,128]{2,1,0:T(8,128)S(1)}, f32[16,24,128]{2,1,0:T(8,128)S(1)}, u32[]{:S(2)}, u32[]{:S(2)}) collective-permute-start(f32[16,24,128]{2,1,0:T(8,128)S(1)} %all_to_all.10.mine), channel_id=1, source_target_pairs={{0,1},{1,0},{2,3},{3,2},{4,5},{5,4},{6,7},{7,6},{8,9},{9,8},{10,11... | collective-permute-start | bytes 589832 | tf_op jit(solution)/shard_map/ppermute | solution.py:534

commit v10 on v8

--- a/solution.py
+++ b/solution.py
@@ -292,12 +292,14 @@
     return inverse, blocks[count][:1]
 
 
-def own_blocks(near_ref):
-    scaled = jnp.concatenate([near_ref[:, n].astype(F32) for n in range(PAIRS - 1)], axis=1)
-    innov = near_ref[:, PAIRS - 1].astype(F32)[:, :1]
-    sub = lax.broadcasted_iota(jnp.int32, scaled.shape, 1)
-    lane = lax.broadcasted_iota(jnp.int32, scaled.shape, 2)
-    return scaled, jnp.where(lane == sub, jnp.broadcast_to(innov, scaled.shape), 0.0)
+def own_blocks(mine, other):
+    scaled = [jnp.concatenate([near[:, n].astype(F32) for n in range(PAIRS - 1)], axis=1) for near in (mine, other)]
+    innov = [jnp.broadcast_to(near[:, PAIRS - 1].astype(F32)[:, :1], scaled[0].shape) for near in (mine, other)]
+    sub = lax.broadcasted_iota(jnp.int32, scaled[0].shape, 1)
+    lane = lax.broadcasted_iota(jnp.int32, scaled[0].shape, 2)
+    innov = [jnp.where(lane == sub, value, 0.0) for value in innov]
+    shape = (2 * mine.shape[0], SUB, LANES)
+    return [jnp.stack(pair, axis=1).reshape(shape) for pair in (scaled, innov)]
 
 
 def summed_blocks(lat_count, mine, other):
@@ -328,12 +330,13 @@
     return (value - mean).astype(BF16).astype(F32), innov
 
 
-def batch_map(batch, lat_count, blocks, pattern, swapped, held_rows):
+def batch_map(batch, lat_count, blocks, pattern, held_rows):
     scaled, innov = blocks
     held = min(WIN, lat_count)
     count = scaled.shape[0]
     my_lat = lax.axis_index("lat")
     start = window_start(lat_count, my_lat)
+    swapped = lax.axis_index("core") == 1
     picked = []
     for j in range(held):
         offset = start + j - my_lat + REACH
@@ -343,9 +346,7 @@
         marks = [jnp.broadcast_to(row[:, e:e + 1], (1, SUB, LANES)) for e in range(count // held)]
         for e in range(0, len(marks), 2):
             first, second = marks[e:e + 2]
-            if swapped is not None:
-                first, second = (jnp.where(swapped, second, first), jnp.where(swapped, first, second))
-            picked.extend((first, second))
+            picked.extend((jnp.where(swapped, second, first), jnp.where(swapped, first, second)))
     weighted = scaled * jnp.concatenate(picked, axis=0)
     both = jnp.concatenate([scaled, innov], axis=2).reshape(count * SUB, 2 * LANES).astype(BF16)
     product = lax.dot_general(
@@ -374,8 +375,8 @@
     )
 
 
-def first_kernel(lat_count, near_ref, pattern, later, map_ref, mid_ref, out_0, out_1, held_rows):
-    flipped = batch_map(0, lat_count, own_blocks(near_ref), pattern, None, held_rows)
+def first_kernel(lat_count, near, other, pattern, later, map_ref, mid_ref, out_0, out_1, held_rows):
+    flipped = batch_map(0, lat_count, own_blocks(near, other), pattern, held_rows)
     map_ref[...] = flipped
     count = len(NEAR) ** 2
     moved = exact_dot(later[pl.ds(0, count)].reshape(-1, LANES), flipped, 1)
@@ -392,9 +393,8 @@
 def last_kernel(lat_count, mine, other, pattern, map_ref, pad, out_ref, result, held_rows, out_sem):
     parts = out_sem.shape[0]
     rows, cols = (pad.shape[0] - 4, pad.shape[1] - 2 * SUB)
-    swapped = lax.axis_index("core") == 1
     blocks = summed_blocks(lat_count, mine, other)
-    flipped = exact_dot(batch_map(1, lat_count, blocks, pattern, swapped, held_rows), map_ref[...], 0)
+    flipped = exact_dot(batch_map(1, lat_count, blocks, pattern, held_rows), map_ref[...], 0)
     high = flipped.astype(BF16)
     low = (flipped - high.astype(F32)).astype(BF16)
     right = jnp.concatenate(
@@ -417,12 +417,13 @@
         out_copy.wait()
 
 
-def window(tiles, lat_count, lon_count):
+def window(blocks, lat_count):
     held = min(WIN, lat_count)
     if held == lat_count:
-        return tiles
+        return blocks
     start = jnp.clip(lax.axis_index("lat") - REACH, 0, lat_count - held)
-    return lax.dynamic_slice_in_dim(tiles, start * lon_count, held * lon_count, axis=0)
+    per_row = blocks.shape[0] // lat_count
+    return lax.dynamic_slice_in_dim(blocks, start * per_row, held * per_row, axis=0)
 
 
 def local(ensemble, observed, precision, interp_weight, stencil, owned, pattern):
@@ -450,7 +451,8 @@
         )(*operands)
 
     def exchange(blocks):
-        return lax.all_to_all(blocks, ("lat",) + LON, split_axis=0, concat_axis=0, tiled=True)
+        mine = lax.all_to_all(blocks, ("lat", "far"), split_axis=0, concat_axis=0, tiled=True)
+        return mine, lax.ppermute(mine, "core", [(0, 1), (1, 0)])
 
     small = (observed, precision, interp_weight, stencil, owned)
     side = shape(rows + SUB, members)
@@ -472,7 +474,7 @@
     end = shape(cols + 3 * SUB, members)
     left, right, *ends = call(rows_kernel, "edge_rows", [vmem] * 4, (side, side, end, end), [], mine, *sides, pad)
     ends = trade(ends, "lat", False)
-    slots = shape(tiles, PAIRS, 2, members, dtype=BF16)
+    slots = shape(tiles // 2, PAIRS, 2, members, dtype=BF16)
     numbers = [pltpu.SMEM((SUB, LANES), F32), pltpu.SemaphoreType.DMA]
     block = shape(SUB, members)
     held_sides = pltpu.VMEM((2, rows + 2 * SUB, members), F32)
@@ -487,7 +489,7 @@
         own,
         *ends,
     )
-    near = window(exchange(blocks), lat_count, lon_count)
+    near = [window(part, lat_count) for part in exchange(blocks)]
     count = len(NEAR) ** 2
     later = call(
         later_kernel,
@@ -506,18 +508,17 @@
     first_map, mid, *sides = call(
         functools.partial(first_kernel, lat_count),
         "first_batch",
-        [vmem] * 3,
+        [vmem] * 4,
         (shape(members, members), column, column, column),
         [held_rows],
-        near,
+        *near,
         pattern,
         later,
     )
     sides = trade(sides, LON, True)
     shares = call(meet_kernel, "meet", [vmem] * 3, shape(tiles // 2, *column.shape), [], mid, *sides)
-    shares = lax.all_to_all(shares, ("lat", "far"), split_axis=0, concat_axis=0, tiled=True)
-    other = lax.ppermute(shares, "core", [(0, 1), (1, 0)])
-    parts = 8
+    near = exchange(shares)
+    parts = 16
     result = call(
         functools.partial(last_kernel, lat_count),
         "second_batch",
@@ -528,8 +529,7 @@
             held_rows,
             pltpu.SemaphoreType.DMA((parts,)),
         ],
-        shares,
-        other,
+        *near,
         pattern,
         first_map,
         pad,

time: 56.6 us -> 58.3 us (1.030)
  blocking collectives: 11.2 us -> 23 us
  waiting for transfers between devices: 12.7 us -> 6.39 us
  starting transfers between devices: 13 us -> 9.83 us
  Pallas kernels: 17.2 us -> 16.6 us
    all_to_all x1 -> x2, blocking collectives: 11.2 us -> 23 us  [exchange(): lax.all_to_all(blocks, ('lat', 'far'), split_axis=0, concat_axis=0, tiled...]
    all_to_all x1 -> x0, waiting for transfers between devices: 6 us -> none  [exchange(): lax.all_to_all(blocks, ('lat',) + LON, split_axis=0, concat_axis=0, tiled...]
    all_to_all x1 -> x0, starting transfers between devices: 3.47 us -> none  [exchange(): lax.all_to_all(blocks, ('lat',) + LON, split_axis=0, concat_axis=0, tiled...]
    pallas_call x9, Pallas kernels: 17.2 us -> 16.6 us  [call(): pl.pallas_call(kernel, out_shape=out_shape, in_specs=specs, out_specs=out...]
    ppermute x1 -> x2, waiting for transfers between devices: 1.44 us -> 1.44 us  [exchange(): return (mine, lax.ppermute(mine, 'core', [(0, 1), (1, 0)]))]
  transfers between devices with their start and end apart: 8 -> 8, of which waited for: 4 -> 3; matrix products, arithmetic and copies ran while one was open for 0% -> 0% of each run, Pallas kernels for 4% -> 4%
where the time goes in v10:
time: 58.3 us; the launch traced here: 57.9 us
  blocking collectives  23 us (39%)
  Pallas kernels  16.6 us (28%)
  starting transfers between devices  9.83 us (17%)
  waiting for transfers between devices  6.39 us (11%)
  local copies, waits for them, and re-layouts  2.06 us (4%)
    all_to_all x2, blocking collectives, exchange(): lax.all_to_all(blocks, ('lat', 'far'), split_axis=0, concat_axis=0, tiled...  23 us
    pallas_call x9, Pallas kernels, call(): pl.pallas_call(kernel, out_shape=out_shape, in_specs=specs, out_specs=out...  16.6 us
    ppermute x6, starting transfers between devices, trade(): results.append(lax.ppermute(block, axis, route))  9.82 us
    ppermute x6, waiting for transfers between devices, trade(): results.append(lax.ppermute(block, axis, route))  4.95 us
    unnamed x7, local copies, waits for them, and re-layouts  2.06 us
    ppermute x2, waiting for transfers between devices, exchange(): return (mine, lax.ppermute(mine, 'core', [(0, 1), (1, 0)]))  1.44 us
  transfers between devices with their start and end apart: 8, of which 3 were waited for; matrix products, arithmetic and copies ran while one was open for 0% of the time, Pallas kernels for 4%

profile of v10, /device:TPU:0, one launch (start us, length us, event | category | flops | bytes accessed | tf_op | source)
XLA Modules:
  0.0 57.9 jit_solution(17915613459556031713)
XLA Ops:
  0.0 1.8 %start.1 = (f32[2,8,128]{2,1,0:T(8,128)}, f32[40,128]{1,0:T(8,128)}, f32[40,128]{1,0:T(8,128)}) custom-call(f32[2,1,1,8]{3,2,1,0:T(1,128)} %observed.1, f32[2,1,1,8]{3,2,1,0:T(1,128)} %precision.1, f32[2,1,1,4,8]{4,3,2,1,0:T(4,128)} %weight.1, s32[2,1,1,4,8]{4,3,2,1,0:T(4,128)} %stencil.1, s32[2,1,1,8]{3,2,1,0:T(1,128)} %owned.1, f32[32,128,128]{2,1,0:T(8,128)} %cells.3), custom_call_target="tpu_custom_call" | custom-call | tf_op jit(solution)/shard_map/start/pallas_call | solution.py:443
  1.8 3.4 %collective-permute-start = (f32[40,128]{1,0:T(8,128)}, f32[40,128]{1,0:T(8,128)S(1)}, u32[]{:S(2)}, u32[]{:S(2)}) collective-permute-start(f32[40,128]{1,0:T(8,128)} %get-tuple-element.17), channel_id=1, source_target_pairs={{0,7},{1,2},{2,1},{3,4},{4,3},{5,6},{6,5},{7,0},{8,15},{9,10},{10,... | collective-permute-start | bytes 61448 | tf_op jit(solution)/shard_map/ppermute | solution.py:31
  5.2 0.0 collective-permute-start.1
  5.2 0.0 copy-start
  5.2 1.6 %copy-done = f32[32,128,128]{2,1,0:T(8,128)S(1)} copy-done((f32[32,128,128]{2,1,0:T(8,128)S(1)}, f32[32,128,128]{2,1,0:T(8,128)}, u32[]{:S(2)}) %copy-start) | copy-done | bytes 2097176
  6.8 0.0 copy-start.1
  6.8 0.2 pad.1
  7.0 0.0 collective-permute-done.sides_0
  7.0 0.0 collective-permute-done.1.sides_1
  7.0 0.5 copy-done.1
  7.5 0.1 edge_rows.1
  7.5 0.0 copy-start.2
  7.5 0.8 %collective-permute-start.2 = (f32[152,128]{1,0:T(8,128)S(1)}, f32[152,128]{1,0:T(8,128)S(1)}, u32[]{:S(2)}, u32[]{:S(2)}) collective-permute-start(f32[152,128]{1,0:T(8,128)S(1)} %get-tuple-element.21), channel_id=1, source_target_pairs={{8,16},{16,8},{9,17},{17,9},{10,18},{18,10},{11,19},{19,11},{12,20... | collective-permute-start | bytes 233480 | tf_op jit(solution)/shard_map/ppermute | solution.py:31
  8.3 4.7 %collective-permute-start.3 = (f32[152,128]{1,0:T(8,128)S(1)}, f32[152,128]{1,0:T(8,128)S(1)}, u32[]{:S(2)}, u32[]{:S(2)}) collective-permute-start(f32[152,128]{1,0:T(8,128)S(1)} %get-tuple-element.22), channel_id=1, source_target_pairs={{0,8},{8,0},{16,24},{24,16},{1,9},{9,1},{17,25},{25,17},{2,10},{10... | collective-permute-start | bytes 233480 | tf_op jit(solution)/shard_map/ppermute | solution.py:31
  13.1 0.7 %row_shares.1.own = f32[8,128]{1,0:T(8,128)S(1)} custom-call(f32[2,8,128]{2,1,0:T(8,128)S(1)} %copy-done.1, f32[40,128]{1,0:T(8,128)S(1)} %get-tuple-element.19.left, f32[40,128]{1,0:T(8,128)S(1)} %get-tuple-element.20.right, f32[36,144,128]{2,1,0:T(8,128)S(1)} %pad.1), custom_call_target="tpu_custom_call" | custom-call | tf_op jit(solution)/shard_map/row_shares/pallas_call | solution.py:443
  13.8 0.0 collective-permute-done.2.ends_0
  13.8 1.8 %collective-permute-done.3.ends_1 = f32[152,128]{1,0:T(8,128)S(1)} collective-permute-done((f32[152,128]{1,0:T(8,128)S(1)}, f32[152,128]{1,0:T(8,128)S(1)}, u32[]{:S(2)}, u32[]{:S(2)}) %collective-permute-start.3) | collective-permute-done | bytes 77856 | tf_op jit(solution)/shard_map/ppermute | solution.py:31
  15.5 0.8 %prior.1 = bf16[16,5,2,128]{3,2,1,0:T(2,128)(2,1)S(1)} custom-call(f32[2,8,128]{2,1,0:T(8,128)S(1)} %copy-done.1, f32[8,128]{1,0:T(8,128)S(1)} %row_shares.1.own, f32[152,128]{1,0:T(8,128)S(1)} %collective-permute-done.2.ends_0, f32[152,128]{1,0:T(8,128)S(1)} %collective-permute-done.3.ends_1), custom_call_target="tpu_custom_call" | custom-call | tf_op jit(solution)/shard_map/prior/pallas_call | solution.py:443
  16.3 11.7 %all_to_all.10.near = bf16[16,5,2,128]{3,2,1,0:T(2,128)(2,1)S(1)} all-to-all(bf16[16,5,2,128]{3,2,1,0:T(2,128)(2,1)S(1)} %prior.1), channel_id=1, replica_groups=mesh['lat'=4,'far'=4,'core'=2] {'lat','far'}, dimensions={0} | all-to-all | bytes 81920 | tf_op jit(solution)/shard_map/all_to_all | solution.py:454
  28.0 0.0 collective-permute-start.4
  28.0 0.0 copy-done.2
  28.0 1.6 %later_shares.1.later = f32[10,8,128]{2,1,0:T(8,128)S(1)} custom-call(f32[2,8,128]{2,1,0:T(8,128)S(1)} %copy-done.1, f32[40,128]{1,0:T(8,128)S(1)} %get-tuple-element.19.left, f32[40,128]{1,0:T(8,128)S(1)} %get-tuple-element.20.right, f32[152,128]{1,0:T(8,128)S(1)} %collective-permute-done.2.ends_0, f32[152,128]{1,0:T(8,128)S(1)} %collective-permute-done.3.ends_1, ...), custom_call_target="tpu_custom_call" | custom-call | tf_op jit(solution)/shard_map/later_shares/pallas_call | solution.py:443
  29.6 0.0 collective-permute-done.4.other
  29.6 4.9 %first_batch.1 = (f32[128,128]{1,0:T(8,128)S(1)}, f32[24,128]{1,0:T(8,128)S(1)}, f32[24,128]{1,0:T(8,128)S(1)}, f32[24,128]{1,0:T(8,128)S(1)}) custom-call(bf16[16,5,2,128]{3,2,1,0:T(2,128)(2,1)S(1)} %all_to_all.10.near, bf16[16,5,2,128]{3,2,1,0:T(2,128)(2,1)S(1)} %collective-permute-done.4.other, s32[2,1,1,5,8]{4,3,2,1,0:T(8,128)S(1)} %copy.8.pattern, ...), custom_call_target="tpu_custom_call" | custom-call | tf_op jit(solution)/shard_map/first_batch/pallas_call | solution.py:443
  34.5 0.8 %collective-permute-start.5 = (f32[24,128]{1,0:T(8,128)S(1)}, f32[24,128]{1,0:T(8,128)S(1)}, u32[]{:S(2)}, u32[]{:S(2)}) collective-permute-start(f32[24,128]{1,0:T(8,128)S(1)} %get-tuple-element.24), channel_id=1, source_target_pairs={{0,7},{1,2},{2,1},{3,4},{4,3},{5,6},{6,5},{7,0},{8,15},{9,10},{10,... | collective-permute-start | bytes 36872 | tf_op jit(solution)/shard_map/ppermute | solution.py:31
  35.3 0.1 collective-permute-start.6
  35.4 3.2 %collective-permute-done.5.sides_0 = f32[24,128]{1,0:T(8,128)S(1)} collective-permute-done((f32[24,128]{1,0:T(8,128)S(1)}, f32[24,128]{1,0:T(8,128)S(1)}, u32[]{:S(2)}, u32[]{:S(2)}) %collective-permute-start.5) | collective-permute-done | bytes 12320 | tf_op jit(solution)/shard_map/ppermute | solution.py:31
  38.6 0.0 collective-permute-done.6.sides_1
  38.6 11.3 %all_to_all.11.mine = f32[16,24,128]{2,1,0:T(8,128)S(1)} all-to-all(f32[16,24,128]{2,1,0:T(8,128)S(1)} %meet.1), channel_id=1, replica_groups=mesh['lat'=4,'far'=4,'core'=2] {'lat','far'}, dimensions={0} | all-to-all | bytes 393216 | tf_op jit(solution)/shard_map/all_to_all | solution.py:454
  49.9 0.0 collective-permute-start.7
  49.9 1.4 %collective-permute-done.7.other = f32[16,24,128]{2,1,0:T(8,128)S(1)} collective-permute-done((f32[16,24,128]{2,1,0:T(8,128)S(1)}, f32[16,24,128]{2,1,0:T(8,128)S(1)}, u32[]{:S(2)}, u32[]{:S(2)}) %collective-permute-start.7) | collective-permute-done | bytes 196640 | tf_op jit(solution)/shard_map/ppermute | solution.py:455
  51.3 6.6 %second_batch.1 = f32[4096,128]{1,0:T(8,128)} custom-call(f32[16,24,128]{2,1,0:T(8,128)S(1)} %all_to_all.11.mine, f32[16,24,128]{2,1,0:T(8,128)S(1)} %collective-permute-done.7.other, s32[2,1,1,5,8]{4,3,2,1,0:T(8,128)S(1)} %copy.8.pattern, f32[128,128]{1,0:T(8,128)S(1)} %get-tuple-element.26.map_ref, f32[36,144,128]{2,1,0:T(8,128)S(1)} %pad.1), custom_call_target="tpu_custom_call" | custom-call | tf_op jit(solution)/shard_map/second_batch/pallas_call | solution.py:443
  (2 shorter events, 0.0 us)
Async XLA Ops:
  1.8 5.2 %collective-permute-start = (f32[40,128]{1,0:T(8,128)}, f32[40,128]{1,0:T(8,128)S(1)}, u32[]{:S(2)}, u32[]{:S(2)}) collective-permute-start(f32[40,128]{1,0:T(8,128)} %get-tuple-element.17), channel_id=1, source_target_pairs={{0,7},{1,2},{2,1},{3,4},{4,3},{5,6},{6,5},{7,0},{8,15},{9,10},{10,... | collective-permute-start | bytes 61448 | tf_op jit(solution)/shard_map/ppermute | solution.py:31
  5.2 1.8 %collective-permute-start.1 = (f32[40,128]{1,0:T(8,128)}, f32[40,128]{1,0:T(8,128)S(1)}, u32[]{:S(2)}, u32[]{:S(2)}) collective-permute-start(f32[40,128]{1,0:T(8,128)} %get-tuple-element.18), channel_id=1, source_target_pairs={{0,1},{1,0},{2,3},{3,2},{4,5},{5,4},{6,7},{7,6},{8,9},{9,8},{10,11... | collective-permute-start | bytes 61448 | tf_op jit(solution)/shard_map/ppermute | solution.py:31
  5.2 1.6 %copy-start = (f32[32,128,128]{2,1,0:T(8,128)S(1)}, f32[32,128,128]{2,1,0:T(8,128)}, u32[]{:S(2)}) copy-start(f32[32,128,128]{2,1,0:T(8,128)} %cells.3) | copy-start | bytes 6291460
  6.8 0.7 %copy-start.1 = (f32[2,8,128]{2,1,0:T(8,128)S(1)}, f32[2,8,128]{2,1,0:T(8,128)}, u32[]{:S(2)}) copy-start(f32[2,8,128]{2,1,0:T(8,128)} %get-tuple-element.16.mine) | copy-start | bytes 24580
  7.5 20.5 %copy-start.2 = (s32[2,1,1,5,8]{4,2,3,1,0:T(1,128)S(1)}, s32[2,1,1,5,8]{4,2,3,1,0:T(1,128)}, u32[]{:S(2)}) copy-start(s32[2,1,1,5,8]{4,2,3,1,0:T(1,128)} %param.13) | copy-start | bytes 964
  7.5 6.2 %collective-permute-start.2 = (f32[152,128]{1,0:T(8,128)S(1)}, f32[152,128]{1,0:T(8,128)S(1)}, u32[]{:S(2)}, u32[]{:S(2)}) collective-permute-start(f32[152,128]{1,0:T(8,128)S(1)} %get-tuple-element.21), channel_id=1, source_target_pairs={{8,16},{16,8},{9,17},{17,9},{10,18},{18,10},{11,19},{19,11},{12,20... | collective-permute-start | bytes 233480 | tf_op jit(solution)/shard_map/ppermute | solution.py:31
  8.3 7.2 %collective-permute-start.3 = (f32[152,128]{1,0:T(8,128)S(1)}, f32[152,128]{1,0:T(8,128)S(1)}, u32[]{:S(2)}, u32[]{:S(2)}) collective-permute-start(f32[152,128]{1,0:T(8,128)S(1)} %get-tuple-element.22), channel_id=1, source_target_pairs={{0,8},{8,0},{16,24},{24,16},{1,9},{9,1},{17,25},{25,17},{2,10},{10... | collective-permute-start | bytes 233480 | tf_op jit(solution)/shard_map/ppermute | solution.py:31
  28.0 1.6 %collective-permute-start.4 = (bf16[16,5,2,128]{3,2,1,0:T(2,128)(2,1)S(1)}, bf16[16,5,2,128]{3,2,1,0:T(2,128)(2,1)S(1)}, u32[]{:S(2)}, u32[]{:S(2)}) collective-permute-start(bf16[16,5,2,128]{3,2,1,0:T(2,128)(2,1)S(1)} %all_to_all.10.near), channel_id=1, source_target_pairs={{0,1},{1,0},{2,3},{3,2},{4,5},{5,4},{6,7},{7,6},{8,9},{9,8},{10,11... | collective-permute-start | bytes 122888 | tf_op jit(solution)/shard_map/ppermute | solution.py:455
  34.5 4.1 %collective-permute-start.5 = (f32[24,128]{1,0:T(8,128)S(1)}, f32[24,128]{1,0:T(8,128)S(1)}, u32[]{:S(2)}, u32[]{:S(2)}) collective-permute-start(f32[24,128]{1,0:T(8,128)S(1)} %get-tuple-element.24), channel_id=1, source_target_pairs={{0,7},{1,2},{2,1},{3,4},{4,3},{5,6},{6,5},{7,0},{8,15},{9,10},{10,... | collective-permute-start | bytes 36872 | tf_op jit(solution)/shard_map/ppermute | solution.py:31
  35.3 3.3 %collective-permute-start.6 = (f32[24,128]{1,0:T(8,128)S(1)}, f32[24,128]{1,0:T(8,128)S(1)}, u32[]{:S(2)}, u32[]{:S(2)}) collective-permute-start(f32[24,128]{1,0:T(8,128)S(1)} %get-tuple-element.25), channel_id=1, source_target_pairs={{0,1},{1,0},{2,3},{3,2},{4,5},{5,4},{6,7},{7,6},{8,9},{9,8},{10,11... | collective-permute-start | bytes 36872 | tf_op jit(solution)/shard_map/ppermute | solution.py:31
  49.9 1.4 %collective-permute-start.7 = (f32[16,24,128]{2,1,0:T(8,128)S(1)}, f32[16,24,128]{2,1,0:T(8,128)S(1)}, u32[]{:S(2)}, u32[]{:S(2)}) collective-permute-start(f32[16,24,128]{2,1,0:T(8,128)S(1)} %all_to_all.11.mine), channel_id=1, source_target_pairs={{0,1},{1,0},{2,3},{3,2},{4,5},{5,4},{6,7},{7,6},{8,9},{9,8},{10,11... | collective-permute-start | bytes 589832 | tf_op jit(solution)/shard_map/ppermute | solution.py:455

commit v11 on v8

--- a/solution.py
+++ b/solution.py
@@ -300,26 +300,25 @@
     return scaled, jnp.where(lane == sub, jnp.broadcast_to(innov, scaled.shape), 0.0)
 
 
-def summed_blocks(lat_count, mine, other):
+def summed_blocks(lat_count, shares):
     held = min(WIN, lat_count)
-    far_count = mine.shape[0] // lat_count
+    far_count = shares.shape[0] // lat_count
     start = window_start(lat_count, lax.axis_index("lat"))
     values = []
     for j in range(held):
         for far in range(far_count):
-            for shares in (mine, other):
-                total = jnp.zeros((SUB, LANES), F32)
-                for n, da in enumerate(NEAR):
-                    source = start + j - da
-                    part = pl.ds(n * SUB, SUB)
-                    if isinstance(source, int):
-                        if 0 <= source < lat_count:
-                            total = total + shares[source * far_count + far, part, :]
-                    else:
-                        inside = (source >= 0) & (source < lat_count)
-                        source = jnp.clip(source, 0, lat_count - 1)
-                        total = total + jnp.where(inside, shares[source * far_count + far, part, :], 0.0)
-                values.append(total[None])
+            total = jnp.zeros((SUB, LANES), F32)
+            for n, da in enumerate(NEAR):
+                source = start + j - da
+                part = pl.ds(n * SUB, SUB)
+                if isinstance(source, int):
+                    if 0 <= source < lat_count:
+                        total = total + shares[source * far_count + far, part, :]
+                else:
+                    inside = (source >= 0) & (source < lat_count)
+                    source = jnp.clip(source, 0, lat_count - 1)
+                    total = total + jnp.where(inside, shares[source * far_count + far, part, :], 0.0)
+            values.append(total[None])
     value = jnp.concatenate(values, axis=0)
     mean = jnp.mean(value, axis=-1, keepdims=True)
     sub = lax.broadcasted_iota(jnp.int32, value.shape, 1)
@@ -328,10 +327,11 @@
     return (value - mean).astype(BF16).astype(F32), innov
 
 
-def batch_map(batch, lat_count, blocks, pattern, swapped, held_rows):
+def marked_product(batch, lat_count, blocks, pattern, place=None):
     scaled, innov = blocks
     held = min(WIN, lat_count)
     count = scaled.shape[0]
+    lon_count = pattern.shape[-1]
     my_lat = lax.axis_index("lat")
     start = window_start(lat_count, my_lat)
     picked = []
@@ -340,12 +340,10 @@
         inside = (offset >= 0) & (offset < WIN)
         row = pattern[batch, 0, 0, pl.ds(jnp.clip(offset, 0, WIN - 1), 1), :].astype(F32)
         row = jnp.where(inside, row, 0.0)
-        marks = [jnp.broadcast_to(row[:, e:e + 1], (1, SUB, LANES)) for e in range(count // held)]
-        for e in range(0, len(marks), 2):
-            first, second = marks[e:e + 2]
-            if swapped is not None:
-                first, second = (jnp.where(swapped, second, first), jnp.where(swapped, first, second))
-            picked.extend((first, second))
+        marks = [jnp.broadcast_to(row[:, e:e + 1], (1, SUB, LANES)) for e in range(lon_count)]
+        if place is not None:
+            marks = [jnp.where(place == 1, marks[e + 1], marks[e]) for e in range(0, lon_count, 2)]
+        picked.extend(marks)
     weighted = scaled * jnp.concatenate(picked, axis=0)
     both = jnp.concatenate([scaled, innov], axis=2).reshape(count * SUB, 2 * LANES).astype(BF16)
     product = lax.dot_general(
@@ -354,6 +352,10 @@
         (((0,), (0,)), ((), ())),
         preferred_element_type=F32,
     )
+    return product[:LANES + SUB]
+
+
+def solved_map(product, held_rows):
     sub = lax.broadcasted_iota(jnp.int32, (SUB, LANES), 0)
     lane = lax.broadcasted_iota(jnp.int32, (SUB, LANES), 1)
     members = LANES
@@ -375,7 +377,7 @@
 
 
 def first_kernel(lat_count, near_ref, pattern, later, map_ref, mid_ref, out_0, out_1, held_rows):
-    flipped = batch_map(0, lat_count, own_blocks(near_ref), pattern, None, held_rows)
+    flipped = solved_map(marked_product(0, lat_count, own_blocks(near_ref), pattern), held_rows)
     map_ref[...] = flipped
     count = len(NEAR) ** 2
     moved = exact_dot(later[pl.ds(0, count)].reshape(-1, LANES), flipped, 1)
@@ -389,12 +391,15 @@
     out_1[...] = jnp.where(forward, left, right)
 
 
-def last_kernel(lat_count, mine, other, pattern, map_ref, pad, out_ref, result, held_rows, out_sem):
+def half_kernel(lat_count, mine, pattern, out_ref):
+    out_ref[...] = marked_product(1, lat_count, summed_blocks(lat_count, mine), pattern, lax.axis_index("core"))
+
+
+def last_kernel(lat_count, half, other, pattern, map_ref, pad, out_ref, result, held_rows, out_sem):
     parts = out_sem.shape[0]
     rows, cols = (pad.shape[0] - 4, pad.shape[1] - 2 * SUB)
-    swapped = lax.axis_index("core") == 1
-    blocks = summed_blocks(lat_count, mine, other)
-    flipped = exact_dot(batch_map(1, lat_count, blocks, pattern, swapped, held_rows), map_ref[...], 0)
+    product = marked_product(1, lat_count, summed_blocks(lat_count, other), pattern, 1 - lax.axis_index("core"))
+    flipped = exact_dot(solved_map(product + half[...], held_rows), map_ref[...], 0)
     high = flipped.astype(BF16)
     low = (flipped - high.astype(F32)).astype(BF16)
     right = jnp.concatenate(
@@ -517,6 +522,15 @@
     shares = call(meet_kernel, "meet", [vmem] * 3, shape(tiles // 2, *column.shape), [], mid, *sides)
     shares = lax.all_to_all(shares, ("lat", "far"), split_axis=0, concat_axis=0, tiled=True)
     other = lax.ppermute(shares, "core", [(0, 1), (1, 0)])
+    half = call(
+        functools.partial(half_kernel, lat_count),
+        "half_product",
+        [vmem] * 2,
+        shape(members + SUB, members),
+        [],
+        shares,
+        pattern,
+    )
     parts = 8
     result = call(
         functools.partial(last_kernel, lat_count),
@@ -528,7 +542,7 @@
             held_rows,
             pltpu.SemaphoreType.DMA((parts,)),
         ],
-        shares,
+        half,
         other,
         pattern,
         first_map,

time: 56.6 us -> 56.5 us (level)
    pallas_call x9 -> x10, Pallas kernels: 17.2 us -> 17.5 us  [call(): pl.pallas_call(kernel, out_shape=out_shape, in_specs=specs, out_specs=out...]
  transfers between devices with their start and end apart: 8 -> 8, of which waited for: 4 -> 4; matrix products, arithmetic and copies ran while one was open for 0% -> 0% of each run, Pallas kernels for 4% -> 5%
where the time goes in v11:
time: 56.5 us; the launch traced here: 56.2 us
  Pallas kernels  17.5 us (31%)
  starting transfers between devices  13 us (23%)
  waiting for transfers between devices  12.3 us (22%)
  blocking collectives  11.2 us (20%)
  local copies, waits for them, and re-layouts  2.06 us (4%)
    pallas_call x10, Pallas kernels, call(): pl.pallas_call(kernel, out_shape=out_shape, in_specs=specs, out_specs=out...  17.5 us
    all_to_all x1, blocking collectives, local(): lax.all_to_all(shares, ('lat', 'far'), split_axis=0, concat_axis=0, tiled...  11.2 us
    ppermute x6, starting transfers between devices, trade(): results.append(lax.ppermute(block, axis, route))  9.49 us
    all_to_all x1, waiting for transfers between devices, exchange(): lax.all_to_all(blocks, ('lat',) + LON, split_axis=0, concat_axis=0, tiled...  6 us
    ppermute x6, waiting for transfers between devices, trade(): results.append(lax.ppermute(block, axis, route))  5.28 us
    all_to_all x1, starting transfers between devices, exchange(): lax.all_to_all(blocks, ('lat',) + LON, split_axis=0, concat_axis=0, tiled...  3.47 us
    unnamed x7, local copies, waits for them, and re-layouts  2.06 us
  transfers between devices with their start and end apart: 8, of which 4 were waited for; matrix products, arithmetic and copies ran while one was open for 0% of the time, Pallas kernels for 5%

profile of v11, /device:TPU:0, one launch (start us, length us, event | category | flops | bytes accessed | tf_op | source)
XLA Modules:
  0.0 56.2 jit_solution(7475318790920617159)
XLA Ops:
  0.0 1.8 %start.1 = (f32[2,8,128]{2,1,0:T(8,128)}, f32[40,128]{1,0:T(8,128)}, f32[40,128]{1,0:T(8,128)}) custom-call(f32[2,1,1,8]{3,2,1,0:T(1,128)} %observed.1, f32[2,1,1,8]{3,2,1,0:T(1,128)} %precision.1, f32[2,1,1,4,8]{4,3,2,1,0:T(4,128)} %weight.1, s32[2,1,1,4,8]{4,3,2,1,0:T(4,128)} %stencil.1, s32[2,1,1,8]{3,2,1,0:T(1,128)} %owned.1, f32[32,128,128]{2,1,0:T(8,128)} %cells.3), custom_call_target="tpu_custom_call" | custom-call | tf_op jit(solution)/shard_map/start/pallas_call | solution.py:447
  1.8 3.4 %collective-permute-start = (f32[40,128]{1,0:T(8,128)}, f32[40,128]{1,0:T(8,128)S(1)}, u32[]{:S(2)}, u32[]{:S(2)}) collective-permute-start(f32[40,128]{1,0:T(8,128)} %get-tuple-element.17), channel_id=1, source_target_pairs={{0,7},{1,2},{2,1},{3,4},{4,3},{5,6},{6,5},{7,0},{8,15},{9,10},{10,... | collective-permute-start | bytes 61448 | tf_op jit(solution)/shard_map/ppermute | solution.py:31
  5.2 0.0 collective-permute-start.1
  5.2 0.0 copy-start
  5.2 1.6 %copy-done = f32[32,128,128]{2,1,0:T(8,128)S(1)} copy-done((f32[32,128,128]{2,1,0:T(8,128)S(1)}, f32[32,128,128]{2,1,0:T(8,128)}, u32[]{:S(2)}) %copy-start) | copy-done | bytes 2097176
  6.8 0.0 copy-start.1
  6.8 0.2 pad.1
  7.0 0.0 collective-permute-done.sides_0
  7.0 0.0 collective-permute-done.1.sides_1
  7.0 0.5 copy-done.1
  7.5 0.1 edge_rows.1
  7.5 0.0 copy-start.2
  7.5 0.8 %collective-permute-start.2 = (f32[152,128]{1,0:T(8,128)S(1)}, f32[152,128]{1,0:T(8,128)S(1)}, u32[]{:S(2)}, u32[]{:S(2)}) collective-permute-start(f32[152,128]{1,0:T(8,128)S(1)} %get-tuple-element.21), channel_id=1, source_target_pairs={{8,16},{16,8},{9,17},{17,9},{10,18},{18,10},{11,19},{19,11},{12,20... | collective-permute-start | bytes 233480 | tf_op jit(solution)/shard_map/ppermute | solution.py:31
  8.3 4.7 %collective-permute-start.3 = (f32[152,128]{1,0:T(8,128)S(1)}, f32[152,128]{1,0:T(8,128)S(1)}, u32[]{:S(2)}, u32[]{:S(2)}) collective-permute-start(f32[152,128]{1,0:T(8,128)S(1)} %get-tuple-element.22), channel_id=1, source_target_pairs={{0,8},{8,0},{16,24},{24,16},{1,9},{9,1},{17,25},{25,17},{2,10},{10... | collective-permute-start | bytes 233480 | tf_op jit(solution)/shard_map/ppermute | solution.py:31
  13.1 0.7 %row_shares.1.own = f32[8,128]{1,0:T(8,128)S(1)} custom-call(f32[2,8,128]{2,1,0:T(8,128)S(1)} %copy-done.1, f32[40,128]{1,0:T(8,128)S(1)} %get-tuple-element.19.left, f32[40,128]{1,0:T(8,128)S(1)} %get-tuple-element.20.right, f32[36,144,128]{2,1,0:T(8,128)S(1)} %pad.1), custom_call_target="tpu_custom_call" | custom-call | tf_op jit(solution)/shard_map/row_shares/pallas_call | solution.py:447
  13.8 0.0 collective-permute-done.2.ends_0
  13.8 1.8 %collective-permute-done.3.ends_1 = f32[152,128]{1,0:T(8,128)S(1)} collective-permute-done((f32[152,128]{1,0:T(8,128)S(1)}, f32[152,128]{1,0:T(8,128)S(1)}, u32[]{:S(2)}, u32[]{:S(2)}) %collective-permute-start.3) | collective-permute-done | bytes 77856 | tf_op jit(solution)/shard_map/ppermute | solution.py:31
  15.5 1.4 %prior.1 = bf16[32,5,2,128]{3,2,1,0:T(2,128)(2,1)} custom-call(f32[2,8,128]{2,1,0:T(8,128)S(1)} %copy-done.1, f32[8,128]{1,0:T(8,128)S(1)} %row_shares.1.own, f32[152,128]{1,0:T(8,128)S(1)} %collective-permute-done.2.ends_0, f32[152,128]{1,0:T(8,128)S(1)} %collective-permute-done.3.ends_1), custom_call_target="tpu_custom_call" | custom-call | tf_op jit(solution)/shard_map/prior/pallas_call | solution.py:447
  17.0 3.5 %all-to-all-start = ((bf16[32,5,2,128]{3,2,1,0:T(2,128)(2,1)}), bf16[32,5,2,128]{3,2,1,0:T(2,128)(2,1)S(1)}, u32[]{:S(2)}, u32[]{:S(2)}) async-start(bf16[32,5,2,128]{3,2,1,0:T(2,128)(2,1)} %prior.1), calls=%async_computation | async-start | bytes 163840 | tf_op jit(solution)/shard_map/all_to_all | solution.py:458
  20.5 0.0 copy-done.2
  20.5 1.6 %later_shares.1.later = f32[10,8,128]{2,1,0:T(8,128)S(1)} custom-call(f32[2,8,128]{2,1,0:T(8,128)S(1)} %copy-done.1, f32[40,128]{1,0:T(8,128)S(1)} %get-tuple-element.19.left, f32[40,128]{1,0:T(8,128)S(1)} %get-tuple-element.20.right, f32[152,128]{1,0:T(8,128)S(1)} %collective-permute-done.2.ends_0, f32[152,128]{1,0:T(8,128)S(1)} %collective-permute-done.3.ends_1, ...), custom_call_target="tpu_custom_call" | custom-call | tf_op jit(solution)/shard_map/later_shares/pallas_call | solution.py:447
  22.1 6.0 %all-to-all-done.near_ref = bf16[32,5,2,128]{3,2,1,0:T(2,128)(2,1)S(1)} async-done(((bf16[32,5,2,128]{3,2,1,0:T(2,128)(2,1)}), bf16[32,5,2,128]{3,2,1,0:T(2,128)(2,1)S(1)}, u32[]{:S(2)}, u32[]{:S(2)}) %all-to-all-start) | async-done | bytes 81952 | tf_op jit(solution)/shard_map/all_to_all | solution.py:458
  28.1 4.9 %first_batch.1 = (f32[128,128]{1,0:T(8,128)S(1)}, f32[24,128]{1,0:T(8,128)S(1)}, f32[24,128]{1,0:T(8,128)S(1)}, f32[24,128]{1,0:T(8,128)S(1)}) custom-call(bf16[32,5,2,128]{3,2,1,0:T(2,128)(2,1)S(1)} %all-to-all-done.near_ref, s32[2,1,1,5,8]{4,3,2,1,0:T(8,128)S(1)} %copy.8.pattern, f32[10,8,128]{2,1,0:T(8,128)S(1)} %later_shares.1.later), custom_call_target="tpu_custom_call" | custom-call | tf_op jit(solution)/shard_map/first_batch/pallas_call | solution.py:447
  32.9 0.4 collective-permute-start.4
  33.3 0.2 collective-permute-start.5
  33.5 3.5 %collective-permute-done.4.sides_0 = f32[24,128]{1,0:T(8,128)S(1)} collective-permute-done((f32[24,128]{1,0:T(8,128)S(1)}, f32[24,128]{1,0:T(8,128)S(1)}, u32[]{:S(2)}, u32[]{:S(2)}) %collective-permute-start.4) | collective-permute-done | bytes 12320 | tf_op jit(solution)/shard_map/ppermute | solution.py:31
  37.0 0.0 collective-permute-done.5.sides_1
  37.0 11.2 %all_to_all.10.mine = f32[16,24,128]{2,1,0:T(8,128)S(1)} all-to-all(f32[16,24,128]{2,1,0:T(8,128)S(1)} %meet.1), channel_id=1, replica_groups=mesh['lat'=4,'far'=4,'core'=2] {'lat','far'}, dimensions={0} | all-to-all | bytes 393216 | tf_op jit(solution)/shard_map/all_to_all | solution.py:523
  48.2 0.0 collective-permute-start.6
  48.2 0.4 half_product.1.half
  48.6 1.1 %collective-permute-done.6.other = f32[16,24,128]{2,1,0:T(8,128)S(1)} collective-permute-done((f32[16,24,128]{2,1,0:T(8,128)S(1)}, f32[16,24,128]{2,1,0:T(8,128)S(1)}, u32[]{:S(2)}, u32[]{:S(2)}) %collective-permute-start.6) | collective-permute-done | bytes 196640 | tf_op jit(solution)/shard_map/ppermute | solution.py:524
  49.7 6.5 %second_batch.1 = f32[4096,128]{1,0:T(8,128)} custom-call(f32[136,128]{1,0:T(8,128)S(1)} %half_product.1.half, f32[16,24,128]{2,1,0:T(8,128)S(1)} %collective-permute-done.6.other, s32[2,1,1,5,8]{4,3,2,1,0:T(8,128)S(1)} %copy.8.pattern, f32[128,128]{1,0:T(8,128)S(1)} %get-tuple-element.26.map_ref, f32[36,144,128]{2,1,0:T(8,128)S(1)} %pad.1), custom_call_target="tpu_custom_call" | custom-call | tf_op jit(solution)/shard_map/second_batch/pallas_call | solution.py:447
  (2 shorter events, 0.0 us)
Async XLA Ops:
  1.8 5.2 %collective-permute-start = (f32[40,128]{1,0:T(8,128)}, f32[40,128]{1,0:T(8,128)S(1)}, u32[]{:S(2)}, u32[]{:S(2)}) collective-permute-start(f32[40,128]{1,0:T(8,128)} %get-tuple-element.17), channel_id=1, source_target_pairs={{0,7},{1,2},{2,1},{3,4},{4,3},{5,6},{6,5},{7,0},{8,15},{9,10},{10,... | collective-permute-start | bytes 61448 | tf_op jit(solution)/shard_map/ppermute | solution.py:31
  5.2 1.8 %collective-permute-start.1 = (f32[40,128]{1,0:T(8,128)}, f32[40,128]{1,0:T(8,128)S(1)}, u32[]{:S(2)}, u32[]{:S(2)}) collective-permute-start(f32[40,128]{1,0:T(8,128)} %get-tuple-element.18), channel_id=1, source_target_pairs={{0,1},{1,0},{2,3},{3,2},{4,5},{5,4},{6,7},{7,6},{8,9},{9,8},{10,11... | collective-permute-start | bytes 61448 | tf_op jit(solution)/shard_map/ppermute | solution.py:31
  5.2 1.6 %copy-start = (f32[32,128,128]{2,1,0:T(8,128)S(1)}, f32[32,128,128]{2,1,0:T(8,128)}, u32[]{:S(2)}) copy-start(f32[32,128,128]{2,1,0:T(8,128)} %cells.3) | copy-start | bytes 6291460
  6.8 0.7 %copy-start.1 = (f32[2,8,128]{2,1,0:T(8,128)S(1)}, f32[2,8,128]{2,1,0:T(8,128)}, u32[]{:S(2)}) copy-start(f32[2,8,128]{2,1,0:T(8,128)} %get-tuple-element.16.mine) | copy-start | bytes 24580
  7.5 12.9 %copy-start.2 = (s32[2,1,1,5,8]{4,2,3,1,0:T(1,128)S(1)}, s32[2,1,1,5,8]{4,2,3,1,0:T(1,128)}, u32[]{:S(2)}) copy-start(s32[2,1,1,5,8]{4,2,3,1,0:T(1,128)} %param.13) | copy-start | bytes 964
  7.5 6.2 %collective-permute-start.2 = (f32[152,128]{1,0:T(8,128)S(1)}, f32[152,128]{1,0:T(8,128)S(1)}, u32[]{:S(2)}, u32[]{:S(2)}) collective-permute-start(f32[152,128]{1,0:T(8,128)S(1)} %get-tuple-element.21), channel_id=1, source_target_pairs={{8,16},{16,8},{9,17},{17,9},{10,18},{18,10},{11,19},{19,11},{12,20... | collective-permute-start | bytes 233480 | tf_op jit(solution)/shard_map/ppermute | solution.py:31
  8.3 7.2 %collective-permute-start.3 = (f32[152,128]{1,0:T(8,128)S(1)}, f32[152,128]{1,0:T(8,128)S(1)}, u32[]{:S(2)}, u32[]{:S(2)}) collective-permute-start(f32[152,128]{1,0:T(8,128)S(1)} %get-tuple-element.22), channel_id=1, source_target_pairs={{0,8},{8,0},{16,24},{24,16},{1,9},{9,1},{17,25},{25,17},{2,10},{10... | collective-permute-start | bytes 233480 | tf_op jit(solution)/shard_map/ppermute | solution.py:31
  17.0 11.1 %all-to-all-start = ((bf16[32,5,2,128]{3,2,1,0:T(2,128)(2,1)}), bf16[32,5,2,128]{3,2,1,0:T(2,128)(2,1)S(1)}, u32[]{:S(2)}, u32[]{:S(2)}) async-start(bf16[32,5,2,128]{3,2,1,0:T(2,128)(2,1)} %prior.1), calls=%async_computation | async-start | bytes 163840 | tf_op jit(solution)/shard_map/all_to_all | solution.py:458
  32.9 4.1 %collective-permute-start.4 = (f32[24,128]{1,0:T(8,128)S(1)}, f32[24,128]{1,0:T(8,128)S(1)}, u32[]{:S(2)}, u32[]{:S(2)}) collective-permute-start(f32[24,128]{1,0:T(8,128)S(1)} %get-tuple-element.24), channel_id=1, source_target_pairs={{0,7},{1,2},{2,1},{3,4},{4,3},{5,6},{6,5},{7,0},{8,15},{9,10},{10,... | collective-permute-start | bytes 36872 | tf_op jit(solution)/shard_map/ppermute | solution.py:31
  33.3 3.7 %collective-permute-start.5 = (f32[24,128]{1,0:T(8,128)S(1)}, f32[24,128]{1,0:T(8,128)S(1)}, u32[]{:S(2)}, u32[]{:S(2)}) collective-permute-start(f32[24,128]{1,0:T(8,128)S(1)} %get-tuple-element.25), channel_id=1, source_target_pairs={{0,1},{1,0},{2,3},{3,2},{4,5},{5,4},{6,7},{7,6},{8,9},{9,8},{10,11... | collective-permute-start | bytes 36872 | tf_op jit(solution)/shard_map/ppermute | solution.py:31
  48.2 1.4 %collective-permute-start.6 = (f32[16,24,128]{2,1,0:T(8,128)S(1)}, f32[16,24,128]{2,1,0:T(8,128)S(1)}, u32[]{:S(2)}, u32[]{:S(2)}) collective-permute-start(f32[16,24,128]{2,1,0:T(8,128)S(1)} %all_to_all.10.mine), channel_id=1, source_target_pairs={{0,1},{1,0},{2,3},{3,2},{4,5},{5,4},{6,7},{7,6},{8,9},{9,8},{10,11... | collective-permute-start | bytes 589832 | tf_op jit(solution)/shard_map/ppermute | solution.py:524

commit v12 on v11

--- a/solution.py
+++ b/solution.py
@@ -51,8 +51,8 @@
         (cells.at[:, pl.ds(cols - SUB, SUB)], right_v),
     )
     copies = [pltpu.make_async_copy(source, target, sems.at[n]) for n, (source, target) in enumerate(pairs)]
-    for copy in copies:
-        copy.start()
+    for n, copy in enumerate(copies):
+        copy.start(priority=n % 2)
     for copy in copies:
         copy.wait()
     params_ref[...] = jnp.zeros_like(params_ref)
@@ -417,7 +417,7 @@
         )
         result[part, :] = both[:, :LANES] + both[:, LANES:]
         copies.append(pltpu.make_async_copy(result.at[part], out_ref.at[part], out_sem.at[n]))
-        copies[-1].start()
+        copies[-1].start(priority=n % 2)
     for out_copy in copies:
         out_copy.wait()
 

time: 56.5 us -> 56.5 us (level)
  no operation moved by 1% of the time
where the time goes in v12:
time: 56.5 us; the launch traced here: 56.2 us
  Pallas kernels  17.5 us (31%)
  starting transfers between devices  13 us (23%)
  waiting for transfers between devices  12.3 us (22%)
  blocking collectives  11.2 us (20%)
  local copies, waits for them, and re-layouts  2.06 us (4%)
    pallas_call x10, Pallas kernels, call(): pl.pallas_call(kernel, out_shape=out_shape, in_specs=specs, out_specs=out...  17.5 us
    all_to_all x1, blocking collectives, local(): lax.all_to_all(shares, ('lat', 'far'), split_axis=0, concat_axis=0, tiled...  11.2 us
    ppermute x6, starting transfers between devices, trade(): results.append(lax.ppermute(block, axis, route))  9.49 us
    all_to_all x1, waiting for transfers between devices, exchange(): lax.all_to_all(blocks, ('lat',) + LON, split_axis=0, concat_axis=0, tiled...  6 us
    ppermute x6, waiting for transfers between devices, trade(): results.append(lax.ppermute(block, axis, route))  5.28 us
    all_to_all x1, starting transfers between devices, exchange(): lax.all_to_all(blocks, ('lat',) + LON, split_axis=0, concat_axis=0, tiled...  3.47 us
    unnamed x7, local copies, waits for them, and re-layouts  2.06 us
  transfers between devices with their start and end apart: 8, of which 4 were waited for; matrix products, arithmetic and copies ran while one was open for 0% of the time, Pallas kernels for 5%

profile of v12, /device:TPU:0, one launch (start us, length us, event | category | flops | bytes accessed | tf_op | source)
XLA Modules:
  0.0 56.2 jit_solution(9205487649925622890)
XLA Ops:
  0.0 1.8 %start.1 = (f32[2,8,128]{2,1,0:T(8,128)}, f32[40,128]{1,0:T(8,128)}, f32[40,128]{1,0:T(8,128)}) custom-call(f32[2,1,1,8]{3,2,1,0:T(1,128)} %observed.1, f32[2,1,1,8]{3,2,1,0:T(1,128)} %precision.1, f32[2,1,1,4,8]{4,3,2,1,0:T(4,128)} %weight.1, s32[2,1,1,4,8]{4,3,2,1,0:T(4,128)} %stencil.1, s32[2,1,1,8]{3,2,1,0:T(1,128)} %owned.1, f32[32,128,128]{2,1,0:T(8,128)} %cells.3), custom_call_target="tpu_custom_call" | custom-call | tf_op jit(solution)/shard_map/start/pallas_call | solution.py:447
  1.8 3.4 %collective-permute-start = (f32[40,128]{1,0:T(8,128)}, f32[40,128]{1,0:T(8,128)S(1)}, u32[]{:S(2)}, u32[]{:S(2)}) collective-permute-start(f32[40,128]{1,0:T(8,128)} %get-tuple-element.17), channel_id=1, source_target_pairs={{0,7},{1,2},{2,1},{3,4},{4,3},{5,6},{6,5},{7,0},{8,15},{9,10},{10,... | collective-permute-start | bytes 61448 | tf_op jit(solution)/shard_map/ppermute | solution.py:31
  5.2 0.0 collective-permute-start.1
  5.2 0.0 copy-start
  5.2 1.6 %copy-done = f32[32,128,128]{2,1,0:T(8,128)S(1)} copy-done((f32[32,128,128]{2,1,0:T(8,128)S(1)}, f32[32,128,128]{2,1,0:T(8,128)}, u32[]{:S(2)}) %copy-start) | copy-done | bytes 2097176
  6.8 0.0 copy-start.1
  6.8 0.2 pad.1
  7.0 0.0 collective-permute-done.sides_0
  7.0 0.0 collective-permute-done.1.sides_1
  7.0 0.5 copy-done.1
  7.5 0.1 edge_rows.1
  7.5 0.0 copy-start.2
  7.5 0.8 %collective-permute-start.2 = (f32[152,128]{1,0:T(8,128)S(1)}, f32[152,128]{1,0:T(8,128)S(1)}, u32[]{:S(2)}, u32[]{:S(2)}) collective-permute-start(f32[152,128]{1,0:T(8,128)S(1)} %get-tuple-element.21), channel_id=1, source_target_pairs={{8,16},{16,8},{9,17},{17,9},{10,18},{18,10},{11,19},{19,11},{12,20... | collective-permute-start | bytes 233480 | tf_op jit(solution)/shard_map/ppermute | solution.py:31
  8.3 4.7 %collective-permute-start.3 = (f32[152,128]{1,0:T(8,128)S(1)}, f32[152,128]{1,0:T(8,128)S(1)}, u32[]{:S(2)}, u32[]{:S(2)}) collective-permute-start(f32[152,128]{1,0:T(8,128)S(1)} %get-tuple-element.22), channel_id=1, source_target_pairs={{0,8},{8,0},{16,24},{24,16},{1,9},{9,1},{17,25},{25,17},{2,10},{10... | collective-permute-start | bytes 233480 | tf_op jit(solution)/shard_map/ppermute | solution.py:31
  13.1 0.7 %row_shares.1.own = f32[8,128]{1,0:T(8,128)S(1)} custom-call(f32[2,8,128]{2,1,0:T(8,128)S(1)} %copy-done.1, f32[40,128]{1,0:T(8,128)S(1)} %get-tuple-element.19.left, f32[40,128]{1,0:T(8,128)S(1)} %get-tuple-element.20.right, f32[36,144,128]{2,1,0:T(8,128)S(1)} %pad.1), custom_call_target="tpu_custom_call" | custom-call | tf_op jit(solution)/shard_map/row_shares/pallas_call | solution.py:447
  13.8 0.0 collective-permute-done.2.ends_0
  13.8 1.8 %collective-permute-done.3.ends_1 = f32[152,128]{1,0:T(8,128)S(1)} collective-permute-done((f32[152,128]{1,0:T(8,128)S(1)}, f32[152,128]{1,0:T(8,128)S(1)}, u32[]{:S(2)}, u32[]{:S(2)}) %collective-permute-start.3) | collective-permute-done | bytes 77856 | tf_op jit(solution)/shard_map/ppermute | solution.py:31
  15.5 1.4 %prior.1 = bf16[32,5,2,128]{3,2,1,0:T(2,128)(2,1)} custom-call(f32[2,8,128]{2,1,0:T(8,128)S(1)} %copy-done.1, f32[8,128]{1,0:T(8,128)S(1)} %row_shares.1.own, f32[152,128]{1,0:T(8,128)S(1)} %collective-permute-done.2.ends_0, f32[152,128]{1,0:T(8,128)S(1)} %collective-permute-done.3.ends_1), custom_call_target="tpu_custom_call" | custom-call | tf_op jit(solution)/shard_map/prior/pallas_call | solution.py:447
  17.0 3.5 %all-to-all-start = ((bf16[32,5,2,128]{3,2,1,0:T(2,128)(2,1)}), bf16[32,5,2,128]{3,2,1,0:T(2,128)(2,1)S(1)}, u32[]{:S(2)}, u32[]{:S(2)}) async-start(bf16[32,5,2,128]{3,2,1,0:T(2,128)(2,1)} %prior.1), calls=%async_computation | async-start | bytes 163840 | tf_op jit(solution)/shard_map/all_to_all | solution.py:458
  20.5 0.0 copy-done.2
  20.5 1.6 %later_shares.1.later = f32[10,8,128]{2,1,0:T(8,128)S(1)} custom-call(f32[2,8,128]{2,1,0:T(8,128)S(1)} %copy-done.1, f32[40,128]{1,0:T(8,128)S(1)} %get-tuple-element.19.left, f32[40,128]{1,0:T(8,128)S(1)} %get-tuple-element.20.right, f32[152,128]{1,0:T(8,128)S(1)} %collective-permute-done.2.ends_0, f32[152,128]{1,0:T(8,128)S(1)} %collective-permute-done.3.ends_1, ...), custom_call_target="tpu_custom_call" | custom-call | tf_op jit(solution)/shard_map/later_shares/pallas_call | solution.py:447
  22.1 6.0 %all-to-all-done.near_ref = bf16[32,5,2,128]{3,2,1,0:T(2,128)(2,1)S(1)} async-done(((bf16[32,5,2,128]{3,2,1,0:T(2,128)(2,1)}), bf16[32,5,2,128]{3,2,1,0:T(2,128)(2,1)S(1)}, u32[]{:S(2)}, u32[]{:S(2)}) %all-to-all-start) | async-done | bytes 81952 | tf_op jit(solution)/shard_map/all_to_all | solution.py:458
  28.1 4.9 %first_batch.1 = (f32[128,128]{1,0:T(8,128)S(1)}, f32[24,128]{1,0:T(8,128)S(1)}, f32[24,128]{1,0:T(8,128)S(1)}, f32[24,128]{1,0:T(8,128)S(1)}) custom-call(bf16[32,5,2,128]{3,2,1,0:T(2,128)(2,1)S(1)} %all-to-all-done.near_ref, s32[2,1,1,5,8]{4,3,2,1,0:T(8,128)S(1)} %copy.8.pattern, f32[10,8,128]{2,1,0:T(8,128)S(1)} %later_shares.1.later), custom_call_target="tpu_custom_call" | custom-call | tf_op jit(solution)/shard_map/first_batch/pallas_call | solution.py:447
  32.9 0.4 collective-permute-start.4
  33.3 0.2 collective-permute-start.5
  33.5 3.5 %collective-permute-done.4.sides_0 = f32[24,128]{1,0:T(8,128)S(1)} collective-permute-done((f32[24,128]{1,0:T(8,128)S(1)}, f32[24,128]{1,0:T(8,128)S(1)}, u32[]{:S(2)}, u32[]{:S(2)}) %collective-permute-start.4) | collective-permute-done | bytes 12320 | tf_op jit(solution)/shard_map/ppermute | solution.py:31
  37.0 0.0 collective-permute-done.5.sides_1
  37.0 11.2 %all_to_all.10.mine = f32[16,24,128]{2,1,0:T(8,128)S(1)} all-to-all(f32[16,24,128]{2,1,0:T(8,128)S(1)} %meet.1), channel_id=1, replica_groups=mesh['lat'=4,'far'=4,'core'=2] {'lat','far'}, dimensions={0} | all-to-all | bytes 393216 | tf_op jit(solution)/shard_map/all_to_all | solution.py:523
  48.2 0.0 collective-permute-start.6
  48.2 0.4 half_product.1.half
  48.6 1.1 %collective-permute-done.6.other = f32[16,24,128]{2,1,0:T(8,128)S(1)} collective-permute-done((f32[16,24,128]{2,1,0:T(8,128)S(1)}, f32[16,24,128]{2,1,0:T(8,128)S(1)}, u32[]{:S(2)}, u32[]{:S(2)}) %collective-permute-start.6) | collective-permute-done | bytes 196640 | tf_op jit(solution)/shard_map/ppermute | solution.py:524
  49.7 6.5 %second_batch.1 = f32[4096,128]{1,0:T(8,128)} custom-call(f32[136,128]{1,0:T(8,128)S(1)} %half_product.1.half, f32[16,24,128]{2,1,0:T(8,128)S(1)} %collective-permute-done.6.other, s32[2,1,1,5,8]{4,3,2,1,0:T(8,128)S(1)} %copy.8.pattern, f32[128,128]{1,0:T(8,128)S(1)} %get-tuple-element.26.map_ref, f32[36,144,128]{2,1,0:T(8,128)S(1)} %pad.1), custom_call_target="tpu_custom_call" | custom-call | tf_op jit(solution)/shard_map/second_batch/pallas_call | solution.py:447
  (2 shorter events, 0.0 us)
Async XLA Ops:
  1.8 5.2 %collective-permute-start = (f32[40,128]{1,0:T(8,128)}, f32[40,128]{1,0:T(8,128)S(1)}, u32[]{:S(2)}, u32[]{:S(2)}) collective-permute-start(f32[40,128]{1,0:T(8,128)} %get-tuple-element.17), channel_id=1, source_target_pairs={{0,7},{1,2},{2,1},{3,4},{4,3},{5,6},{6,5},{7,0},{8,15},{9,10},{10,... | collective-permute-start | bytes 61448 | tf_op jit(solution)/shard_map/ppermute | solution.py:31
  5.2 1.8 %collective-permute-start.1 = (f32[40,128]{1,0:T(8,128)}, f32[40,128]{1,0:T(8,128)S(1)}, u32[]{:S(2)}, u32[]{:S(2)}) collective-permute-start(f32[40,128]{1,0:T(8,128)} %get-tuple-element.18), channel_id=1, source_target_pairs={{0,1},{1,0},{2,3},{3,2},{4,5},{5,4},{6,7},{7,6},{8,9},{9,8},{10,11... | collective-permute-start | bytes 61448 | tf_op jit(solution)/shard_map/ppermute | solution.py:31
  5.2 1.6 %copy-start = (f32[32,128,128]{2,1,0:T(8,128)S(1)}, f32[32,128,128]{2,1,0:T(8,128)}, u32[]{:S(2)}) copy-start(f32[32,128,128]{2,1,0:T(8,128)} %cells.3) | copy-start | bytes 6291460
  6.8 0.7 %copy-start.1 = (f32[2,8,128]{2,1,0:T(8,128)S(1)}, f32[2,8,128]{2,1,0:T(8,128)}, u32[]{:S(2)}) copy-start(f32[2,8,128]{2,1,0:T(8,128)} %get-tuple-element.16.mine) | copy-start | bytes 24580
  7.5 12.9 %copy-start.2 = (s32[2,1,1,5,8]{4,2,3,1,0:T(1,128)S(1)}, s32[2,1,1,5,8]{4,2,3,1,0:T(1,128)}, u32[]{:S(2)}) copy-start(s32[2,1,1,5,8]{4,2,3,1,0:T(1,128)} %param.13) | copy-start | bytes 964
  7.5 6.2 %collective-permute-start.2 = (f32[152,128]{1,0:T(8,128)S(1)}, f32[152,128]{1,0:T(8,128)S(1)}, u32[]{:S(2)}, u32[]{:S(2)}) collective-permute-start(f32[152,128]{1,0:T(8,128)S(1)} %get-tuple-element.21), channel_id=1, source_target_pairs={{8,16},{16,8},{9,17},{17,9},{10,18},{18,10},{11,19},{19,11},{12,20... | collective-permute-start | bytes 233480 | tf_op jit(solution)/shard_map/ppermute | solution.py:31
  8.3 7.2 %collective-permute-start.3 = (f32[152,128]{1,0:T(8,128)S(1)}, f32[152,128]{1,0:T(8,128)S(1)}, u32[]{:S(2)}, u32[]{:S(2)}) collective-permute-start(f32[152,128]{1,0:T(8,128)S(1)} %get-tuple-element.22), channel_id=1, source_target_pairs={{0,8},{8,0},{16,24},{24,16},{1,9},{9,1},{17,25},{25,17},{2,10},{10... | collective-permute-start | bytes 233480 | tf_op jit(solution)/shard_map/ppermute | solution.py:31
  17.0 11.1 %all-to-all-start = ((bf16[32,5,2,128]{3,2,1,0:T(2,128)(2,1)}), bf16[32,5,2,128]{3,2,1,0:T(2,128)(2,1)S(1)}, u32[]{:S(2)}, u32[]{:S(2)}) async-start(bf16[32,5,2,128]{3,2,1,0:T(2,128)(2,1)} %prior.1), calls=%async_computation | async-start | bytes 163840 | tf_op jit(solution)/shard_map/all_to_all | solution.py:458
  32.9 4.1 %collective-permute-start.4 = (f32[24,128]{1,0:T(8,128)S(1)}, f32[24,128]{1,0:T(8,128)S(1)}, u32[]{:S(2)}, u32[]{:S(2)}) collective-permute-start(f32[24,128]{1,0:T(8,128)S(1)} %get-tuple-element.24), channel_id=1, source_target_pairs={{0,7},{1,2},{2,1},{3,4},{4,3},{5,6},{6,5},{7,0},{8,15},{9,10},{10,... | collective-permute-start | bytes 36872 | tf_op jit(solution)/shard_map/ppermute | solution.py:31
  33.3 3.7 %collective-permute-start.5 = (f32[24,128]{1,0:T(8,128)S(1)}, f32[24,128]{1,0:T(8,128)S(1)}, u32[]{:S(2)}, u32[]{:S(2)}) collective-permute-start(f32[24,128]{1,0:T(8,128)S(1)} %get-tuple-element.25), channel_id=1, source_target_pairs={{0,1},{1,0},{2,3},{3,2},{4,5},{5,4},{6,7},{7,6},{8,9},{9,8},{10,11... | collective-permute-start | bytes 36872 | tf_op jit(solution)/shard_map/ppermute | solution.py:31
  48.2 1.4 %collective-permute-start.6 = (f32[16,24,128]{2,1,0:T(8,128)S(1)}, f32[16,24,128]{2,1,0:T(8,128)S(1)}, u32[]{:S(2)}, u32[]{:S(2)}) collective-permute-start(f32[16,24,128]{2,1,0:T(8,128)S(1)} %all_to_all.10.mine), channel_id=1, source_target_pairs={{0,1},{1,0},{2,3},{3,2},{4,5},{5,4},{6,7},{7,6},{8,9},{9,8},{10,11... | collective-permute-start | bytes 589832 | tf_op jit(solution)/shard_map/ppermute | solution.py:524

commit v13 on v11

--- a/solution.py
+++ b/solution.py
@@ -184,8 +184,9 @@
     send_block(value[...], out_ref)
 
 
-def meet_kernel(mid, sides_0, sides_1, out_ref):
-    out_ref[...] = jnp.broadcast_to(mid[...] + sides_0[...] + sides_1[...], out_ref.shape)
+def meet_kernel(mid, sides_0, sides_1, done, out_ref):
+    total = mid[...] + sides_0[...] + sides_1[...] + done[pl.ds(0, 1), :]
+    out_ref[...] = jnp.broadcast_to(total, out_ref.shape)
 
 
 def later_kernel(mine, left, right, ends_0, ends_1, pad, out_ref, params, sems):
@@ -395,27 +396,39 @@
     out_ref[...] = marked_product(1, lat_count, summed_blocks(lat_count, mine), pattern, lax.axis_index("core"))
 
 
-def last_kernel(lat_count, half, other, pattern, map_ref, pad, out_ref, result, held_rows, out_sem):
-    parts = out_sem.shape[0]
-    rows, cols = (pad.shape[0] - 4, pad.shape[1] - 2 * SUB)
-    product = marked_product(1, lat_count, summed_blocks(lat_count, other), pattern, 1 - lax.axis_index("core"))
-    flipped = exact_dot(solved_map(product + half[...], held_rows), map_ref[...], 0)
+def halves(value):
+    upper = value.astype(BF16)
+    return jnp.concatenate([upper, (value - upper.astype(F32)).astype(BF16)], axis=1)
+
+
+def mapped(both, flipped):
     high = flipped.astype(BF16)
     low = (flipped - high.astype(F32)).astype(BF16)
     right = jnp.concatenate(
         [jnp.concatenate([high, high], axis=1), jnp.concatenate([low, jnp.zeros_like(low)], axis=1)], axis=0
     )
+    product = lax.dot_general(both, right, (((1,), (1,)), ((), ())), preferred_element_type=F32)
+    return product[:, :LANES] + product[:, LANES:]
+
+
+def apply_kernel(map_ref, pad, out_ref, done_ref):
+    rows, cols = (pad.shape[0] - 4, pad.shape[1] - 2 * SUB)
+    size = 4
+    for n in range(0, rows, size):
+        value = pad[pl.ds(2 + n, size), pl.ds(SUB, cols), :].reshape(size * cols, LANES)
+        out_ref[pl.ds(n * cols, size * cols), :] = halves(mapped(halves(value), map_ref[...]))
+    done_ref[...] = jnp.zeros_like(done_ref)
+
+
+def last_kernel(lat_count, half, other, pattern, cells, out_ref, result, held_rows, out_sem):
+    parts = out_sem.shape[0]
+    size = result.shape[0] // parts
+    product = marked_product(1, lat_count, summed_blocks(lat_count, other), pattern, 1 - lax.axis_index("core"))
+    flipped = solved_map(product + half[...], held_rows)
     copies = []
-    size = rows // parts
     for n in range(parts):
-        part = pl.ds(n * size * cols, size * cols)
-        value = pad[pl.ds(2 + n * size, size), pl.ds(SUB, cols), :].reshape(size * cols, LANES)
-        upper = value.astype(BF16)
-        rest = (value - upper.astype(F32)).astype(BF16)
-        both = lax.dot_general(
-            jnp.concatenate([upper, rest], axis=1), right, (((1,), (1,)), ((), ())), preferred_element_type=F32
-        )
-        result[part, :] = both[:, :LANES] + both[:, LANES:]
+        part = pl.ds(n * size, size)
+        result[part, :] = mapped(cells[part, :], flipped)
         copies.append(pltpu.make_async_copy(result.at[part], out_ref.at[part], out_sem.at[n]))
         copies[-1].start()
     for out_copy in copies:
@@ -519,7 +532,16 @@
         later,
     )
     sides = trade(sides, LON, True)
-    shares = call(meet_kernel, "meet", [vmem] * 3, shape(tiles // 2, *column.shape), [], mid, *sides)
+    cells, done = call(
+        apply_kernel,
+        "apply_first",
+        [vmem] * 2,
+        (shape(rows * cols, 2 * members, dtype=BF16), shape(SUB, members)),
+        [],
+        first_map,
+        pad,
+    )
+    shares = call(meet_kernel, "meet", [vmem] * 4, shape(tiles // 2, *column.shape), [], mid, *sides, done)
     shares = lax.all_to_all(shares, ("lat", "far"), split_axis=0, concat_axis=0, tiled=True)
     other = lax.ppermute(shares, "core", [(0, 1), (1, 0)])
     half = call(
@@ -535,7 +557,7 @@
     result = call(
         functools.partial(last_kernel, lat_count),
         "second_batch",
-        [vmem] * 5,
+        [vmem] * 4,
         shape(rows * cols, members),
         [
             pltpu.VMEM((rows * cols, members), F32),
@@ -545,8 +567,7 @@
         half,
         other,
         pattern,
-        first_map,
-        pad,
+        cells,
         out_specs=anywhere,
     )
     return result.reshape(rows, cols, members)

time: 56.5 us -> 56.3 us (level)
  waiting for transfers between devices: 12.3 us -> 11.6 us
  Pallas kernels: 17.5 us -> 18.1 us
    ppermute x6, waiting for transfers between devices: 5.28 us -> 4.52 us  [trade(): results.append(lax.ppermute(block, axis, route))]
    pallas_call x10 -> x11, Pallas kernels: 17.5 us -> 18.1 us  [call(): pl.pallas_call(kernel, out_shape=out_shape, in_specs=specs, out_specs=out...]
  transfers between devices with their start and end apart: 8 -> 8, of which waited for: 4 -> 4; matrix products, arithmetic and copies ran while one was open for 0% -> 0% of each run, Pallas kernels for 5% -> 6%
where the time goes in v13:
time: 56.3 us; the launch traced here: 56 us
  Pallas kernels  18.1 us (32%)
  starting transfers between devices  13 us (23%)
  waiting for transfers between devices  11.6 us (21%)
  blocking collectives  11.2 us (20%)
  local copies, waits for them, and re-layouts  2.06 us (4%)
    pallas_call x11, Pallas kernels, call(): pl.pallas_call(kernel, out_shape=out_shape, in_specs=specs, out_specs=out...  18.1 us
    all_to_all x1, blocking collectives, local(): lax.all_to_all(shares, ('lat', 'far'), split_axis=0, concat_axis=0, tiled...  11.2 us
    ppermute x6, starting transfers between devices, trade(): results.append(lax.ppermute(block, axis, route))  9.49 us
    all_to_all x1, waiting for transfers between devices, exchange(): lax.all_to_all(blocks, ('lat',) + LON, split_axis=0, concat_axis=0, tiled...  6 us
    ppermute x6, waiting for transfers between devices, trade(): results.append(lax.ppermute(block, axis, route))  4.52 us
    all_to_all x1, starting transfers between devices, exchange(): lax.all_to_all(blocks, ('lat',) + LON, split_axis=0, concat_axis=0, tiled...  3.47 us
    unnamed x7, local copies, waits for them, and re-layouts  2.06 us
  transfers between devices with their start and end apart: 8, of which 4 were waited for; matrix products, arithmetic and copies ran while one was open for 0% of the time, Pallas kernels for 6%

profile of v13, /device:TPU:0, one launch (start us, length us, event | category | flops | bytes accessed | tf_op | source)
XLA Modules:
  0.0 56.0 jit_solution(5911548128864112971)
XLA Ops:
  0.0 1.8 %start.1 = (f32[2,8,128]{2,1,0:T(8,128)}, f32[40,128]{1,0:T(8,128)}, f32[40,128]{1,0:T(8,128)}) custom-call(f32[2,1,1,8]{3,2,1,0:T(1,128)} %observed.1, f32[2,1,1,8]{3,2,1,0:T(1,128)} %precision.1, f32[2,1,1,4,8]{4,3,2,1,0:T(4,128)} %weight.1, s32[2,1,1,4,8]{4,3,2,1,0:T(4,128)} %stencil.1, s32[2,1,1,8]{3,2,1,0:T(1,128)} %owned.1, f32[32,128,128]{2,1,0:T(8,128)} %cells.3), custom_call_target="tpu_custom_call" | custom-call | tf_op jit(solution)/shard_map/start/pallas_call | solution.py:460
  1.8 3.4 %collective-permute-start = (f32[40,128]{1,0:T(8,128)}, f32[40,128]{1,0:T(8,128)S(1)}, u32[]{:S(2)}, u32[]{:S(2)}) collective-permute-start(f32[40,128]{1,0:T(8,128)} %get-tuple-element.19), channel_id=1, source_target_pairs={{0,7},{1,2},{2,1},{3,4},{4,3},{5,6},{6,5},{7,0},{8,15},{9,10},{10,... | collective-permute-start | bytes 61448 | tf_op jit(solution)/shard_map/ppermute | solution.py:31
  5.2 0.0 collective-permute-start.1
  5.2 0.0 copy-start
  5.2 1.6 %copy-done = f32[32,128,128]{2,1,0:T(8,128)S(1)} copy-done((f32[32,128,128]{2,1,0:T(8,128)S(1)}, f32[32,128,128]{2,1,0:T(8,128)}, u32[]{:S(2)}) %copy-start) | copy-done | bytes 2097176
  6.8 0.0 copy-start.1
  6.8 0.2 pad.1
  7.0 0.0 collective-permute-done.sides_0
  7.0 0.0 collective-permute-done.1.sides_1
  7.0 0.5 copy-done.1
  7.5 0.1 edge_rows.1
  7.5 0.0 copy-start.2
  7.5 0.8 %collective-permute-start.2 = (f32[152,128]{1,0:T(8,128)S(1)}, f32[152,128]{1,0:T(8,128)S(1)}, u32[]{:S(2)}, u32[]{:S(2)}) collective-permute-start(f32[152,128]{1,0:T(8,128)S(1)} %get-tuple-element.23), channel_id=1, source_target_pairs={{8,16},{16,8},{9,17},{17,9},{10,18},{18,10},{11,19},{19,11},{12,20... | collective-permute-start | bytes 233480 | tf_op jit(solution)/shard_map/ppermute | solution.py:31
  8.3 4.7 %collective-permute-start.3 = (f32[152,128]{1,0:T(8,128)S(1)}, f32[152,128]{1,0:T(8,128)S(1)}, u32[]{:S(2)}, u32[]{:S(2)}) collective-permute-start(f32[152,128]{1,0:T(8,128)S(1)} %get-tuple-element.24), channel_id=1, source_target_pairs={{0,8},{8,0},{16,24},{24,16},{1,9},{9,1},{17,25},{25,17},{2,10},{10... | collective-permute-start | bytes 233480 | tf_op jit(solution)/shard_map/ppermute | solution.py:31
  13.0 0.7 %row_shares.1.own = f32[8,128]{1,0:T(8,128)S(1)} custom-call(f32[2,8,128]{2,1,0:T(8,128)S(1)} %copy-done.1, f32[40,128]{1,0:T(8,128)S(1)} %get-tuple-element.21.left, f32[40,128]{1,0:T(8,128)S(1)} %get-tuple-element.22.right, f32[36,144,128]{2,1,0:T(8,128)S(1)} %pad.1), custom_call_target="tpu_custom_call" | custom-call | tf_op jit(solution)/shard_map/row_shares/pallas_call | solution.py:460
  13.8 0.0 collective-permute-done.2.ends_0
  13.8 1.8 %collective-permute-done.3.ends_1 = f32[152,128]{1,0:T(8,128)S(1)} collective-permute-done((f32[152,128]{1,0:T(8,128)S(1)}, f32[152,128]{1,0:T(8,128)S(1)}, u32[]{:S(2)}, u32[]{:S(2)}) %collective-permute-start.3) | collective-permute-done | bytes 77856 | tf_op jit(solution)/shard_map/ppermute | solution.py:31
  15.5 1.4 %prior.1 = bf16[32,5,2,128]{3,2,1,0:T(2,128)(2,1)} custom-call(f32[2,8,128]{2,1,0:T(8,128)S(1)} %copy-done.1, f32[8,128]{1,0:T(8,128)S(1)} %row_shares.1.own, f32[152,128]{1,0:T(8,128)S(1)} %collective-permute-done.2.ends_0, f32[152,128]{1,0:T(8,128)S(1)} %collective-permute-done.3.ends_1), custom_call_target="tpu_custom_call" | custom-call | tf_op jit(solution)/shard_map/prior/pallas_call | solution.py:460
  17.0 3.5 %all-to-all-start = ((bf16[32,5,2,128]{3,2,1,0:T(2,128)(2,1)}), bf16[32,5,2,128]{3,2,1,0:T(2,128)(2,1)S(1)}, u32[]{:S(2)}, u32[]{:S(2)}) async-start(bf16[32,5,2,128]{3,2,1,0:T(2,128)(2,1)} %prior.1), calls=%async_computation | async-start | bytes 163840 | tf_op jit(solution)/shard_map/all_to_all | solution.py:471
  20.4 0.0 copy-done.2
  20.5 1.6 %later_shares.1.later = f32[10,8,128]{2,1,0:T(8,128)S(1)} custom-call(f32[2,8,128]{2,1,0:T(8,128)S(1)} %copy-done.1, f32[40,128]{1,0:T(8,128)S(1)} %get-tuple-element.21.left, f32[40,128]{1,0:T(8,128)S(1)} %get-tuple-element.22.right, f32[152,128]{1,0:T(8,128)S(1)} %collective-permute-done.2.ends_0, f32[152,128]{1,0:T(8,128)S(1)} %collective-permute-done.3.ends_1, ...), custom_call_target="tpu_custom_call" | custom-call | tf_op jit(solution)/shard_map/later_shares/pallas_call | solution.py:460
  22.1 6.0 %all-to-all-done.near_ref = bf16[32,5,2,128]{3,2,1,0:T(2,128)(2,1)S(1)} async-done(((bf16[32,5,2,128]{3,2,1,0:T(2,128)(2,1)}), bf16[32,5,2,128]{3,2,1,0:T(2,128)(2,1)S(1)}, u32[]{:S(2)}, u32[]{:S(2)}) %all-to-all-start) | async-done | bytes 81952 | tf_op jit(solution)/shard_map/all_to_all | solution.py:471
  28.1 4.9 %first_batch.1 = (f32[128,128]{1,0:T(8,128)S(1)}, f32[24,128]{1,0:T(8,128)S(1)}, f32[24,128]{1,0:T(8,128)S(1)}, f32[24,128]{1,0:T(8,128)S(1)}) custom-call(bf16[32,5,2,128]{3,2,1,0:T(2,128)(2,1)S(1)} %all-to-all-done.near_ref, s32[2,1,1,5,8]{4,3,2,1,0:T(8,128)S(1)} %copy.8.pattern, f32[10,8,128]{2,1,0:T(8,128)S(1)} %later_shares.1.later), custom_call_target="tpu_custom_call" | custom-call | tf_op jit(solution)/shard_map/first_batch/pallas_call | solution.py:460
  32.9 0.4 collective-permute-start.4
  33.3 0.2 collective-permute-start.5
  33.5 0.8 %apply_first.1 = (bf16[4096,256]{1,0:T(8,128)(2,1)S(1)}, f32[8,128]{1,0:T(8,128)S(1)}) custom-call(f32[128,128]{1,0:T(8,128)S(1)} %get-tuple-element.28.map_ref, f32[36,144,128]{2,1,0:T(8,128)S(1)} %pad.1), custom_call_target="tpu_custom_call" | custom-call | tf_op jit(solution)/shard_map/apply_first/pallas_call | solution.py:460
  34.3 2.7 %collective-permute-done.4.sides_0 = f32[24,128]{1,0:T(8,128)S(1)} collective-permute-done((f32[24,128]{1,0:T(8,128)S(1)}, f32[24,128]{1,0:T(8,128)S(1)}, u32[]{:S(2)}, u32[]{:S(2)}) %collective-permute-start.4) | collective-permute-done | bytes 12320 | tf_op jit(solution)/shard_map/ppermute | solution.py:31
  37.0 0.0 collective-permute-done.5.sides_1
  37.0 11.2 %all_to_all.10.mine = f32[16,24,128]{2,1,0:T(8,128)S(1)} all-to-all(f32[16,24,128]{2,1,0:T(8,128)S(1)} %meet.1), channel_id=1, replica_groups=mesh['lat'=4,'far'=4,'core'=2] {'lat','far'}, dimensions={0} | all-to-all | bytes 393216 | tf_op jit(solution)/shard_map/all_to_all | solution.py:545
  48.2 0.0 collective-permute-start.6
  48.2 0.4 half_product.1.half
  48.6 1.1 %collective-permute-done.6.other = f32[16,24,128]{2,1,0:T(8,128)S(1)} collective-permute-done((f32[16,24,128]{2,1,0:T(8,128)S(1)}, f32[16,24,128]{2,1,0:T(8,128)S(1)}, u32[]{:S(2)}, u32[]{:S(2)}) %collective-permute-start.6) | collective-permute-done | bytes 196640 | tf_op jit(solution)/shard_map/ppermute | solution.py:546
  49.7 6.3 %second_batch.1 = f32[4096,128]{1,0:T(8,128)} custom-call(f32[136,128]{1,0:T(8,128)S(1)} %half_product.1.half, f32[16,24,128]{2,1,0:T(8,128)S(1)} %collective-permute-done.6.other, s32[2,1,1,5,8]{4,3,2,1,0:T(8,128)S(1)} %copy.8.pattern, bf16[4096,256]{1,0:T(8,128)(2,1)S(1)} %get-tuple-element.30.cells), custom_call_target="tpu_custom_call" | custom-call | tf_op jit(solution)/shard_map/second_batch/pallas_call | solution.py:460
  (2 shorter events, 0.0 us)
Async XLA Ops:
  1.8 5.2 %collective-permute-start = (f32[40,128]{1,0:T(8,128)}, f32[40,128]{1,0:T(8,128)S(1)}, u32[]{:S(2)}, u32[]{:S(2)}) collective-permute-start(f32[40,128]{1,0:T(8,128)} %get-tuple-element.19), channel_id=1, source_target_pairs={{0,7},{1,2},{2,1},{3,4},{4,3},{5,6},{6,5},{7,0},{8,15},{9,10},{10,... | collective-permute-start | bytes 61448 | tf_op jit(solution)/shard_map/ppermute | solution.py:31
  5.2 1.8 %collective-permute-start.1 = (f32[40,128]{1,0:T(8,128)}, f32[40,128]{1,0:T(8,128)S(1)}, u32[]{:S(2)}, u32[]{:S(2)}) collective-permute-start(f32[40,128]{1,0:T(8,128)} %get-tuple-element.20), channel_id=1, source_target_pairs={{0,1},{1,0},{2,3},{3,2},{4,5},{5,4},{6,7},{7,6},{8,9},{9,8},{10,11... | collective-permute-start | bytes 61448 | tf_op jit(solution)/shard_map/ppermute | solution.py:31
  5.2 1.6 %copy-start = (f32[32,128,128]{2,1,0:T(8,128)S(1)}, f32[32,128,128]{2,1,0:T(8,128)}, u32[]{:S(2)}) copy-start(f32[32,128,128]{2,1,0:T(8,128)} %cells.3) | copy-start | bytes 6291460
  6.8 0.7 %copy-start.1 = (f32[2,8,128]{2,1,0:T(8,128)S(1)}, f32[2,8,128]{2,1,0:T(8,128)}, u32[]{:S(2)}) copy-start(f32[2,8,128]{2,1,0:T(8,128)} %get-tuple-element.18.mine) | copy-start | bytes 24580
  7.5 12.9 %copy-start.2 = (s32[2,1,1,5,8]{4,2,3,1,0:T(1,128)S(1)}, s32[2,1,1,5,8]{4,2,3,1,0:T(1,128)}, u32[]{:S(2)}) copy-start(s32[2,1,1,5,8]{4,2,3,1,0:T(1,128)} %param.13) | copy-start | bytes 964
  7.5 6.2 %collective-permute-start.2 = (f32[152,128]{1,0:T(8,128)S(1)}, f32[152,128]{1,0:T(8,128)S(1)}, u32[]{:S(2)}, u32[]{:S(2)}) collective-permute-start(f32[152,128]{1,0:T(8,128)S(1)} %get-tuple-element.23), channel_id=1, source_target_pairs={{8,16},{16,8},{9,17},{17,9},{10,18},{18,10},{11,19},{19,11},{12,20... | collective-permute-start | bytes 233480 | tf_op jit(solution)/shard_map/ppermute | solution.py:31
  8.3 7.2 %collective-permute-start.3 = (f32[152,128]{1,0:T(8,128)S(1)}, f32[152,128]{1,0:T(8,128)S(1)}, u32[]{:S(2)}, u32[]{:S(2)}) collective-permute-start(f32[152,128]{1,0:T(8,128)S(1)} %get-tuple-element.24), channel_id=1, source_target_pairs={{0,8},{8,0},{16,24},{24,16},{1,9},{9,1},{17,25},{25,17},{2,10},{10... | collective-permute-start | bytes 233480 | tf_op jit(solution)/shard_map/ppermute | solution.py:31
  17.0 11.1 %all-to-all-start = ((bf16[32,5,2,128]{3,2,1,0:T(2,128)(2,1)}), bf16[32,5,2,128]{3,2,1,0:T(2,128)(2,1)S(1)}, u32[]{:S(2)}, u32[]{:S(2)}) async-start(bf16[32,5,2,128]{3,2,1,0:T(2,128)(2,1)} %prior.1), calls=%async_computation | async-start | bytes 163840 | tf_op jit(solution)/shard_map/all_to_all | solution.py:471
  32.9 4.1 %collective-permute-start.4 = (f32[24,128]{1,0:T(8,128)S(1)}, f32[24,128]{1,0:T(8,128)S(1)}, u32[]{:S(2)}, u32[]{:S(2)}) collective-permute-start(f32[24,128]{1,0:T(8,128)S(1)} %get-tuple-element.26), channel_id=1, source_target_pairs={{0,7},{1,2},{2,1},{3,4},{4,3},{5,6},{6,5},{7,0},{8,15},{9,10},{10,... | collective-permute-start | bytes 36872 | tf_op jit(solution)/shard_map/ppermute | solution.py:31
  33.3 3.7 %collective-permute-start.5 = (f32[24,128]{1,0:T(8,128)S(1)}, f32[24,128]{1,0:T(8,128)S(1)}, u32[]{:S(2)}, u32[]{:S(2)}) collective-permute-start(f32[24,128]{1,0:T(8,128)S(1)} %get-tuple-element.27), channel_id=1, source_target_pairs={{0,1},{1,0},{2,3},{3,2},{4,5},{5,4},{6,7},{7,6},{8,9},{9,8},{10,11... | collective-permute-start | bytes 36872 | tf_op jit(solution)/shard_map/ppermute | solution.py:31
  48.2 1.4 %collective-permute-start.6 = (f32[16,24,128]{2,1,0:T(8,128)S(1)}, f32[16,24,128]{2,1,0:T(8,128)S(1)}, u32[]{:S(2)}, u32[]{:S(2)}) collective-permute-start(f32[16,24,128]{2,1,0:T(8,128)S(1)} %all_to_all.10.mine), channel_id=1, source_target_pairs={{0,1},{1,0},{2,3},{3,2},{4,5},{5,4},{6,7},{7,6},{8,9},{9,8},{10,11... | collective-permute-start | bytes 589832 | tf_op jit(solution)/shard_map/ppermute | solution.py:546

commit v14 on v13

--- a/solution.py
+++ b/solution.py
@@ -47,8 +47,8 @@
         (weight, weight_v),
         (stencil, stencil_v),
         (owned, owned_v),
-        (cells.at[:, pl.ds(0, SUB)], left_v),
-        (cells.at[:, pl.ds(cols - SUB, SUB)], right_v),
+        (cells.at[:, pl.ds(0, 1)], left_v),
+        (cells.at[:, pl.ds(cols - 1, 1)], right_v),
     )
     copies = [pltpu.make_async_copy(source, target, sems.at[n]) for n, (source, target) in enumerate(pairs)]
     for copy in copies:
@@ -66,7 +66,7 @@
         params_ref[b, pl.ds(AT_OBS, 1), pl.ds(0, SUB)] = observed_v[b, 0] * root
     rows = cells.shape[0]
     forward = next_first("core")
-    left, right = (left_v[:, 0, :], right_v[:, SUB - 1, :])
+    left, right = (left_v[:, 0, :], right_v[:, 0, :])
     sides_0[pl.ds(0, rows), :] = jnp.where(forward, right, left)
     sides_1[pl.ds(0, rows), :] = jnp.where(forward, left, right)
     sides_0[pl.ds(rows, SUB), :] = params_ref[1]
@@ -218,7 +218,7 @@
     return jnp.broadcast_to(block[:, j:j + 1], block.shape)
 
 
-def pivot_rows(block, k, held, between):
+def pivot_rows(block, after, k, held, between):
     sub = lax.broadcasted_iota(jnp.int32, block.shape, 0)
     lane = lax.broadcasted_iota(jnp.int32, block.shape, 1) - k * SUB
     held[pl.ds(k * SUB, SUB), :] = block
@@ -227,6 +227,8 @@
     here = (lane >= 0) & (lane < SUB)
     rows = [jnp.where(here, jnp.where(lane == r, 1.0, 0.0), row) for r, row in enumerate(rows)]
     inverse, scale = (jnp.zeros(block.shape, F32), jnp.ones(block.shape, F32))
+    beside = [column_of(after, k * SUB + n) for n in range(SUB)]
+    after = jnp.where(here, 0.0, after)
     for j in range(0, SUB, 2):
         a, b, c = (at[j, j], at[j + 1, j], at[j + 1, j + 1])
         det = a * c - b * b
@@ -247,6 +249,11 @@
                 for n in range(j + 2, r + 1):
                     at[r, n] = at[r, n] - (first * upper[n][0] + second * upper[n][1])
             rows[r] = rows[r] - (first * top + second * bottom)
+        first, second = (beside[j] * c - beside[j + 1] * b, beside[j + 1] * a - beside[j] * b)
+        first, second = (first * over_det, second * over_det)
+        for n in rest:
+            beside[n] = beside[n] - (first * upper[n][0] + second * upper[n][1])
+        after = after - (first * top + second * bottom)
         a_part, b_part, c_part = (a * over_det, b * over_det, c * over_det)
         for r in range(j):
             first = at[r, j] * c_part - at[r, j + 1] * b_part
@@ -262,7 +269,7 @@
         inverse = jnp.where(sub == j, top, jnp.where(sub == j + 1, a * bottom - b * top, inverse))
         scale = jnp.where(sub == j, a, jnp.where(sub == j + 1, a * det, scale))
         between()
-    return rows, jnp.where(lane < SUB, inverse * lax.rsqrt(scale), 0.0)
+    return rows, jnp.where(lane < SUB, inverse * lax.rsqrt(scale), 0.0), after
 
 
 def eliminate(blocks, held):
@@ -279,6 +286,8 @@
         blocks[i] = jnp.where(here, 0.0, blocks[i]) - terms[0]
 
     for k in range(count):
+        if waiting:
+            update(*waiting.pop(0))
         share_of = -(-len(waiting) // 4)
 
         def between():
@@ -286,8 +295,7 @@
                 update(*task)
             del waiting[:share_of]
 
-        pivot, rows = pivot_rows(blocks[k], k, held, between)
-        update(k + 1, k, pivot)
+        pivot, rows, blocks[k + 1] = pivot_rows(blocks[k], blocks[k + 1], k, held, between)
         waiting = [(i, k, pivot) for i in range(k + 2, count + 1)]
         inverse.append(rows)
     return inverse, blocks[count][:1]
@@ -478,7 +486,7 @@
         [hbm] * 6,
         (shape(batches, SUB, LANES), side, side),
         [pltpu.VMEM(array.shape, array.dtype) for array in small]
-        + [pltpu.VMEM((rows, SUB, members), F32)] * 2
+        + [pltpu.VMEM((rows, 1, members), F32)] * 2
         + [pltpu.SemaphoreType.DMA((7,))],
         *small,
         ensemble,

time: 56.3 us -> 55.7 us (0.989)
  Pallas kernels: 18.1 us -> 17.4 us
    pallas_call x11, Pallas kernels: 18.1 us -> 17.4 us  [call(): pl.pallas_call(kernel, out_shape=out_shape, in_specs=specs, out_specs=out...]
  transfers between devices with their start and end apart: 8 -> 8, of which waited for: 4 -> 4; matrix products, arithmetic and copies ran while one was open for 0% -> 0% of each run, Pallas kernels for 6% -> 7%
where the time goes in v14:
time: 55.7 us; the launch traced here: 55.3 us
  Pallas kernels  17.4 us (31%)
  starting transfers between devices  13 us (23%)
  waiting for transfers between devices  11.6 us (21%)
  blocking collectives  11.2 us (20%)
  local copies, waits for them, and re-layouts  2.06 us (4%)
    pallas_call x11, Pallas kernels, call(): pl.pallas_call(kernel, out_shape=out_shape, in_specs=specs, out_specs=out...  17.4 us
    all_to_all x1, blocking collectives, local(): lax.all_to_all(shares, ('lat', 'far'), split_axis=0, concat_axis=0, tiled...  11.2 us
    ppermute x6, starting transfers between devices, trade(): results.append(lax.ppermute(block, axis, route))  9.49 us
    all_to_all x1, waiting for transfers between devices, exchange(): lax.all_to_all(blocks, ('lat',) + LON, split_axis=0, concat_axis=0, tiled...  6 us
    ppermute x6, waiting for transfers between devices, trade(): results.append(lax.ppermute(block, axis, route))  4.52 us
    all_to_all x1, starting transfers between devices, exchange(): lax.all_to_all(blocks, ('lat',) + LON, split_axis=0, concat_axis=0, tiled...  3.47 us
    unnamed x7, local copies, waits for them, and re-layouts  2.06 us
  transfers between devices with their start and end apart: 8, of which 4 were waited for; matrix products, arithmetic and copies ran while one was open for 0% of the time, Pallas kernels for 7%

profile of v14, /device:TPU:0, one launch (start us, length us, event | category | flops | bytes accessed | tf_op | source)
XLA Modules:
  0.0 55.3 jit_solution(2950516685258624825)
XLA Ops:
  0.0 1.5 %start.1 = (f32[2,8,128]{2,1,0:T(8,128)}, f32[40,128]{1,0:T(8,128)}, f32[40,128]{1,0:T(8,128)}) custom-call(f32[2,1,1,8]{3,2,1,0:T(1,128)} %observed.1, f32[2,1,1,8]{3,2,1,0:T(1,128)} %precision.1, f32[2,1,1,4,8]{4,3,2,1,0:T(4,128)} %weight.1, s32[2,1,1,4,8]{4,3,2,1,0:T(4,128)} %stencil.1, s32[2,1,1,8]{3,2,1,0:T(1,128)} %owned.1, f32[32,128,128]{2,1,0:T(8,128)} %cells.3), custom_call_target="tpu_custom_call" | custom-call | tf_op jit(solution)/shard_map/start/pallas_call | solution.py:468
  1.5 3.4 %collective-permute-start = (f32[40,128]{1,0:T(8,128)}, f32[40,128]{1,0:T(8,128)S(1)}, u32[]{:S(2)}, u32[]{:S(2)}) collective-permute-start(f32[40,128]{1,0:T(8,128)} %get-tuple-element.19), channel_id=1, source_target_pairs={{0,7},{1,2},{2,1},{3,4},{4,3},{5,6},{6,5},{7,0},{8,15},{9,10},{10,... | collective-permute-start | bytes 61448 | tf_op jit(solution)/shard_map/ppermute | solution.py:31
  4.9 0.0 collective-permute-start.1
  4.9 0.0 copy-start
  4.9 1.6 %copy-done = f32[32,128,128]{2,1,0:T(8,128)S(1)} copy-done((f32[32,128,128]{2,1,0:T(8,128)S(1)}, f32[32,128,128]{2,1,0:T(8,128)}, u32[]{:S(2)}) %copy-start) | copy-done | bytes 2097176
  6.5 0.0 copy-start.1
  6.5 0.2 pad.1
  6.7 0.0 collective-permute-done.sides_0
  6.7 0.0 collective-permute-done.1.sides_1
  6.8 0.5 copy-done.1
  7.2 0.1 edge_rows.1
  7.3 0.0 copy-start.2
  7.3 0.8 %collective-permute-start.2 = (f32[152,128]{1,0:T(8,128)S(1)}, f32[152,128]{1,0:T(8,128)S(1)}, u32[]{:S(2)}, u32[]{:S(2)}) collective-permute-start(f32[152,128]{1,0:T(8,128)S(1)} %get-tuple-element.23), channel_id=1, source_target_pairs={{8,16},{16,8},{9,17},{17,9},{10,18},{18,10},{11,19},{19,11},{12,20... | collective-permute-start | bytes 233480 | tf_op jit(solution)/shard_map/ppermute | solution.py:31
  8.1 4.7 %collective-permute-start.3 = (f32[152,128]{1,0:T(8,128)S(1)}, f32[152,128]{1,0:T(8,128)S(1)}, u32[]{:S(2)}, u32[]{:S(2)}) collective-permute-start(f32[152,128]{1,0:T(8,128)S(1)} %get-tuple-element.24), channel_id=1, source_target_pairs={{0,8},{8,0},{16,24},{24,16},{1,9},{9,1},{17,25},{25,17},{2,10},{10... | collective-permute-start | bytes 233480 | tf_op jit(solution)/shard_map/ppermute | solution.py:31
  12.8 0.7 %row_shares.1.own = f32[8,128]{1,0:T(8,128)S(1)} custom-call(f32[2,8,128]{2,1,0:T(8,128)S(1)} %copy-done.1, f32[40,128]{1,0:T(8,128)S(1)} %get-tuple-element.21.left, f32[40,128]{1,0:T(8,128)S(1)} %get-tuple-element.22.right, f32[36,144,128]{2,1,0:T(8,128)S(1)} %pad.1), custom_call_target="tpu_custom_call" | custom-call | tf_op jit(solution)/shard_map/row_shares/pallas_call | solution.py:468
  13.5 0.0 collective-permute-done.2.ends_0
  13.5 1.8 %collective-permute-done.3.ends_1 = f32[152,128]{1,0:T(8,128)S(1)} collective-permute-done((f32[152,128]{1,0:T(8,128)S(1)}, f32[152,128]{1,0:T(8,128)S(1)}, u32[]{:S(2)}, u32[]{:S(2)}) %collective-permute-start.3) | collective-permute-done | bytes 77856 | tf_op jit(solution)/shard_map/ppermute | solution.py:31
  15.3 1.4 %prior.1 = bf16[32,5,2,128]{3,2,1,0:T(2,128)(2,1)} custom-call(f32[2,8,128]{2,1,0:T(8,128)S(1)} %copy-done.1, f32[8,128]{1,0:T(8,128)S(1)} %row_shares.1.own, f32[152,128]{1,0:T(8,128)S(1)} %collective-permute-done.2.ends_0, f32[152,128]{1,0:T(8,128)S(1)} %collective-permute-done.3.ends_1), custom_call_target="tpu_custom_call" | custom-call | tf_op jit(solution)/shard_map/prior/pallas_call | solution.py:468
  16.7 3.5 %all-to-all-start = ((bf16[32,5,2,128]{3,2,1,0:T(2,128)(2,1)}), bf16[32,5,2,128]{3,2,1,0:T(2,128)(2,1)S(1)}, u32[]{:S(2)}, u32[]{:S(2)}) async-start(bf16[32,5,2,128]{3,2,1,0:T(2,128)(2,1)} %prior.1), calls=%async_computation | async-start | bytes 163840 | tf_op jit(solution)/shard_map/all_to_all | solution.py:479
  20.2 0.0 copy-done.2
  20.2 1.6 %later_shares.1.later = f32[10,8,128]{2,1,0:T(8,128)S(1)} custom-call(f32[2,8,128]{2,1,0:T(8,128)S(1)} %copy-done.1, f32[40,128]{1,0:T(8,128)S(1)} %get-tuple-element.21.left, f32[40,128]{1,0:T(8,128)S(1)} %get-tuple-element.22.right, f32[152,128]{1,0:T(8,128)S(1)} %collective-permute-done.2.ends_0, f32[152,128]{1,0:T(8,128)S(1)} %collective-permute-done.3.ends_1, ...), custom_call_target="tpu_custom_call" | custom-call | tf_op jit(solution)/shard_map/later_shares/pallas_call | solution.py:468
  21.8 6.0 %all-to-all-done.near_ref = bf16[32,5,2,128]{3,2,1,0:T(2,128)(2,1)S(1)} async-done(((bf16[32,5,2,128]{3,2,1,0:T(2,128)(2,1)}), bf16[32,5,2,128]{3,2,1,0:T(2,128)(2,1)S(1)}, u32[]{:S(2)}, u32[]{:S(2)}) %all-to-all-start) | async-done | bytes 81952 | tf_op jit(solution)/shard_map/all_to_all | solution.py:479
  27.8 4.5 %first_batch.1 = (f32[128,128]{1,0:T(8,128)S(1)}, f32[24,128]{1,0:T(8,128)S(1)}, f32[24,128]{1,0:T(8,128)S(1)}, f32[24,128]{1,0:T(8,128)S(1)}) custom-call(bf16[32,5,2,128]{3,2,1,0:T(2,128)(2,1)S(1)} %all-to-all-done.near_ref, s32[2,1,1,5,8]{4,3,2,1,0:T(8,128)S(1)} %copy.8.pattern, f32[10,8,128]{2,1,0:T(8,128)S(1)} %later_shares.1.later), custom_call_target="tpu_custom_call" | custom-call | tf_op jit(solution)/shard_map/first_batch/pallas_call | solution.py:468
  32.4 0.4 collective-permute-start.4
  32.7 0.2 collective-permute-start.5
  32.9 0.8 %apply_first.1 = (bf16[4096,256]{1,0:T(8,128)(2,1)S(1)}, f32[8,128]{1,0:T(8,128)S(1)}) custom-call(f32[128,128]{1,0:T(8,128)S(1)} %get-tuple-element.28.map_ref, f32[36,144,128]{2,1,0:T(8,128)S(1)} %pad.1), custom_call_target="tpu_custom_call" | custom-call | tf_op jit(solution)/shard_map/apply_first/pallas_call | solution.py:468
  33.7 2.7 %collective-permute-done.4.sides_0 = f32[24,128]{1,0:T(8,128)S(1)} collective-permute-done((f32[24,128]{1,0:T(8,128)S(1)}, f32[24,128]{1,0:T(8,128)S(1)}, u32[]{:S(2)}, u32[]{:S(2)}) %collective-permute-start.4) | collective-permute-done | bytes 12320 | tf_op jit(solution)/shard_map/ppermute | solution.py:31
  36.4 0.0 collective-permute-done.5.sides_1
  36.5 11.2 %all_to_all.10.mine = f32[16,24,128]{2,1,0:T(8,128)S(1)} all-to-all(f32[16,24,128]{2,1,0:T(8,128)S(1)} %meet.1), channel_id=1, replica_groups=mesh['lat'=4,'far'=4,'core'=2] {'lat','far'}, dimensions={0} | all-to-all | bytes 393216 | tf_op jit(solution)/shard_map/all_to_all | solution.py:553
  47.7 0.0 collective-permute-start.6
  47.7 0.4 half_product.1.half
  48.1 1.1 %collective-permute-done.6.other = f32[16,24,128]{2,1,0:T(8,128)S(1)} collective-permute-done((f32[16,24,128]{2,1,0:T(8,128)S(1)}, f32[16,24,128]{2,1,0:T(8,128)S(1)}, u32[]{:S(2)}, u32[]{:S(2)}) %collective-permute-start.6) | collective-permute-done | bytes 196640 | tf_op jit(solution)/shard_map/ppermute | solution.py:554
  49.1 6.2 %second_batch.1 = f32[4096,128]{1,0:T(8,128)} custom-call(f32[136,128]{1,0:T(8,128)S(1)} %half_product.1.half, f32[16,24,128]{2,1,0:T(8,128)S(1)} %collective-permute-done.6.other, s32[2,1,1,5,8]{4,3,2,1,0:T(8,128)S(1)} %copy.8.pattern, bf16[4096,256]{1,0:T(8,128)(2,1)S(1)} %get-tuple-element.30.cells), custom_call_target="tpu_custom_call" | custom-call | tf_op jit(solution)/shard_map/second_batch/pallas_call | solution.py:468
  (2 shorter events, 0.0 us)
Async XLA Ops:
  1.5 5.2 %collective-permute-start = (f32[40,128]{1,0:T(8,128)}, f32[40,128]{1,0:T(8,128)S(1)}, u32[]{:S(2)}, u32[]{:S(2)}) collective-permute-start(f32[40,128]{1,0:T(8,128)} %get-tuple-element.19), channel_id=1, source_target_pairs={{0,7},{1,2},{2,1},{3,4},{4,3},{5,6},{6,5},{7,0},{8,15},{9,10},{10,... | collective-permute-start | bytes 61448 | tf_op jit(solution)/shard_map/ppermute | solution.py:31
  4.9 1.8 %collective-permute-start.1 = (f32[40,128]{1,0:T(8,128)}, f32[40,128]{1,0:T(8,128)S(1)}, u32[]{:S(2)}, u32[]{:S(2)}) collective-permute-start(f32[40,128]{1,0:T(8,128)} %get-tuple-element.20), channel_id=1, source_target_pairs={{0,1},{1,0},{2,3},{3,2},{4,5},{5,4},{6,7},{7,6},{8,9},{9,8},{10,11... | collective-permute-start | bytes 61448 | tf_op jit(solution)/shard_map/ppermute | solution.py:31
  4.9 1.6 %copy-start = (f32[32,128,128]{2,1,0:T(8,128)S(1)}, f32[32,128,128]{2,1,0:T(8,128)}, u32[]{:S(2)}) copy-start(f32[32,128,128]{2,1,0:T(8,128)} %cells.3) | copy-start | bytes 6291460
  6.5 0.7 %copy-start.1 = (f32[2,8,128]{2,1,0:T(8,128)S(1)}, f32[2,8,128]{2,1,0:T(8,128)}, u32[]{:S(2)}) copy-start(f32[2,8,128]{2,1,0:T(8,128)} %get-tuple-element.18.mine) | copy-start | bytes 24580
  7.3 12.9 %copy-start.2 = (s32[2,1,1,5,8]{4,2,3,1,0:T(1,128)S(1)}, s32[2,1,1,5,8]{4,2,3,1,0:T(1,128)}, u32[]{:S(2)}) copy-start(s32[2,1,1,5,8]{4,2,3,1,0:T(1,128)} %param.13) | copy-start | bytes 964
  7.3 6.2 %collective-permute-start.2 = (f32[152,128]{1,0:T(8,128)S(1)}, f32[152,128]{1,0:T(8,128)S(1)}, u32[]{:S(2)}, u32[]{:S(2)}) collective-permute-start(f32[152,128]{1,0:T(8,128)S(1)} %get-tuple-element.23), channel_id=1, source_target_pairs={{8,16},{16,8},{9,17},{17,9},{10,18},{18,10},{11,19},{19,11},{12,20... | collective-permute-start | bytes 233480 | tf_op jit(solution)/shard_map/ppermute | solution.py:31
  8.1 7.2 %collective-permute-start.3 = (f32[152,128]{1,0:T(8,128)S(1)}, f32[152,128]{1,0:T(8,128)S(1)}, u32[]{:S(2)}, u32[]{:S(2)}) collective-permute-start(f32[152,128]{1,0:T(8,128)S(1)} %get-tuple-element.24), channel_id=1, source_target_pairs={{0,8},{8,0},{16,24},{24,16},{1,9},{9,1},{17,25},{25,17},{2,10},{10... | collective-permute-start | bytes 233480 | tf_op jit(solution)/shard_map/ppermute | solution.py:31
  16.7 11.1 %all-to-all-start = ((bf16[32,5,2,128]{3,2,1,0:T(2,128)(2,1)}), bf16[32,5,2,128]{3,2,1,0:T(2,128)(2,1)S(1)}, u32[]{:S(2)}, u32[]{:S(2)}) async-start(bf16[32,5,2,128]{3,2,1,0:T(2,128)(2,1)} %prior.1), calls=%async_computation | async-start | bytes 163840 | tf_op jit(solution)/shard_map/all_to_all | solution.py:479
  32.4 4.1 %collective-permute-start.4 = (f32[24,128]{1,0:T(8,128)S(1)}, f32[24,128]{1,0:T(8,128)S(1)}, u32[]{:S(2)}, u32[]{:S(2)}) collective-permute-start(f32[24,128]{1,0:T(8,128)S(1)} %get-tuple-element.26), channel_id=1, source_target_pairs={{0,7},{1,2},{2,1},{3,4},{4,3},{5,6},{6,5},{7,0},{8,15},{9,10},{10,... | collective-permute-start | bytes 36872 | tf_op jit(solution)/shard_map/ppermute | solution.py:31
  32.7 3.7 %collective-permute-start.5 = (f32[24,128]{1,0:T(8,128)S(1)}, f32[24,128]{1,0:T(8,128)S(1)}, u32[]{:S(2)}, u32[]{:S(2)}) collective-permute-start(f32[24,128]{1,0:T(8,128)S(1)} %get-tuple-element.27), channel_id=1, source_target_pairs={{0,1},{1,0},{2,3},{3,2},{4,5},{5,4},{6,7},{7,6},{8,9},{9,8},{10,11... | collective-permute-start | bytes 36872 | tf_op jit(solution)/shard_map/ppermute | solution.py:31
  47.7 1.4 %collective-permute-start.6 = (f32[16,24,128]{2,1,0:T(8,128)S(1)}, f32[16,24,128]{2,1,0:T(8,128)S(1)}, u32[]{:S(2)}, u32[]{:S(2)}) collective-permute-start(f32[16,24,128]{2,1,0:T(8,128)S(1)} %all_to_all.10.mine), channel_id=1, source_target_pairs={{0,1},{1,0},{2,3},{3,2},{4,5},{5,4},{6,7},{7,6},{8,9},{9,8},{10,11... | collective-permute-start | bytes 589832 | tf_op jit(solution)/shard_map/ppermute | solution.py:554

commit v15 on v14

--- a/solution.py
+++ b/solution.py
@@ -250,10 +250,10 @@
                     at[r, n] = at[r, n] - (first * upper[n][0] + second * upper[n][1])
             rows[r] = rows[r] - (first * top + second * bottom)
         first, second = (beside[j] * c - beside[j + 1] * b, beside[j + 1] * a - beside[j] * b)
+        after = after - ((first * top + second * bottom) * guess) * better
         first, second = (first * over_det, second * over_det)
         for n in rest:
             beside[n] = beside[n] - (first * upper[n][0] + second * upper[n][1])
-        after = after - (first * top + second * bottom)
         a_part, b_part, c_part = (a * over_det, b * over_det, c * over_det)
         for r in range(j):
             first = at[r, j] * c_part - at[r, j + 1] * b_part

time: 55.7 us -> 55.6 us (level)
  no operation moved by 1% of the time
where the time goes in v15:
time: 55.6 us; the launch traced here: 55.2 us
  Pallas kernels  17.3 us (31%)
  starting transfers between devices  13 us (23%)
  waiting for transfers between devices  11.6 us (21%)
  blocking collectives  11.2 us (20%)
  local copies, waits for them, and re-layouts  2.06 us (4%)
    pallas_call x11, Pallas kernels, call(): pl.pallas_call(kernel, out_shape=out_shape, in_specs=specs, out_specs=out...  17.3 us
    all_to_all x1, blocking collectives, local(): lax.all_to_all(shares, ('lat', 'far'), split_axis=0, concat_axis=0, tiled...  11.2 us
    ppermute x6, starting transfers between devices, trade(): results.append(lax.ppermute(block, axis, route))  9.49 us
    all_to_all x1, waiting for transfers between devices, exchange(): lax.all_to_all(blocks, ('lat',) + LON, split_axis=0, concat_axis=0, tiled...  6 us
    ppermute x6, waiting for transfers between devices, trade(): results.append(lax.ppermute(block, axis, route))  4.52 us
    all_to_all x1, starting transfers between devices, exchange(): lax.all_to_all(blocks, ('lat',) + LON, split_axis=0, concat_axis=0, tiled...  3.47 us
    unnamed x7, local copies, waits for them, and re-layouts  2.06 us
  transfers between devices with their start and end apart: 8, of which 4 were waited for; matrix products, arithmetic and copies ran while one was open for 0% of the time, Pallas kernels for 7%

profile of v15, /device:TPU:0, one launch (start us, length us, event | category | flops | bytes accessed | tf_op | source)
XLA Modules:
  0.0 55.2 jit_solution(3200425552636545302)
XLA Ops:
  0.0 1.5 %start.1 = (f32[2,8,128]{2,1,0:T(8,128)}, f32[40,128]{1,0:T(8,128)}, f32[40,128]{1,0:T(8,128)}) custom-call(f32[2,1,1,8]{3,2,1,0:T(1,128)} %observed.1, f32[2,1,1,8]{3,2,1,0:T(1,128)} %precision.1, f32[2,1,1,4,8]{4,3,2,1,0:T(4,128)} %weight.1, s32[2,1,1,4,8]{4,3,2,1,0:T(4,128)} %stencil.1, s32[2,1,1,8]{3,2,1,0:T(1,128)} %owned.1, f32[32,128,128]{2,1,0:T(8,128)} %cells.3), custom_call_target="tpu_custom_call" | custom-call | tf_op jit(solution)/shard_map/start/pallas_call | solution.py:468
  1.5 3.4 %collective-permute-start = (f32[40,128]{1,0:T(8,128)}, f32[40,128]{1,0:T(8,128)S(1)}, u32[]{:S(2)}, u32[]{:S(2)}) collective-permute-start(f32[40,128]{1,0:T(8,128)} %get-tuple-element.19), channel_id=1, source_target_pairs={{0,7},{1,2},{2,1},{3,4},{4,3},{5,6},{6,5},{7,0},{8,15},{9,10},{10,... | collective-permute-start | bytes 61448 | tf_op jit(solution)/shard_map/ppermute | solution.py:31
  4.9 0.0 collective-permute-start.1
  4.9 0.0 copy-start
  4.9 1.6 %copy-done = f32[32,128,128]{2,1,0:T(8,128)S(1)} copy-done((f32[32,128,128]{2,1,0:T(8,128)S(1)}, f32[32,128,128]{2,1,0:T(8,128)}, u32[]{:S(2)}) %copy-start) | copy-done | bytes 2097176
  6.5 0.0 copy-start.1
  6.5 0.2 pad.1
  6.7 0.0 collective-permute-done.sides_0
  6.7 0.0 collective-permute-done.1.sides_1
  6.8 0.5 copy-done.1
  7.2 0.1 edge_rows.1
  7.3 0.0 copy-start.2
  7.3 0.8 %collective-permute-start.2 = (f32[152,128]{1,0:T(8,128)S(1)}, f32[152,128]{1,0:T(8,128)S(1)}, u32[]{:S(2)}, u32[]{:S(2)}) collective-permute-start(f32[152,128]{1,0:T(8,128)S(1)} %get-tuple-element.23), channel_id=1, source_target_pairs={{8,16},{16,8},{9,17},{17,9},{10,18},{18,10},{11,19},{19,11},{12,20... | collective-permute-start | bytes 233480 | tf_op jit(solution)/shard_map/ppermute | solution.py:31
  8.1 4.7 %collective-permute-start.3 = (f32[152,128]{1,0:T(8,128)S(1)}, f32[152,128]{1,0:T(8,128)S(1)}, u32[]{:S(2)}, u32[]{:S(2)}) collective-permute-start(f32[152,128]{1,0:T(8,128)S(1)} %get-tuple-element.24), channel_id=1, source_target_pairs={{0,8},{8,0},{16,24},{24,16},{1,9},{9,1},{17,25},{25,17},{2,10},{10... | collective-permute-start | bytes 233480 | tf_op jit(solution)/shard_map/ppermute | solution.py:31
  12.8 0.7 %row_shares.1.own = f32[8,128]{1,0:T(8,128)S(1)} custom-call(f32[2,8,128]{2,1,0:T(8,128)S(1)} %copy-done.1, f32[40,128]{1,0:T(8,128)S(1)} %get-tuple-element.21.left, f32[40,128]{1,0:T(8,128)S(1)} %get-tuple-element.22.right, f32[36,144,128]{2,1,0:T(8,128)S(1)} %pad.1), custom_call_target="tpu_custom_call" | custom-call | tf_op jit(solution)/shard_map/row_shares/pallas_call | solution.py:468
  13.5 0.0 collective-permute-done.2.ends_0
  13.5 1.8 %collective-permute-done.3.ends_1 = f32[152,128]{1,0:T(8,128)S(1)} collective-permute-done((f32[152,128]{1,0:T(8,128)S(1)}, f32[152,128]{1,0:T(8,128)S(1)}, u32[]{:S(2)}, u32[]{:S(2)}) %collective-permute-start.3) | collective-permute-done | bytes 77856 | tf_op jit(solution)/shard_map/ppermute | solution.py:31
  15.3 1.4 %prior.1 = bf16[32,5,2,128]{3,2,1,0:T(2,128)(2,1)} custom-call(f32[2,8,128]{2,1,0:T(8,128)S(1)} %copy-done.1, f32[8,128]{1,0:T(8,128)S(1)} %row_shares.1.own, f32[152,128]{1,0:T(8,128)S(1)} %collective-permute-done.2.ends_0, f32[152,128]{1,0:T(8,128)S(1)} %collective-permute-done.3.ends_1), custom_call_target="tpu_custom_call" | custom-call | tf_op jit(solution)/shard_map/prior/pallas_call | solution.py:468
  16.7 3.5 %all-to-all-start = ((bf16[32,5,2,128]{3,2,1,0:T(2,128)(2,1)}), bf16[32,5,2,128]{3,2,1,0:T(2,128)(2,1)S(1)}, u32[]{:S(2)}, u32[]{:S(2)}) async-start(bf16[32,5,2,128]{3,2,1,0:T(2,128)(2,1)} %prior.1), calls=%async_computation | async-start | bytes 163840 | tf_op jit(solution)/shard_map/all_to_all | solution.py:479
  20.2 0.0 copy-done.2
  20.2 1.6 %later_shares.1.later = f32[10,8,128]{2,1,0:T(8,128)S(1)} custom-call(f32[2,8,128]{2,1,0:T(8,128)S(1)} %copy-done.1, f32[40,128]{1,0:T(8,128)S(1)} %get-tuple-element.21.left, f32[40,128]{1,0:T(8,128)S(1)} %get-tuple-element.22.right, f32[152,128]{1,0:T(8,128)S(1)} %collective-permute-done.2.ends_0, f32[152,128]{1,0:T(8,128)S(1)} %collective-permute-done.3.ends_1, ...), custom_call_target="tpu_custom_call" | custom-call | tf_op jit(solution)/shard_map/later_shares/pallas_call | solution.py:468
  21.8 6.0 %all-to-all-done.near_ref = bf16[32,5,2,128]{3,2,1,0:T(2,128)(2,1)S(1)} async-done(((bf16[32,5,2,128]{3,2,1,0:T(2,128)(2,1)}), bf16[32,5,2,128]{3,2,1,0:T(2,128)(2,1)S(1)}, u32[]{:S(2)}, u32[]{:S(2)}) %all-to-all-start) | async-done | bytes 81952 | tf_op jit(solution)/shard_map/all_to_all | solution.py:479
  27.8 4.6 %first_batch.1 = (f32[128,128]{1,0:T(8,128)S(1)}, f32[24,128]{1,0:T(8,128)S(1)}, f32[24,128]{1,0:T(8,128)S(1)}, f32[24,128]{1,0:T(8,128)S(1)}) custom-call(bf16[32,5,2,128]{3,2,1,0:T(2,128)(2,1)S(1)} %all-to-all-done.near_ref, s32[2,1,1,5,8]{4,3,2,1,0:T(8,128)S(1)} %copy.8.pattern, f32[10,8,128]{2,1,0:T(8,128)S(1)} %later_shares.1.later), custom_call_target="tpu_custom_call" | custom-call | tf_op jit(solution)/shard_map/first_batch/pallas_call | solution.py:468
  32.4 0.4 collective-permute-start.4
  32.8 0.2 collective-permute-start.5
  33.0 0.8 %apply_first.1 = (bf16[4096,256]{1,0:T(8,128)(2,1)S(1)}, f32[8,128]{1,0:T(8,128)S(1)}) custom-call(f32[128,128]{1,0:T(8,128)S(1)} %get-tuple-element.28.map_ref, f32[36,144,128]{2,1,0:T(8,128)S(1)} %pad.1), custom_call_target="tpu_custom_call" | custom-call | tf_op jit(solution)/shard_map/apply_first/pallas_call | solution.py:468
  33.8 2.7 %collective-permute-done.4.sides_0 = f32[24,128]{1,0:T(8,128)S(1)} collective-permute-done((f32[24,128]{1,0:T(8,128)S(1)}, f32[24,128]{1,0:T(8,128)S(1)}, u32[]{:S(2)}, u32[]{:S(2)}) %collective-permute-start.4) | collective-permute-done | bytes 12320 | tf_op jit(solution)/shard_map/ppermute | solution.py:31
  36.5 0.0 collective-permute-done.5.sides_1
  36.5 11.2 %all_to_all.10.mine = f32[16,24,128]{2,1,0:T(8,128)S(1)} all-to-all(f32[16,24,128]{2,1,0:T(8,128)S(1)} %meet.1), channel_id=1, replica_groups=mesh['lat'=4,'far'=4,'core'=2] {'lat','far'}, dimensions={0} | all-to-all | bytes 393216 | tf_op jit(solution)/shard_map/all_to_all | solution.py:553
  47.7 0.0 collective-permute-start.6
  47.7 0.4 half_product.1.half
  48.1 1.1 %collective-permute-done.6.other = f32[16,24,128]{2,1,0:T(8,128)S(1)} collective-permute-done((f32[16,24,128]{2,1,0:T(8,128)S(1)}, f32[16,24,128]{2,1,0:T(8,128)S(1)}, u32[]{:S(2)}, u32[]{:S(2)}) %collective-permute-start.6) | collective-permute-done | bytes 196640 | tf_op jit(solution)/shard_map/ppermute | solution.py:554
  49.2 6.0 %second_batch.1 = f32[4096,128]{1,0:T(8,128)} custom-call(f32[136,128]{1,0:T(8,128)S(1)} %half_product.1.half, f32[16,24,128]{2,1,0:T(8,128)S(1)} %collective-permute-done.6.other, s32[2,1,1,5,8]{4,3,2,1,0:T(8,128)S(1)} %copy.8.pattern, bf16[4096,256]{1,0:T(8,128)(2,1)S(1)} %get-tuple-element.30.cells), custom_call_target="tpu_custom_call" | custom-call | tf_op jit(solution)/shard_map/second_batch/pallas_call | solution.py:468
  (2 shorter events, 0.0 us)
Async XLA Ops:
  1.5 5.2 %collective-permute-start = (f32[40,128]{1,0:T(8,128)}, f32[40,128]{1,0:T(8,128)S(1)}, u32[]{:S(2)}, u32[]{:S(2)}) collective-permute-start(f32[40,128]{1,0:T(8,128)} %get-tuple-element.19), channel_id=1, source_target_pairs={{0,7},{1,2},{2,1},{3,4},{4,3},{5,6},{6,5},{7,0},{8,15},{9,10},{10,... | collective-permute-start | bytes 61448 | tf_op jit(solution)/shard_map/ppermute | solution.py:31
  4.9 1.8 %collective-permute-start.1 = (f32[40,128]{1,0:T(8,128)}, f32[40,128]{1,0:T(8,128)S(1)}, u32[]{:S(2)}, u32[]{:S(2)}) collective-permute-start(f32[40,128]{1,0:T(8,128)} %get-tuple-element.20), channel_id=1, source_target_pairs={{0,1},{1,0},{2,3},{3,2},{4,5},{5,4},{6,7},{7,6},{8,9},{9,8},{10,11... | collective-permute-start | bytes 61448 | tf_op jit(solution)/shard_map/ppermute | solution.py:31
  4.9 1.6 %copy-start = (f32[32,128,128]{2,1,0:T(8,128)S(1)}, f32[32,128,128]{2,1,0:T(8,128)}, u32[]{:S(2)}) copy-start(f32[32,128,128]{2,1,0:T(8,128)} %cells.3) | copy-start | bytes 6291460
  6.5 0.7 %copy-start.1 = (f32[2,8,128]{2,1,0:T(8,128)S(1)}, f32[2,8,128]{2,1,0:T(8,128)}, u32[]{:S(2)}) copy-start(f32[2,8,128]{2,1,0:T(8,128)} %get-tuple-element.18.mine) | copy-start | bytes 24580
  7.3 12.9 %copy-start.2 = (s32[2,1,1,5,8]{4,2,3,1,0:T(1,128)S(1)}, s32[2,1,1,5,8]{4,2,3,1,0:T(1,128)}, u32[]{:S(2)}) copy-start(s32[2,1,1,5,8]{4,2,3,1,0:T(1,128)} %param.13) | copy-start | bytes 964
  7.3 6.2 %collective-permute-start.2 = (f32[152,128]{1,0:T(8,128)S(1)}, f32[152,128]{1,0:T(8,128)S(1)}, u32[]{:S(2)}, u32[]{:S(2)}) collective-permute-start(f32[152,128]{1,0:T(8,128)S(1)} %get-tuple-element.23), channel_id=1, source_target_pairs={{8,16},{16,8},{9,17},{17,9},{10,18},{18,10},{11,19},{19,11},{12,20... | collective-permute-start | bytes 233480 | tf_op jit(solution)/shard_map/ppermute | solution.py:31
  8.1 7.2 %collective-permute-start.3 = (f32[152,128]{1,0:T(8,128)S(1)}, f32[152,128]{1,0:T(8,128)S(1)}, u32[]{:S(2)}, u32[]{:S(2)}) collective-permute-start(f32[152,128]{1,0:T(8,128)S(1)} %get-tuple-element.24), channel_id=1, source_target_pairs={{0,8},{8,0},{16,24},{24,16},{1,9},{9,1},{17,25},{25,17},{2,10},{10... | collective-permute-start | bytes 233480 | tf_op jit(solution)/shard_map/ppermute | solution.py:31
  16.7 11.1 %all-to-all-start = ((bf16[32,5,2,128]{3,2,1,0:T(2,128)(2,1)}), bf16[32,5,2,128]{3,2,1,0:T(2,128)(2,1)S(1)}, u32[]{:S(2)}, u32[]{:S(2)}) async-start(bf16[32,5,2,128]{3,2,1,0:T(2,128)(2,1)} %prior.1), calls=%async_computation | async-start | bytes 163840 | tf_op jit(solution)/shard_map/all_to_all | solution.py:479
  32.4 4.1 %collective-permute-start.4 = (f32[24,128]{1,0:T(8,128)S(1)}, f32[24,128]{1,0:T(8,128)S(1)}, u32[]{:S(2)}, u32[]{:S(2)}) collective-permute-start(f32[24,128]{1,0:T(8,128)S(1)} %get-tuple-element.26), channel_id=1, source_target_pairs={{0,7},{1,2},{2,1},{3,4},{4,3},{5,6},{6,5},{7,0},{8,15},{9,10},{10,... | collective-permute-start | bytes 36872 | tf_op jit(solution)/shard_map/ppermute | solution.py:31
  32.8 3.7 %collective-permute-start.5 = (f32[24,128]{1,0:T(8,128)S(1)}, f32[24,128]{1,0:T(8,128)S(1)}, u32[]{:S(2)}, u32[]{:S(2)}) collective-permute-start(f32[24,128]{1,0:T(8,128)S(1)} %get-tuple-element.27), channel_id=1, source_target_pairs={{0,1},{1,0},{2,3},{3,2},{4,5},{5,4},{6,7},{7,6},{8,9},{9,8},{10,11... | collective-permute-start | bytes 36872 | tf_op jit(solution)/shard_map/ppermute | solution.py:31
  47.7 1.4 %collective-permute-start.6 = (f32[16,24,128]{2,1,0:T(8,128)S(1)}, f32[16,24,128]{2,1,0:T(8,128)S(1)}, u32[]{:S(2)}, u32[]{:S(2)}) collective-permute-start(f32[16,24,128]{2,1,0:T(8,128)S(1)} %all_to_all.10.mine), channel_id=1, source_target_pairs={{0,1},{1,0},{2,3},{3,2},{4,5},{5,4},{6,7},{7,6},{8,9},{9,8},{10,11... | collective-permute-start | bytes 589832 | tf_op jit(solution)/shard_map/ppermute | solution.py:554

commit v16 on v15

--- a/solution.py
+++ b/solution.py
@@ -430,12 +430,13 @@
 
 def last_kernel(lat_count, half, other, pattern, cells, out_ref, result, held_rows, out_sem):
     parts = out_sem.shape[0]
-    size = result.shape[0] // parts
+    unit = result.shape[0] // 2 ** parts
     product = marked_product(1, lat_count, summed_blocks(lat_count, other), pattern, 1 - lax.axis_index("core"))
     flipped = solved_map(product + half[...], held_rows)
     copies = []
     for n in range(parts):
-        part = pl.ds(n * size, size)
+        size = unit * 2 ** max(n - 1, 0) * 2
+        part = pl.ds(size if n else 0, size)
         result[part, :] = mapped(cells[part, :], flipped)
         copies.append(pltpu.make_async_copy(result.at[part], out_ref.at[part], out_sem.at[n]))
         copies[-1].start()
@@ -561,7 +562,7 @@
         shares,
         pattern,
     )
-    parts = 8
+    parts = 5
     result = call(
         functools.partial(last_kernel, lat_count),
         "second_batch",

time: 55.6 us -> 55.6 us (level)
  no operation moved by 1% of the time
where the time goes in v16:
time: 55.6 us; the launch traced here: 55.3 us
  Pallas kernels  17.4 us (31%)
  starting transfers between devices  13 us (23%)
  waiting for transfers between devices  11.6 us (21%)
  blocking collectives  11.2 us (20%)
  local copies, waits for them, and re-layouts  2.06 us (4%)
    pallas_call x11, Pallas kernels, call(): pl.pallas_call(kernel, out_shape=out_shape, in_specs=specs, out_specs=out...  17.4 us
    all_to_all x1, blocking collectives, local(): lax.all_to_all(shares, ('lat', 'far'), split_axis=0, concat_axis=0, tiled...  11.2 us
    ppermute x6, starting transfers between devices, trade(): results.append(lax.ppermute(block, axis, route))  9.49 us
    all_to_all x1, waiting for transfers between devices, exchange(): lax.all_to_all(blocks, ('lat',) + LON, split_axis=0, concat_axis=0, tiled...  6 us
    ppermute x6, waiting for transfers between devices, trade(): results.append(lax.ppermute(block, axis, route))  4.52 us
    all_to_all x1, starting transfers between devices, exchange(): lax.all_to_all(blocks, ('lat',) + LON, split_axis=0, concat_axis=0, tiled...  3.47 us
    unnamed x7, local copies, waits for them, and re-layouts  2.06 us
  transfers between devices with their start and end apart: 8, of which 4 were waited for; matrix products, arithmetic and copies ran while one was open for 0% of the time, Pallas kernels for 7%

profile of v16, /device:TPU:0, one launch (start us, length us, event | category | flops | bytes accessed | tf_op | source)
XLA Modules:
  0.0 55.3 jit_solution(6687228250679785370)
XLA Ops:
  0.0 1.5 %start.1 = (f32[2,8,128]{2,1,0:T(8,128)}, f32[40,128]{1,0:T(8,128)}, f32[40,128]{1,0:T(8,128)}) custom-call(f32[2,1,1,8]{3,2,1,0:T(1,128)} %observed.1, f32[2,1,1,8]{3,2,1,0:T(1,128)} %precision.1, f32[2,1,1,4,8]{4,3,2,1,0:T(4,128)} %weight.1, s32[2,1,1,4,8]{4,3,2,1,0:T(4,128)} %stencil.1, s32[2,1,1,8]{3,2,1,0:T(1,128)} %owned.1, f32[32,128,128]{2,1,0:T(8,128)} %cells.3), custom_call_target="tpu_custom_call" | custom-call | tf_op jit(solution)/shard_map/start/pallas_call | solution.py:469
  1.5 3.4 %collective-permute-start = (f32[40,128]{1,0:T(8,128)}, f32[40,128]{1,0:T(8,128)S(1)}, u32[]{:S(2)}, u32[]{:S(2)}) collective-permute-start(f32[40,128]{1,0:T(8,128)} %get-tuple-element.19), channel_id=1, source_target_pairs={{0,7},{1,2},{2,1},{3,4},{4,3},{5,6},{6,5},{7,0},{8,15},{9,10},{10,... | collective-permute-start | bytes 61448 | tf_op jit(solution)/shard_map/ppermute | solution.py:31
  4.9 0.0 collective-permute-start.1
  4.9 0.0 copy-start
  4.9 1.6 %copy-done = f32[32,128,128]{2,1,0:T(8,128)S(1)} copy-done((f32[32,128,128]{2,1,0:T(8,128)S(1)}, f32[32,128,128]{2,1,0:T(8,128)}, u32[]{:S(2)}) %copy-start) | copy-done | bytes 2097176
  6.5 0.0 copy-start.1
  6.5 0.2 pad.1
  6.7 0.0 collective-permute-done.sides_0
  6.7 0.0 collective-permute-done.1.sides_1
  6.8 0.5 copy-done.1
  7.2 0.1 edge_rows.1
  7.3 0.0 copy-start.2
  7.3 0.8 %collective-permute-start.2 = (f32[152,128]{1,0:T(8,128)S(1)}, f32[152,128]{1,0:T(8,128)S(1)}, u32[]{:S(2)}, u32[]{:S(2)}) collective-permute-start(f32[152,128]{1,0:T(8,128)S(1)} %get-tuple-element.23), channel_id=1, source_target_pairs={{8,16},{16,8},{9,17},{17,9},{10,18},{18,10},{11,19},{19,11},{12,20... | collective-permute-start | bytes 233480 | tf_op jit(solution)/shard_map/ppermute | solution.py:31
  8.1 4.7 %collective-permute-start.3 = (f32[152,128]{1,0:T(8,128)S(1)}, f32[152,128]{1,0:T(8,128)S(1)}, u32[]{:S(2)}, u32[]{:S(2)}) collective-permute-start(f32[152,128]{1,0:T(8,128)S(1)} %get-tuple-element.24), channel_id=1, source_target_pairs={{0,8},{8,0},{16,24},{24,16},{1,9},{9,1},{17,25},{25,17},{2,10},{10... | collective-permute-start | bytes 233480 | tf_op jit(solution)/shard_map/ppermute | solution.py:31
  12.8 0.7 %row_shares.1.own = f32[8,128]{1,0:T(8,128)S(1)} custom-call(f32[2,8,128]{2,1,0:T(8,128)S(1)} %copy-done.1, f32[40,128]{1,0:T(8,128)S(1)} %get-tuple-element.21.left, f32[40,128]{1,0:T(8,128)S(1)} %get-tuple-element.22.right, f32[36,144,128]{2,1,0:T(8,128)S(1)} %pad.1), custom_call_target="tpu_custom_call" | custom-call | tf_op jit(solution)/shard_map/row_shares/pallas_call | solution.py:469
  13.5 0.0 collective-permute-done.2.ends_0
  13.5 1.8 %collective-permute-done.3.ends_1 = f32[152,128]{1,0:T(8,128)S(1)} collective-permute-done((f32[152,128]{1,0:T(8,128)S(1)}, f32[152,128]{1,0:T(8,128)S(1)}, u32[]{:S(2)}, u32[]{:S(2)}) %collective-permute-start.3) | collective-permute-done | bytes 77856 | tf_op jit(solution)/shard_map/ppermute | solution.py:31
  15.3 1.4 %prior.1 = bf16[32,5,2,128]{3,2,1,0:T(2,128)(2,1)} custom-call(f32[2,8,128]{2,1,0:T(8,128)S(1)} %copy-done.1, f32[8,128]{1,0:T(8,128)S(1)} %row_shares.1.own, f32[152,128]{1,0:T(8,128)S(1)} %collective-permute-done.2.ends_0, f32[152,128]{1,0:T(8,128)S(1)} %collective-permute-done.3.ends_1), custom_call_target="tpu_custom_call" | custom-call | tf_op jit(solution)/shard_map/prior/pallas_call | solution.py:469
  16.7 3.5 %all-to-all-start = ((bf16[32,5,2,128]{3,2,1,0:T(2,128)(2,1)}), bf16[32,5,2,128]{3,2,1,0:T(2,128)(2,1)S(1)}, u32[]{:S(2)}, u32[]{:S(2)}) async-start(bf16[32,5,2,128]{3,2,1,0:T(2,128)(2,1)} %prior.1), calls=%async_computation | async-start | bytes 163840 | tf_op jit(solution)/shard_map/all_to_all | solution.py:480
  20.2 0.0 copy-done.2
  20.2 1.6 %later_shares.1.later = f32[10,8,128]{2,1,0:T(8,128)S(1)} custom-call(f32[2,8,128]{2,1,0:T(8,128)S(1)} %copy-done.1, f32[40,128]{1,0:T(8,128)S(1)} %get-tuple-element.21.left, f32[40,128]{1,0:T(8,128)S(1)} %get-tuple-element.22.right, f32[152,128]{1,0:T(8,128)S(1)} %collective-permute-done.2.ends_0, f32[152,128]{1,0:T(8,128)S(1)} %collective-permute-done.3.ends_1, ...), custom_call_target="tpu_custom_call" | custom-call | tf_op jit(solution)/shard_map/later_shares/pallas_call | solution.py:469
  21.8 6.0 %all-to-all-done.near_ref = bf16[32,5,2,128]{3,2,1,0:T(2,128)(2,1)S(1)} async-done(((bf16[32,5,2,128]{3,2,1,0:T(2,128)(2,1)}), bf16[32,5,2,128]{3,2,1,0:T(2,128)(2,1)S(1)}, u32[]{:S(2)}, u32[]{:S(2)}) %all-to-all-start) | async-done | bytes 81952 | tf_op jit(solution)/shard_map/all_to_all | solution.py:480
  27.8 4.6 %first_batch.1 = (f32[128,128]{1,0:T(8,128)S(1)}, f32[24,128]{1,0:T(8,128)S(1)}, f32[24,128]{1,0:T(8,128)S(1)}, f32[24,128]{1,0:T(8,128)S(1)}) custom-call(bf16[32,5,2,128]{3,2,1,0:T(2,128)(2,1)S(1)} %all-to-all-done.near_ref, s32[2,1,1,5,8]{4,3,2,1,0:T(8,128)S(1)} %copy.8.pattern, f32[10,8,128]{2,1,0:T(8,128)S(1)} %later_shares.1.later), custom_call_target="tpu_custom_call" | custom-call | tf_op jit(solution)/shard_map/first_batch/pallas_call | solution.py:469
  32.4 0.4 collective-permute-start.4
  32.8 0.2 collective-permute-start.5
  33.0 0.8 %apply_first.1 = (bf16[4096,256]{1,0:T(8,128)(2,1)S(1)}, f32[8,128]{1,0:T(8,128)S(1)}) custom-call(f32[128,128]{1,0:T(8,128)S(1)} %get-tuple-element.28.map_ref, f32[36,144,128]{2,1,0:T(8,128)S(1)} %pad.1), custom_call_target="tpu_custom_call" | custom-call | tf_op jit(solution)/shard_map/apply_first/pallas_call | solution.py:469
  33.8 2.7 %collective-permute-done.4.sides_0 = f32[24,128]{1,0:T(8,128)S(1)} collective-permute-done((f32[24,128]{1,0:T(8,128)S(1)}, f32[24,128]{1,0:T(8,128)S(1)}, u32[]{:S(2)}, u32[]{:S(2)}) %collective-permute-start.4) | collective-permute-done | bytes 12320 | tf_op jit(solution)/shard_map/ppermute | solution.py:31
  36.5 0.0 collective-permute-done.5.sides_1
  36.5 11.2 %all_to_all.10.mine = f32[16,24,128]{2,1,0:T(8,128)S(1)} all-to-all(f32[16,24,128]{2,1,0:T(8,128)S(1)} %meet.1), channel_id=1, replica_groups=mesh['lat'=4,'far'=4,'core'=2] {'lat','far'}, dimensions={0} | all-to-all | bytes 393216 | tf_op jit(solution)/shard_map/all_to_all | solution.py:554
  47.7 0.0 collective-permute-start.6
  47.7 0.4 half_product.1.half
  48.1 1.1 %collective-permute-done.6.other = f32[16,24,128]{2,1,0:T(8,128)S(1)} collective-permute-done((f32[16,24,128]{2,1,0:T(8,128)S(1)}, f32[16,24,128]{2,1,0:T(8,128)S(1)}, u32[]{:S(2)}, u32[]{:S(2)}) %collective-permute-start.6) | collective-permute-done | bytes 196640 | tf_op jit(solution)/shard_map/ppermute | solution.py:555
  49.2 6.1 %second_batch.1 = f32[4096,128]{1,0:T(8,128)} custom-call(f32[136,128]{1,0:T(8,128)S(1)} %half_product.1.half, f32[16,24,128]{2,1,0:T(8,128)S(1)} %collective-permute-done.6.other, s32[2,1,1,5,8]{4,3,2,1,0:T(8,128)S(1)} %copy.8.pattern, bf16[4096,256]{1,0:T(8,128)(2,1)S(1)} %get-tuple-element.30.cells), custom_call_target="tpu_custom_call" | custom-call | tf_op jit(solution)/shard_map/second_batch/pallas_call | solution.py:469
  (2 shorter events, 0.0 us)
Async XLA Ops:
  1.5 5.2 %collective-permute-start = (f32[40,128]{1,0:T(8,128)}, f32[40,128]{1,0:T(8,128)S(1)}, u32[]{:S(2)}, u32[]{:S(2)}) collective-permute-start(f32[40,128]{1,0:T(8,128)} %get-tuple-element.19), channel_id=1, source_target_pairs={{0,7},{1,2},{2,1},{3,4},{4,3},{5,6},{6,5},{7,0},{8,15},{9,10},{10,... | collective-permute-start | bytes 61448 | tf_op jit(solution)/shard_map/ppermute | solution.py:31
  4.9 1.8 %collective-permute-start.1 = (f32[40,128]{1,0:T(8,128)}, f32[40,128]{1,0:T(8,128)S(1)}, u32[]{:S(2)}, u32[]{:S(2)}) collective-permute-start(f32[40,128]{1,0:T(8,128)} %get-tuple-element.20), channel_id=1, source_target_pairs={{0,1},{1,0},{2,3},{3,2},{4,5},{5,4},{6,7},{7,6},{8,9},{9,8},{10,11... | collective-permute-start | bytes 61448 | tf_op jit(solution)/shard_map/ppermute | solution.py:31
  4.9 1.6 %copy-start = (f32[32,128,128]{2,1,0:T(8,128)S(1)}, f32[32,128,128]{2,1,0:T(8,128)}, u32[]{:S(2)}) copy-start(f32[32,128,128]{2,1,0:T(8,128)} %cells.3) | copy-start | bytes 6291460
  6.5 0.7 %copy-start.1 = (f32[2,8,128]{2,1,0:T(8,128)S(1)}, f32[2,8,128]{2,1,0:T(8,128)}, u32[]{:S(2)}) copy-start(f32[2,8,128]{2,1,0:T(8,128)} %get-tuple-element.18.mine) | copy-start | bytes 24580
  7.3 12.9 %copy-start.2 = (s32[2,1,1,5,8]{4,2,3,1,0:T(1,128)S(1)}, s32[2,1,1,5,8]{4,2,3,1,0:T(1,128)}, u32[]{:S(2)}) copy-start(s32[2,1,1,5,8]{4,2,3,1,0:T(1,128)} %param.13) | copy-start | bytes 964
  7.3 6.2 %collective-permute-start.2 = (f32[152,128]{1,0:T(8,128)S(1)}, f32[152,128]{1,0:T(8,128)S(1)}, u32[]{:S(2)}, u32[]{:S(2)}) collective-permute-start(f32[152,128]{1,0:T(8,128)S(1)} %get-tuple-element.23), channel_id=1, source_target_pairs={{8,16},{16,8},{9,17},{17,9},{10,18},{18,10},{11,19},{19,11},{12,20... | collective-permute-start | bytes 233480 | tf_op jit(solution)/shard_map/ppermute | solution.py:31
  8.1 7.2 %collective-permute-start.3 = (f32[152,128]{1,0:T(8,128)S(1)}, f32[152,128]{1,0:T(8,128)S(1)}, u32[]{:S(2)}, u32[]{:S(2)}) collective-permute-start(f32[152,128]{1,0:T(8,128)S(1)} %get-tuple-element.24), channel_id=1, source_target_pairs={{0,8},{8,0},{16,24},{24,16},{1,9},{9,1},{17,25},{25,17},{2,10},{10... | collective-permute-start | bytes 233480 | tf_op jit(solution)/shard_map/ppermute | solution.py:31
  16.7 11.1 %all-to-all-start = ((bf16[32,5,2,128]{3,2,1,0:T(2,128)(2,1)}), bf16[32,5,2,128]{3,2,1,0:T(2,128)(2,1)S(1)}, u32[]{:S(2)}, u32[]{:S(2)}) async-start(bf16[32,5,2,128]{3,2,1,0:T(2,128)(2,1)} %prior.1), calls=%async_computation | async-start | bytes 163840 | tf_op jit(solution)/shard_map/all_to_all | solution.py:480
  32.4 4.1 %collective-permute-start.4 = (f32[24,128]{1,0:T(8,128)S(1)}, f32[24,128]{1,0:T(8,128)S(1)}, u32[]{:S(2)}, u32[]{:S(2)}) collective-permute-start(f32[24,128]{1,0:T(8,128)S(1)} %get-tuple-element.26), channel_id=1, source_target_pairs={{0,7},{1,2},{2,1},{3,4},{4,3},{5,6},{6,5},{7,0},{8,15},{9,10},{10,... | collective-permute-start | bytes 36872 | tf_op jit(solution)/shard_map/ppermute | solution.py:31
  32.8 3.7 %collective-permute-start.5 = (f32[24,128]{1,0:T(8,128)S(1)}, f32[24,128]{1,0:T(8,128)S(1)}, u32[]{:S(2)}, u32[]{:S(2)}) collective-permute-start(f32[24,128]{1,0:T(8,128)S(1)} %get-tuple-element.27), channel_id=1, source_target_pairs={{0,1},{1,0},{2,3},{3,2},{4,5},{5,4},{6,7},{7,6},{8,9},{9,8},{10,11... | collective-permute-start | bytes 36872 | tf_op jit(solution)/shard_map/ppermute | solution.py:31
  47.7 1.4 %collective-permute-start.6 = (f32[16,24,128]{2,1,0:T(8,128)S(1)}, f32[16,24,128]{2,1,0:T(8,128)S(1)}, u32[]{:S(2)}, u32[]{:S(2)}) collective-permute-start(f32[16,24,128]{2,1,0:T(8,128)S(1)} %all_to_all.10.mine), channel_id=1, source_target_pairs={{0,1},{1,0},{2,3},{3,2},{4,5},{5,4},{6,7},{7,6},{8,9},{9,8},{10,11... | collective-permute-start | bytes 589832 | tf_op jit(solution)/shard_map/ppermute | solution.py:555
